TPU v7x, 32 devices: a whole 2x2x4 slice. The times are simulated.
32 devices in a mesh: grid: 2 (over x), gx: 4 (over z), gy: 4 (over y, core).
Axes of the slice: x: 2, y: 2, z: 4, core: 2. Of those that a mesh axis runs over, the one named last changes fastest.
Arguments:
- fields: float32 [2, 9, 24, 96, 384], P('grid', None, 'gx', 'gy'), may hold values from -6 to 6
- material: int32 [2, 24, 96, 384], P('grid', 'gx', 'gy'), may hold values from 0 to 7
- permittivity: float32 [8], replicated, may hold values from 4 to 81
- conductivity: float32 [8], replicated, may hold values from 0.02 to 0.6
- relax_rate: float32 [8], replicated, may hold values from 0.05 to 0.8
- debye_strength: float32 [8], replicated, may hold values from 0.5 to 4
- subgrids: int32 [4, 4, 6], P('gx', 'gy'), may hold values from 0 to 256, as said below
Outputs:
- fields_out: float32 [2, 9, 24, 96, 384], P('grid', None, 'gx', 'gy')
Inputs may be any that keep to these rules, and one draw needn't show every extreme that they name: subgrids[a, b] = (x0, y0, z0, lx, ly, lz): x0 <= 4, y0 <= 16, z0 <= 256; lx is at least 1 and at most 2, ly at least 4 and at most 8, lz at least 64 and at most 128; some block reaches every upper bound.
All inputs are finite; a program needn't handle non-finite values.
Results may differ from a plain program's by a relative error of at most 0.0003.
Values sent between devices are 32-bit elements; how exact they have to be, the bound alone decides.
No kernel may reach another device: no remote copies, remote signals or barrier semaphores. Data moves between devices by JAX's collectives and lax.ppermute only.
A program may use at most 128 MiB of HBM per device.

v0:
```python
import jax
import jax.numpy as jnp
from jax import lax
from jax.sharding import PartitionSpec as P

COARSE_STEPS = 3


courant = 0.5
one_third = 1.0 / 3.0


def shifted(value, axis, by):
    peers = lax.axis_size(axis)
    pairs = [(i, i + by) for i in range(peers) if 0 <= i + by < peers]
    return lax.ppermute(value, axis, pairs)


def lookup(material, entries):
    picked = jnp.zeros(material.shape, entries.dtype)
    for candidate in range(entries.shape[0]):
        picked = jnp.where(material == candidate, entries[candidate], picked)
    return picked


def material_factors(material, permittivity, conductivity, relax_rate, debye_strength, factor):
    permit = lookup(material, permittivity)
    damping = lookup(material, conductivity) * factor / (2.0 * permit)
    relaxing = lookup(material, relax_rate) * factor
    return jnp.stack(
        [
            (1.0 - damping) / (1.0 + damping),
            1.0 / (permit * (1.0 + damping)),
            relaxing,
            jnp.exp(-relaxing),
            lookup(material, debye_strength),
        ]
    )


def diff_ahead(values, direction):
    base_cut = [slice(0, -1)] * 3
    moved_cut = [slice(0, -1)] * 3
    moved_cut[direction] = slice(1, None)
    return values[tuple(moved_cut)] - values[tuple(base_cut)]


def diff_behind(values, direction):
    base_cut = [slice(1, None)] * 3
    moved_cut = [slice(1, None)] * 3
    moved_cut[direction] = slice(0, -1)
    return values[tuple(base_cut)] - values[tuple(moved_cut)]


def curl_ahead(padded):
    return jnp.stack(
        [
            diff_ahead(padded[2], 1) - diff_ahead(padded[1], 2),
            diff_ahead(padded[0], 2) - diff_ahead(padded[2], 0),
            diff_ahead(padded[1], 0) - diff_ahead(padded[0], 1),
        ]
    )


def curl_behind(padded):
    return jnp.stack(
        [
            diff_behind(padded[2], 1) - diff_behind(padded[1], 2),
            diff_behind(padded[0], 2) - diff_behind(padded[2], 0),
            diff_behind(padded[1], 0) - diff_behind(padded[0], 1),
        ]
    )


def electric(efield, polarization, rotation, factors):
    return factors[0] * efield + factors[1] * (
        courant * rotation - factors[2] * (factors[4] * efield - polarization)
    )


def relaxation(polarization, efield, factors):
    return factors[3] * polarization + (1.0 - factors[3]) * factors[4] * efield


def fine_update(fields, factors, inside, border, driven):
    efield, hfield, polarization = (fields[0:3], fields[3:6], fields[6:9])
    hfield = inside * (
        hfield - courant * curl_ahead(jnp.pad(efield, ((0, 0), (0, 1), (0, 1), (0, 1))))
    )
    rotation = curl_behind(jnp.pad(hfield, ((0, 0), (1, 0), (1, 0), (1, 0))))
    efield = jnp.where(border, driven, inside * electric(efield, polarization, rotation, factors))
    polarization = inside * relaxation(polarization, efield, factors)
    return jnp.concatenate([efield, hfield, polarization])


def subgrid_masks(extent, cell_shape):
    along_x = lax.broadcasted_iota(jnp.int32, cell_shape, 0)
    along_y = lax.broadcasted_iota(jnp.int32, cell_shape, 1)
    along_z = lax.broadcasted_iota(jnp.int32, cell_shape, 2)
    xlength = 3 * extent[3]
    ylength = 3 * extent[4]
    zlength = 3 * extent[5]
    covered = (along_x < xlength) & (along_y < ylength) & (along_z < zlength)
    xfaces = (along_x == 0) | (along_x == xlength - 1)
    yfaces = (along_y == 0) | (along_y == ylength - 1)
    zfaces = (along_z == 0) | (along_z == zlength - 1)
    border = jnp.stack(
        [covered & (yfaces | zfaces), covered & (xfaces | zfaces), covered & (xfaces | yfaces)]
    )
    return (covered.astype(jnp.float32), border)


def cut_region(efield, extent):
    region_shape = (3, efield.shape[1] // 3, efield.shape[2] // 3, efield.shape[3] // 3)
    return lax.dynamic_slice(efield, (jnp.int32(0), extent[0], extent[1], extent[2]), region_shape)


def upsample(region):
    sizes = region.shape
    spread = jnp.broadcast_to(
        region[:, :, None, :, None, :, None], (sizes[0], sizes[1], 3, sizes[2], 3, sizes[3], 3)
    )
    return spread.reshape(sizes[0], 3 * sizes[1], 3 * sizes[2], 3 * sizes[3])


def restrict(efield):
    sizes = efield.shape
    grouped = efield.reshape(sizes[0], sizes[1] // 3, 3, sizes[2] // 3, 3, sizes[3] // 3, 3)
    return grouped.mean(axis=(2, 4, 6))


def overwrite(fields, restricted, extent):
    region = cut_region(fields[0:3], extent)
    along_x = lax.broadcasted_iota(jnp.int32, region.shape, 1)
    along_y = lax.broadcasted_iota(jnp.int32, region.shape, 2)
    along_z = lax.broadcasted_iota(jnp.int32, region.shape, 3)
    covered = (along_x < extent[3]) & (along_y < extent[4]) & (along_z < extent[5])
    updated = jnp.where(covered, restricted, region)
    return lax.dynamic_update_slice(
        fields, updated, (jnp.int32(0), extent[0], extent[1], extent[2])
    )


def ahead_extend(values, next_x, next_y):
    upper_rows = jnp.concatenate([values, next_x], axis=1)
    corner = jnp.zeros((values.shape[0], 1, 1, values.shape[3]), values.dtype)
    side_rows = jnp.concatenate([next_y, corner], axis=1)
    return jnp.pad(
        jnp.concatenate([upper_rows, side_rows], axis=2), ((0, 0), (0, 0), (0, 0), (0, 1))
    )


def behind_extend(values, prev_x, prev_y):
    upper_rows = jnp.concatenate([prev_x, values], axis=1)
    corner = jnp.zeros((values.shape[0], 1, 1, values.shape[3]), values.dtype)
    side_rows = jnp.concatenate([corner, prev_y], axis=1)
    return jnp.pad(
        jnp.concatenate([side_rows, upper_rows], axis=2), ((0, 0), (0, 0), (0, 0), (1, 0))
    )


def coarse_step(local, factors, coarse):
    efield, hfield, polarization = (local[0:3], local[3:6], local[6:9])
    ahead_x = shifted(efield[:, 0:1], "gx", -1)
    ahead_y = shifted(efield[:, :, 0:1], "gy", -1)
    hfield = lax.cond(
        coarse,
        lambda: hfield - courant * curl_ahead(ahead_extend(efield, ahead_x, ahead_y)),
        lambda: hfield,
    )
    behind_x = shifted(hfield[:, -1:], "gx", 1)
    behind_y = shifted(hfield[:, :, -1:], "gy", 1)
    rotation = lax.cond(
        coarse,
        lambda: curl_behind(behind_extend(hfield, behind_x, behind_y)),
        lambda: jnp.zeros_like(hfield),
    )

    def advance():
        updated = electric(efield, polarization, rotation, factors)
        return (updated, relaxation(polarization, updated, factors))

    efield, polarization = lax.cond(coarse, advance, lambda: (efield, polarization))
    return jnp.concatenate([efield, hfield, polarization])


def body(fields, material, permittivity, conductivity, relax_rate, debye_strength, subgrids):
    coarse = lax.axis_index("grid") == 0
    local = fields[0]
    factor = jnp.where(coarse, 1.0, one_third).astype(local.dtype)
    factors = material_factors(
        material[0], permittivity, conductivity, relax_rate, debye_strength, factor
    )
    extent = subgrids[0, 0]
    inside, border = subgrid_masks(extent, local.shape[1:])
    local = lax.cond(coarse, lambda: local, lambda: local * inside)
    for number in range(COARSE_STEPS):
        earlier = cut_region(local[0:3], extent)
        local = coarse_step(local, factors, coarse)
        latest = cut_region(local[0:3], extent)
        incoming = shifted(jnp.stack([earlier, latest]), "grid", 1)
        for substep in range(1, 4):
            weight = substep / 3.0
            local = lax.cond(
                coarse,
                lambda: local,
                lambda: fine_update(
                    local,
                    factors,
                    inside,
                    border,
                    upsample(incoming[0] + weight * (incoming[1] - incoming[0])),
                ),
            )
        restricted = lax.cond(coarse, lambda: jnp.zeros_like(earlier), lambda: restrict(local[0:3]))
        received = shifted(restricted, "grid", -1)
        local = lax.cond(coarse, lambda: overwrite(local, received, extent), lambda: local)
    return local[None]


def solution(mesh):
    in_specs = (
        P("grid", None, "gx", "gy", None),
        P("grid", "gx", "gy", None),
        P(),
        P(),
        P(),
        P(),
        P("gx", "gy", None),
    )
    out_specs = P("grid", None, "gx", "gy", None)
    return jax.shard_map(body, mesh=mesh, in_specs=in_specs, out_specs=out_specs, check_vma=False)
```

profile of v0, /device:TPU:16, one launch (start us, length us, event | category | flops | bytes accessed | tf_op | source)
XLA Modules:
  0.0 645.2 jit_solution(64120027623318477)
XLA Ops:
  3.6 1.6 conditional.25
  5.8 2.3 collective-permute-start
  10.3 2.5 fusion.309
  14.8 5.4 exponential_bitcast_fusion
  20.2 10.2 %subtract_divide_fusion = f32[1,6,24,384]{3,2,1,0:T(8,128)S(1)} fusion(pred[1,6,24,384]{3,2,1,0:T(8,128)(4,1)S(1)} %get-tuple-element.651, pred[1,6,24,384]{3,2,1,0:T(8,128)(4,1)S(1)} %get-tuple-element.650, pred[1,6,24,384]{3,2,1,0:T(8,128)(4,1)S(1)} %get-tuple-element.649, pred[1,6,24,384]{3,2,1,0:T(8,128)(4,1)S(1)} %get-tuple-element.648, ...), kind=kLoop, calls=%fused_computation.615 | loop fusion | flops 1216512 | bytes 663620 | tf_op jit(solution)/shard_map/div | solution.py:32
  30.4 10.2 %multiply_divide_fusion = f32[1,6,24,384]{3,2,1,0:T(8,128)S(1)} fusion(pred[1,6,24,384]{3,2,1,0:T(8,128)(4,1)S(1)} %get-tuple-element.651, pred[1,6,24,384]{3,2,1,0:T(8,128)(4,1)S(1)} %get-tuple-element.650, pred[1,6,24,384]{3,2,1,0:T(8,128)(4,1)S(1)} %get-tuple-element.649, pred[1,6,24,384]{3,2,1,0:T(8,128)(4,1)S(1)} %get-tuple-element.648, ...), kind=kLoop, calls=%fused_computation.614 | loop fusion | flops 1216512 | bytes 663620 | tf_op jit(solution)/shard_map/div | solution.py:33
  41.4 5.3 select_select_fusion
  52.9 3.4 conditional.26
  54.3 2.0 fusion
  58.1 3.0 collective-permute-start.2
  61.2 4.1 collective-permute-start.3
  66.0 2.8 collective-permute-done.3
  68.8 2.2 conditional.27
  72.6 1.9 collective-permute-start.4
  74.5 1.6 pad_maximum_fusion.12
  76.5 8.7 %conditional.32 = (f32[3,2,8,128]{3,2,1,0:T(8,128)}) conditional(s32[]{:T(128)} %convert_element_type.32, f32[9,6,24,384]{3,2,1,0:T(8,128)S(1)} %get-tuple-element.895, () %tuple.169), branch_computations={%region_14.16_spmd, %region_16.17_spmd} | conditional | flops 165888 | bytes 3391500 | solution.py:215
  86.5 148.5 %collective-permute-done.5 = f32[3,2,8,128]{3,2,1,0:T(8,128)} collective-permute-done((f32[3,2,8,128]{3,2,1,0:T(8,128)}, f32[3,2,8,128]{3,2,1,0:T(8,128)}, u32[]{:S(2)}, u32[]{:S(2)}) %collective-permute-start.5) | collective-permute-done | bytes 24608 | tf_op jit(solution)/shard_map/ppermute | solution.py:16
  235.0 13.3 %conditional.33 = (f32[9,6,24,384]{3,2,1,0:T(8,128)S(1)}) conditional(s32[]{:T(128)} %convert_element_type.32, f32[9,6,24,384]{3,2,1,0:T(8,128)S(1)} %get-tuple-element.895, (s32[6]{0:T(128)S(1)}, f32[9,6,24,384]{3,2,1,0:T(8,128)S(1)}, f32[3,2,8,128]{3,2,1,0:T(8,128)}) %tuple.455), branch_computations={%region_17.18_spmd, %region_18.19_spmd} | conditional | flops 18579 | bytes 1450446 | solution.py:217
  243.7 1.6 dynamic-slice_select_fusion
  245.3 3.0 dynamic_update_slice.7
  248.4 1.9 collective-permute-start.6
  253.4 1.6 collective-permute-done.6
  255.0 3.2 conditional.34
  260.1 2.3 collective-permute-start.8
  262.4 3.5 collective-permute-start.9
  265.9 1.6 dynamic-slice_bitcast_fusion.3
  267.5 2.6 collective-permute-done.9
  270.8 2.3 conditional.35
  274.7 1.9 collective-permute-start.10
  276.6 1.6 pad_maximum_fusion.13
  278.5 8.5 %conditional.40 = (f32[3,2,8,128]{3,2,1,0:T(8,128)}) conditional(s32[]{:T(128)} %convert_element_type.32, f32[9,6,24,384]{3,2,1,0:T(8,128)S(1)} %get-tuple-element.903, () %tuple.179), branch_computations={%region_31.33_spmd, %region_33.34_spmd} | conditional | flops 165888 | bytes 3391500 | solution.py:215
  288.3 148.1 %collective-permute-done.11 = f32[3,2,8,128]{3,2,1,0:T(8,128)} collective-permute-done((f32[3,2,8,128]{3,2,1,0:T(8,128)}, f32[3,2,8,128]{3,2,1,0:T(8,128)}, u32[]{:S(2)}, u32[]{:S(2)}) %collective-permute-start.11) | collective-permute-done | bytes 24608 | tf_op jit(solution)/shard_map/ppermute | solution.py:16
  436.5 13.3 %conditional.41 = (f32[9,6,24,384]{3,2,1,0:T(8,128)S(1)}) conditional(s32[]{:T(128)} %convert_element_type.32, f32[9,6,24,384]{3,2,1,0:T(8,128)S(1)} %get-tuple-element.903, (s32[6]{0:T(128)S(1)}, f32[9,6,24,384]{3,2,1,0:T(8,128)S(1)}, f32[3,2,8,128]{3,2,1,0:T(8,128)}) %tuple.456), branch_computations={%region_34.35_spmd, %region_35.36_spmd} | conditional | flops 18579 | bytes 1450446 | solution.py:217
  445.2 1.6 dynamic-slice_select_fusion.1
  446.8 3.0 dynamic_update_slice.8
  449.8 1.9 collective-permute-start.12
  454.8 1.6 collective-permute-done.12
  456.5 3.2 conditional.42
  462.9 3.6 collective-permute-start.15
  466.5 1.6 dynamic-slice_bitcast_fusion.1
  468.1 2.1 collective-permute-done.15
  470.8 2.3 conditional.43
  474.8 1.9 collective-permute-start.16
  476.7 1.6 pad_maximum_fusion.14
  478.6 2.8 conditional.48
  482.7 150.3 %collective-permute-done.17 = f32[3,2,8,128]{3,2,1,0:T(8,128)S(1)} collective-permute-done((f32[3,2,8,128]{3,2,1,0:T(8,128)S(1)}, f32[3,2,8,128]{3,2,1,0:T(8,128)S(1)}, u32[]{:S(2)}, u32[]{:S(2)}) %collective-permute-start.17) | collective-permute-done | bytes 24608 | tf_op jit(solution)/shard_map/ppermute | solution.py:16
  633.1 10.4 %conditional.49 = (f32[1,9,6,24,384]{4,3,2,1,0:T(8,128)S(1)}) conditional(s32[]{:T(128)} %convert_element_type.32, f32[9,6,24,384]{3,2,1,0:T(8,128)S(1)} %get-tuple-element.911, (f32[9,6,24,384]{3,2,1,0:T(8,128)S(1)}, s32[6]{0:T(128)S(1)}, f32[3,2,8,128]{3,2,1,0:T(8,128)S(1)}) %tuple.457), branch_computations={%region_51.52_spmd, %region_52.53_spmd} | conditional | flops 18579 | bytes 1450446 | solution.py:217
  641.2 2.2 dynamic_update_slice.9
  (162 shorter events, 62.8 us)
Async XLA Ops:
  5.2 3.7 copy-start.32
  5.8 47.0 %collective-permute-start = (f32[3,1,24,384]{3,2,1,0:T(8,128)}, f32[3,1,24,384]{3,2,1,0:T(8,128)}, u32[]{:S(2)}, u32[]{:S(2)}) collective-permute-start(f32[3,1,24,384]{3,2,1,0:T(8,128)} %slice.1700), channel_id=1, source_target_pairs={{4,0},{8,4},{12,8},{5,1},{9,5},{13,9},{6,2},{10,6},{14,10},{7,3},{... | collective-permute-start | bytes 331784 | tf_op jit(solution)/shard_map/ppermute | solution.py:16
  8.8 3.9 copy-start.55
  8.8 4.6 copy-start.56
  8.8 5.2 copy-start.57
  8.8 5.9 copy-start.52
  8.8 44.0 %collective-permute-start.1 = (f32[3,6,1,384]{3,2,1,0:T(1,128)}, f32[3,6,1,384]{3,2,1,0:T(1,128)}, u32[]{:S(2)}, u32[]{:S(2)}) collective-permute-start(f32[3,6,1,384]{3,2,1,0:T(1,128)} %slice.1701), channel_id=1, source_target_pairs={{1,0},{2,1},{3,2},{5,4},{6,5},{7,6},{9,8},{10,9},{11,10},{13,12},{... | collective-permute-start | bytes 82952 | tf_op jit(solution)/shard_map/ppermute | solution.py:16
  12.7 27.8 %copy-start.58 = (f32[8]{0:T(128)S(1)}, f32[8]{0:T(128)}, u32[]{:S(2)}) copy-start(f32[8]{0:T(128)} %param.62) | copy-start | bytes 100
  58.1 7.8 %collective-permute-start.2 = (f32[3,6,1,384]{3,2,1,0:T(1,128)S(1)}, f32[3,6,1,384]{3,2,1,0:T(1,128)S(1)}, u32[]{:S(2)}, u32[]{:S(2)}) collective-permute-start(f32[3,6,1,384]{3,2,1,0:T(1,128)S(1)} %slice.1702), channel_id=1, source_target_pairs={{0,1},{1,2},{2,3},{4,5},{5,6},{6,7},{8,9},{9,10},{10,11},{12,13},{... | collective-permute-start | bytes 82952 | tf_op jit(solution)/shard_map/ppermute | solution.py:16
  61.2 7.7 %collective-permute-start.3 = (f32[3,1,24,384]{3,2,1,0:T(8,128)S(1)}, f32[3,1,24,384]{3,2,1,0:T(8,128)S(1)}, u32[]{:S(2)}, u32[]{:S(2)}) collective-permute-start(f32[3,1,24,384]{3,2,1,0:T(8,128)S(1)} %slice.1703), channel_id=1, source_target_pairs={{0,4},{4,8},{8,12},{1,5},{5,9},{9,13},{2,6},{6,10},{10,14},{3,7},{... | collective-permute-start | bytes 331784 | tf_op jit(solution)/shard_map/ppermute | solution.py:16
  71.7 2.8 copy-start.1
  71.8 2.8 copy-start.24
  72.6 3.5 collective-permute-start.4
  76.5 158.5 %copy-start.51 = (s32[1,1,6]{2,1,0:T(1,128)S(1)}, s32[1,1,6]{2,1,0:T(1,128)}, u32[]{:S(2)}) copy-start(s32[1,1,6]{2,1,0:T(1,128)} %param.63) | copy-start | bytes 76
  85.2 149.8 %collective-permute-start.5 = (f32[3,2,8,128]{3,2,1,0:T(8,128)}, f32[3,2,8,128]{3,2,1,0:T(8,128)}, u32[]{:S(2)}, u32[]{:S(2)}) collective-permute-start(f32[3,2,8,128]{3,2,1,0:T(8,128)} %get-tuple-element.896), channel_id=1, source_target_pairs={{16,0},{17,1},{18,2},{19,3},{20,4},{21,5},{22,6},{23,7},{24,8},{25... | collective-permute-start | bytes 73736 | tf_op jit(solution)/shard_map/ppermute | solution.py:16
  248.4 6.6 %collective-permute-start.6 = (f32[3,1,24,384]{3,2,1,0:T(8,128)S(1)}, f32[3,1,24,384]{3,2,1,0:T(8,128)S(1)}, u32[]{:S(2)}, u32[]{:S(2)}) collective-permute-start(f32[3,1,24,384]{3,2,1,0:T(8,128)S(1)} %slice.1707), channel_id=1, source_target_pairs={{4,0},{8,4},{12,8},{5,1},{9,5},{13,9},{6,2},{10,6},{14,10},{7,3},{... | collective-permute-start | bytes 331784 | tf_op jit(solution)/shard_map/ppermute | solution.py:16
  250.3 3.1 collective-permute-start.7
  256.2 1.1 copy-start.9
  257.4 0.8 copy-start.10
  260.1 7.4 %collective-permute-start.8 = (f32[3,6,1,384]{3,2,1,0:T(1,128)S(1)}, f32[3,6,1,384]{3,2,1,0:T(1,128)S(1)}, u32[]{:S(2)}, u32[]{:S(2)}) collective-permute-start(f32[3,6,1,384]{3,2,1,0:T(1,128)S(1)} %slice.1709), channel_id=1, source_target_pairs={{0,1},{1,2},{2,3},{4,5},{5,6},{6,7},{8,9},{9,10},{10,11},{12,13},{... | collective-permute-start | bytes 82952 | tf_op jit(solution)/shard_map/ppermute | solution.py:16
  262.4 7.7 %collective-permute-start.9 = (f32[3,1,24,384]{3,2,1,0:T(8,128)S(1)}, f32[3,1,24,384]{3,2,1,0:T(8,128)S(1)}, u32[]{:S(2)}, u32[]{:S(2)}) collective-permute-start(f32[3,1,24,384]{3,2,1,0:T(8,128)S(1)} %slice.1710), channel_id=1, source_target_pairs={{0,4},{4,8},{8,12},{1,5},{5,9},{9,13},{2,6},{6,10},{10,14},{3,7},{... | collective-permute-start | bytes 331784 | tf_op jit(solution)/shard_map/ppermute | solution.py:16
  267.5 2.6 copy-start.59
  270.1 0.6 copy-start.53
  270.8 2.3 copy-start.3
  270.8 2.3 copy-start.26
  273.8 2.8 copy-start.4
  273.8 2.8 copy-start.27
  274.7 3.5 collective-permute-start.10
  287.0 149.4 %collective-permute-start.11 = (f32[3,2,8,128]{3,2,1,0:T(8,128)}, f32[3,2,8,128]{3,2,1,0:T(8,128)}, u32[]{:S(2)}, u32[]{:S(2)}) collective-permute-start(f32[3,2,8,128]{3,2,1,0:T(8,128)} %get-tuple-element.904), channel_id=1, source_target_pairs={{16,0},{17,1},{18,2},{19,3},{20,4},{21,5},{22,6},{23,7},{24,8},{25... | collective-permute-start | bytes 73736 | tf_op jit(solution)/shard_map/ppermute | solution.py:16
  449.8 6.6 %collective-permute-start.12 = (f32[3,1,24,384]{3,2,1,0:T(8,128)S(1)}, f32[3,1,24,384]{3,2,1,0:T(8,128)S(1)}, u32[]{:S(2)}, u32[]{:S(2)}) collective-permute-start(f32[3,1,24,384]{3,2,1,0:T(8,128)S(1)} %slice.1714), channel_id=1, source_target_pairs={{4,0},{8,4},{12,8},{5,1},{9,5},{13,9},{6,2},{10,6},{14,10},{7,3},{... | collective-permute-start | bytes 331784 | tf_op jit(solution)/shard_map/ppermute | solution.py:16
  451.8 3.1 collective-permute-start.13
  457.7 1.1 copy-start.12
  458.9 0.8 copy-start.13
  461.6 6.5 %collective-permute-start.14 = (f32[3,6,1,384]{3,2,1,0:T(1,128)S(1)}, f32[3,6,1,384]{3,2,1,0:T(1,128)S(1)}, u32[]{:S(2)}, u32[]{:S(2)}) collective-permute-start(f32[3,6,1,384]{3,2,1,0:T(1,128)S(1)} %slice.1716), channel_id=1, source_target_pairs={{0,1},{1,2},{2,3},{4,5},{5,6},{6,7},{8,9},{9,10},{10,11},{12,13},{... | collective-permute-start | bytes 82952 | tf_op jit(solution)/shard_map/ppermute | solution.py:16
  462.9 7.3 %collective-permute-start.15 = (f32[3,1,24,384]{3,2,1,0:T(8,128)S(1)}, f32[3,1,24,384]{3,2,1,0:T(8,128)S(1)}, u32[]{:S(2)}, u32[]{:S(2)}) collective-permute-start(f32[3,1,24,384]{3,2,1,0:T(8,128)S(1)} %slice.1717), channel_id=1, source_target_pairs={{0,4},{4,8},{8,12},{1,5},{5,9},{9,13},{2,6},{6,10},{10,14},{3,7},{... | collective-permute-start | bytes 331784 | tf_op jit(solution)/shard_map/ppermute | solution.py:16
  468.1 2.1 copy-start.60
  470.2 0.6 copy-start.54
  470.8 2.3 copy-start.6
  470.8 2.3 copy-start.29
  473.9 2.8 copy-start.7
  473.9 2.8 copy-start.30
  474.8 3.5 collective-permute-start.16
  481.4 151.6 %collective-permute-start.17 = (f32[3,2,8,128]{3,2,1,0:T(8,128)S(1)}, f32[3,2,8,128]{3,2,1,0:T(8,128)S(1)}, u32[]{:S(2)}, u32[]{:S(2)}) collective-permute-start(f32[3,2,8,128]{3,2,1,0:T(8,128)S(1)} %get-tuple-element.912), channel_id=1, source_target_pairs={{16,0},{17,1},{18,2},{19,3},{20,4},{21,5},{22,6},{23,7},{24,8},{25... | collective-permute-start | bytes 73736 | tf_op jit(solution)/shard_map/ppermute | solution.py:16
  643.4 1.3 copy-start
where the time goes:
time: 658 us; the launch traced here: 645 us
  waiting for transfers between devices  459 us (70%)
  other arithmetic  62.1 us (9%)
  local copies, waits for them, and re-layouts  42.7 us (6%)
  starting transfers between devices  37.5 us (6%)
  loops' own time  35.8 us (5%)
  between operations  8.4 us (1%)
    ppermute x18, waiting for transfers between devices, shifted(): return lax.ppermute(value, axis, pairs)  459 us
    ppermute x18, starting transfers between devices, shifted(): return lax.ppermute(value, axis, pairs)  37.5 us
    another operation x3, loops' own time, body(): lax.cond(coarse, lambda: jnp.zeros_like(earlier), lambda: restrict(local[...  18.8 us
    another operation x3, loops' own time, body(): lax.cond(coarse, lambda: overwrite(local, received, extent), lambda: local)  15.9 us
  transfers between devices with their start and end apart: 18, of which 10 were waited for; matrix products, arithmetic and copies ran while one was open for 8% of the time, Pallas kernels for 0%

commit v1 on v0

v1 whole, which is shorter than its diff:
```python
import functools

import jax
import jax.numpy as jnp
from jax import lax
from jax.experimental import pallas as pl
from jax.experimental.pallas import tpu as pltpu
from jax.sharding import PartitionSpec as P

COARSE_STEPS = 3
LIMIT = 40 * 1024 * 1024
VM = pl.BlockSpec(memory_space=pltpu.VMEM)
SM = pl.BlockSpec(memory_space=pltpu.SMEM)
F32 = jnp.float32


def shifted(value, axis, by):
    peers = lax.axis_size(axis)
    pairs = [(i, i + by) for i in range(peers) if 0 <= i + by < peers]
    return lax.ppermute(value, axis, pairs)


def lanes(shape=(8, 128)):
    return lax.broadcasted_iota(jnp.int32, shape, len(shape) - 1)


def rows(shape=(8, 128)):
    return lax.broadcasted_iota(jnp.int32, shape, len(shape) - 2)


def gather(tile, index):
    return jnp.take_along_axis(tile, index, axis=1)


def tables(perm, cond, relax, debye, factor):
    lane = lanes()

    def spread(ref):
        value = jnp.full((8, 128), ref[0], F32)
        for k in range(1, ref.shape[0]):
            value = jnp.where(lane == k, ref[k], value)
        return value

    eps = spread(perm)
    damp = spread(cond) * factor / (2.0 * eps)
    rate = spread(relax) * factor
    f0 = (1.0 - damp) / (1.0 + damp)
    f1 = 1.0 / (eps * (1.0 + damp))
    f3 = jnp.exp(-rate)
    f4 = spread(debye)
    c = f1 * rate
    return (f0 - c * f4, 0.5 * f1, c, f3, (1.0 - f3) * f4)


def to_tiles(parts):
    lane = lanes()
    kind = lane % 3
    out = []
    for t in range(3):
        mixed = jnp.where(
            kind == t, parts[0], jnp.where(kind == (t + 1) % 3, parts[1], parts[2])
        )
        out.append(gather(mixed, (3 * lane + t) & 127))
    return out


def from_tiles(tiles):
    lane = lanes()
    spread = [gather(tiles[t], (43 * (lane - t + 128)) & 127) for t in range(3)]
    out = []
    for a in range(3):
        kind = (2 * a + lane) % 3
        out.append(jnp.where(kind == 0, spread[0], jnp.where(kind == 1, spread[1], spread[2])))
    return out


def prep_kernel(f0, f1, f2, m0, m1, m2, perm, cond, relax, debye, sub, slab_e, slab_h, slab_p, box, coef):
    coarse = lax.axis_index("grid") == 0
    fields, material = (f0, f1, f2), (m0, m1, m2)

    @pl.when(coarse)
    def _():
        table = tables(perm, cond, relax, debye, 1.0)
        for x in range(6):
            for yt in range(3):
                for zt in range(3):
                    index = material[zt][0, x, pl.ds(8 * yt, 8)]
                    for k in range(5):
                        coef[k, x, 3 * yt + zt] = gather(table[k], index)
        for a in range(3):
            for k, part in enumerate((slab_e, slab_h, slab_p)):
                part[:, :, :, pl.ds(128 * a, 128)] = fields[a][0, 3 * k : 3 * k + 3]

    @pl.when(jnp.logical_not(coarse))
    def _():
        table = tables(perm, cond, relax, debye, F32(1.0 / 3.0))
        row, lane = rows(), lanes()
        ly, lz = sub[0, 0, 4], sub[0, 0, 5]
        within = (row < ly) & (lane < lz)
        for x in range(6):
            inside = within & (x < 3 * sub[0, 0, 3])
            for u in range(3):
                cut = pl.ds(u, 8, stride=3)
                parts = [material[a][0, x, cut] for a in range(3)]
                for t, index in enumerate(to_tiles(parts)):
                    for k in range(5):
                        coef[k, x, 3 * u + t] = gather(table[k], index)
                for c in range(9):
                    parts = [fields[a][0, c, x, cut] for a in range(3)]
                    for t, tile in enumerate(to_tiles(parts)):
                        box[c, x, 3 * u + t] = jnp.where(inside, tile, 0.0)


def whole(ref, *index):
    return jnp.concatenate(
        [
            jnp.concatenate([ref[(*index, 3 * yt + zt)] for zt in range(3)], axis=1)
            for yt in range(3)
        ],
        axis=0,
    )


def magnetic_kernel(slab_e, slab_h, next_x, next_y, out_h, last_x, last_y):
    coarse = lax.axis_index("grid") == 0

    @pl.when(coarse)
    def _():
        row, lane = rows((24, 384)), lanes((24, 384))

        def ahead_y(value, edge):
            return jnp.where(row == 23, edge, pltpu.roll(value, 23, 0))

        def ahead_z(value):
            return jnp.where(lane == 383, 0.0, pltpu.roll(value, 383, 1))

        for x in range(6):
            ex, ey, ez = (slab_e[c, x] for c in range(3))
            if x < 5:
                ey_x, ez_x = slab_e[1, x + 1], slab_e[2, x + 1]
            else:
                ey_x, ez_x = next_x[1, 0], next_x[2, 0]
            ex_y = ahead_y(ex, next_y[0, x : x + 1])
            ez_y = ahead_y(ez, next_y[2, x : x + 1])
            ex_z, ey_z = ahead_z(ex), ahead_z(ey)
            hx = slab_h[0, x] - 0.5 * ((ez_y - ez) - (ey_z - ey))
            hy = slab_h[1, x] - 0.5 * ((ex_z - ex) - (ez_x - ez))
            hz = slab_h[2, x] - 0.5 * ((ey_x - ey) - (ex_y - ex))
            for c, value in enumerate((hx, hy, hz)):
                out_h[c, x] = value
                last_y[c, x : x + 1] = value[23:24]
                if x == 5:
                    last_x[c, 0] = value


def row_pair(sub):
    y0 = sub[0, 0, 1]
    base = pl.multiple_of(8 * jnp.minimum(y0 // 8, 1), 8)
    return base, y0 - base


def region_of(slab, sub):
    x0, z0 = sub[0, 0, 0], sub[0, 0, 2]
    base, over = row_pair(sub)
    place = lanes() + z0
    index, part = place & 127, place >> 7

    def cut(c, i):
        tiles = []
        for a in range(3):
            pair = slab[c, x0 + i, pl.ds(base, 16), pl.ds(128 * a, 128)]
            tiles.append(gather(pltpu.roll(pair, (16 - over) & 15, 0)[0:8], index))
        return jnp.where(part == 0, tiles[0], jnp.where(part == 1, tiles[1], tiles[2]))

    return cut


def electric_kernel(slab_e, slab_h, slab_p, coef, prev_x, prev_y, sub, out_e, out_p, sent):
    coarse = lax.axis_index("grid") == 0

    @pl.when(coarse)
    def _():
        row, lane = rows((24, 384)), lanes((24, 384))
        cut = region_of(slab_e, sub)
        for c in range(3):
            for i in range(2):
                sent[0, c, i] = cut(c, i)

        def behind_y(value, edge):
            return jnp.where(row == 0, edge, pltpu.roll(value, 1, 0))

        def behind_z(value):
            return jnp.where(lane == 0, 0.0, pltpu.roll(value, 1, 1))

        for x in range(6):
            hx, hy, hz = (slab_h[c, x] for c in range(3))
            if x > 0:
                hy_x, hz_x = slab_h[1, x - 1], slab_h[2, x - 1]
            else:
                hy_x, hz_x = prev_x[1, 0], prev_x[2, 0]
            hx_y = behind_y(hx, prev_y[0, x : x + 1])
            hz_y = behind_y(hz, prev_y[2, x : x + 1])
            hx_z, hy_z = behind_z(hx), behind_z(hy)
            rotation = (
                (hz - hz_y) - (hy - hy_z),
                (hx - hx_z) - (hz - hz_x),
                (hy - hy_x) - (hx - hx_y),
            )
            a, b, p, f3, g = (whole(coef, k, x) for k in range(5))
            for c in range(3):
                old = slab_p[c, x]
                new = a * slab_e[c, x] + b * rotation[c] + p * old
                out_e[c, x] = new
                out_p[c, x] = f3 * old + g * new
        cut = region_of(out_e, sub)
        for c in range(3):
            for i in range(2):
                sent[1, c, i] = cut(c, i)


def put_back(slab, received, sub):
    x0, z0 = sub[0, 0, 0], sub[0, 0, 2]
    lx, ly, lz = sub[0, 0, 3], sub[0, 0, 4], sub[0, 0, 5]
    base, over = row_pair(sub)
    row, lane = rows((16, 128)) - over, lanes()
    for i in range(2):
        for a in range(3):
            place = lane + (128 * a) - z0
            index = place & 127
            wide = lanes((16, 128)) + (128 * a) - z0
            covered = (wide >= 0) & (wide < lz) & (row >= 0) & (row < ly) & (i < lx)
            for c in range(3):
                spot = (c, x0 + i, pl.ds(base, 16), pl.ds(128 * a, 128))
                tile = gather(received[c, i], index)
                pair = pltpu.roll(jnp.concatenate([tile, tile]), over, 0)
                slab[spot] = jnp.where(covered, pair, slab[spot])


def overwrite_kernel(slab_e, received, sub, slab, first_x, first_y):
    coarse = lax.axis_index("grid") == 0

    @pl.when(coarse)
    def _():
        slab[...] = slab_e[...]
        put_back(slab, received, sub)
        for c in range(3):
            first_x[c, 0] = slab[c, 0]
            for x in range(6):
                first_y[c, x : x + 1] = slab[c, x, 0:1]


def fine_kernel(box_in, coef, region, sub, box, restricted):
    coarse = lax.axis_index("grid") == 0

    @pl.when(jnp.logical_not(coarse))
    def _():
        box[...] = box_in[...]
        row, lane = rows(), lanes()
        lx, ly, lz = sub[0, 0, 3], sub[0, 0, 4], sub[0, 0, 5]
        within = (row < ly) & (lane < lz)
        inside = [within, within & (lx == 2)]
        y_face = [row == 0, None, row == ly - 1]
        z_face = [lane == 0, None, lane == lz - 1]

        def up(value):
            return jnp.where(row == 7, 0.0, pltpu.roll(value, 7, 0))

        def left(value):
            return jnp.where(lane == 127, 0.0, pltpu.roll(value, 127, 1))

        def down(value):
            return jnp.where(row == 0, 0.0, pltpu.roll(value, 1, 0))

        def right(value):
            return jnp.where(lane == 0, 0.0, pltpu.roll(value, 1, 1))

        def ahead_y(values, u, t):
            return values[3 * u + 3 + t] if u < 2 else up(values[t])

        def ahead_z(values, u, t):
            return values[3 * u + t + 1] if t < 2 else left(values[3 * u])

        def behind_y(values, u, t):
            return values[3 * u - 3 + t] if u > 0 else down(values[6 + t])

        def behind_z(values, u, t):
            return values[3 * u + t - 1] if t > 0 else right(values[3 * u + 2])

        def either(p, q):
            if p is None:
                return q
            return p if q is None else p | q

        zero = jnp.zeros((8, 128), F32)

        def substep(number, carry):
            weight = (number.astype(F32) + 1.0) / 3.0
            driven = [
                [region[0, c, i] + weight * (region[1, c, i] - region[0, c, i]) for i in range(2)]
                for c in range(3)
            ]
            for x in range(6):
                part = x // 3
                e = [[box[c, x, k] for k in range(9)] for c in range(3)]
                if x < 5:
                    ey_x = [box[1, x + 1, k] for k in range(9)]
                    ez_x = [box[2, x + 1, k] for k in range(9)]
                else:
                    ey_x = ez_x = [zero] * 9
                h = [[], [], []]
                for u in range(3):
                    for t in range(3):
                        k = 3 * u + t
                        ex, ey, ez = e[0][k], e[1][k], e[2][k]
                        turn = (
                            (ahead_y(e[2], u, t) - ez) - (ahead_z(e[1], u, t) - ey),
                            (ahead_z(e[0], u, t) - ex) - (ez_x[k] - ez),
                            (ey_x[k] - ey) - (ahead_y(e[0], u, t) - ex),
                        )
                        for c in range(3):
                            value = box[3 + c, x, k] - 0.5 * turn[c]
                            box[3 + c, x, k] = value
                            h[c].append(value)
                x_face = x == 0
                if x in (2, 5):
                    x_face = jnp.full((8, 128), 3 * lx - 1, jnp.int32) == x
                for u in range(3):
                    for t in range(3):
                        k = 3 * u + t
                        hx, hy, hz = h[0][k], h[1][k], h[2][k]
                        hy_x = box[4, x - 1, k] if x > 0 else zero
                        hz_x = box[5, x - 1, k] if x > 0 else zero
                        rotation = (
                            (hz - behind_y(h[2], u, t)) - (hy - behind_z(h[1], u, t)),
                            (hx - behind_z(h[0], u, t)) - (hz - hz_x),
                            (hy - hy_x) - (hx - behind_y(h[0], u, t)),
                        )
                        a, b, p, f3, g = (coef[q, x, k] for q in range(5))
                        faces = (
                            either(y_face[u], z_face[t]),
                            None if x_face is True else either(x_face if x in (2, 5) else None, z_face[t]),
                            None if x_face is True else either(x_face if x in (2, 5) else None, y_face[u]),
                        )
                        for c in range(3):
                            old = box[6 + c, x, k]
                            new = a * e[c][k] + b * rotation[c] + p * old
                            if c > 0 and x_face is True:
                                new = driven[c][part]
                            elif faces[c] is not None:
                                new = jnp.where(faces[c], driven[c][part], new)
                            new = jnp.where(inside[part], new, 0.0)
                            box[c, x, k] = new
                            box[6 + c, x, k] = f3 * old + g * new
            return carry

        lax.fori_loop(0, 3, substep, 0)
        for c in range(3):
            for i in range(2):
                total = zero
                for x in range(3 * i, 3 * i + 3):
                    for k in range(9):
                        total = total + box[c, x, k]
                restricted[c, i] = total * F32(1.0 / 27.0)


def finish_kernel(slab_e, slab_h, slab_p, box, received, sub, out, mixed):
    coarse = lax.axis_index("grid") == 0

    @pl.when(coarse)
    def _():
        for k, part in enumerate((slab_e, slab_h, slab_p)):
            out[3 * k : 3 * k + 3] = part[...]
        put_back(out, received, sub)

    @pl.when(jnp.logical_not(coarse))
    def _():
        for c in range(9):
            for x in range(6):
                for u in range(3):
                    parts = from_tiles([box[c, x, 3 * u + t] for t in range(3)])
                    for a in range(3):
                        mixed[c, x, a, pl.ds(u, 8, stride=3)] = parts[a]
                for a in range(3):
                    out[c, x, :, pl.ds(128 * a, 128)] = mixed[c, x, a]


def third(shape, a):
    return pl.BlockSpec(shape, lambda i: (0,) * (len(shape) - 1) + (a,))


def call(kernel, operands, specs, outs, scratch=(), grid=()):
    params = pltpu.CompilerParams(vmem_limit_bytes=LIMIT)
    return pl.pallas_call(
        kernel,
        out_shape=[jax.ShapeDtypeStruct(shape, F32) for shape in outs],
        in_specs=specs,
        out_specs=[VM] * len(outs),
        grid=grid,
        scratch_shapes=scratch,
        compiler_params=params,
    )(*operands)


PART = (3, 6, 24, 384)
SLAB = (9, 6, 24, 384)
BOX = (9, 6, 9, 8, 128)
COEF = (5, 6, 9, 8, 128)
REGION = (3, 2, 8, 128)
X_EDGE = (3, 1, 24, 384)
Y_EDGE = (3, 6, 384)


def body(fields, material, permittivity, conductivity, relax_rate, debye_strength, subgrids):
    first_x = fields[0, 0:3, 0:1]
    first_y = fields[0, 0:3, :, 0]
    slab_e, slab_h, slab_p, box, coef = call(
        prep_kernel,
        (fields,) * 3
        + (material,) * 3
        + (permittivity, conductivity, relax_rate, debye_strength, subgrids),
        [third((1, 9, 6, 24, 128), a) for a in range(3)]
        + [third((1, 6, 24, 128), a) for a in range(3)]
        + [SM] * 5,
        [PART] * 3 + [BOX, COEF],
        grid=(1,),
    )
    for number in range(COARSE_STEPS):
        next_x = shifted(first_x, "gx", -1)
        next_y = shifted(first_y, "gy", -1)
        slab_h, last_x, last_y = call(
            magnetic_kernel,
            (slab_e, slab_h, next_x, next_y),
            [VM] * 4,
            [PART, X_EDGE, Y_EDGE],
        )
        prev_x = shifted(last_x, "gx", 1)
        prev_y = shifted(last_y, "gy", 1)
        slab_e, slab_p, sent = call(
            electric_kernel,
            (slab_e, slab_h, slab_p, coef, prev_x, prev_y, subgrids),
            [VM] * 6 + [SM],
            [PART, PART, (2, *REGION)],
        )
        region = shifted(sent, "grid", 1)
        box, restricted = call(
            fine_kernel, (box, coef, region, subgrids), [VM] * 3 + [SM], [BOX, REGION]
        )
        received = shifted(restricted, "grid", -1)
        if number < COARSE_STEPS - 1:
            slab_e, first_x, first_y = call(
                overwrite_kernel,
                (slab_e, received, subgrids),
                [VM] * 2 + [SM],
                [PART, X_EDGE, Y_EDGE],
            )
    (out,) = call(
        finish_kernel,
        (slab_e, slab_h, slab_p, box, received, subgrids),
        [VM] * 5 + [SM],
        [SLAB],
        scratch=[pltpu.VMEM((9, 6, 3, 24, 128), F32)],
    )
    return out[None]


def solution(mesh):
    in_specs = (
        P("grid", None, "gx", "gy", None),
        P("grid", "gx", "gy", None),
        P(),
        P(),
        P(),
        P(),
        P("gx", "gy", None),
    )
    out_specs = P("grid", None, "gx", "gy", None)
    return jax.shard_map(body, mesh=mesh, in_specs=in_specs, out_specs=out_specs, check_vma=False)
```

time: 658 us -> 96.6 us (0.15)
  the two profiles are of different devices: /device:TPU:16 before, /device:TPU:0 now
where the time goes in v1:
time: 96.6 us; the launch traced here: 95.6 us
  starting transfers between devices  43.8 us (45%)
  waiting for transfers between devices  33.8 us (35%)
  Pallas kernels  10.1 us (10%)
  local copies, waits for them, and re-layouts  7.63 us (8%)
    ppermute x18, starting transfers between devices, shifted(): return lax.ppermute(value, axis, pairs)  43.8 us
    ppermute x18, waiting for transfers between devices, shifted(): return lax.ppermute(value, axis, pairs)  33.8 us
    pallas_call x13, Pallas kernels, call(): pl.pallas_call(kernel, out_shape=[jax.ShapeDtypeStruct(shape, F32) for sh...  10.1 us
    unnamed x17, local copies, waits for them, and re-layouts  5.77 us
  transfers between devices with their start and end apart: 18, of which 13 were waited for; matrix products, arithmetic and copies ran while one was open for 1% of the time, Pallas kernels for 1%

profile of v1, /device:TPU:0, one launch (start us, length us, event | category | flops | bytes accessed | tf_op | source)
XLA Modules:
  0.0 95.6 jit_solution(15851057147263646650)
XLA Ops:
  0.0 0.9 slice_bitcast_fusion
  0.9 1.3 %collective-permute-start = (f32[3,1,24,384]{3,2,1,0:T(8,128)S(1)}, f32[3,1,24,384]{3,2,1,0:T(8,128)S(1)}, u32[]{:S(2)}, u32[]{:S(2)}) collective-permute-start(f32[3,1,24,384]{3,2,1,0:T(8,128)S(1)} %slice_bitcast_fusion), channel_id=1, source_target_pairs={{4,0},{8,4},{12,8},{5,1},{9,5},{13,9},{6,2},{10,6},{14,10},{7,3},{... | collective-permute-start | bytes 331784 | tf_op jit(solution)/shard_map/ppermute | solution.py:20
  2.2 1.0 slice.7
  3.2 1.3 %collective-permute-start.1 = (f32[3,6,384]{2,1,0:T(8,128)S(1)}, f32[3,6,384]{2,1,0:T(8,128)S(1)}, u32[]{:S(2)}, u32[]{:S(2)}) collective-permute-start(f32[3,6,384]{2,1,0:T(8,128)S(1)} %bitcast.8), channel_id=1, source_target_pairs={{1,0},{2,1},{3,2},{5,4},{6,5},{7,6},{9,8},{10,9},{11,10},{13,12},{... | collective-permute-start | bytes 82952 | tf_op jit(solution)/shard_map/ppermute | solution.py:20
  4.5 1.5 %copy-done = f32[1,9,6,24,384]{4,3,2,1,0:T(8,128)S(1)} copy-done((f32[1,9,6,24,384]{4,3,2,1,0:T(8,128)S(1)}, f32[1,9,6,24,384]{4,3,2,1,0:T(8,128)}, u32[]{:S(2)}) %copy-start) | copy-done | bytes 1990680
  6.0 0.9 copy-done.1
  7.0 0.7 copy-done.2
  7.6 0.7 copy-done.4
  8.3 0.7 copy-done.5
  8.9 0.7 copy-done.6
  9.6 0.7 copy-done.7
  10.2 1.1 %shard_map.73 = (f32[3,6,24,384]{3,2,1,0:T(8,128)S(1)}, f32[3,6,24,384]{3,2,1,0:T(8,128)S(1)}, f32[3,6,24,384]{3,2,1,0:T(8,128)S(1)}, f32[9,6,9,8,128]{4,3,2,1,0:T(8,128)S(1)}, f32[5,6,9,8,128]{4,3,2,1,0:T(8,128)S(1)}) custom-call(f32[1,9,6,24,384]{4,3,2,1,0:T(8,128)S(1)} %copy-done, f32[1,9,6,24,384]{4,3,2,1,0:T(8,128)S(1)} %copy-done, ...), custom_call_target="tpu_custom_call" | custom-call | tf_op jit(solution)/shard_map/pallas_call | solution.py:393
  11.6 5.6 %collective-permute-start.2 = (f32[3,1,24,384]{3,2,1,0:T(8,128)S(1)}, f32[3,1,24,384]{3,2,1,0:T(8,128)S(1)}, u32[]{:S(2)}, u32[]{:S(2)}) collective-permute-start(f32[3,1,24,384]{3,2,1,0:T(8,128)S(1)} %get-tuple-element.45), channel_id=1, source_target_pairs={{0,4},{4,8},{8,12},{1,5},{5,9},{9,13},{2,6},{6,10},{10,14},{3,7},{... | collective-permute-start | bytes 331784 | tf_op jit(solution)/shard_map/ppermute | solution.py:20
  17.2 2.8 %collective-permute-start.3 = (f32[3,6,384]{2,1,0:T(8,128)S(1)}, f32[3,6,384]{2,1,0:T(8,128)S(1)}, u32[]{:S(2)}, u32[]{:S(2)}) collective-permute-start(f32[3,6,384]{2,1,0:T(8,128)S(1)} %get-tuple-element.46), channel_id=1, source_target_pairs={{0,1},{1,2},{2,3},{4,5},{5,6},{6,7},{8,9},{9,10},{10,11},{12,13},{... | collective-permute-start | bytes 82952 | tf_op jit(solution)/shard_map/ppermute | solution.py:20
  20.0 0.8 collective-permute-done.3.prev_y
  20.8 1.1 %shard_map.75 = (f32[3,6,24,384]{3,2,1,0:T(8,128)S(1)}, f32[3,6,24,384]{3,2,1,0:T(8,128)S(1)}, f32[2,3,2,8,128]{4,3,2,1,0:T(8,128)S(1)}) custom-call(f32[3,6,24,384]{3,2,1,0:T(8,128)S(1)} %get-tuple-element.40.slab_e, f32[3,6,24,384]{3,2,1,0:T(8,128)S(1)} %get-tuple-element.42.slab_h, f32[3,6,24,384]{3,2,1,0:T(8,128)S(1)} %get-tuple-element.43.slab_p, ...), custom_call_target="tpu_custom_call" | custom-call | tf_op jit(solution)/shard_map/pallas_call | solution.py:393
  21.9 5.7 %collective-permute-start.4 = (f32[2,3,2,8,128]{4,3,2,1,0:T(8,128)S(1)}, f32[2,3,2,8,128]{4,3,2,1,0:T(8,128)S(1)}, u32[]{:S(2)}, u32[]{:S(2)}) collective-permute-start(f32[2,3,2,8,128]{4,3,2,1,0:T(8,128)S(1)} %get-tuple-element.49), channel_id=1, source_target_pairs={{0,16},{1,17},{2,18},{3,19},{4,20},{5,21},{6,22},{7,23},{8,24},{9,... | collective-permute-start | bytes 147464 | tf_op jit(solution)/shard_map/ppermute | solution.py:20
  27.6 1.7 %collective-permute-done.4.region = f32[2,3,2,8,128]{4,3,2,1,0:T(8,128)S(1)} collective-permute-done((f32[2,3,2,8,128]{4,3,2,1,0:T(8,128)S(1)}, f32[2,3,2,8,128]{4,3,2,1,0:T(8,128)S(1)}, u32[]{:S(2)}, u32[]{:S(2)}) %collective-permute-start.4) | collective-permute-done | bytes 49184 | tf_op jit(solution)/shard_map/ppermute | solution.py:20
  29.4 0.6 shard_map.76
  29.9 1.3 %collective-permute-start.5 = (f32[3,2,8,128]{3,2,1,0:T(8,128)S(1)}, f32[3,2,8,128]{3,2,1,0:T(8,128)S(1)}, u32[]{:S(2)}, u32[]{:S(2)}) collective-permute-start(f32[3,2,8,128]{3,2,1,0:T(8,128)S(1)} %get-tuple-element.50), channel_id=1, source_target_pairs={{16,0},{17,1},{18,2},{19,3},{20,4},{21,5},{22,6},{23,7},{24,8},{25... | collective-permute-start | bytes 73736 | tf_op jit(solution)/shard_map/ppermute | solution.py:20
  31.2 5.8 %collective-permute-done.5.received = f32[3,2,8,128]{3,2,1,0:T(8,128)S(1)} collective-permute-done((f32[3,2,8,128]{3,2,1,0:T(8,128)S(1)}, f32[3,2,8,128]{3,2,1,0:T(8,128)S(1)}, u32[]{:S(2)}, u32[]{:S(2)}) %collective-permute-start.5) | collective-permute-done | bytes 24608 | tf_op jit(solution)/shard_map/ppermute | solution.py:20
  37.0 0.7 shard_map.77
  37.7 1.3 %collective-permute-start.6 = (f32[3,1,24,384]{3,2,1,0:T(8,128)S(1)}, f32[3,1,24,384]{3,2,1,0:T(8,128)S(1)}, u32[]{:S(2)}, u32[]{:S(2)}) collective-permute-start(f32[3,1,24,384]{3,2,1,0:T(8,128)S(1)} %get-tuple-element.52), channel_id=1, source_target_pairs={{4,0},{8,4},{12,8},{5,1},{9,5},{13,9},{6,2},{10,6},{14,10},{7,3},{... | collective-permute-start | bytes 331784 | tf_op jit(solution)/shard_map/ppermute | solution.py:20
  39.0 1.3 %collective-permute-start.7 = (f32[3,6,384]{2,1,0:T(8,128)S(1)}, f32[3,6,384]{2,1,0:T(8,128)S(1)}, u32[]{:S(2)}, u32[]{:S(2)}) collective-permute-start(f32[3,6,384]{2,1,0:T(8,128)S(1)} %get-tuple-element.53), channel_id=1, source_target_pairs={{1,0},{2,1},{3,2},{5,4},{6,5},{7,6},{9,8},{10,9},{11,10},{13,12},{... | collective-permute-start | bytes 82952 | tf_op jit(solution)/shard_map/ppermute | solution.py:20
  40.3 1.8 %collective-permute-done.7.next_y = f32[3,6,384]{2,1,0:T(8,128)S(1)} collective-permute-done((f32[3,6,384]{2,1,0:T(8,128)S(1)}, f32[3,6,384]{2,1,0:T(8,128)S(1)}, u32[]{:S(2)}, u32[]{:S(2)}) %collective-permute-start.7) | collective-permute-done | bytes 27680 | tf_op jit(solution)/shard_map/ppermute | solution.py:20
  42.1 2.8 %collective-permute-done.6.next_x = f32[3,1,24,384]{3,2,1,0:T(8,128)S(1)} collective-permute-done((f32[3,1,24,384]{3,2,1,0:T(8,128)S(1)}, f32[3,1,24,384]{3,2,1,0:T(8,128)S(1)}, u32[]{:S(2)}, u32[]{:S(2)}) %collective-permute-start.6) | collective-permute-done | bytes 110624 | tf_op jit(solution)/shard_map/ppermute | solution.py:20
  45.1 3.9 %collective-permute-start.8 = (f32[3,1,24,384]{3,2,1,0:T(8,128)S(1)}, f32[3,1,24,384]{3,2,1,0:T(8,128)S(1)}, u32[]{:S(2)}, u32[]{:S(2)}) collective-permute-start(f32[3,1,24,384]{3,2,1,0:T(8,128)S(1)} %get-tuple-element.56), channel_id=1, source_target_pairs={{0,4},{4,8},{8,12},{1,5},{5,9},{9,13},{2,6},{6,10},{10,14},{3,7},{... | collective-permute-start | bytes 331784 | tf_op jit(solution)/shard_map/ppermute | solution.py:20
  49.0 3.8 %collective-permute-start.9 = (f32[3,6,384]{2,1,0:T(8,128)S(1)}, f32[3,6,384]{2,1,0:T(8,128)S(1)}, u32[]{:S(2)}, u32[]{:S(2)}) collective-permute-start(f32[3,6,384]{2,1,0:T(8,128)S(1)} %get-tuple-element.57), channel_id=1, source_target_pairs={{0,1},{1,2},{2,3},{4,5},{5,6},{6,7},{8,9},{9,10},{10,11},{12,13},{... | collective-permute-start | bytes 82952 | tf_op jit(solution)/shard_map/ppermute | solution.py:20
  52.9 0.8 collective-permute-done.9.prev_y
  53.7 1.1 %shard_map.79 = (f32[3,6,24,384]{3,2,1,0:T(8,128)S(1)}, f32[3,6,24,384]{3,2,1,0:T(8,128)S(1)}, f32[2,3,2,8,128]{4,3,2,1,0:T(8,128)S(1)}) custom-call(f32[3,6,24,384]{3,2,1,0:T(8,128)S(1)} %get-tuple-element.51.slab_e, f32[3,6,24,384]{3,2,1,0:T(8,128)S(1)} %get-tuple-element.54.slab_h, f32[3,6,24,384]{3,2,1,0:T(8,128)S(1)} %get-tuple-element.55.slab_p, ...), custom_call_target="tpu_custom_call" | custom-call | tf_op jit(solution)/shard_map/pallas_call | solution.py:393
  54.8 1.3 %collective-permute-start.10 = (f32[2,3,2,8,128]{4,3,2,1,0:T(8,128)S(1)}, f32[2,3,2,8,128]{4,3,2,1,0:T(8,128)S(1)}, u32[]{:S(2)}, u32[]{:S(2)}) collective-permute-start(f32[2,3,2,8,128]{4,3,2,1,0:T(8,128)S(1)} %get-tuple-element.60), channel_id=1, source_target_pairs={{0,16},{1,17},{2,18},{3,19},{4,20},{5,21},{6,22},{7,23},{8,24},{9,... | collective-permute-start | bytes 147464 | tf_op jit(solution)/shard_map/ppermute | solution.py:20
  56.1 1.7 %collective-permute-done.10.region = f32[2,3,2,8,128]{4,3,2,1,0:T(8,128)S(1)} collective-permute-done((f32[2,3,2,8,128]{4,3,2,1,0:T(8,128)S(1)}, f32[2,3,2,8,128]{4,3,2,1,0:T(8,128)S(1)}, u32[]{:S(2)}, u32[]{:S(2)}) %collective-permute-start.10) | collective-permute-done | bytes 49184 | tf_op jit(solution)/shard_map/ppermute | solution.py:20
  58.4 1.3 %collective-permute-start.11 = (f32[3,2,8,128]{3,2,1,0:T(8,128)S(1)}, f32[3,2,8,128]{3,2,1,0:T(8,128)S(1)}, u32[]{:S(2)}, u32[]{:S(2)}) collective-permute-start(f32[3,2,8,128]{3,2,1,0:T(8,128)S(1)} %get-tuple-element.61), channel_id=1, source_target_pairs={{16,0},{17,1},{18,2},{19,3},{20,4},{21,5},{22,6},{23,7},{24,8},{25... | collective-permute-start | bytes 73736 | tf_op jit(solution)/shard_map/ppermute | solution.py:20
  59.7 5.7 %collective-permute-done.11.received = f32[3,2,8,128]{3,2,1,0:T(8,128)S(1)} collective-permute-done((f32[3,2,8,128]{3,2,1,0:T(8,128)S(1)}, f32[3,2,8,128]{3,2,1,0:T(8,128)S(1)}, u32[]{:S(2)}, u32[]{:S(2)}) %collective-permute-start.11) | collective-permute-done | bytes 24608 | tf_op jit(solution)/shard_map/ppermute | solution.py:20
  65.5 0.7 shard_map.81
  66.2 1.3 %collective-permute-start.12 = (f32[3,1,24,384]{3,2,1,0:T(8,128)S(1)}, f32[3,1,24,384]{3,2,1,0:T(8,128)S(1)}, u32[]{:S(2)}, u32[]{:S(2)}) collective-permute-start(f32[3,1,24,384]{3,2,1,0:T(8,128)S(1)} %get-tuple-element.63), channel_id=1, source_target_pairs={{4,0},{8,4},{12,8},{5,1},{9,5},{13,9},{6,2},{10,6},{14,10},{7,3},{... | collective-permute-start | bytes 331784 | tf_op jit(solution)/shard_map/ppermute | solution.py:20
  67.5 1.3 %collective-permute-start.13 = (f32[3,6,384]{2,1,0:T(8,128)S(1)}, f32[3,6,384]{2,1,0:T(8,128)S(1)}, u32[]{:S(2)}, u32[]{:S(2)}) collective-permute-start(f32[3,6,384]{2,1,0:T(8,128)S(1)} %get-tuple-element.64), channel_id=1, source_target_pairs={{1,0},{2,1},{3,2},{5,4},{6,5},{7,6},{9,8},{10,9},{11,10},{13,12},{... | collective-permute-start | bytes 82952 | tf_op jit(solution)/shard_map/ppermute | solution.py:20
  68.8 1.8 %collective-permute-done.13.next_y = f32[3,6,384]{2,1,0:T(8,128)S(1)} collective-permute-done((f32[3,6,384]{2,1,0:T(8,128)S(1)}, f32[3,6,384]{2,1,0:T(8,128)S(1)}, u32[]{:S(2)}, u32[]{:S(2)}) %collective-permute-start.13) | collective-permute-done | bytes 27680 | tf_op jit(solution)/shard_map/ppermute | solution.py:20
  70.6 2.2 %collective-permute-done.12.next_x = f32[3,1,24,384]{3,2,1,0:T(8,128)S(1)} collective-permute-done((f32[3,1,24,384]{3,2,1,0:T(8,128)S(1)}, f32[3,1,24,384]{3,2,1,0:T(8,128)S(1)}, u32[]{:S(2)}, u32[]{:S(2)}) %collective-permute-start.12) | collective-permute-done | bytes 110624 | tf_op jit(solution)/shard_map/ppermute | solution.py:20
  73.0 3.5 %collective-permute-start.14 = (f32[3,1,24,384]{3,2,1,0:T(8,128)S(1)}, f32[3,1,24,384]{3,2,1,0:T(8,128)S(1)}, u32[]{:S(2)}, u32[]{:S(2)}) collective-permute-start(f32[3,1,24,384]{3,2,1,0:T(8,128)S(1)} %get-tuple-element.67), channel_id=1, source_target_pairs={{0,4},{4,8},{8,12},{1,5},{5,9},{9,13},{2,6},{6,10},{10,14},{3,7},{... | collective-permute-start | bytes 331784 | tf_op jit(solution)/shard_map/ppermute | solution.py:20
  76.5 4.3 %collective-permute-start.15 = (f32[3,6,384]{2,1,0:T(8,128)S(1)}, f32[3,6,384]{2,1,0:T(8,128)S(1)}, u32[]{:S(2)}, u32[]{:S(2)}) collective-permute-start(f32[3,6,384]{2,1,0:T(8,128)S(1)} %get-tuple-element.68), channel_id=1, source_target_pairs={{0,1},{1,2},{2,3},{4,5},{5,6},{6,7},{8,9},{9,10},{10,11},{12,13},{... | collective-permute-start | bytes 82952 | tf_op jit(solution)/shard_map/ppermute | solution.py:20
  80.9 0.8 collective-permute-done.15.prev_y
  81.7 1.1 %shard_map.83 = (f32[3,6,24,384]{3,2,1,0:T(8,128)S(1)}, f32[3,6,24,384]{3,2,1,0:T(8,128)S(1)}, f32[2,3,2,8,128]{4,3,2,1,0:T(8,128)S(1)}) custom-call(f32[3,6,24,384]{3,2,1,0:T(8,128)S(1)} %get-tuple-element.62.slab_e, f32[3,6,24,384]{3,2,1,0:T(8,128)S(1)} %get-tuple-element.65.slab_h, f32[3,6,24,384]{3,2,1,0:T(8,128)S(1)} %get-tuple-element.66.slab_p, ...), custom_call_target="tpu_custom_call" | custom-call | tf_op jit(solution)/shard_map/pallas_call | solution.py:393
  82.8 1.3 %collective-permute-start.16 = (f32[2,3,2,8,128]{4,3,2,1,0:T(8,128)S(1)}, f32[2,3,2,8,128]{4,3,2,1,0:T(8,128)S(1)}, u32[]{:S(2)}, u32[]{:S(2)}) collective-permute-start(f32[2,3,2,8,128]{4,3,2,1,0:T(8,128)S(1)} %get-tuple-element.72), channel_id=1, source_target_pairs={{0,16},{1,17},{2,18},{3,19},{4,20},{5,21},{6,22},{7,23},{8,24},{9,... | collective-permute-start | bytes 147464 | tf_op jit(solution)/shard_map/ppermute | solution.py:20
  84.1 1.7 %collective-permute-done.16.region = f32[2,3,2,8,128]{4,3,2,1,0:T(8,128)S(1)} collective-permute-done((f32[2,3,2,8,128]{4,3,2,1,0:T(8,128)S(1)}, f32[2,3,2,8,128]{4,3,2,1,0:T(8,128)S(1)}, u32[]{:S(2)}, u32[]{:S(2)}) %collective-permute-start.16) | collective-permute-done | bytes 49184 | tf_op jit(solution)/shard_map/ppermute | solution.py:20
  86.4 1.3 %collective-permute-start.17 = (f32[3,2,8,128]{3,2,1,0:T(8,128)S(1)}, f32[3,2,8,128]{3,2,1,0:T(8,128)S(1)}, u32[]{:S(2)}, u32[]{:S(2)}) collective-permute-start(f32[3,2,8,128]{3,2,1,0:T(8,128)S(1)} %get-tuple-element.74), channel_id=1, source_target_pairs={{16,0},{17,1},{18,2},{19,3},{20,4},{21,5},{22,6},{23,7},{24,8},{25... | collective-permute-start | bytes 73736 | tf_op jit(solution)/shard_map/ppermute | solution.py:20
  87.7 5.9 %collective-permute-done.17.received = f32[3,2,8,128]{3,2,1,0:T(8,128)S(1)} collective-permute-done((f32[3,2,8,128]{3,2,1,0:T(8,128)S(1)}, f32[3,2,8,128]{3,2,1,0:T(8,128)S(1)}, u32[]{:S(2)}, u32[]{:S(2)}) %collective-permute-start.17) | collective-permute-done | bytes 24608 | tf_op jit(solution)/shard_map/ppermute | solution.py:20
  93.6 2.0 %shard_map.85 = f32[9,6,24,384]{3,2,1,0:T(8,128)} custom-call(f32[3,6,24,384]{3,2,1,0:T(8,128)S(1)} %get-tuple-element.69.slab_e, f32[3,6,24,384]{3,2,1,0:T(8,128)S(1)} %get-tuple-element.65.slab_h, f32[3,6,24,384]{3,2,1,0:T(8,128)S(1)} %get-tuple-element.70.slab_p, f32[9,6,9,8,128]{4,3,2,1,0:T(8,128)S(1)} %get-tuple-element.73.box, ...), custom_call_target="tpu_custom_call" | custom-call | tf_op jit(solution)/shard_map/pallas_call | solution.py:393
  (20 shorter events, 1.8 us)
Async XLA Ops:
  0.9 10.5 %collective-permute-start = (f32[3,1,24,384]{3,2,1,0:T(8,128)S(1)}, f32[3,1,24,384]{3,2,1,0:T(8,128)S(1)}, u32[]{:S(2)}, u32[]{:S(2)}) collective-permute-start(f32[3,1,24,384]{3,2,1,0:T(8,128)S(1)} %slice_bitcast_fusion), channel_id=1, source_target_pairs={{4,0},{8,4},{12,8},{5,1},{9,5},{13,9},{6,2},{10,6},{14,10},{7,3},{... | collective-permute-start | bytes 331784 | tf_op jit(solution)/shard_map/ppermute | solution.py:20
  3.2 8.2 %collective-permute-start.1 = (f32[3,6,384]{2,1,0:T(8,128)S(1)}, f32[3,6,384]{2,1,0:T(8,128)S(1)}, u32[]{:S(2)}, u32[]{:S(2)}) collective-permute-start(f32[3,6,384]{2,1,0:T(8,128)S(1)} %bitcast.8), channel_id=1, source_target_pairs={{1,0},{2,1},{3,2},{5,4},{6,5},{7,6},{9,8},{10,9},{11,10},{13,12},{... | collective-permute-start | bytes 82952 | tf_op jit(solution)/shard_map/ppermute | solution.py:20
  4.5 1.6 %copy-start = (f32[1,9,6,24,384]{4,3,2,1,0:T(8,128)S(1)}, f32[1,9,6,24,384]{4,3,2,1,0:T(8,128)}, u32[]{:S(2)}) copy-start(f32[1,9,6,24,384]{4,3,2,1,0:T(8,128)} %f2.1) | copy-start | bytes 5971972
  6.0 0.9 copy-start.1
  7.0 0.7 copy-start.2
  7.6 0.7 copy-start.4
  8.3 0.7 copy-start.5
  8.9 0.7 copy-start.6
  9.6 0.7 copy-start.7
  10.2 10.6 %copy-start.3 = (s32[1,1,6]{2,1,0:T(1,128)S(1)}, s32[1,1,6]{2,1,0:T(1,128)}, u32[]{:S(2)}) copy-start(s32[1,1,6]{2,1,0:T(1,128)} %sub.19) | copy-start | bytes 76
  11.6 9.2 %collective-permute-start.2 = (f32[3,1,24,384]{3,2,1,0:T(8,128)S(1)}, f32[3,1,24,384]{3,2,1,0:T(8,128)S(1)}, u32[]{:S(2)}, u32[]{:S(2)}) collective-permute-start(f32[3,1,24,384]{3,2,1,0:T(8,128)S(1)} %get-tuple-element.45), channel_id=1, source_target_pairs={{0,4},{4,8},{8,12},{1,5},{5,9},{9,13},{2,6},{6,10},{10,14},{3,7},{... | collective-permute-start | bytes 331784 | tf_op jit(solution)/shard_map/ppermute | solution.py:20
  17.2 3.6 %collective-permute-start.3 = (f32[3,6,384]{2,1,0:T(8,128)S(1)}, f32[3,6,384]{2,1,0:T(8,128)S(1)}, u32[]{:S(2)}, u32[]{:S(2)}) collective-permute-start(f32[3,6,384]{2,1,0:T(8,128)S(1)} %get-tuple-element.46), channel_id=1, source_target_pairs={{0,1},{1,2},{2,3},{4,5},{5,6},{6,7},{8,9},{9,10},{10,11},{12,13},{... | collective-permute-start | bytes 82952 | tf_op jit(solution)/shard_map/ppermute | solution.py:20
  21.9 7.4 %collective-permute-start.4 = (f32[2,3,2,8,128]{4,3,2,1,0:T(8,128)S(1)}, f32[2,3,2,8,128]{4,3,2,1,0:T(8,128)S(1)}, u32[]{:S(2)}, u32[]{:S(2)}) collective-permute-start(f32[2,3,2,8,128]{4,3,2,1,0:T(8,128)S(1)} %get-tuple-element.49), channel_id=1, source_target_pairs={{0,16},{1,17},{2,18},{3,19},{4,20},{5,21},{6,22},{7,23},{8,24},{9,... | collective-permute-start | bytes 147464 | tf_op jit(solution)/shard_map/ppermute | solution.py:20
  29.9 7.1 %collective-permute-start.5 = (f32[3,2,8,128]{3,2,1,0:T(8,128)S(1)}, f32[3,2,8,128]{3,2,1,0:T(8,128)S(1)}, u32[]{:S(2)}, u32[]{:S(2)}) collective-permute-start(f32[3,2,8,128]{3,2,1,0:T(8,128)S(1)} %get-tuple-element.50), channel_id=1, source_target_pairs={{16,0},{17,1},{18,2},{19,3},{20,4},{21,5},{22,6},{23,7},{24,8},{25... | collective-permute-start | bytes 73736 | tf_op jit(solution)/shard_map/ppermute | solution.py:20
  37.7 7.2 %collective-permute-start.6 = (f32[3,1,24,384]{3,2,1,0:T(8,128)S(1)}, f32[3,1,24,384]{3,2,1,0:T(8,128)S(1)}, u32[]{:S(2)}, u32[]{:S(2)}) collective-permute-start(f32[3,1,24,384]{3,2,1,0:T(8,128)S(1)} %get-tuple-element.52), channel_id=1, source_target_pairs={{4,0},{8,4},{12,8},{5,1},{9,5},{13,9},{6,2},{10,6},{14,10},{7,3},{... | collective-permute-start | bytes 331784 | tf_op jit(solution)/shard_map/ppermute | solution.py:20
  39.0 3.1 %collective-permute-start.7 = (f32[3,6,384]{2,1,0:T(8,128)S(1)}, f32[3,6,384]{2,1,0:T(8,128)S(1)}, u32[]{:S(2)}, u32[]{:S(2)}) collective-permute-start(f32[3,6,384]{2,1,0:T(8,128)S(1)} %get-tuple-element.53), channel_id=1, source_target_pairs={{1,0},{2,1},{3,2},{5,4},{6,5},{7,6},{9,8},{10,9},{11,10},{13,12},{... | collective-permute-start | bytes 82952 | tf_op jit(solution)/shard_map/ppermute | solution.py:20
  45.1 8.6 %collective-permute-start.8 = (f32[3,1,24,384]{3,2,1,0:T(8,128)S(1)}, f32[3,1,24,384]{3,2,1,0:T(8,128)S(1)}, u32[]{:S(2)}, u32[]{:S(2)}) collective-permute-start(f32[3,1,24,384]{3,2,1,0:T(8,128)S(1)} %get-tuple-element.56), channel_id=1, source_target_pairs={{0,4},{4,8},{8,12},{1,5},{5,9},{9,13},{2,6},{6,10},{10,14},{3,7},{... | collective-permute-start | bytes 331784 | tf_op jit(solution)/shard_map/ppermute | solution.py:20
  49.0 4.7 %collective-permute-start.9 = (f32[3,6,384]{2,1,0:T(8,128)S(1)}, f32[3,6,384]{2,1,0:T(8,128)S(1)}, u32[]{:S(2)}, u32[]{:S(2)}) collective-permute-start(f32[3,6,384]{2,1,0:T(8,128)S(1)} %get-tuple-element.57), channel_id=1, source_target_pairs={{0,1},{1,2},{2,3},{4,5},{5,6},{6,7},{8,9},{9,10},{10,11},{12,13},{... | collective-permute-start | bytes 82952 | tf_op jit(solution)/shard_map/ppermute | solution.py:20
  54.8 3.0 %collective-permute-start.10 = (f32[2,3,2,8,128]{4,3,2,1,0:T(8,128)S(1)}, f32[2,3,2,8,128]{4,3,2,1,0:T(8,128)S(1)}, u32[]{:S(2)}, u32[]{:S(2)}) collective-permute-start(f32[2,3,2,8,128]{4,3,2,1,0:T(8,128)S(1)} %get-tuple-element.60), channel_id=1, source_target_pairs={{0,16},{1,17},{2,18},{3,19},{4,20},{5,21},{6,22},{7,23},{8,24},{9,... | collective-permute-start | bytes 147464 | tf_op jit(solution)/shard_map/ppermute | solution.py:20
  58.4 7.0 %collective-permute-start.11 = (f32[3,2,8,128]{3,2,1,0:T(8,128)S(1)}, f32[3,2,8,128]{3,2,1,0:T(8,128)S(1)}, u32[]{:S(2)}, u32[]{:S(2)}) collective-permute-start(f32[3,2,8,128]{3,2,1,0:T(8,128)S(1)} %get-tuple-element.61), channel_id=1, source_target_pairs={{16,0},{17,1},{18,2},{19,3},{20,4},{21,5},{22,6},{23,7},{24,8},{25... | collective-permute-start | bytes 73736 | tf_op jit(solution)/shard_map/ppermute | solution.py:20
  66.2 6.6 %collective-permute-start.12 = (f32[3,1,24,384]{3,2,1,0:T(8,128)S(1)}, f32[3,1,24,384]{3,2,1,0:T(8,128)S(1)}, u32[]{:S(2)}, u32[]{:S(2)}) collective-permute-start(f32[3,1,24,384]{3,2,1,0:T(8,128)S(1)} %get-tuple-element.63), channel_id=1, source_target_pairs={{4,0},{8,4},{12,8},{5,1},{9,5},{13,9},{6,2},{10,6},{14,10},{7,3},{... | collective-permute-start | bytes 331784 | tf_op jit(solution)/shard_map/ppermute | solution.py:20
  67.5 3.1 %collective-permute-start.13 = (f32[3,6,384]{2,1,0:T(8,128)S(1)}, f32[3,6,384]{2,1,0:T(8,128)S(1)}, u32[]{:S(2)}, u32[]{:S(2)}) collective-permute-start(f32[3,6,384]{2,1,0:T(8,128)S(1)} %get-tuple-element.64), channel_id=1, source_target_pairs={{1,0},{2,1},{3,2},{5,4},{6,5},{7,6},{9,8},{10,9},{11,10},{13,12},{... | collective-permute-start | bytes 82952 | tf_op jit(solution)/shard_map/ppermute | solution.py:20
  73.0 8.7 %collective-permute-start.14 = (f32[3,1,24,384]{3,2,1,0:T(8,128)S(1)}, f32[3,1,24,384]{3,2,1,0:T(8,128)S(1)}, u32[]{:S(2)}, u32[]{:S(2)}) collective-permute-start(f32[3,1,24,384]{3,2,1,0:T(8,128)S(1)} %get-tuple-element.67), channel_id=1, source_target_pairs={{0,4},{4,8},{8,12},{1,5},{5,9},{9,13},{2,6},{6,10},{10,14},{3,7},{... | collective-permute-start | bytes 331784 | tf_op jit(solution)/shard_map/ppermute | solution.py:20
  76.5 5.2 %collective-permute-start.15 = (f32[3,6,384]{2,1,0:T(8,128)S(1)}, f32[3,6,384]{2,1,0:T(8,128)S(1)}, u32[]{:S(2)}, u32[]{:S(2)}) collective-permute-start(f32[3,6,384]{2,1,0:T(8,128)S(1)} %get-tuple-element.68), channel_id=1, source_target_pairs={{0,1},{1,2},{2,3},{4,5},{5,6},{6,7},{8,9},{9,10},{10,11},{12,13},{... | collective-permute-start | bytes 82952 | tf_op jit(solution)/shard_map/ppermute | solution.py:20
  82.8 3.0 %collective-permute-start.16 = (f32[2,3,2,8,128]{4,3,2,1,0:T(8,128)S(1)}, f32[2,3,2,8,128]{4,3,2,1,0:T(8,128)S(1)}, u32[]{:S(2)}, u32[]{:S(2)}) collective-permute-start(f32[2,3,2,8,128]{4,3,2,1,0:T(8,128)S(1)} %get-tuple-element.72), channel_id=1, source_target_pairs={{0,16},{1,17},{2,18},{3,19},{4,20},{5,21},{6,22},{7,23},{8,24},{9,... | collective-permute-start | bytes 147464 | tf_op jit(solution)/shard_map/ppermute | solution.py:20
  86.4 7.2 %collective-permute-start.17 = (f32[3,2,8,128]{3,2,1,0:T(8,128)S(1)}, f32[3,2,8,128]{3,2,1,0:T(8,128)S(1)}, u32[]{:S(2)}, u32[]{:S(2)}) collective-permute-start(f32[3,2,8,128]{3,2,1,0:T(8,128)S(1)} %get-tuple-element.74), channel_id=1, source_target_pairs={{16,0},{17,1},{18,2},{19,3},{20,4},{21,5},{22,6},{23,7},{24,8},{25... | collective-permute-start | bytes 73736 | tf_op jit(solution)/shard_map/ppermute | solution.py:20

commit v2 on v1

--- a/solution.py
+++ b/solution.py
@@ -121,45 +121,163 @@
     )
 
 
-def magnetic_kernel(slab_e, slab_h, next_x, next_y, out_h, last_x, last_y):
+def row_pair(sub):
+    y0 = sub[0, 0, 1]
+    base = pl.multiple_of(8 * jnp.minimum(y0 // 8, 1), 8)
+    return base, y0 - base
+
+
+def neighbour(da, db):
+    a, b = lax.axis_index("gx") + da, lax.axis_index("gy") + db
+    na, nb = lax.axis_size("gx"), lax.axis_size("gy")
+    there = (a >= 0) & (a < na) & (b >= 0) & (b < nb)
+    return there, jnp.clip(a, 0, na - 1) * nb + jnp.clip(b, 0, nb - 1)
+
+
+def lay_over(wide, boxes, subs, da, db, kinds):
+    there, block = neighbour(da, db)
+    x0, y0, z0, lx, ly, lz = (subs[block, 0, k] for k in range(6))
+    if da == 1:
+        there = there & (x0 == 0)
+    if da == -1:
+        there = there & (x0 + lx == 6)
+    if db == 1:
+        there = there & (y0 == 0)
+    if db == -1:
+        there = there & (y0 + ly == 24)
+
+    @pl.when(there)
+    def _():
+        base = pl.multiple_of(8 * jnp.minimum(y0 // 8, 1), 8)
+        over = y0 - base
+        row = rows((16, 128)) - over
+        for a in range(3):
+            index = (lanes() + (128 * a) - z0) & 127
+            place = lanes((16, 128)) + (128 * a) - z0
+            flat = (place >= 0) & (place < lz) & (row >= 0) & (row < ly)
+            for i in range(2):
+                covered = flat & (i < lx)
+                for c in kinds:
+                    spot = (
+                        c,
+                        6 + 6 * da + x0 + i,
+                        pl.ds(24 + 24 * db + base, 16),
+                        pl.ds(128 * a, 128),
+                    )
+                    tile = gather(boxes[block, c, i], index)
+                    pair = pltpu.roll(jnp.concatenate([tile, tile]), over, 0)
+                    wide[spot] = jnp.where(covered, pair, wide[spot])
+
+
+def step_kernel(with_boxes, *refs):
+    slab_e, slab_h, slab_p, coef, ax, ay, bx, by, d1, d2, sub = refs[:11]
+    refs = refs[11:]
+    if with_boxes:
+        boxes, subs = refs[:2]
+        refs = refs[2:]
+    out_e, out_h, out_p, sent, oax, oay, obx, oby, od1, od2, wide = refs
     coarse = lax.axis_index("grid") == 0
 
     @pl.when(coarse)
     def _():
         row, lane = rows((24, 384)), lanes((24, 384))
+        edge_lane = lanes((1, 384))
+        own = pl.ds(24, 24)
+        for c in range(3):
+            for x in range(6):
+                wide[c, 6 + x, own] = slab_e[c, x]
+                wide[c, 6 + x, 23:24] = by[c, x : x + 1]
+            wide[c, 5, own] = bx[c]
+        for k, c in enumerate((1, 2)):
+            wide[c, 12, own] = ax[k]
+        for k, c in enumerate((0, 2)):
+            for x in range(6):
+                wide[c, 6 + x, 48:49] = ay[k, x : x + 1]
+        wide[0, 5, 48:49] = d1[...]
+        wide[1, 12, 23:24] = d2[...]
+        if with_boxes:
+            lay_over(wide, boxes, subs, 0, 0, (0, 1, 2))
+            lay_over(wide, boxes, subs, 1, 0, (1, 2))
+            lay_over(wide, boxes, subs, 0, 1, (0, 2))
+            lay_over(wide, boxes, subs, -1, 0, (0, 1, 2))
+            lay_over(wide, boxes, subs, 0, -1, (0, 1, 2))
+            lay_over(wide, boxes, subs, -1, 1, (0,))
+            lay_over(wide, boxes, subs, 1, -1, (1,))
+
+        cut = region_of(wide, sub, 6, 24)
+        for c in range(3):
+            for i in range(2):
+                sent[0, c, i] = cut(c, i)
 
         def ahead_y(value, edge):
             return jnp.where(row == 23, edge, pltpu.roll(value, 23, 0))
 
         def ahead_z(value):
-            return jnp.where(lane == 383, 0.0, pltpu.roll(value, 383, 1))
-
+            last = lanes(value.shape) == 383
+            return jnp.where(last, 0.0, pltpu.roll(value, 383, 1))
+
+        def behind_y(value, edge):
+            return jnp.where(row == 0, edge, pltpu.roll(value, 1, 0))
+
+        def behind_z(value):
+            return jnp.where(lane == 0, 0.0, pltpu.roll(value, 1, 1))
+
+        has_x = (lax.axis_index("gx") > 0).astype(F32)
+        has_y = (lax.axis_index("gy") > 0).astype(F32)
+        ex, ey, ez = (wide[c, 5, own] for c in range(3))
+        hy_b = bx[3] - 0.5 * ((ahead_z(ex) - ex) - (wide[2, 6, own] - ez))
+        hz_b = bx[4] - 0.5 * ((wide[1, 6, own] - ey) - (ahead_y(ex, wide[0, 5, 48:49]) - ex))
+        hy_b, hz_b = hy_b * has_x, hz_b * has_x
         for x in range(6):
-            ex, ey, ez = (slab_e[c, x] for c in range(3))
-            if x < 5:
-                ey_x, ez_x = slab_e[1, x + 1], slab_e[2, x + 1]
-            else:
-                ey_x, ez_x = next_x[1, 0], next_x[2, 0]
-            ex_y = ahead_y(ex, next_y[0, x : x + 1])
-            ez_y = ahead_y(ez, next_y[2, x : x + 1])
+            ex, ey, ez = (wide[c, 6 + x, own] for c in range(3))
+            ey_x, ez_x = wide[1, 7 + x, own], wide[2, 7 + x, own]
+            ex_y = ahead_y(ex, wide[0, 6 + x, 48:49])
+            ez_y = ahead_y(ez, wide[2, 6 + x, 48:49])
             ex_z, ey_z = ahead_z(ex), ahead_z(ey)
             hx = slab_h[0, x] - 0.5 * ((ez_y - ez) - (ey_z - ey))
             hy = slab_h[1, x] - 0.5 * ((ex_z - ex) - (ez_x - ez))
             hz = slab_h[2, x] - 0.5 * ((ey_x - ey) - (ex_y - ex))
-            for c, value in enumerate((hx, hy, hz)):
-                out_h[c, x] = value
-                last_y[c, x : x + 1] = value[23:24]
+            out_h[0, x], out_h[1, x], out_h[2, x] = hx, hy, hz
+            ex_r, ey_r, ez_r = (wide[c, 6 + x, 23:24] for c in range(3))
+            hx_r = by[3, x : x + 1] - 0.5 * ((ez[0:1] - ez_r) - (ahead_z(ey_r) - ey_r))
+            hz_r = by[4, x : x + 1] - 0.5 * ((wide[1, 7 + x, 23:24] - ey_r) - (ex[0:1] - ex_r))
+            hx_y = behind_y(hx, hx_r * has_y)
+            hz_y = behind_y(hz, hz_r * has_y)
+            hx_z, hy_z = behind_z(hx), behind_z(hy)
+            rotation = (
+                (hz - hz_y) - (hy - hy_z),
+                (hx - hx_z) - (hz - hz_b),
+                (hy - hy_b) - (hx - hx_y),
+            )
+            hy_b, hz_b = hy, hz
+            a, b, p, f3, g = (whole(coef, k, x) for k in range(5))
+            for c, old_e in enumerate((ex, ey, ez)):
+                old = slab_p[c, x]
+                new = a * old_e + b * rotation[c] + p * old
+                out_e[c, x] = new
+                out_p[c, x] = f3 * old + g * new
                 if x == 5:
-                    last_x[c, 0] = value
-
-
-def row_pair(sub):
-    y0 = sub[0, 0, 1]
-    base = pl.multiple_of(8 * jnp.minimum(y0 // 8, 1), 8)
-    return base, y0 - base
-
-
-def region_of(slab, sub):
+                    obx[c] = new
+                if x == 0 and c > 0:
+                    oax[c - 1] = new
+                oby[c, x : x + 1] = new[23:24]
+                if c != 1:
+                    oay[c // 2, x : x + 1] = new[0:1]
+                if c == 0 and x == 5:
+                    od1[...] = new[0:1]
+                if c == 1 and x == 0:
+                    od2[...] = new[23:24]
+            oby[3, x : x + 1] = hx[23:24]
+            oby[4, x : x + 1] = hz[23:24]
+            if x == 5:
+                obx[3], obx[4] = hy, hz
+        cut = region_of(out_e, sub, 0, 0)
+        for c in range(3):
+            for i in range(2):
+                sent[1, c, i] = cut(c, i)
+
+
+def region_of(slab, sub, x_base, y_base):
     x0, z0 = sub[0, 0, 0], sub[0, 0, 2]
     base, over = row_pair(sub)
     place = lanes() + z0
@@ -168,54 +286,11 @@
     def cut(c, i):
         tiles = []
         for a in range(3):
-            pair = slab[c, x0 + i, pl.ds(base, 16), pl.ds(128 * a, 128)]
+            pair = slab[c, x_base + x0 + i, pl.ds(y_base + base, 16), pl.ds(128 * a, 128)]
             tiles.append(gather(pltpu.roll(pair, (16 - over) & 15, 0)[0:8], index))
         return jnp.where(part == 0, tiles[0], jnp.where(part == 1, tiles[1], tiles[2]))
 
     return cut
-
-
-def electric_kernel(slab_e, slab_h, slab_p, coef, prev_x, prev_y, sub, out_e, out_p, sent):
-    coarse = lax.axis_index("grid") == 0
-
-    @pl.when(coarse)
-    def _():
-        row, lane = rows((24, 384)), lanes((24, 384))
-        cut = region_of(slab_e, sub)
-        for c in range(3):
-            for i in range(2):
-                sent[0, c, i] = cut(c, i)
-
-        def behind_y(value, edge):
-            return jnp.where(row == 0, edge, pltpu.roll(value, 1, 0))
-
-        def behind_z(value):
-            return jnp.where(lane == 0, 0.0, pltpu.roll(value, 1, 1))
-
-        for x in range(6):
-            hx, hy, hz = (slab_h[c, x] for c in range(3))
-            if x > 0:
-                hy_x, hz_x = slab_h[1, x - 1], slab_h[2, x - 1]
-            else:
-                hy_x, hz_x = prev_x[1, 0], prev_x[2, 0]
-            hx_y = behind_y(hx, prev_y[0, x : x + 1])
-            hz_y = behind_y(hz, prev_y[2, x : x + 1])
-            hx_z, hy_z = behind_z(hx), behind_z(hy)
-            rotation = (
-                (hz - hz_y) - (hy - hy_z),
-                (hx - hx_z) - (hz - hz_x),
-                (hy - hy_x) - (hx - hx_y),
-            )
-            a, b, p, f3, g = (whole(coef, k, x) for k in range(5))
-            for c in range(3):
-                old = slab_p[c, x]
-                new = a * slab_e[c, x] + b * rotation[c] + p * old
-                out_e[c, x] = new
-                out_p[c, x] = f3 * old + g * new
-        cut = region_of(out_e, sub)
-        for c in range(3):
-            for i in range(2):
-                sent[1, c, i] = cut(c, i)
 
 
 def put_back(slab, received, sub):
@@ -234,19 +309,6 @@
                 tile = gather(received[c, i], index)
                 pair = pltpu.roll(jnp.concatenate([tile, tile]), over, 0)
                 slab[spot] = jnp.where(covered, pair, slab[spot])
-
-
-def overwrite_kernel(slab_e, received, sub, slab, first_x, first_y):
-    coarse = lax.axis_index("grid") == 0
-
-    @pl.when(coarse)
-    def _():
-        slab[...] = slab_e[...]
-        put_back(slab, received, sub)
-        for c in range(3):
-            first_x[c, 0] = slab[c, 0]
-            for x in range(6):
-                first_y[c, x : x + 1] = slab[c, x, 0:1]
 
 
 def fine_kernel(box_in, coef, region, sub, box, restricted):
@@ -406,13 +468,34 @@
 BOX = (9, 6, 9, 8, 128)
 COEF = (5, 6, 9, 8, 128)
 REGION = (3, 2, 8, 128)
-X_EDGE = (3, 1, 24, 384)
-Y_EDGE = (3, 6, 384)
+EDGES = [(2, 24, 384), (2, 6, 384), (5, 24, 384), (5, 6, 384), (1, 384), (1, 384)]
+WAYS = [(-1, 0), (0, -1), (1, 0), (0, 1), (1, -1), (-1, 1)]
+AXES = ("grid", "gx", "gy")
+
+
+def between_coarse(value, da, db):
+    na, nb = lax.axis_size("gx"), lax.axis_size("gy")
+    pairs = [
+        (a * nb + b, (a + da) * nb + b + db)
+        for a in range(na)
+        for b in range(nb)
+        if 0 <= a + da < na and 0 <= b + db < nb
+    ]
+    return lax.ppermute(value, AXES, pairs)
 
 
 def body(fields, material, permittivity, conductivity, relax_rate, debye_strength, subgrids):
-    first_x = fields[0, 0:3, 0:1]
-    first_y = fields[0, 0:3, :, 0]
+    blocks = lax.axis_size("gx") * lax.axis_size("gy")
+    subs = lax.all_gather(subgrids[0], ("gx", "gy"))
+    f = fields[0]
+    edges = [
+        f[1:3, 0],
+        f[0:3:2, :, 0],
+        jnp.concatenate([f[0:3, 5], f[4:6, 5]]),
+        jnp.concatenate([f[0:4, :, 23], f[5:6, :, 23]]),
+        f[0, 5, 0:1],
+        f[1, 0, 23:24],
+    ]
     slab_e, slab_h, slab_p, box, coef = call(
         prep_kernel,
         (fields,) * 3
@@ -424,35 +507,24 @@
         [PART] * 3 + [BOX, COEF],
         grid=(1,),
     )
+    boxes = None
     for number in range(COARSE_STEPS):
-        next_x = shifted(first_x, "gx", -1)
-        next_y = shifted(first_y, "gy", -1)
-        slab_h, last_x, last_y = call(
-            magnetic_kernel,
-            (slab_e, slab_h, next_x, next_y),
-            [VM] * 4,
-            [PART, X_EDGE, Y_EDGE],
-        )
-        prev_x = shifted(last_x, "gx", 1)
-        prev_y = shifted(last_y, "gy", 1)
-        slab_e, slab_p, sent = call(
-            electric_kernel,
-            (slab_e, slab_h, slab_p, coef, prev_x, prev_y, subgrids),
-            [VM] * 6 + [SM],
-            [PART, PART, (2, *REGION)],
+        edges = [between_coarse(edge, *way) for edge, way in zip(edges, WAYS)]
+        extra = () if number == 0 else (boxes, subs)
+        slab_e, slab_h, slab_p, sent, *edges = call(
+            functools.partial(step_kernel, number > 0),
+            (slab_e, slab_h, slab_p, coef, *edges, subgrids, *extra),
+            [VM] * 10 + [SM] + [VM, SM][: len(extra)],
+            [PART] * 3 + [(2, *REGION)] + EDGES,
+            scratch=[pltpu.VMEM((3, 18, 72, 384), F32)],
         )
         region = shifted(sent, "grid", 1)
         box, restricted = call(
             fine_kernel, (box, coef, region, subgrids), [VM] * 3 + [SM], [BOX, REGION]
         )
-        received = shifted(restricted, "grid", -1)
         if number < COARSE_STEPS - 1:
-            slab_e, first_x, first_y = call(
-                overwrite_kernel,
-                (slab_e, received, subgrids),
-                [VM] * 2 + [SM],
-                [PART, X_EDGE, Y_EDGE],
-            )
+            boxes = lax.all_gather(restricted, AXES)[blocks:]
+    received = shifted(restricted, "grid", -1)
     (out,) = call(
         finish_kernel,
         (slab_e, slab_h, slab_p, box, received, subgrids),

time: 96.6 us -> 180 us (1.86)
  blocking collectives: 0 us -> 111 us
  waiting for transfers between devices: 33.8 us -> 9.9 us
  local copies, waits for them, and re-layouts: 7.63 us -> 2.58 us
    all_gather x0 -> x3, blocking collectives: none -> 111 us  [the longest x2 83.5 us: body(): boxes = lax.all_gather(restricted, AXES)[blocks:]]
    ppermute x18 -> x4, starting transfers between devices: 43.8 us -> 5.16 us  [shifted(): return lax.ppermute(value, axis, pairs)]
    ppermute x0 -> x18, starting transfers between devices: none -> 38.6 us  [between_coarse(): return lax.ppermute(value, AXES, pairs)]
    ppermute x18 -> x4, waiting for transfers between devices: 33.8 us -> 7.79 us  [shifted(): return lax.ppermute(value, axis, pairs)]
    unnamed x17 -> x18, local copies, waits for them, and re-layouts: 5.77 us -> 2.25 us
    ppermute x0 -> x18, waiting for transfers between devices: none -> 2.11 us  [between_coarse(): return lax.ppermute(value, AXES, pairs)]
    pallas_call x13 -> x8, Pallas kernels: 10.1 us -> 11 us  [call(): pl.pallas_call(kernel, out_shape=[jax.ShapeDtypeStruct(shape, F32) for sh...]
  transfers between devices with their start and end apart: 18 -> 22, of which waited for: 13 -> 3; matrix products, arithmetic and copies ran while one was open for 1% -> 0% of each run, Pallas kernels for 1% -> 1%
where the time goes in v2:
time: 180 us; the launch traced here: 179 us
  blocking collectives  111 us (62%)
  starting transfers between devices  43.8 us (24%)
  Pallas kernels  11 us (6%)
  waiting for transfers between devices  9.9 us (6%)
  local copies, waits for them, and re-layouts  2.58 us (1%)
    all_gather x2, blocking collectives, body(): boxes = lax.all_gather(restricted, AXES)[blocks:]  83.5 us
    ppermute x18, starting transfers between devices, between_coarse(): return lax.ppermute(value, AXES, pairs)  38.6 us
    all_gather x1, blocking collectives, body(): subs = lax.all_gather(subgrids[0], ('gx', 'gy'))  27.9 us
    pallas_call x8, Pallas kernels, call(): pl.pallas_call(kernel, out_shape=[jax.ShapeDtypeStruct(shape, F32) for sh...  11 us
    ppermute x4, waiting for transfers between devices, shifted(): return lax.ppermute(value, axis, pairs)  7.79 us
    ppermute x4, starting transfers between devices, shifted(): return lax.ppermute(value, axis, pairs)  5.16 us
  transfers between devices with their start and end apart: 22, of which 3 were waited for; matrix products, arithmetic and copies ran while one was open for 0% of the time, Pallas kernels for 1%

profile of v2, /device:TPU:0, one launch (start us, length us, event | category | flops | bytes accessed | tf_op | source)
XLA Modules:
  0.0 179.3 jit_solution(4591100904546033947)
XLA Ops:
  0.0 2.2 %copy.17 = f32[1,9,6,24,384]{4,2,3,1,0:T(8,128)S(1)} copy(f32[1,9,6,24,384]{4,3,2,1,0:T(8,128)} %f2.1) | data formatting | bytes 3981312 | tf_op args[0]
  2.3 1.3 collective-permute-start.1
  3.6 3.0 %collective-permute-start.3 = (f32[5,6,384]{2,1,0:T(8,128)S(1)}, f32[5,6,384]{2,1,0:T(8,128)S(1)}, u32[]{:S(2)}, u32[]{:S(2)}) collective-permute-start(f32[5,6,384]{2,1,0:T(8,128)S(1)} %pad_maximum_fusion.1), channel_id=1, source_target_pairs={{0,1},{1,2},{2,3},{4,5},{5,6},{6,7},{8,9},{9,10},{10,11},{12,13},{... | collective-permute-start | bytes 138248 | tf_op jit(solution)/shard_map/ppermute | solution.py:484
  6.6 0.1 fusion
  6.8 1.3 collective-permute-start
  8.1 0.1 slice.43
  8.3 5.6 %collective-permute-start.2 = (f32[5,24,384]{2,1,0:T(8,128)S(1)}, f32[5,24,384]{2,1,0:T(8,128)S(1)}, u32[]{:S(2)}, u32[]{:S(2)}) collective-permute-start(f32[5,24,384]{2,1,0:T(8,128)S(1)} %pad_maximum_fusion), channel_id=1, source_target_pairs={{0,4},{1,5},{2,6},{3,7},{4,8},{5,9},{6,10},{7,11},{8,12},{9,13},{1... | collective-permute-start | bytes 552968 | tf_op jit(solution)/shard_map/ppermute | solution.py:484
  13.9 0.7 collective-permute-start.5
  14.5 0.0 collective-permute-done.5.refs_9_
  14.6 0.7 collective-permute-start.4
  15.3 1.1 shard_map.73
  16.5 0.0 collective-permute-done.3.refs_7_
  16.5 0.0 collective-permute-done.refs_4_
  16.5 2.1 %collective-permute-done.2.refs_6_ = f32[5,24,384]{2,1,0:T(8,128)S(1)} collective-permute-done((f32[5,24,384]{2,1,0:T(8,128)S(1)}, f32[5,24,384]{2,1,0:T(8,128)S(1)}, u32[]{:S(2)}, u32[]{:S(2)}) %collective-permute-start.2) | collective-permute-done | bytes 184352 | tf_op jit(solution)/shard_map/ppermute | solution.py:484
  18.5 1.5 shard_map.74
  20.1 1.3 collective-permute-start.12
  21.4 0.7 collective-permute-start.10
  22.1 27.9 %all_gather.17.refs_12_ = s32[16,1,6]{2,1,0:T(1,128)S(1)} all-gather(s32[1,1,6]{2,1,0:T(1,128)S(1)} %copy-done.2), channel_id=1, replica_groups=mesh['grid'=2,'gx'=4,'gy'=4] {'gx','gy'}, dimensions={0}, use_global_device_ids=true | all-gather | bytes 408 | tf_op jit(solution)/shard_map/all_gather | solution.py:489
  50.0 0.6 collective-permute-start.11
  50.7 1.3 collective-permute-start.7
  52.0 3.5 %collective-permute-start.9 = (f32[5,6,384]{2,1,0:T(8,128)S(1)}, f32[5,6,384]{2,1,0:T(8,128)S(1)}, u32[]{:S(2)}, u32[]{:S(2)}) collective-permute-start(f32[5,6,384]{2,1,0:T(8,128)S(1)} %get-tuple-element.50), channel_id=1, source_target_pairs={{0,1},{1,2},{2,3},{4,5},{5,6},{6,7},{8,9},{9,10},{10,11},{12,13},{... | collective-permute-start | bytes 138248 | tf_op jit(solution)/shard_map/ppermute | solution.py:484
  55.4 1.3 collective-permute-start.6
  56.7 0.6 shard_map.75
  57.3 5.3 %collective-permute-start.8 = (f32[5,24,384]{2,1,0:T(8,128)S(1)}, f32[5,24,384]{2,1,0:T(8,128)S(1)}, u32[]{:S(2)}, u32[]{:S(2)}) collective-permute-start(f32[5,24,384]{2,1,0:T(8,128)S(1)} %get-tuple-element.49), channel_id=1, source_target_pairs={{0,4},{1,5},{2,6},{3,7},{4,8},{5,9},{6,10},{7,11},{8,12},{9,13},{1... | collective-permute-start | bytes 552968 | tf_op jit(solution)/shard_map/ppermute | solution.py:484
  62.6 41.7 %all-gather = f32[96,2,8,128]{3,2,1,0:T(8,128)S(1)} all-gather(f32[3,2,8,128]{3,2,1,0:T(8,128)S(1)} %get-tuple-element.55), channel_id=2, replica_groups=mesh['grid'=2,'gx'=4,'gy'=4] {'grid','gx','gy'}, dimensions={0}, use_global_device_ids=true | all-gather | bytes 811008 | tf_op jit(solution)/shard_map/all_gather | solution.py:526
  104.4 0.0 collective-permute-done.11.refs_9_
  104.4 0.0 collective-permute-done.7.refs_5_
  104.4 0.0 collective-permute-done.6.refs_4_
  104.4 0.0 collective-permute-done.8.refs_6_
  104.4 2.0 %shard_map.76 = (f32[3,6,24,384]{3,2,1,0:T(8,128)S(1)}, f32[3,6,24,384]{3,2,1,0:T(8,128)S(1)}, f32[3,6,24,384]{3,2,1,0:T(8,128)S(1)}, f32[2,3,2,8,128]{4,3,2,1,0...) custom-call(f32[3,6,24,384]{3,2,1,0:T(8,128)S(1)} %get-tuple-element, ...), custom_call_target="tpu_custom_call" | custom-call | tf_op jit(solution)/shard_map/pallas_call | solution.py:455
  106.4 1.3 collective-permute-start.19
  107.7 0.7 collective-permute-start.17
  108.4 0.7 collective-permute-start.18
  109.0 1.3 collective-permute-start.14
  110.3 4.2 %collective-permute-start.16 = (f32[5,6,384]{2,1,0:T(8,128)S(1)}, f32[5,6,384]{2,1,0:T(8,128)S(1)}, u32[]{:S(2)}, u32[]{:S(2)}) collective-permute-start(f32[5,6,384]{2,1,0:T(8,128)S(1)} %get-tuple-element.62), channel_id=1, source_target_pairs={{0,1},{1,2},{2,3},{4,5},{5,6},{6,7},{8,9},{9,10},{10,11},{12,13},{... | collective-permute-start | bytes 138248 | tf_op jit(solution)/shard_map/ppermute | solution.py:484
  114.6 1.3 collective-permute-start.13
  115.9 0.6 shard_map.77
  116.5 5.3 %collective-permute-start.15 = (f32[5,24,384]{2,1,0:T(8,128)S(1)}, f32[5,24,384]{2,1,0:T(8,128)S(1)}, u32[]{:S(2)}, u32[]{:S(2)}) collective-permute-start(f32[5,24,384]{2,1,0:T(8,128)S(1)} %get-tuple-element.61), channel_id=1, source_target_pairs={{0,4},{1,5},{2,6},{3,7},{4,8},{5,9},{6,10},{7,11},{8,12},{9,13},{1... | collective-permute-start | bytes 552968 | tf_op jit(solution)/shard_map/ppermute | solution.py:484
  121.7 41.8 %all-gather.1 = f32[96,2,8,128]{3,2,1,0:T(8,128)S(1)} all-gather(f32[3,2,8,128]{3,2,1,0:T(8,128)S(1)} %get-tuple-element.67), channel_id=3, replica_groups=mesh['grid'=2,'gx'=4,'gy'=4] {'grid','gx','gy'}, dimensions={0}, use_global_device_ids=true | all-gather | bytes 811008 | tf_op jit(solution)/shard_map/all_gather | solution.py:526
  163.6 0.0 collective-permute-done.14.refs_5_
  163.6 0.0 collective-permute-done.15.refs_6_
  163.6 2.7 %shard_map.78 = (f32[3,6,24,384]{3,2,1,0:T(8,128)S(1)}, f32[3,6,24,384]{3,2,1,0:T(8,128)S(1)}, f32[3,6,24,384]{3,2,1,0:T(8,128)S(1)}, f32[2,3,2,8,128]{4,3,2,1,0...) custom-call(f32[3,6,24,384]{3,2,1,0:T(8,128)S(1)} %get-tuple-element, ...), custom_call_target="tpu_custom_call" | custom-call | tf_op jit(solution)/shard_map/pallas_call | solution.py:455
  166.3 1.3 collective-permute-start.20
  167.6 1.9 %collective-permute-done.20.region = f32[2,3,2,8,128]{4,3,2,1,0:T(8,128)S(1)} collective-permute-done((f32[2,3,2,8,128]{4,3,2,1,0:T(8,128)S(1)}, f32[2,3,2,8,128]{4,3,2,1,0:T(8,128)S(1)}, u32[]{:S(2)}, u32[]{:S(2)}) %collective-permute-start.20) | collective-permute-done | bytes 49184 | tf_op jit(solution)/shard_map/ppermute | solution.py:20
  169.5 0.6 shard_map.79
  170.0 1.3 collective-permute-start.21
  171.3 5.9 %collective-permute-done.21.received = f32[3,2,8,128]{3,2,1,0:T(8,128)S(1)} collective-permute-done((f32[3,2,8,128]{3,2,1,0:T(8,128)S(1)}, f32[3,2,8,128]{3,2,1,0:T(8,128)S(1)}, u32[]{:S(2)}, u32[]{:S(2)}) %collective-permute-start.21) | collective-permute-done | bytes 24608 | tf_op jit(solution)/shard_map/ppermute | solution.py:20
  177.3 2.0 %shard_map.80 = f32[9,6,24,384]{3,2,1,0:T(8,128)} custom-call(f32[3,6,24,384]{3,2,1,0:T(8,128)S(1)} %get-tuple-element.68.slab_e, f32[3,6,24,384]{3,2,1,0:T(8,128)S(1)} %get-tuple-element.69.slab_h, f32[3,6,24,384]{3,2,1,0:T(8,128)S(1)} %get-tuple-element.70.slab_p, f32[9,6,9,8,128]{4,3,2,1,0:T(8,128)S(1)} %get-tuple-element.73.box, ...), custom_call_target="tpu_custom_call" | custom-call | tf_op jit(solution)/shard_map/pallas_call | solution.py:455
  (35 shorter events, 0.2 us)
Async XLA Ops:
  0.0 15.2 %copy-start.2 = (s32[1,1,6]{2,1,0:T(1,128)S(1)}, s32[1,1,6]{2,1,0:T(1,128)}, u32[]{:S(2)}) copy-start(s32[1,1,6]{2,1,0:T(1,128)} %sub.9) | copy-start | bytes 76
  0.0 15.2 %copy-start.6 = (f32[8]{0:T(128)S(1)}, f32[8]{0:T(128)}, u32[]{:S(2)}) copy-start(f32[8]{0:T(128)} %debye.1) | copy-start | bytes 100
  0.0 15.2 %copy-start.5 = (f32[8]{0:T(128)S(1)}, f32[8]{0:T(128)}, u32[]{:S(2)}) copy-start(f32[8]{0:T(128)} %relax.1) | copy-start | bytes 100
  0.0 15.2 %copy-start.4 = (f32[8]{0:T(128)S(1)}, f32[8]{0:T(128)}, u32[]{:S(2)}) copy-start(f32[8]{0:T(128)} %cond.1) | copy-start | bytes 100
  0.0 15.3 %copy-start.3 = (f32[8]{0:T(128)S(1)}, f32[8]{0:T(128)}, u32[]{:S(2)}) copy-start(f32[8]{0:T(128)} %perm.1) | copy-start | bytes 100
  0.0 15.3 %copy-start = (f32[1,9,6,24,384]{4,3,2,1,0:T(8,128)S(1)}, f32[1,9,6,24,384]{4,3,2,1,0:T(8,128)}, u32[]{:S(2)}) copy-start(f32[1,9,6,24,384]{4,3,2,1,0:T(8,128)} %f2.1) | copy-start | bytes 5971972
  0.0 15.3 %copy-start.1 = (s32[1,6,24,384]{3,2,1,0:T(8,128)S(1)}, s32[1,6,24,384]{3,2,1,0:T(8,128)}, u32[]{:S(2)}) copy-start(s32[1,6,24,384]{3,2,1,0:T(8,128)} %m2.1) | copy-start | bytes 663556
  2.3 14.2 %collective-permute-start.1 = (f32[2,6,384]{2,1,0:T(8,128)S(1)}, f32[2,6,384]{2,1,0:T(8,128)S(1)}, u32[]{:S(2)}, u32[]{:S(2)}) collective-permute-start(f32[2,6,384]{2,1,0:T(8,128)S(1)} %slice_bitcast_fusion.1), channel_id=1, source_target_pairs={{1,0},{2,1},{3,2},{5,4},{6,5},{7,6},{9,8},{10,9},{11,10},{13,12},{... | collective-permute-start | bytes 55304 | tf_op jit(solution)/shard_map/ppermute | solution.py:484
  3.6 12.9 %collective-permute-start.3 = (f32[5,6,384]{2,1,0:T(8,128)S(1)}, f32[5,6,384]{2,1,0:T(8,128)S(1)}, u32[]{:S(2)}, u32[]{:S(2)}) collective-permute-start(f32[5,6,384]{2,1,0:T(8,128)S(1)} %pad_maximum_fusion.1), channel_id=1, source_target_pairs={{0,1},{1,2},{2,3},{4,5},{5,6},{6,7},{8,9},{9,10},{10,11},{12,13},{... | collective-permute-start | bytes 138248 | tf_op jit(solution)/shard_map/ppermute | solution.py:484
  6.8 9.7 %collective-permute-start = (f32[2,24,384]{2,1,0:T(8,128)S(1)}, f32[2,24,384]{2,1,0:T(8,128)S(1)}, u32[]{:S(2)}, u32[]{:S(2)}) collective-permute-start(f32[2,24,384]{2,1,0:T(8,128)S(1)} %bitcast.35), channel_id=1, source_target_pairs={{4,0},{5,1},{6,2},{7,3},{8,4},{9,5},{10,6},{11,7},{12,8},{13,9},{1... | collective-permute-start | bytes 221192 | tf_op jit(solution)/shard_map/ppermute | solution.py:484
  8.3 10.3 %collective-permute-start.2 = (f32[5,24,384]{2,1,0:T(8,128)S(1)}, f32[5,24,384]{2,1,0:T(8,128)S(1)}, u32[]{:S(2)}, u32[]{:S(2)}) collective-permute-start(f32[5,24,384]{2,1,0:T(8,128)S(1)} %pad_maximum_fusion), channel_id=1, source_target_pairs={{0,4},{1,5},{2,6},{3,7},{4,8},{5,9},{6,10},{7,11},{8,12},{9,13},{1... | collective-permute-start | bytes 552968 | tf_op jit(solution)/shard_map/ppermute | solution.py:484
  13.9 0.7 collective-permute-start.5
  14.6 1.9 %collective-permute-start.4 = (f32[1,384]{1,0:T(1,128)S(1)}, f32[1,384]{1,0:T(1,128)S(1)}, u32[]{:S(2)}, u32[]{:S(2)}) collective-permute-start(f32[1,384]{1,0:T(1,128)S(1)} %get-tuple-element.76), channel_id=1, source_target_pairs={{1,4},{2,5},{3,6},{5,8},{6,9},{7,10},{9,12},{10,13},{11,14}} | collective-permute-start | bytes 4616 | tf_op jit(solution)/shard_map/ppermute | solution.py:484
  20.1 35.4 %collective-permute-start.12 = (f32[2,3,2,8,128]{4,3,2,1,0:T(8,128)S(1)}, f32[2,3,2,8,128]{4,3,2,1,0:T(8,128)S(1)}, u32[]{:S(2)}, u32[]{:S(2)}) collective-permute-start(f32[2,3,2,8,128]{4,3,2,1,0:T(8,128)S(1)} %get-tuple-element.54), channel_id=1, source_target_pairs={{0,16},{1,17},{2,18},{3,19},{4,20},{5,21},{6,22},{7,23},{8,24},{9,... | collective-permute-start | bytes 147464 | tf_op jit(solution)/shard_map/ppermute | solution.py:20
  21.4 35.9 %collective-permute-start.10 = (f32[1,384]{1,0:T(1,128)S(1)}, f32[1,384]{1,0:T(1,128)S(1)}, u32[]{:S(2)}, u32[]{:S(2)}) collective-permute-start(f32[1,384]{1,0:T(1,128)S(1)} %get-tuple-element.51), channel_id=1, source_target_pairs={{1,4},{2,5},{3,6},{5,8},{6,9},{7,10},{9,12},{10,13},{11,14}} | collective-permute-start | bytes 4616 | tf_op jit(solution)/shard_map/ppermute | solution.py:484
  50.0 54.4 %collective-permute-start.11 = (f32[1,384]{1,0:T(1,128)S(1)}, f32[1,384]{1,0:T(1,128)S(1)}, u32[]{:S(2)}, u32[]{:S(2)}) collective-permute-start(f32[1,384]{1,0:T(1,128)S(1)} %get-tuple-element.52), channel_id=1, source_target_pairs={{4,1},{5,2},{6,3},{8,5},{9,6},{10,7},{12,9},{13,10},{14,11}} | collective-permute-start | bytes 4616 | tf_op jit(solution)/shard_map/ppermute | solution.py:484
  50.7 53.7 %collective-permute-start.7 = (f32[2,6,384]{2,1,0:T(8,128)S(1)}, f32[2,6,384]{2,1,0:T(8,128)S(1)}, u32[]{:S(2)}, u32[]{:S(2)}) collective-permute-start(f32[2,6,384]{2,1,0:T(8,128)S(1)} %get-tuple-element.48), channel_id=1, source_target_pairs={{1,0},{2,1},{3,2},{5,4},{6,5},{7,6},{9,8},{10,9},{11,10},{13,12},{... | collective-permute-start | bytes 55304 | tf_op jit(solution)/shard_map/ppermute | solution.py:484
  52.0 52.4 %collective-permute-start.9 = (f32[5,6,384]{2,1,0:T(8,128)S(1)}, f32[5,6,384]{2,1,0:T(8,128)S(1)}, u32[]{:S(2)}, u32[]{:S(2)}) collective-permute-start(f32[5,6,384]{2,1,0:T(8,128)S(1)} %get-tuple-element.50), channel_id=1, source_target_pairs={{0,1},{1,2},{2,3},{4,5},{5,6},{6,7},{8,9},{9,10},{10,11},{12,13},{... | collective-permute-start | bytes 138248 | tf_op jit(solution)/shard_map/ppermute | solution.py:484
  55.4 48.9 %collective-permute-start.6 = (f32[2,24,384]{2,1,0:T(8,128)S(1)}, f32[2,24,384]{2,1,0:T(8,128)S(1)}, u32[]{:S(2)}, u32[]{:S(2)}) collective-permute-start(f32[2,24,384]{2,1,0:T(8,128)S(1)} %get-tuple-element.47), channel_id=1, source_target_pairs={{4,0},{5,1},{6,2},{7,3},{8,4},{9,5},{10,6},{11,7},{12,8},{13,9},{1... | collective-permute-start | bytes 221192 | tf_op jit(solution)/shard_map/ppermute | solution.py:484
  57.3 47.1 %collective-permute-start.8 = (f32[5,24,384]{2,1,0:T(8,128)S(1)}, f32[5,24,384]{2,1,0:T(8,128)S(1)}, u32[]{:S(2)}, u32[]{:S(2)}) collective-permute-start(f32[5,24,384]{2,1,0:T(8,128)S(1)} %get-tuple-element.49), channel_id=1, source_target_pairs={{0,4},{1,5},{2,6},{3,7},{4,8},{5,9},{6,10},{7,11},{8,12},{9,13},{1... | collective-permute-start | bytes 552968 | tf_op jit(solution)/shard_map/ppermute | solution.py:484
  106.4 8.2 %collective-permute-start.19 = (f32[2,3,2,8,128]{4,3,2,1,0:T(8,128)S(1)}, f32[2,3,2,8,128]{4,3,2,1,0:T(8,128)S(1)}, u32[]{:S(2)}, u32[]{:S(2)}) collective-permute-start(f32[2,3,2,8,128]{4,3,2,1,0:T(8,128)S(1)} %get-tuple-element.66), channel_id=1, source_target_pairs={{0,16},{1,17},{2,18},{3,19},{4,20},{5,21},{6,22},{7,23},{8,24},{9,... | collective-permute-start | bytes 147464 | tf_op jit(solution)/shard_map/ppermute | solution.py:20
  107.7 8.8 %collective-permute-start.17 = (f32[1,384]{1,0:T(1,128)S(1)}, f32[1,384]{1,0:T(1,128)S(1)}, u32[]{:S(2)}, u32[]{:S(2)}) collective-permute-start(f32[1,384]{1,0:T(1,128)S(1)} %get-tuple-element.63), channel_id=1, source_target_pairs={{1,4},{2,5},{3,6},{5,8},{6,9},{7,10},{9,12},{10,13},{11,14}} | collective-permute-start | bytes 4616 | tf_op jit(solution)/shard_map/ppermute | solution.py:484
  108.4 55.2 %collective-permute-start.18 = (f32[1,384]{1,0:T(1,128)S(1)}, f32[1,384]{1,0:T(1,128)S(1)}, u32[]{:S(2)}, u32[]{:S(2)}) collective-permute-start(f32[1,384]{1,0:T(1,128)S(1)} %get-tuple-element.64), channel_id=1, source_target_pairs={{4,1},{5,2},{6,3},{8,5},{9,6},{10,7},{12,9},{13,10},{14,11}} | collective-permute-start | bytes 4616 | tf_op jit(solution)/shard_map/ppermute | solution.py:484
  109.0 54.6 %collective-permute-start.14 = (f32[2,6,384]{2,1,0:T(8,128)S(1)}, f32[2,6,384]{2,1,0:T(8,128)S(1)}, u32[]{:S(2)}, u32[]{:S(2)}) collective-permute-start(f32[2,6,384]{2,1,0:T(8,128)S(1)} %get-tuple-element.60), channel_id=1, source_target_pairs={{1,0},{2,1},{3,2},{5,4},{6,5},{7,6},{9,8},{10,9},{11,10},{13,12},{... | collective-permute-start | bytes 55304 | tf_op jit(solution)/shard_map/ppermute | solution.py:484
  110.3 53.3 %collective-permute-start.16 = (f32[5,6,384]{2,1,0:T(8,128)S(1)}, f32[5,6,384]{2,1,0:T(8,128)S(1)}, u32[]{:S(2)}, u32[]{:S(2)}) collective-permute-start(f32[5,6,384]{2,1,0:T(8,128)S(1)} %get-tuple-element.62), channel_id=1, source_target_pairs={{0,1},{1,2},{2,3},{4,5},{5,6},{6,7},{8,9},{9,10},{10,11},{12,13},{... | collective-permute-start | bytes 138248 | tf_op jit(solution)/shard_map/ppermute | solution.py:484
  114.6 49.0 %collective-permute-start.13 = (f32[2,24,384]{2,1,0:T(8,128)S(1)}, f32[2,24,384]{2,1,0:T(8,128)S(1)}, u32[]{:S(2)}, u32[]{:S(2)}) collective-permute-start(f32[2,24,384]{2,1,0:T(8,128)S(1)} %get-tuple-element.59), channel_id=1, source_target_pairs={{4,0},{5,1},{6,2},{7,3},{8,4},{9,5},{10,6},{11,7},{12,8},{13,9},{1... | collective-permute-start | bytes 221192 | tf_op jit(solution)/shard_map/ppermute | solution.py:484
  116.5 47.2 %collective-permute-start.15 = (f32[5,24,384]{2,1,0:T(8,128)S(1)}, f32[5,24,384]{2,1,0:T(8,128)S(1)}, u32[]{:S(2)}, u32[]{:S(2)}) collective-permute-start(f32[5,24,384]{2,1,0:T(8,128)S(1)} %get-tuple-element.61), channel_id=1, source_target_pairs={{0,4},{1,5},{2,6},{3,7},{4,8},{5,9},{6,10},{7,11},{8,12},{9,13},{1... | collective-permute-start | bytes 552968 | tf_op jit(solution)/shard_map/ppermute | solution.py:484
  166.3 3.2 %collective-permute-start.20 = (f32[2,3,2,8,128]{4,3,2,1,0:T(8,128)S(1)}, f32[2,3,2,8,128]{4,3,2,1,0:T(8,128)S(1)}, u32[]{:S(2)}, u32[]{:S(2)}) collective-permute-start(f32[2,3,2,8,128]{4,3,2,1,0:T(8,128)S(1)} %get-tuple-element.72), channel_id=1, source_target_pairs={{0,16},{1,17},{2,18},{3,19},{4,20},{5,21},{6,22},{7,23},{8,24},{9,... | collective-permute-start | bytes 147464 | tf_op jit(solution)/shard_map/ppermute | solution.py:20
  170.0 7.2 %collective-permute-start.21 = (f32[3,2,8,128]{3,2,1,0:T(8,128)S(1)}, f32[3,2,8,128]{3,2,1,0:T(8,128)S(1)}, u32[]{:S(2)}, u32[]{:S(2)}) collective-permute-start(f32[3,2,8,128]{3,2,1,0:T(8,128)S(1)} %get-tuple-element.74), channel_id=1, source_target_pairs={{16,0},{17,1},{18,2},{19,3},{20,4},{21,5},{22,6},{23,7},{24,8},{25... | collective-permute-start | bytes 73736 | tf_op jit(solution)/shard_map/ppermute | solution.py:20

commit v3 on v1

v3 whole, which is shorter than its diff:
```python
import functools

import jax
import jax.numpy as jnp
from jax import lax
from jax.experimental import pallas as pl
from jax.experimental.pallas import tpu as pltpu
from jax.sharding import PartitionSpec as P

COARSE_STEPS = 3
LIMIT = 40 * 1024 * 1024
VM = pl.BlockSpec(memory_space=pltpu.VMEM)
SM = pl.BlockSpec(memory_space=pltpu.SMEM)
F32 = jnp.float32


def shifted(value, axis, by):
    peers = lax.axis_size(axis)
    pairs = [(i, i + by) for i in range(peers) if 0 <= i + by < peers]
    return lax.ppermute(value, axis, pairs)


def lanes(shape=(8, 128)):
    return lax.broadcasted_iota(jnp.int32, shape, len(shape) - 1)


def rows(shape=(8, 128)):
    return lax.broadcasted_iota(jnp.int32, shape, len(shape) - 2)


def gather(tile, index):
    return jnp.take_along_axis(tile, index, axis=1)


def tables(perm, cond, relax, debye, factor):
    lane = lanes()

    def spread(ref):
        value = jnp.full((8, 128), ref[0], F32)
        for k in range(1, ref.shape[0]):
            value = jnp.where(lane == k, ref[k], value)
        return value

    eps = spread(perm)
    damp = spread(cond) * factor / (2.0 * eps)
    rate = spread(relax) * factor
    f0 = (1.0 - damp) / (1.0 + damp)
    f1 = 1.0 / (eps * (1.0 + damp))
    f3 = jnp.exp(-rate)
    f4 = spread(debye)
    c = f1 * rate
    return (f0 - c * f4, 0.5 * f1, c, f3, (1.0 - f3) * f4)


def to_tiles(parts):
    lane = lanes()
    kind = lane % 3
    out = []
    for t in range(3):
        mixed = jnp.where(
            kind == t, parts[0], jnp.where(kind == (t + 1) % 3, parts[1], parts[2])
        )
        out.append(gather(mixed, (3 * lane + t) & 127))
    return out


def from_tiles(tiles):
    lane = lanes()
    spread = [gather(tiles[t], (43 * (lane - t + 128)) & 127) for t in range(3)]
    out = []
    for a in range(3):
        kind = (2 * a + lane) % 3
        out.append(jnp.where(kind == 0, spread[0], jnp.where(kind == 1, spread[1], spread[2])))
    return out


def prep_kernel(f0, f1, f2, m0, m1, m2, perm, cond, relax, debye, sub, e, h, p, box, coef, desc, wide):
    coarse = lax.axis_index("grid") == 0
    fields, material = (f0, f1, f2), (m0, m1, m2)
    for k in range(6):
        desc[k] = jnp.full((8, 128), sub[0, 0, k], jnp.int32)

    @pl.when(coarse)
    def _():
        table = tables(perm, cond, relax, debye, 1.0)
        for x in range(6):
            for yt in range(3):
                for zt in range(3):
                    index = material[zt][0, x, pl.ds(8 * yt, 8)]
                    for k in range(5):
                        coef[k, x, 3 * yt + zt] = gather(table[k], index)
        for a in range(3):
            for k, part in enumerate((e, h, p)):
                part[:, :, :, pl.ds(128 * a, 128)] = fields[a][0, 3 * k : 3 * k + 3]

    @pl.when(jnp.logical_not(coarse))
    def _():
        for k, tile in enumerate(tables(perm, cond, relax, debye, 1.0)):
            wide[k] = tile
        table = tables(perm, cond, relax, debye, F32(1.0 / 3.0))
        row, lane = rows(), lanes()
        ly, lz = sub[0, 0, 4], sub[0, 0, 5]
        within = (row < ly) & (lane < lz)
        for x in range(6):
            inside = within & (x < 3 * sub[0, 0, 3])
            for u in range(3):
                cut = pl.ds(u, 8, stride=3)
                parts = [material[a][0, x, cut] for a in range(3)]
                for t, index in enumerate(to_tiles(parts)):
                    for k in range(5):
                        coef[k, x, 3 * u + t] = gather(table[k], index)
                for c in range(9):
                    parts = [fields[a][0, c, x, cut] for a in range(3)]
                    for t, tile in enumerate(to_tiles(parts)):
                        box[c, x, 3 * u + t] = jnp.where(inside, tile, 0.0)


def whole(ref, *index):
    return jnp.concatenate(
        [
            jnp.concatenate([ref[(*index, 3 * yt + zt)] for zt in range(3)], axis=1)
            for yt in range(3)
        ],
        axis=0,
    )


def magnetic(e, h, next_x, next_y, out):
    row, lane = rows((24, 384)), lanes((24, 384))

    def ahead_y(value, edge):
        return jnp.where(row == 23, edge, pltpu.roll(value, 23, 0))

    def ahead_z(value):
        return jnp.where(lane == 383, 0.0, pltpu.roll(value, 383, 1))

    for x in range(6):
        ex, ey, ez = (e[c, x] for c in range(3))
        if x < 5:
            ey_x, ez_x = e[1, x + 1], e[2, x + 1]
        else:
            ey_x, ez_x = next_x(0), next_x(1)
        ex_y = ahead_y(ex, next_y(0, x))
        ez_y = ahead_y(ez, next_y(1, x))
        ex_z, ey_z = ahead_z(ex), ahead_z(ey)
        turn = ((ez_y - ez) - (ey_z - ey), (ex_z - ex) - (ez_x - ez), (ey_x - ey) - (ex_y - ex))
        for c in range(3):
            if h is None:
                out[c, x] = -0.5 * turn[c]
            else:
                out[c, x] = h[c, x] - 0.5 * turn[c]


def last_layers(h, out_x, out_y):
    out_x[0], out_x[1] = h[1, 5], h[2, 5]
    for x in range(6):
        out_y[0, x : x + 1] = h[0, x, 23:24]
        out_y[1, x : x + 1] = h[2, x, 23:24]


def first_layers(e, out_x, out_y):
    out_x[0], out_x[1] = e[1, 0], e[2, 0]
    for x in range(6):
        out_y[0, x : x + 1] = e[0, x, 0:1]
        out_y[1, x : x + 1] = e[2, x, 0:1]


def curl_behind(h, x, prev_x, prev_y):
    row, lane = rows((24, 384)), lanes((24, 384))

    def behind_y(value, edge):
        return jnp.where(row == 0, edge, pltpu.roll(value, 1, 0))

    def behind_z(value):
        return jnp.where(lane == 0, 0.0, pltpu.roll(value, 1, 1))

    hx, hy, hz = (h[c, x] for c in range(3))
    if isinstance(x, int):
        hy_x, hz_x = (h[1, x - 1], h[2, x - 1]) if x > 0 else (prev_x(0), prev_x(1))
    else:
        before = jnp.maximum(x - 1, 0)
        first = jnp.full((24, 384), x, jnp.int32) == 0
        hy_x = jnp.where(first, prev_x(0), h[1, before])
        hz_x = jnp.where(first, prev_x(1), h[2, before])
    hx_y = behind_y(hx, prev_y(0, x))
    hz_y = behind_y(hz, prev_y(1, x))
    hx_z, hy_z = behind_z(hx), behind_z(hy)
    return ((hz - hz_y) - (hy - hy_z), (hx - hx_z) - (hz - hz_x), (hy - hy_x) - (hx - hx_y))


def electric(e, h, p, coef, prev_x, prev_y, out_e, out_p, more=None):
    for x in range(6):
        rotation = curl_behind(h, x, prev_x, prev_y)
        a, b, q, f3, g = (whole(coef, k, x) for k in range(5))
        for c in range(3):
            new = a * e[c, x] + b * rotation[c]
            old = None if p is None else p[c, x]
            if old is not None:
                new = new + q * old
            last = g * new if old is None else f3 * old + g * new
            if more is not None:
                new, last = new + more[0][c, x], last + more[1][c, x]
            out_e[c, x] = new
            out_p[c, x] = last


def edge_x(ref):
    return lambda k: ref[k]


def edge_y(ref):
    return lambda k, x: ref[k, pl.ds(x, 1)]


def corner(desc):
    x0 = jnp.max(desc[0].astype(F32)).astype(jnp.int32)
    y0 = jnp.max(desc[1].astype(F32)).astype(jnp.int32)
    base = pl.multiple_of(8 * jnp.minimum(y0 // 8, 1), 8)
    return x0, base, y0 - base


def cut_region(e, desc, spot):
    x0, base, over = spot
    place = lanes() + desc[2]
    index, part = place & 127, place >> 7

    def cut(c, i):
        tiles = []
        for a in range(3):
            pair = e[c, x0 + i, pl.ds(base, 16), pl.ds(128 * a, 128)]
            tiles.append(gather(pltpu.roll(pair, (16 - over) & 15, 0)[0:8], index))
        return jnp.where(part == 0, tiles[0], jnp.where(part == 1, tiles[1], tiles[2]))

    return [[cut(c, i) for i in range(2)] for c in range(3)]


def covered_of(desc):
    within = (rows() < desc[4]) & (lanes() < desc[5])
    return [within & (desc[3] > i) for i in range(2)]


def put(e, values, desc, spot, replace=None):
    x0, base, over = spot
    empty = jnp.zeros((8, 128), F32)
    for a in range(3):
        place = lanes() + (128 * a) - desc[2]
        index = place & 127
        here = (place >= 0) & (place < 128)
        for i in range(2):
            keep = None
            if replace is not None:
                keep = jnp.where(here, gather(replace[i], index), 0.0)
                keep = pltpu.roll(jnp.concatenate([keep, empty]), over, 0) > 0.5
            for c in range(3):
                spot = (c, x0 + i, pl.ds(base, 16), pl.ds(128 * a, 128))
                tile = jnp.where(here, gather(values(c, i), index), 0.0)
                pair = pltpu.roll(jnp.concatenate([tile, empty]), over, 0)
                if replace is None:
                    e[spot] = e[spot] + pair
                else:
                    e[spot] = jnp.where(keep, pair, e[spot])


def pack(out, box, in_x, in_y, at=0):
    if box is not None:
        for c in range(3):
            for i in range(2):
                out[pl.ds(8 * i, 8), pl.ds(128 * c, 128)] = box[c][i]
        at += 16
    for k in range(2):
        out[pl.ds(at + 24 * k, 24)] = in_x[k]
        out[pl.ds(at + 48 + 8 * k, 6)] = in_y[k]


def packed_box(ref):
    return lambda c, i: ref[pl.ds(8 * i, 8), pl.ds(128 * c, 128)]


def packed_x(ref, at):
    return lambda k: ref[pl.ds(at + 24 * k, 24)]


def packed_y(ref, at):
    return lambda k, x: ref[pl.ds(at + 48 + 8 * k + x, 1)]


def fine_steps(box, coef, desc, earlier, latest):
    row, lane = rows(), lanes()
    lx, ly, lz = desc[3], desc[4], desc[5]
    inside = covered_of(desc)
    y_face = [row == 0, None, row == ly - 1]
    z_face = [lane == 0, None, lane == lz - 1]

    def up(value):
        return jnp.where(row == 7, 0.0, pltpu.roll(value, 7, 0))

    def left(value):
        return jnp.where(lane == 127, 0.0, pltpu.roll(value, 127, 1))

    def down(value):
        return jnp.where(row == 0, 0.0, pltpu.roll(value, 1, 0))

    def right(value):
        return jnp.where(lane == 0, 0.0, pltpu.roll(value, 1, 1))

    def ahead_y(values, u, t):
        return values[3 * u + 3 + t] if u < 2 else up(values[t])

    def ahead_z(values, u, t):
        return values[3 * u + t + 1] if t < 2 else left(values[3 * u])

    def behind_y(values, u, t):
        return values[3 * u - 3 + t] if u > 0 else down(values[6 + t])

    def behind_z(values, u, t):
        return values[3 * u + t - 1] if t > 0 else right(values[3 * u + 2])

    def either(p, q):
        if p is None:
            return q
        return p if q is None else p | q

    zero = jnp.zeros((8, 128), F32)

    def substep(number, carry):
        weight = (number.astype(F32) + 1.0) / 3.0
        driven = [
            [earlier[c][i] + weight * (latest[c][i] - earlier[c][i]) for i in range(2)]
            for c in range(3)
        ]
        for x in range(6):
            part = x // 3
            e = [[box[c, x, k] for k in range(9)] for c in range(3)]
            if x < 5:
                ey_x = [box[1, x + 1, k] for k in range(9)]
                ez_x = [box[2, x + 1, k] for k in range(9)]
            else:
                ey_x = ez_x = [zero] * 9
            h = [[], [], []]
            for u in range(3):
                for t in range(3):
                    k = 3 * u + t
                    ex, ey, ez = e[0][k], e[1][k], e[2][k]
                    turn = (
                        (ahead_y(e[2], u, t) - ez) - (ahead_z(e[1], u, t) - ey),
                        (ahead_z(e[0], u, t) - ex) - (ez_x[k] - ez),
                        (ey_x[k] - ey) - (ahead_y(e[0], u, t) - ex),
                    )
                    for c in range(3):
                        value = box[3 + c, x, k] - 0.5 * turn[c]
                        box[3 + c, x, k] = value
                        h[c].append(value)
            x_face = x == 0
            if x in (2, 5):
                x_face = 3 * lx - 1 == x
            for u in range(3):
                for t in range(3):
                    k = 3 * u + t
                    hx, hy, hz = h[0][k], h[1][k], h[2][k]
                    hy_x = box[4, x - 1, k] if x > 0 else zero
                    hz_x = box[5, x - 1, k] if x > 0 else zero
                    rotation = (
                        (hz - behind_y(h[2], u, t)) - (hy - behind_z(h[1], u, t)),
                        (hx - behind_z(h[0], u, t)) - (hz - hz_x),
                        (hy - hy_x) - (hx - behind_y(h[0], u, t)),
                    )
                    a, b, p, f3, g = (coef[q, x, k] for q in range(5))
                    faces = (
                        either(y_face[u], z_face[t]),
                        None if x_face is True else either(x_face if x in (2, 5) else None, z_face[t]),
                        None if x_face is True else either(x_face if x in (2, 5) else None, y_face[u]),
                    )
                    for c in range(3):
                        old = box[6 + c, x, k]
                        new = a * e[c][k] + b * rotation[c] + p * old
                        if c > 0 and x_face is True:
                            new = driven[c][part]
                        elif faces[c] is not None:
                            new = jnp.where(faces[c], driven[c][part], new)
                        new = jnp.where(inside[part], new, 0.0)
                        box[c, x, k] = new
                        box[6 + c, x, k] = f3 * old + g * new
        return carry

    lax.fori_loop(0, 3, substep, 0)
    restricted = [[zero, zero] for c in range(3)]
    for c in range(3):
        for i in range(2):
            total = zero
            for x in range(3 * i, 3 * i + 3):
                for k in range(9):
                    total = total + box[c, x, k]
            restricted[c][i] = total * F32(1.0 / 27.0)
    return restricted


def feed_back(restricted, latest, desc):
    covered = covered_of(desc)
    after = [[jnp.where(covered[i], restricted[c][i], latest[c][i]) for i in range(2)] for c in range(3)]
    return after, [[after[c][i] - latest[c][i] for i in range(2)] for c in range(3)]


def store_box(ref, values):
    for c in range(3):
        for i in range(2):
            ref[c, i] = values[c][i]


def load_box(ref):
    return [[ref[c, i] for i in range(2)] for c in range(3)]


def is_coarse():
    return lax.axis_index("grid") == 0


def is_fine():
    return lax.axis_index("grid") == 1


def h1_kernel(e, h, ax, ay, out_h, bx, by):
    @pl.when(is_coarse())
    def _():
        magnetic(e, h, edge_x(ax), edge_y(ay), out_h)
        last_layers(out_h, bx, by)


def e1_kernel(e, h, p, coef, bx, by, desc, out_e, out_p, ax, ay, sent):
    @pl.when(is_coarse())
    def _():
        spot = corner(desc)
        before = cut_region(e, desc, spot)
        electric(e, h, p, coef, edge_x(bx), edge_y(by), out_e, out_p)
        first_layers(out_e, ax, ay)
        after = cut_region(out_e, desc, spot)
        for c in range(3):
            for i in range(2):
                sent[0, c, i] = before[c][i]
                sent[1, c, i] = after[c][i]


def h2_kernel(e, h, ax, ay, box_in, coef, region, desc, out_e, out_h, bx, by, box, now, change):
    @pl.when(is_coarse())
    def _():
        out_e[...] = e[...]
        magnetic(e, h, edge_x(ax), edge_y(ay), out_h)
        last_layers(out_h, bx, by)

    @pl.when(is_fine())
    def _():
        box[...] = box_in[...]
        out_e[...] = jnp.zeros(out_e.shape, F32)
        out_h[...] = jnp.zeros(out_h.shape, F32)
        earlier = [[region[0, c, i] for i in range(2)] for c in range(3)]
        latest = [[region[1, c, i] for i in range(2)] for c in range(3)]
        restricted = fine_steps(box, coef, desc, earlier, latest)
        after, delta = feed_back(restricted, latest, desc)
        store_box(now, after)
        store_box(change, delta)
        put(out_e, lambda c, i: delta[c][i], desc, corner(desc))


def e2_kernel(e, h, p, coef, bx, by, desc, material, table, out_e, out_p, ax, ay, sent, wide_coef):
    @pl.when(is_coarse())
    def _():
        electric(e, h, p, coef, edge_x(bx), edge_y(by), out_e, out_p)
        first_layers(out_e, ax, ay)
        store_box(sent, cut_region(out_e, desc, corner(desc)))

    @pl.when(is_fine())
    def _():
        out_e[...] = e[...]
        out_p[...] = jnp.zeros(out_p.shape, F32)
        first_layers(e, ax, ay)
        tiles = [table[k] for k in range(5)]
        for x in range(6):
            for yt in range(3):
                for zt in range(3):
                    index = material[0, x, pl.ds(8 * yt, 8), pl.ds(128 * zt, 128)]
                    for k in range(5):
                        wide_coef[k, x, 3 * yt + zt] = gather(tiles[k], index)


def h3_kernel(e, h, ax, ay, change, out_h, bx, by, relay):
    magnetic(e, h, edge_x(ax), edge_y(ay), out_h)
    last_layers(out_h, bx, by)

    @pl.when(is_fine())
    def _():
        pack(relay, load_box(change), ax, ay)


def e3_kernel(
    e, h, p, coef, wide_coef, bx, by, desc, box_in, region, was,
    out_e, out_p, ax, ay, sent, box, now, relay,
):
    @pl.when(is_coarse())
    def _():
        electric(e, h, p, coef, edge_x(bx), edge_y(by), out_e, out_p)
        store_box(sent, cut_region(out_e, desc, corner(desc)))

    @pl.when(is_fine())
    def _():
        box[...] = box_in[...]
        spot = corner(desc)
        electric(e, h, p, wide_coef, edge_x(bx), edge_y(by), out_e, out_p)
        fix = cut_region(out_e, desc, spot)
        latest = [[region[c, i] + fix[c][i] for i in range(2)] for c in range(3)]
        restricted = fine_steps(box, coef, desc, load_box(was), latest)
        after, delta = feed_back(restricted, latest, desc)
        store_box(now, after)
        put(out_e, lambda c, i: delta[c][i], desc, spot)
        first_layers(out_e, ax, ay)
        pack(relay, delta, bx, by)


def h4_kernel(e, h, ax, ay, out_h, bx, by, relay):
    @pl.when(is_fine())
    def _():
        magnetic(e, h, edge_x(ax), edge_y(ay), out_h)
        last_layers(out_h, bx, by)
        pack(relay, None, ax, ay)


def e4_kernel(e, h, p, coef, wide_coef, bx, by, desc, box_in, region, was, box, relay, layer):
    @pl.when(is_fine())
    def _():
        box[...] = box_in[...]
        spot = corner(desc)
        x0 = spot[0]
        for i in range(2):
            x = x0 + i
            rotation = curl_behind(h, x, edge_x(bx), edge_y(by))
            a, b, q = (whole(wide_coef, k, x) for k in range(3))
            for c in range(3):
                layer[c, i] = a * e[c, x] + b * rotation[c] + q * p[c, x]
        fix = cut_region(layer, desc, (0, *spot[1:]))
        latest = [[region[c, i] + fix[c][i] for i in range(2)] for c in range(3)]
        restricted = fine_steps(box, coef, desc, load_box(was), latest)
        pack(relay, restricted, bx, by)


def redo_kernel(coef, desc, relay1, relay2, relay3, out_e, out_h, out_p, one_e, one_h):
    @pl.when(is_coarse())
    def _():
        spot = corner(desc)
        one_e[...] = jnp.zeros(one_e.shape, F32)
        put(one_e, packed_box(relay1), desc, spot)
        magnetic(one_e, None, packed_x(relay1, 16), packed_y(relay1, 16), one_h)
        electric(
            one_e, one_h, None, coef, packed_x(relay2, 16), packed_y(relay2, 16), out_e, out_p
        )
        put(out_e, packed_box(relay2), desc, spot)
        magnetic(out_e, one_h, packed_x(relay3, 0), packed_y(relay3, 0), out_h)


def finish_kernel(e, h, p, fix_e, fix_h, fix_p, coef, desc, relay, box, out, mixed):
    @pl.when(is_coarse())
    def _():
        view_e, view_p = out.at[pl.ds(0, 3)], out.at[pl.ds(6, 3)]
        electric(
            fix_e, fix_h, fix_p, coef, packed_x(relay, 16), packed_y(relay, 16),
            view_e, view_p, (e, p),
        )
        out[3:6] = h[...] + fix_h[...]
        covered = [jnp.where(value, F32(1.0), 0.0) for value in covered_of(desc)]
        put(view_e, packed_box(relay), desc, corner(desc), covered)

    @pl.when(is_fine())
    def _():
        for c in range(9):
            for x in range(6):
                for u in range(3):
                    parts = from_tiles([box[c, x, 3 * u + t] for t in range(3)])
                    for a in range(3):
                        mixed[c, x, a, pl.ds(u, 8, stride=3)] = parts[a]
                for a in range(3):
                    out[c, x, :, pl.ds(128 * a, 128)] = mixed[c, x, a]


def third(shape, a):
    return pl.BlockSpec(shape, lambda i: (0,) * (len(shape) - 1) + (a,))


def call(kernel, operands, outs, specs=None, scratch=(), grid=()):
    shapes = [out if isinstance(out, jax.ShapeDtypeStruct) else jax.ShapeDtypeStruct(out, F32) for out in outs]
    return pl.pallas_call(
        kernel,
        out_shape=shapes,
        in_specs=specs or [VM] * len(operands),
        out_specs=[VM] * len(outs),
        grid=grid,
        scratch_shapes=scratch,
        compiler_params=pltpu.CompilerParams(vmem_limit_bytes=LIMIT),
    )(*operands)


PART = (3, 6, 24, 384)
SLAB = (9, 6, 24, 384)
BOX = (9, 6, 9, 8, 128)
COEF = (5, 6, 9, 8, 128)
REGION = (3, 2, 8, 128)
X_EDGE = (2, 24, 384)
Y_EDGE = (2, 6, 384)
EDGES = [X_EDGE, Y_EDGE]
AXES = ("grid", "gx", "gy")


def exchange(x_edge, y_edge, by, groups):
    na, nb = lax.axis_size("gx"), lax.axis_size("gy")

    def pairs(da, db):
        return [
            ((g * na + a) * nb + b, (g * na + a + da) * nb + b + db)
            for g in groups
            for a in range(na)
            for b in range(nb)
            if 0 <= a + da < na and 0 <= b + db < nb
        ]

    return (
        lax.ppermute(x_edge, AXES, pairs(by, 0)),
        lax.ppermute(y_edge, AXES, pairs(0, by)),
    )


def to_fine(value):
    return shifted(value, "grid", 1)


def to_coarse(value):
    return shifted(value, "grid", -1)


def body(fields, material, permittivity, conductivity, relax_rate, debye_strength, subgrids):
    f = fields[0]
    ax, ay = exchange(f[1:3, 0], f[0:3:2, :, 0], -1, (0,))
    e, h, p, box, coef, desc, table = call(
        prep_kernel,
        (fields,) * 3
        + (material,) * 3
        + (permittivity, conductivity, relax_rate, debye_strength, subgrids),
        [PART] * 3
        + [BOX, COEF, jax.ShapeDtypeStruct((6, 8, 128), jnp.int32), (5, 8, 128)],
        [third((1, 9, 6, 24, 128), a) for a in range(3)]
        + [third((1, 6, 24, 128), a) for a in range(3)]
        + [SM] * 5,
        grid=(1,),
    )
    h, bx, by = call(h1_kernel, (e, h, ax, ay), [PART] + EDGES)
    bx, by = exchange(bx, by, 1, (0,))
    e, p, ax, ay, sent = call(
        e1_kernel, (e, h, p, coef, bx, by, desc), [PART] * 2 + EDGES + [(2, *REGION)]
    )
    region = to_fine(sent)
    ax, ay = exchange(ax, ay, -1, (0,))
    slab_material = to_fine(material)
    e, h, bx, by, box, now, change = call(
        h2_kernel,
        (e, h, ax, ay, box, coef, region, desc),
        [PART] * 2 + EDGES + [BOX, REGION, REGION],
    )
    bx, by = exchange(bx, by, 1, (0,))
    e, p, ax, ay, sent, wide_coef = call(
        e2_kernel,
        (e, h, p, coef, bx, by, desc, slab_material, table),
        [PART] * 2 + EDGES + [REGION, COEF],
    )
    region = to_fine(sent)
    ax, ay = exchange(ax, ay, -1, (0, 1))
    h, bx, by, relay1 = call(h3_kernel, (e, h, ax, ay, change), [PART] + EDGES + [(80, 384)])
    bx, by = exchange(bx, by, 1, (0, 1))
    relay1 = to_coarse(relay1)
    e, p, ax, ay, sent, box, now, relay2 = call(
        e3_kernel,
        (e, h, p, coef, wide_coef, bx, by, desc, box, region, now),
        [PART] * 2 + EDGES + [REGION, BOX, REGION, (80, 384)],
    )
    base_e, base_h, base_p = e, h, p
    region = to_fine(sent)
    ax, ay = exchange(ax, ay, -1, (1,))
    relay2 = to_coarse(relay2)
    h, bx, by, relay3 = call(h4_kernel, (e, h, ax, ay), [PART] + EDGES + [(64, 384)])
    bx, by = exchange(bx, by, 1, (1,))
    relay3 = to_coarse(relay3)
    box, relay4 = call(
        e4_kernel,
        (e, h, p, coef, wide_coef, bx, by, desc, box, region, now),
        [BOX, (80, 384)],
        scratch=[pltpu.VMEM((3, 2, 24, 384), F32)],
    )
    relay4 = to_coarse(relay4)
    fix = call(
        redo_kernel,
        (coef, desc, relay1, relay2, relay3),
        [PART] * 3,
        scratch=[pltpu.VMEM(PART, F32)] * 2,
    )
    (out,) = call(
        finish_kernel,
        (base_e, base_h, base_p, *fix, coef, desc, relay4, box),
        [SLAB],
        scratch=[pltpu.VMEM((9, 6, 3, 24, 128), F32)],
    )
    return out[None]


def solution(mesh):
    in_specs = (
        P("grid", None, "gx", "gy", None),
        P("grid", "gx", "gy", None),
        P(),
        P(),
        P(),
        P(),
        P("gx", "gy", None),
    )
    out_specs = P("grid", None, "gx", "gy", None)
    return jax.shard_map(body, mesh=mesh, in_specs=in_specs, out_specs=out_specs, check_vma=False)
```

time: 96.6 us -> 84.8 us (0.88)
  waiting for transfers between devices: 33.8 us -> 22.7 us
  starting transfers between devices: 43.8 us -> 52.6 us
  local copies, waits for them, and re-layouts: 7.63 us -> 2.35 us
  Pallas kernels: 10.1 us -> 6.23 us
    ppermute x0 -> x16, starting transfers between devices: none -> 32.7 us  [the longest x8 16.6 us: exchange(): lax.ppermute(y_edge, AXES, pairs(0, by))]
    ppermute x18 -> x8, waiting for transfers between devices: 33.8 us -> 9.83 us  [shifted(): return lax.ppermute(value, axis, pairs)]
    ppermute x18 -> x8, starting transfers between devices: 43.8 us -> 19.9 us  [shifted(): return lax.ppermute(value, axis, pairs)]
    ppermute x0 -> x16, waiting for transfers between devices: none -> 12.8 us  [the longest x8 6.42 us: exchange(): lax.ppermute(y_edge, AXES, pairs(0, by))]
    pallas_call x13 -> x11, Pallas kernels: 10.1 us -> 6.23 us  [call(): pl.pallas_call(kernel, out_shape=shapes, in_specs=specs or [VM] * len(ope...]
    unnamed x17 -> x16, local copies, waits for them, and re-layouts: 5.77 us -> 2.29 us
  transfers between devices with their start and end apart: 18 -> 24, of which waited for: 13 -> 11; matrix products, arithmetic and copies ran while one was open for 1% -> 0% of each run, Pallas kernels for 1% -> 3%
where the time goes in v3:
time: 84.8 us; the launch traced here: 84.2 us
  starting transfers between devices  52.6 us (62%)
  waiting for transfers between devices  22.7 us (27%)
  Pallas kernels  6.23 us (7%)
  local copies, waits for them, and re-layouts  2.35 us (3%)
    ppermute x8, starting transfers between devices, shifted(): return lax.ppermute(value, axis, pairs)  19.9 us
    ppermute x8, starting transfers between devices, exchange(): lax.ppermute(y_edge, AXES, pairs(0, by))  16.6 us
    ppermute x8, starting transfers between devices, exchange(): lax.ppermute(x_edge, AXES, pairs(by, 0))  16.1 us
    ppermute x8, waiting for transfers between devices, shifted(): return lax.ppermute(value, axis, pairs)  9.83 us
    ppermute x8, waiting for transfers between devices, exchange(): lax.ppermute(y_edge, AXES, pairs(0, by))  6.42 us
    ppermute x8, waiting for transfers between devices, exchange(): lax.ppermute(x_edge, AXES, pairs(by, 0))  6.4 us
    pallas_call x11, Pallas kernels, call(): pl.pallas_call(kernel, out_shape=shapes, in_specs=specs or [VM] * len(ope...  6.23 us
    unnamed x16, local copies, waits for them, and re-layouts  2.29 us
  transfers between devices with their start and end apart: 24, of which 11 were waited for; matrix products, arithmetic and copies ran while one was open for 0% of the time, Pallas kernels for 3%

profile of v3, /device:TPU:0, one launch (start us, length us, event | category | flops | bytes accessed | tf_op | source)
XLA Modules:
  0.0 84.2 jit_solution(15985136475146154186)
XLA Ops:
  0.0 2.2 %copy.13 = f32[1,9,6,24,384]{4,2,1,3,0:T(8,128)S(1)} copy(f32[1,9,6,24,384]{4,3,2,1,0:T(8,128)} %f2.1) | data formatting | bytes 3981312 | tf_op args[0]
  2.3 0.1 slice.8
  2.4 1.3 %collective-permute-start = (f32[2,24,384]{2,0,1:T(2,128)S(1)}, f32[2,24,384]{2,0,1:T(2,128)S(1)}, u32[]{:S(2)}, u32[]{:S(2)}) collective-permute-start(f32[2,24,384]{2,0,1:T(2,128)S(1)} %bitcast.11), channel_id=1, source_target_pairs={{4,0},{5,1},{6,2},{7,3},{8,4},{9,5},{10,6},{11,7},{12,8},{13,9},{1... | collective-permute-start | bytes 221192 | tf_op jit(solution)/shard_map/ppermute | solution.py:622
  3.7 1.3 %collective-permute-start.1 = (f32[2,6,384]{2,1,0:T(8,128)S(1)}, f32[2,6,384]{2,1,0:T(8,128)S(1)}, u32[]{:S(2)}, u32[]{:S(2)}) collective-permute-start(f32[2,6,384]{2,1,0:T(8,128)S(1)} %slice_bitcast_fusion), channel_id=1, source_target_pairs={{1,0},{2,1},{3,2},{5,4},{6,5},{7,6},{9,8},{10,9},{11,10},{13,12},{... | collective-permute-start | bytes 55304 | tf_op jit(solution)/shard_map/ppermute | solution.py:623
  5.0 1.1 %shard_map.73 = (f32[3,6,24,384]{3,2,1,0:T(8,128)S(1)}, f32[3,6,24,384]{3,2,1,0:T(8,128)S(1)}, f32[3,6,24,384]{3,2,1,0:T(8,128)S(1)}, f32[9,6,9,8,128]{4,3,2,1,0...) custom-call(f32[1,9,6,24,384]{4,3,2,1,0:T(8,128)S(1)} %copy-done, ...), custom_call_target="tpu_custom_call" | custom-call | tf_op jit(solution)/shard_map/pallas_call | solution.py:587
  6.2 3.4 %collective-permute-done = f32[2,24,384]{2,0,1:T(2,128)S(1)} collective-permute-done((f32[2,24,384]{2,0,1:T(2,128)S(1)}, f32[2,24,384]{2,0,1:T(2,128)S(1)}, u32[]{:S(2)}, u32[]{:S(2)}) %collective-permute-start) | collective-permute-done | bytes 73760 | tf_op jit(solution)/shard_map/ppermute | solution.py:622
  9.6 0.2 shard_map.74
  9.9 3.9 %collective-permute-start.2 = (f32[2,24,384]{2,1,0:T(8,128)S(1)}, f32[2,24,384]{2,1,0:T(8,128)S(1)}, u32[]{:S(2)}, u32[]{:S(2)}) collective-permute-start(f32[2,24,384]{2,1,0:T(8,128)S(1)} %get-tuple-element.59), channel_id=1, source_target_pairs={{0,4},{1,5},{2,6},{3,7},{4,8},{5,9},{6,10},{7,11},{8,12},{9,13},{1... | collective-permute-start | bytes 221192 | tf_op jit(solution)/shard_map/ppermute | solution.py:622
  13.8 1.3 %collective-permute-start.9 = (s32[1,6,24,384]{3,2,1,0:T(8,128)S(1)}, s32[1,6,24,384]{3,2,1,0:T(8,128)S(1)}, u32[]{:S(2)}, u32[]{:S(2)}) collective-permute-start(s32[1,6,24,384]{3,2,1,0:T(8,128)S(1)} %copy-done.1), channel_id=1, source_target_pairs={{0,16},{1,17},{2,18},{3,19},{4,20},{5,21},{6,22},{7,23},{8,24},{9,... | collective-permute-start | bytes 663560 | tf_op jit(solution)/shard_map/ppermute | solution.py:20
  15.1 2.8 %collective-permute-start.3 = (f32[2,6,384]{2,1,0:T(8,128)S(1)}, f32[2,6,384]{2,1,0:T(8,128)S(1)}, u32[]{:S(2)}, u32[]{:S(2)}) collective-permute-start(f32[2,6,384]{2,1,0:T(8,128)S(1)} %get-tuple-element.60), channel_id=1, source_target_pairs={{0,1},{1,2},{2,3},{4,5},{5,6},{6,7},{8,9},{9,10},{10,11},{12,13},{... | collective-permute-start | bytes 55304 | tf_op jit(solution)/shard_map/ppermute | solution.py:623
  17.9 0.8 collective-permute-done.3.by
  18.7 0.0 collective-permute-done.2.bx
  18.7 0.6 shard_map.75
  19.3 1.3 %collective-permute-start.4 = (f32[2,24,384]{2,1,0:T(8,128)S(1)}, f32[2,24,384]{2,1,0:T(8,128)S(1)}, u32[]{:S(2)}, u32[]{:S(2)}) collective-permute-start(f32[2,24,384]{2,1,0:T(8,128)S(1)} %get-tuple-element.63), channel_id=1, source_target_pairs={{4,0},{5,1},{6,2},{7,3},{8,4},{9,5},{10,6},{11,7},{12,8},{13,9},{1... | collective-permute-start | bytes 221192 | tf_op jit(solution)/shard_map/ppermute | solution.py:622
  20.6 1.3 %collective-permute-start.6 = (f32[2,3,2,8,128]{4,3,2,1,0:T(8,128)S(1)}, f32[2,3,2,8,128]{4,3,2,1,0:T(8,128)S(1)}, u32[]{:S(2)}, u32[]{:S(2)}) collective-permute-start(f32[2,3,2,8,128]{4,3,2,1,0:T(8,128)S(1)} %get-tuple-element.66), channel_id=1, source_target_pairs={{0,16},{1,17},{2,18},{3,19},{4,20},{5,21},{6,22},{7,23},{8,24},{9,... | collective-permute-start | bytes 147464 | tf_op jit(solution)/shard_map/ppermute | solution.py:20
  21.9 1.3 %collective-permute-start.5 = (f32[2,6,384]{2,1,0:T(8,128)S(1)}, f32[2,6,384]{2,1,0:T(8,128)S(1)}, u32[]{:S(2)}, u32[]{:S(2)}) collective-permute-start(f32[2,6,384]{2,1,0:T(8,128)S(1)} %get-tuple-element.64), channel_id=1, source_target_pairs={{1,0},{2,1},{3,2},{5,4},{6,5},{7,6},{9,8},{10,9},{11,10},{13,12},{... | collective-permute-start | bytes 55304 | tf_op jit(solution)/shard_map/ppermute | solution.py:623
  23.2 2.2 %collective-permute-done.5.ay = f32[2,6,384]{2,1,0:T(8,128)S(1)} collective-permute-done((f32[2,6,384]{2,1,0:T(8,128)S(1)}, f32[2,6,384]{2,1,0:T(8,128)S(1)}, u32[]{:S(2)}, u32[]{:S(2)}) %collective-permute-start.5) | collective-permute-done | bytes 18464 | tf_op jit(solution)/shard_map/ppermute | solution.py:623
  25.4 0.9 %collective-permute-done.4.ax = f32[2,24,384]{2,1,0:T(8,128)S(1)} collective-permute-done((f32[2,24,384]{2,1,0:T(8,128)S(1)}, f32[2,24,384]{2,1,0:T(8,128)S(1)}, u32[]{:S(2)}, u32[]{:S(2)}) %collective-permute-start.4) | collective-permute-done | bytes 73760 | tf_op jit(solution)/shard_map/ppermute | solution.py:622
  26.2 0.2 shard_map.76
  26.5 3.5 %collective-permute-start.7 = (f32[2,24,384]{2,1,0:T(8,128)S(1)}, f32[2,24,384]{2,1,0:T(8,128)S(1)}, u32[]{:S(2)}, u32[]{:S(2)}) collective-permute-start(f32[2,24,384]{2,1,0:T(8,128)S(1)} %get-tuple-element.70), channel_id=1, source_target_pairs={{0,4},{1,5},{2,6},{3,7},{4,8},{5,9},{6,10},{7,11},{8,12},{9,13},{1... | collective-permute-start | bytes 221192 | tf_op jit(solution)/shard_map/ppermute | solution.py:622
  30.0 5.0 %collective-permute-start.8 = (f32[2,6,384]{2,1,0:T(8,128)S(1)}, f32[2,6,384]{2,1,0:T(8,128)S(1)}, u32[]{:S(2)}, u32[]{:S(2)}) collective-permute-start(f32[2,6,384]{2,1,0:T(8,128)S(1)} %get-tuple-element.71), channel_id=1, source_target_pairs={{0,1},{1,2},{2,3},{4,5},{5,6},{6,7},{8,9},{9,10},{10,11},{12,13},{... | collective-permute-start | bytes 55304 | tf_op jit(solution)/shard_map/ppermute | solution.py:623
  34.9 0.8 collective-permute-done.8.by
  35.8 0.0 collective-permute-done.7.bx
  35.8 0.5 shard_map.77
  36.3 1.3 %collective-permute-start.10 = (f32[2,24,384]{2,1,0:T(8,128)S(1)}, f32[2,24,384]{2,1,0:T(8,128)S(1)}, u32[]{:S(2)}, u32[]{:S(2)}) collective-permute-start(f32[2,24,384]{2,1,0:T(8,128)S(1)} %get-tuple-element.74), channel_id=1, source_target_pairs={{4,0},{5,1},{6,2},{7,3},{8,4},{9,5},{10,6},{11,7},{12,8},{13,9},{1... | collective-permute-start | bytes 221192 | tf_op jit(solution)/shard_map/ppermute | solution.py:622
  37.6 1.3 %collective-permute-start.11 = (f32[2,6,384]{2,1,0:T(8,128)S(1)}, f32[2,6,384]{2,1,0:T(8,128)S(1)}, u32[]{:S(2)}, u32[]{:S(2)}) collective-permute-start(f32[2,6,384]{2,1,0:T(8,128)S(1)} %get-tuple-element.75), channel_id=1, source_target_pairs={{1,0},{2,1},{3,2},{5,4},{6,5},{7,6},{9,8},{10,9},{11,10},{13,12},{... | collective-permute-start | bytes 55304 | tf_op jit(solution)/shard_map/ppermute | solution.py:623
  38.9 1.8 %collective-permute-done.11.ay = f32[2,6,384]{2,1,0:T(8,128)S(1)} collective-permute-done((f32[2,6,384]{2,1,0:T(8,128)S(1)}, f32[2,6,384]{2,1,0:T(8,128)S(1)}, u32[]{:S(2)}, u32[]{:S(2)}) %collective-permute-start.11) | collective-permute-done | bytes 18464 | tf_op jit(solution)/shard_map/ppermute | solution.py:623
  40.7 2.1 %collective-permute-done.10.ax = f32[2,24,384]{2,1,0:T(8,128)S(1)} collective-permute-done((f32[2,24,384]{2,1,0:T(8,128)S(1)}, f32[2,24,384]{2,1,0:T(8,128)S(1)}, u32[]{:S(2)}, u32[]{:S(2)}) %collective-permute-start.10) | collective-permute-done | bytes 73760 | tf_op jit(solution)/shard_map/ppermute | solution.py:622
  42.8 0.2 shard_map.78
  43.0 3.5 %collective-permute-start.12 = (f32[2,24,384]{2,1,0:T(8,128)S(1)}, f32[2,24,384]{2,1,0:T(8,128)S(1)}, u32[]{:S(2)}, u32[]{:S(2)}) collective-permute-start(f32[2,24,384]{2,1,0:T(8,128)S(1)} %get-tuple-element.80), channel_id=1, source_target_pairs={{0,4},{1,5},{2,6},{3,7},{4,8},{5,9},{6,10},{7,11},{8,12},{9,13},{1... | collective-permute-start | bytes 221192 | tf_op jit(solution)/shard_map/ppermute | solution.py:622
  46.5 1.3 %collective-permute-start.14 = (f32[3,2,8,128]{3,2,1,0:T(8,128)S(1)}, f32[3,2,8,128]{3,2,1,0:T(8,128)S(1)}, u32[]{:S(2)}, u32[]{:S(2)}) collective-permute-start(f32[3,2,8,128]{3,2,1,0:T(8,128)S(1)} %get-tuple-element.83), channel_id=1, source_target_pairs={{0,16},{1,17},{2,18},{3,19},{4,20},{5,21},{6,22},{7,23},{8,24},{9,... | collective-permute-start | bytes 73736 | tf_op jit(solution)/shard_map/ppermute | solution.py:20
  47.8 3.6 %collective-permute-start.13 = (f32[2,6,384]{2,1,0:T(8,128)S(1)}, f32[2,6,384]{2,1,0:T(8,128)S(1)}, u32[]{:S(2)}, u32[]{:S(2)}) collective-permute-start(f32[2,6,384]{2,1,0:T(8,128)S(1)} %get-tuple-element.81), channel_id=1, source_target_pairs={{0,1},{1,2},{2,3},{4,5},{5,6},{6,7},{8,9},{9,10},{10,11},{12,13},{... | collective-permute-start | bytes 55304 | tf_op jit(solution)/shard_map/ppermute | solution.py:623
  51.5 0.8 collective-permute-done.13.by
  52.3 0.5 shard_map.79
  52.8 0.7 collective-permute-start.17
  53.5 0.7 collective-permute-start.18
  54.2 0.7 collective-permute-start.20
  54.9 10.8 %collective-permute-start.22 = (f32[3,2,8,128]{3,2,1,0:T(8,128)S(1)}, f32[3,2,8,128]{3,2,1,0:T(8,128)S(1)}, u32[]{:S(2)}, u32[]{:S(2)}) collective-permute-start(f32[3,2,8,128]{3,2,1,0:T(8,128)S(1)} %get-tuple-element.99), channel_id=1, source_target_pairs={{0,16},{1,17},{2,18},{3,19},{4,20},{5,21},{6,22},{7,23},{8,24},{9,... | collective-permute-start | bytes 73736 | tf_op jit(solution)/shard_map/ppermute | solution.py:20
  65.7 0.7 collective-permute-start.21
  66.4 1.3 %collective-permute-start.15 = (f32[80,384]{1,0:T(8,128)S(1)}, f32[80,384]{1,0:T(8,128)S(1)}, u32[]{:S(2)}, u32[]{:S(2)}) collective-permute-start(f32[80,384]{1,0:T(8,128)S(1)} %get-tuple-element.87), channel_id=1, source_target_pairs={{16,0},{17,1},{18,2},{19,3},{20,4},{21,5},{22,6},{23,7},{24,8},{25... | collective-permute-start | bytes 368648 | tf_op jit(solution)/shard_map/ppermute | solution.py:20
  67.7 1.3 %collective-permute-start.16 = (f32[80,384]{1,0:T(8,128)S(1)}, f32[80,384]{1,0:T(8,128)S(1)}, u32[]{:S(2)}, u32[]{:S(2)}) collective-permute-start(f32[80,384]{1,0:T(8,128)S(1)} %get-tuple-element.88), channel_id=1, source_target_pairs={{16,0},{17,1},{18,2},{19,3},{20,4},{21,5},{22,6},{23,7},{24,8},{25... | collective-permute-start | bytes 368648 | tf_op jit(solution)/shard_map/ppermute | solution.py:20
  69.1 1.3 %collective-permute-start.23 = (f32[80,384]{1,0:T(8,128)S(1)}, f32[80,384]{1,0:T(8,128)S(1)}, u32[]{:S(2)}, u32[]{:S(2)}) collective-permute-start(f32[80,384]{1,0:T(8,128)S(1)} %get-tuple-element.101), channel_id=1, source_target_pairs={{16,0},{17,1},{18,2},{19,3},{20,4},{21,5},{22,6},{23,7},{24,8},{25... | collective-permute-start | bytes 368648 | tf_op jit(solution)/shard_map/ppermute | solution.py:20
  70.4 1.3 %collective-permute-start.19 = (f32[64,384]{1,0:T(8,128)S(1)}, f32[64,384]{1,0:T(8,128)S(1)}, u32[]{:S(2)}, u32[]{:S(2)}) collective-permute-start(f32[64,384]{1,0:T(8,128)S(1)} %get-tuple-element.91), channel_id=1, source_target_pairs={{16,0},{17,1},{18,2},{19,3},{20,4},{21,5},{22,6},{23,7},{24,8},{25... | collective-permute-start | bytes 294920 | tf_op jit(solution)/shard_map/ppermute | solution.py:20
  71.7 2.4 %collective-permute-done.15.relay1 = f32[80,384]{1,0:T(8,128)S(1)} collective-permute-done((f32[80,384]{1,0:T(8,128)S(1)}, f32[80,384]{1,0:T(8,128)S(1)}, u32[]{:S(2)}, u32[]{:S(2)}) %collective-permute-start.15) | collective-permute-done | bytes 122912 | tf_op jit(solution)/shard_map/ppermute | solution.py:20
  74.1 2.6 %collective-permute-done.16.relay2 = f32[80,384]{1,0:T(8,128)S(1)} collective-permute-done((f32[80,384]{1,0:T(8,128)S(1)}, f32[80,384]{1,0:T(8,128)S(1)}, u32[]{:S(2)}, u32[]{:S(2)}) %collective-permute-start.16) | collective-permute-done | bytes 122912 | tf_op jit(solution)/shard_map/ppermute | solution.py:20
  76.7 4.7 %collective-permute-done.19.relay3 = f32[64,384]{1,0:T(8,128)S(1)} collective-permute-done((f32[64,384]{1,0:T(8,128)S(1)}, f32[64,384]{1,0:T(8,128)S(1)}, u32[]{:S(2)}, u32[]{:S(2)}) %collective-permute-start.19) | collective-permute-done | bytes 98336 | tf_op jit(solution)/shard_map/ppermute | solution.py:20
  81.5 0.8 %shard_map.81 = (f32[3,6,24,384]{3,2,1,0:T(8,128)S(1)}, f32[3,6,24,384]{3,2,1,0:T(8,128)S(1)}, f32[3,6,24,384]{3,2,1,0:T(8,128)S(1)}) custom-call(f32[5,6,9,8,128]{4,3,2,1,0:T(8,128)S(1)} %get-tuple-element.58.coef, s32[6,8,128]{2,1,0:T(8,128)S(1)} %get-tuple-element.61.desc, f32[80,384]{1,0:T(8,128)S(1)} %collective-permute-done.15.relay1, ...), custom_call_target="tpu_custom_call" | custom-call | tf_op jit(solution)/shard_map/pallas_call | solution.py:587
  82.3 1.9 %shard_map.83 = f32[9,6,24,384]{3,2,1,0:T(8,128)} custom-call(f32[3,6,24,384]{3,2,1,0:T(8,128)S(1)} %get-tuple-element.85.e, f32[3,6,24,384]{3,2,1,0:T(8,128)S(1)} %get-tuple-element.77.h, f32[3,6,24,384]{3,2,1,0:T(8,128)S(1)} %get-tuple-element.86.p, f32[3,6,24,384]{3,2,1,0:T(8,128)S(1)} %get-tuple-element.92.fix_e, ...), custom_call_target="tpu_custom_call" | custom-call | tf_op jit(solution)/shard_map/pallas_call | solution.py:587
  (30 shorter events, 0.1 us)
Async XLA Ops:
  0.0 5.0 %copy-start = (f32[1,9,6,24,384]{4,3,2,1,0:T(8,128)S(1)}, f32[1,9,6,24,384]{4,3,2,1,0:T(8,128)}, u32[]{:S(2)}) copy-start(f32[1,9,6,24,384]{4,3,2,1,0:T(8,128)} %f2.1) | copy-start | bytes 5971972
  0.0 5.0 %copy-start.1 = (s32[1,6,24,384]{3,2,1,0:T(8,128)S(1)}, s32[1,6,24,384]{3,2,1,0:T(8,128)}, u32[]{:S(2)}) copy-start(s32[1,6,24,384]{3,2,1,0:T(8,128)} %m2.1) | copy-start | bytes 663556
  0.0 5.0 %copy-start.6 = (s32[1,1,6]{2,1,0:T(1,128)S(1)}, s32[1,1,6]{2,1,0:T(1,128)}, u32[]{:S(2)}) copy-start(s32[1,1,6]{2,1,0:T(1,128)} %sub.1) | copy-start | bytes 76
  0.0 5.0 %copy-start.5 = (f32[8]{0:T(128)S(1)}, f32[8]{0:T(128)}, u32[]{:S(2)}) copy-start(f32[8]{0:T(128)} %debye.1) | copy-start | bytes 100
  0.0 5.0 %copy-start.4 = (f32[8]{0:T(128)S(1)}, f32[8]{0:T(128)}, u32[]{:S(2)}) copy-start(f32[8]{0:T(128)} %relax.1) | copy-start | bytes 100
  0.0 5.0 %copy-start.3 = (f32[8]{0:T(128)S(1)}, f32[8]{0:T(128)}, u32[]{:S(2)}) copy-start(f32[8]{0:T(128)} %cond.1) | copy-start | bytes 100
  0.0 5.0 %copy-start.2 = (f32[8]{0:T(128)S(1)}, f32[8]{0:T(128)}, u32[]{:S(2)}) copy-start(f32[8]{0:T(128)} %perm.1) | copy-start | bytes 100
  2.4 7.3 %collective-permute-start = (f32[2,24,384]{2,0,1:T(2,128)S(1)}, f32[2,24,384]{2,0,1:T(2,128)S(1)}, u32[]{:S(2)}, u32[]{:S(2)}) collective-permute-start(f32[2,24,384]{2,0,1:T(2,128)S(1)} %bitcast.11), channel_id=1, source_target_pairs={{4,0},{5,1},{6,2},{7,3},{8,4},{9,5},{10,6},{11,7},{12,8},{13,9},{1... | collective-permute-start | bytes 221192 | tf_op jit(solution)/shard_map/ppermute | solution.py:622
  3.7 6.0 %collective-permute-start.1 = (f32[2,6,384]{2,1,0:T(8,128)S(1)}, f32[2,6,384]{2,1,0:T(8,128)S(1)}, u32[]{:S(2)}, u32[]{:S(2)}) collective-permute-start(f32[2,6,384]{2,1,0:T(8,128)S(1)} %slice_bitcast_fusion), channel_id=1, source_target_pairs={{1,0},{2,1},{3,2},{5,4},{6,5},{7,6},{9,8},{10,9},{11,10},{13,12},{... | collective-permute-start | bytes 55304 | tf_op jit(solution)/shard_map/ppermute | solution.py:623
  9.9 8.9 %collective-permute-start.2 = (f32[2,24,384]{2,1,0:T(8,128)S(1)}, f32[2,24,384]{2,1,0:T(8,128)S(1)}, u32[]{:S(2)}, u32[]{:S(2)}) collective-permute-start(f32[2,24,384]{2,1,0:T(8,128)S(1)} %get-tuple-element.59), channel_id=1, source_target_pairs={{0,4},{1,5},{2,6},{3,7},{4,8},{5,9},{6,10},{7,11},{8,12},{9,13},{1... | collective-permute-start | bytes 221192 | tf_op jit(solution)/shard_map/ppermute | solution.py:622
  13.8 21.1 %collective-permute-start.9 = (s32[1,6,24,384]{3,2,1,0:T(8,128)S(1)}, s32[1,6,24,384]{3,2,1,0:T(8,128)S(1)}, u32[]{:S(2)}, u32[]{:S(2)}) collective-permute-start(s32[1,6,24,384]{3,2,1,0:T(8,128)S(1)} %copy-done.1), channel_id=1, source_target_pairs={{0,16},{1,17},{2,18},{3,19},{4,20},{5,21},{6,22},{7,23},{8,24},{9,... | collective-permute-start | bytes 663560 | tf_op jit(solution)/shard_map/ppermute | solution.py:20
  15.1 3.6 %collective-permute-start.3 = (f32[2,6,384]{2,1,0:T(8,128)S(1)}, f32[2,6,384]{2,1,0:T(8,128)S(1)}, u32[]{:S(2)}, u32[]{:S(2)}) collective-permute-start(f32[2,6,384]{2,1,0:T(8,128)S(1)} %get-tuple-element.60), channel_id=1, source_target_pairs={{0,1},{1,2},{2,3},{4,5},{5,6},{6,7},{8,9},{9,10},{10,11},{12,13},{... | collective-permute-start | bytes 55304 | tf_op jit(solution)/shard_map/ppermute | solution.py:623
  19.3 6.9 %collective-permute-start.4 = (f32[2,24,384]{2,1,0:T(8,128)S(1)}, f32[2,24,384]{2,1,0:T(8,128)S(1)}, u32[]{:S(2)}, u32[]{:S(2)}) collective-permute-start(f32[2,24,384]{2,1,0:T(8,128)S(1)} %get-tuple-element.63), channel_id=1, source_target_pairs={{4,0},{5,1},{6,2},{7,3},{8,4},{9,5},{10,6},{11,7},{12,8},{13,9},{1... | collective-permute-start | bytes 221192 | tf_op jit(solution)/shard_map/ppermute | solution.py:622
  20.6 4.8 %collective-permute-start.6 = (f32[2,3,2,8,128]{4,3,2,1,0:T(8,128)S(1)}, f32[2,3,2,8,128]{4,3,2,1,0:T(8,128)S(1)}, u32[]{:S(2)}, u32[]{:S(2)}) collective-permute-start(f32[2,3,2,8,128]{4,3,2,1,0:T(8,128)S(1)} %get-tuple-element.66), channel_id=1, source_target_pairs={{0,16},{1,17},{2,18},{3,19},{4,20},{5,21},{6,22},{7,23},{8,24},{9,... | collective-permute-start | bytes 147464 | tf_op jit(solution)/shard_map/ppermute | solution.py:20
  21.9 3.5 %collective-permute-start.5 = (f32[2,6,384]{2,1,0:T(8,128)S(1)}, f32[2,6,384]{2,1,0:T(8,128)S(1)}, u32[]{:S(2)}, u32[]{:S(2)}) collective-permute-start(f32[2,6,384]{2,1,0:T(8,128)S(1)} %get-tuple-element.64), channel_id=1, source_target_pairs={{1,0},{2,1},{3,2},{5,4},{6,5},{7,6},{9,8},{10,9},{11,10},{13,12},{... | collective-permute-start | bytes 55304 | tf_op jit(solution)/shard_map/ppermute | solution.py:623
  26.5 9.3 %collective-permute-start.7 = (f32[2,24,384]{2,1,0:T(8,128)S(1)}, f32[2,24,384]{2,1,0:T(8,128)S(1)}, u32[]{:S(2)}, u32[]{:S(2)}) collective-permute-start(f32[2,24,384]{2,1,0:T(8,128)S(1)} %get-tuple-element.70), channel_id=1, source_target_pairs={{0,4},{1,5},{2,6},{3,7},{4,8},{5,9},{6,10},{7,11},{8,12},{9,13},{1... | collective-permute-start | bytes 221192 | tf_op jit(solution)/shard_map/ppermute | solution.py:622
  30.0 5.8 %collective-permute-start.8 = (f32[2,6,384]{2,1,0:T(8,128)S(1)}, f32[2,6,384]{2,1,0:T(8,128)S(1)}, u32[]{:S(2)}, u32[]{:S(2)}) collective-permute-start(f32[2,6,384]{2,1,0:T(8,128)S(1)} %get-tuple-element.71), channel_id=1, source_target_pairs={{0,1},{1,2},{2,3},{4,5},{5,6},{6,7},{8,9},{9,10},{10,11},{12,13},{... | collective-permute-start | bytes 55304 | tf_op jit(solution)/shard_map/ppermute | solution.py:623
  36.3 6.5 %collective-permute-start.10 = (f32[2,24,384]{2,1,0:T(8,128)S(1)}, f32[2,24,384]{2,1,0:T(8,128)S(1)}, u32[]{:S(2)}, u32[]{:S(2)}) collective-permute-start(f32[2,24,384]{2,1,0:T(8,128)S(1)} %get-tuple-element.74), channel_id=1, source_target_pairs={{4,0},{5,1},{6,2},{7,3},{8,4},{9,5},{10,6},{11,7},{12,8},{13,9},{1... | collective-permute-start | bytes 221192 | tf_op jit(solution)/shard_map/ppermute | solution.py:622
  37.6 3.1 %collective-permute-start.11 = (f32[2,6,384]{2,1,0:T(8,128)S(1)}, f32[2,6,384]{2,1,0:T(8,128)S(1)}, u32[]{:S(2)}, u32[]{:S(2)}) collective-permute-start(f32[2,6,384]{2,1,0:T(8,128)S(1)} %get-tuple-element.75), channel_id=1, source_target_pairs={{1,0},{2,1},{3,2},{5,4},{6,5},{7,6},{9,8},{10,9},{11,10},{13,12},{... | collective-permute-start | bytes 55304 | tf_op jit(solution)/shard_map/ppermute | solution.py:623
  43.0 9.3 %collective-permute-start.12 = (f32[2,24,384]{2,1,0:T(8,128)S(1)}, f32[2,24,384]{2,1,0:T(8,128)S(1)}, u32[]{:S(2)}, u32[]{:S(2)}) collective-permute-start(f32[2,24,384]{2,1,0:T(8,128)S(1)} %get-tuple-element.80), channel_id=1, source_target_pairs={{0,4},{1,5},{2,6},{3,7},{4,8},{5,9},{6,10},{7,11},{8,12},{9,13},{1... | collective-permute-start | bytes 221192 | tf_op jit(solution)/shard_map/ppermute | solution.py:622
  46.5 5.0 %collective-permute-start.14 = (f32[3,2,8,128]{3,2,1,0:T(8,128)S(1)}, f32[3,2,8,128]{3,2,1,0:T(8,128)S(1)}, u32[]{:S(2)}, u32[]{:S(2)}) collective-permute-start(f32[3,2,8,128]{3,2,1,0:T(8,128)S(1)} %get-tuple-element.83), channel_id=1, source_target_pairs={{0,16},{1,17},{2,18},{3,19},{4,20},{5,21},{6,22},{7,23},{8,24},{9,... | collective-permute-start | bytes 73736 | tf_op jit(solution)/shard_map/ppermute | solution.py:20
  47.8 4.5 %collective-permute-start.13 = (f32[2,6,384]{2,1,0:T(8,128)S(1)}, f32[2,6,384]{2,1,0:T(8,128)S(1)}, u32[]{:S(2)}, u32[]{:S(2)}) collective-permute-start(f32[2,6,384]{2,1,0:T(8,128)S(1)} %get-tuple-element.81), channel_id=1, source_target_pairs={{0,1},{1,2},{2,3},{4,5},{5,6},{6,7},{8,9},{9,10},{10,11},{12,13},{... | collective-permute-start | bytes 55304 | tf_op jit(solution)/shard_map/ppermute | solution.py:623
  52.8 1.4 %collective-permute-start.17 = (f32[2,24,384]{2,1,0:T(8,128)S(1)}, f32[2,24,384]{2,1,0:T(8,128)S(1)}, u32[]{:S(2)}, u32[]{:S(2)}) collective-permute-start(f32[2,24,384]{2,1,0:T(8,128)S(1)} %get-tuple-element.89), channel_id=1, source_target_pairs={{20,16},{21,17},{22,18},{23,19},{24,20},{25,21},{26,22},{27,23},{2... | collective-permute-start | bytes 221192 | tf_op jit(solution)/shard_map/ppermute | solution.py:622
  53.5 0.7 collective-permute-start.18
  54.2 14.8 %collective-permute-start.20 = (f32[2,24,384]{2,1,0:T(8,128)S(1)}, f32[2,24,384]{2,1,0:T(8,128)S(1)}, u32[]{:S(2)}, u32[]{:S(2)}) collective-permute-start(f32[2,24,384]{2,1,0:T(8,128)S(1)} %get-tuple-element.96), channel_id=1, source_target_pairs={{16,20},{17,21},{18,22},{19,23},{20,24},{21,25},{22,26},{23,27},{2... | collective-permute-start | bytes 221192 | tf_op jit(solution)/shard_map/ppermute | solution.py:622
  54.9 14.1 %collective-permute-start.22 = (f32[3,2,8,128]{3,2,1,0:T(8,128)S(1)}, f32[3,2,8,128]{3,2,1,0:T(8,128)S(1)}, u32[]{:S(2)}, u32[]{:S(2)}) collective-permute-start(f32[3,2,8,128]{3,2,1,0:T(8,128)S(1)} %get-tuple-element.99), channel_id=1, source_target_pairs={{0,16},{1,17},{2,18},{3,19},{4,20},{5,21},{6,22},{7,23},{8,24},{9,... | collective-permute-start | bytes 73736 | tf_op jit(solution)/shard_map/ppermute | solution.py:20
  65.7 3.3 %collective-permute-start.21 = (f32[2,6,384]{2,1,0:T(8,128)S(1)}, f32[2,6,384]{2,1,0:T(8,128)S(1)}, u32[]{:S(2)}, u32[]{:S(2)}) collective-permute-start(f32[2,6,384]{2,1,0:T(8,128)S(1)} %get-tuple-element.97), channel_id=1, source_target_pairs={{16,17},{17,18},{18,19},{20,21},{21,22},{22,23},{24,25},{25,26},{2... | collective-permute-start | bytes 55304 | tf_op jit(solution)/shard_map/ppermute | solution.py:623
  66.4 7.7 %collective-permute-start.15 = (f32[80,384]{1,0:T(8,128)S(1)}, f32[80,384]{1,0:T(8,128)S(1)}, u32[]{:S(2)}, u32[]{:S(2)}) collective-permute-start(f32[80,384]{1,0:T(8,128)S(1)} %get-tuple-element.87), channel_id=1, source_target_pairs={{16,0},{17,1},{18,2},{19,3},{20,4},{21,5},{22,6},{23,7},{24,8},{25... | collective-permute-start | bytes 368648 | tf_op jit(solution)/shard_map/ppermute | solution.py:20
  67.7 9.0 %collective-permute-start.16 = (f32[80,384]{1,0:T(8,128)S(1)}, f32[80,384]{1,0:T(8,128)S(1)}, u32[]{:S(2)}, u32[]{:S(2)}) collective-permute-start(f32[80,384]{1,0:T(8,128)S(1)} %get-tuple-element.88), channel_id=1, source_target_pairs={{16,0},{17,1},{18,2},{19,3},{20,4},{21,5},{22,6},{23,7},{24,8},{25... | collective-permute-start | bytes 368648 | tf_op jit(solution)/shard_map/ppermute | solution.py:20
  69.1 13.3 %collective-permute-start.23 = (f32[80,384]{1,0:T(8,128)S(1)}, f32[80,384]{1,0:T(8,128)S(1)}, u32[]{:S(2)}, u32[]{:S(2)}) collective-permute-start(f32[80,384]{1,0:T(8,128)S(1)} %get-tuple-element.101), channel_id=1, source_target_pairs={{16,0},{17,1},{18,2},{19,3},{20,4},{21,5},{22,6},{23,7},{24,8},{25... | collective-permute-start | bytes 368648 | tf_op jit(solution)/shard_map/ppermute | solution.py:20
  70.4 11.1 %collective-permute-start.19 = (f32[64,384]{1,0:T(8,128)S(1)}, f32[64,384]{1,0:T(8,128)S(1)}, u32[]{:S(2)}, u32[]{:S(2)}) collective-permute-start(f32[64,384]{1,0:T(8,128)S(1)} %get-tuple-element.91), channel_id=1, source_target_pairs={{16,0},{17,1},{18,2},{19,3},{20,4},{21,5},{22,6},{23,7},{24,8},{25... | collective-permute-start | bytes 294920 | tf_op jit(solution)/shard_map/ppermute | solution.py:20

commit v4 on v3

--- a/solution.py
+++ b/solution.py
@@ -418,6 +418,15 @@
     return lax.axis_index("grid") == 1
 
 
+def edge_kernel(near_x, near_y, ax, ay):
+    @pl.when(is_coarse())
+    def _():
+        ax[0], ax[1] = near_x[0, 1, 0], near_x[0, 2, 0]
+        for x in range(6):
+            ay[0, x : x + 1] = near_y[0, 0, x, 0:1]
+            ay[1, x : x + 1] = near_y[0, 2, x, 0:1]
+
+
 def h1_kernel(e, h, ax, ay, out_h, bx, by):
     @pl.when(is_coarse())
     def _():
@@ -425,32 +434,31 @@
         last_layers(out_h, bx, by)
 
 
-def e1_kernel(e, h, p, coef, bx, by, desc, out_e, out_p, ax, ay, sent):
+def e1_kernel(e, h, p, coef, bx, by, desc, material, out_e, out_p, sent, out_material):
     @pl.when(is_coarse())
     def _():
         spot = corner(desc)
         before = cut_region(e, desc, spot)
         electric(e, h, p, coef, edge_x(bx), edge_y(by), out_e, out_p)
-        first_layers(out_e, ax, ay)
         after = cut_region(out_e, desc, spot)
         for c in range(3):
             for i in range(2):
                 sent[0, c, i] = before[c][i]
                 sent[1, c, i] = after[c][i]
-
-
-def h2_kernel(e, h, ax, ay, box_in, coef, region, desc, out_e, out_h, bx, by, box, now, change):
-    @pl.when(is_coarse())
-    def _():
-        out_e[...] = e[...]
-        magnetic(e, h, edge_x(ax), edge_y(ay), out_h)
-        last_layers(out_h, bx, by)
+        out_material[...] = material[...]
+
+
+def f1_kernel(e, h, p, box_in, coef, region, desc, out_e, out_h, out_p, ax, ay, box, now, change):
+    @pl.when(is_coarse())
+    def _():
+        out_e[...], out_h[...], out_p[...] = e[...], h[...], p[...]
+        first_layers(e, ax, ay)
 
     @pl.when(is_fine())
     def _():
         box[...] = box_in[...]
-        out_e[...] = jnp.zeros(out_e.shape, F32)
-        out_h[...] = jnp.zeros(out_h.shape, F32)
+        for out in (out_e, out_h, out_p):
+            out[...] = jnp.zeros(out.shape, F32)
         earlier = [[region[0, c, i] for i in range(2)] for c in range(3)]
         latest = [[region[1, c, i] for i in range(2)] for c in range(3)]
         restricted = fine_steps(box, coef, desc, earlier, latest)
@@ -458,52 +466,53 @@
         store_box(now, after)
         store_box(change, delta)
         put(out_e, lambda c, i: delta[c][i], desc, corner(desc))
-
-
-def e2_kernel(e, h, p, coef, bx, by, desc, material, table, out_e, out_p, ax, ay, sent, wide_coef):
-    @pl.when(is_coarse())
-    def _():
-        electric(e, h, p, coef, edge_x(bx), edge_y(by), out_e, out_p)
         first_layers(out_e, ax, ay)
-        store_box(sent, cut_region(out_e, desc, corner(desc)))
+
+
+def h2_kernel(e, h, ax, ay, change, coef, material, table, out_h, bx, by, relay, slab_coef):
+    magnetic(e, h, edge_x(ax), edge_y(ay), out_h)
+    last_layers(out_h, bx, by)
+
+    @pl.when(is_coarse())
+    def _():
+        slab_coef[...] = coef[...]
 
     @pl.when(is_fine())
     def _():
-        out_e[...] = e[...]
-        out_p[...] = jnp.zeros(out_p.shape, F32)
-        first_layers(e, ax, ay)
+        pack(relay, load_box(change), ax, ay)
         tiles = [table[k] for k in range(5)]
         for x in range(6):
             for yt in range(3):
                 for zt in range(3):
                     index = material[0, x, pl.ds(8 * yt, 8), pl.ds(128 * zt, 128)]
                     for k in range(5):
-                        wide_coef[k, x, 3 * yt + zt] = gather(tiles[k], index)
-
-
-def h3_kernel(e, h, ax, ay, change, out_h, bx, by, relay):
-    magnetic(e, h, edge_x(ax), edge_y(ay), out_h)
-    last_layers(out_h, bx, by)
-
-    @pl.when(is_fine())
-    def _():
-        pack(relay, load_box(change), ax, ay)
-
-
-def e3_kernel(
-    e, h, p, coef, wide_coef, bx, by, desc, box_in, region, was,
-    out_e, out_p, ax, ay, sent, box, now, relay,
-):
+                        slab_coef[k, x, 3 * yt + zt] = gather(tiles[k], index)
+
+
+def base_kernel(e, h, p, coef, bx, by, desc, out_e, out_p, sent):
     @pl.when(is_coarse())
     def _():
         electric(e, h, p, coef, edge_x(bx), edge_y(by), out_e, out_p)
         store_box(sent, cut_region(out_e, desc, corner(desc)))
 
+
+def f2_kernel(
+    e, h, p, base_e, base_p, coef, slab_coef, bx, by, desc, box_in, region, was, relay1,
+    out_e, out_p, ax, ay, box, now, relay, fix_h, one_e,
+):
+    @pl.when(is_coarse())
+    def _():
+        out_e[...], out_p[...] = base_e[...], base_p[...]
+        first_layers(base_e, ax, ay)
+        one_e[...] = jnp.zeros(one_e.shape, F32)
+        put(one_e, packed_box(relay1), desc, corner(desc))
+        magnetic(one_e, None, packed_x(relay1, 16), packed_y(relay1, 16), fix_h)
+
     @pl.when(is_fine())
     def _():
         box[...] = box_in[...]
         spot = corner(desc)
-        electric(e, h, p, wide_coef, edge_x(bx), edge_y(by), out_e, out_p)
+        electric(e, h, p, slab_coef, edge_x(bx), edge_y(by), out_e, out_p)
         fix = cut_region(out_e, desc, spot)
         latest = [[region[c, i] + fix[c][i] for i in range(2)] for c in range(3)]
         restricted = fine_steps(box, coef, desc, load_box(was), latest)
@@ -514,15 +523,30 @@
         pack(relay, delta, bx, by)
 
 
-def h4_kernel(e, h, ax, ay, out_h, bx, by, relay):
+def h3_kernel(e, h, ax, ay, out_h, bx, by, relay):
+    magnetic(e, h, edge_x(ax), edge_y(ay), out_h)
+    last_layers(out_h, bx, by)
+
     @pl.when(is_fine())
     def _():
-        magnetic(e, h, edge_x(ax), edge_y(ay), out_h)
-        last_layers(out_h, bx, by)
         pack(relay, None, ax, ay)
 
 
-def e4_kernel(e, h, p, coef, wide_coef, bx, by, desc, box_in, region, was, box, relay, layer):
+def f3_kernel(
+    e, h, p, coef, slab_coef, bx, by, desc, box_in, region, was, relay1, relay2, relay3, one_h,
+    box, relay, fix_e, fix_h, fix_p, layer, one_e,
+):
+    @pl.when(is_coarse())
+    def _():
+        one_e[...] = jnp.zeros(one_e.shape, F32)
+        spot = corner(desc)
+        put(one_e, packed_box(relay1), desc, spot)
+        electric(
+            one_e, one_h, None, coef, packed_x(relay2, 16), packed_y(relay2, 16), fix_e, fix_p
+        )
+        put(fix_e, packed_box(relay2), desc, spot)
+        magnetic(fix_e, one_h, packed_x(relay3, 0), packed_y(relay3, 0), fix_h)
+
     @pl.when(is_fine())
     def _():
         box[...] = box_in[...]
@@ -531,27 +555,13 @@
         for i in range(2):
             x = x0 + i
             rotation = curl_behind(h, x, edge_x(bx), edge_y(by))
-            a, b, q = (whole(wide_coef, k, x) for k in range(3))
+            a, b, q = (whole(slab_coef, k, x) for k in range(3))
             for c in range(3):
                 layer[c, i] = a * e[c, x] + b * rotation[c] + q * p[c, x]
         fix = cut_region(layer, desc, (0, *spot[1:]))
         latest = [[region[c, i] + fix[c][i] for i in range(2)] for c in range(3)]
         restricted = fine_steps(box, coef, desc, load_box(was), latest)
         pack(relay, restricted, bx, by)
-
-
-def redo_kernel(coef, desc, relay1, relay2, relay3, out_e, out_h, out_p, one_e, one_h):
-    @pl.when(is_coarse())
-    def _():
-        spot = corner(desc)
-        one_e[...] = jnp.zeros(one_e.shape, F32)
-        put(one_e, packed_box(relay1), desc, spot)
-        magnetic(one_e, None, packed_x(relay1, 16), packed_y(relay1, 16), one_h)
-        electric(
-            one_e, one_h, None, coef, packed_x(relay2, 16), packed_y(relay2, 16), out_e, out_p
-        )
-        put(out_e, packed_box(relay2), desc, spot)
-        magnetic(out_e, one_h, packed_x(relay3, 0), packed_y(relay3, 0), out_h)
 
 
 def finish_kernel(e, h, p, fix_e, fix_h, fix_p, coef, desc, relay, box, out, mixed):
@@ -633,8 +643,17 @@
 
 
 def body(fields, material, permittivity, conductivity, relax_rate, debye_strength, subgrids):
-    f = fields[0]
-    ax, ay = exchange(f[1:3, 0], f[0:3:2, :, 0], -1, (0,))
+    ax, ay = call(
+        edge_kernel,
+        (fields, fields),
+        EDGES,
+        [
+            pl.BlockSpec((1, 3, 1, 24, 384), lambda i: (0, 0, 0, 0, 0)),
+            pl.BlockSpec((1, 3, 6, 8, 384), lambda i: (0, 0, 0, 0, 0)),
+        ],
+        grid=(1,),
+    )
+    ax, ay = exchange(ax, ay, -1, (0,))
     e, h, p, box, coef, desc, table = call(
         prep_kernel,
         (fields,) * 3
@@ -649,56 +668,58 @@
     )
     h, bx, by = call(h1_kernel, (e, h, ax, ay), [PART] + EDGES)
     bx, by = exchange(bx, by, 1, (0,))
-    e, p, ax, ay, sent = call(
-        e1_kernel, (e, h, p, coef, bx, by, desc), [PART] * 2 + EDGES + [(2, *REGION)]
+    e, p, sent, slab_material = call(
+        e1_kernel,
+        (e, h, p, coef, bx, by, desc, material),
+        [PART] * 2 + [(2, *REGION), jax.ShapeDtypeStruct(material.shape, jnp.int32)],
     )
     region = to_fine(sent)
-    ax, ay = exchange(ax, ay, -1, (0,))
-    slab_material = to_fine(material)
-    e, h, bx, by, box, now, change = call(
+    slab_material = to_fine(slab_material)
+    e, h, p, ax, ay, box, now, change = call(
+        f1_kernel,
+        (e, h, p, box, coef, region, desc),
+        [PART] * 3 + EDGES + [BOX, REGION, REGION],
+    )
+    ax, ay = exchange(ax, ay, -1, (0, 1))
+    h, bx, by, relay1, slab_coef = call(
         h2_kernel,
-        (e, h, ax, ay, box, coef, region, desc),
-        [PART] * 2 + EDGES + [BOX, REGION, REGION],
-    )
+        (e, h, ax, ay, change, coef, slab_material, table),
+        [PART] + EDGES + [(80, 384), COEF],
+    )
+    fine_bx, fine_by = exchange(bx, by, 1, (1,))
     bx, by = exchange(bx, by, 1, (0,))
-    e, p, ax, ay, sent, wide_coef = call(
-        e2_kernel,
-        (e, h, p, coef, bx, by, desc, slab_material, table),
-        [PART] * 2 + EDGES + [REGION, COEF],
+    base_e, base_p, sent = call(
+        base_kernel, (e, h, p, slab_coef, bx, by, desc), [PART] * 2 + [REGION]
     )
     region = to_fine(sent)
+    relay1 = to_coarse(relay1)
+    e, p, ax, ay, box, now, relay2, fix_h = call(
+        f2_kernel,
+        (e, h, p, base_e, base_p, coef, slab_coef, fine_bx, fine_by, desc, box, region, now, relay1),
+        [PART] * 2 + EDGES + [BOX, REGION, (80, 384), PART],
+        scratch=[pltpu.VMEM(PART, F32)],
+    )
     ax, ay = exchange(ax, ay, -1, (0, 1))
-    h, bx, by, relay1 = call(h3_kernel, (e, h, ax, ay, change), [PART] + EDGES + [(80, 384)])
-    bx, by = exchange(bx, by, 1, (0, 1))
-    relay1 = to_coarse(relay1)
-    e, p, ax, ay, sent, box, now, relay2 = call(
-        e3_kernel,
-        (e, h, p, coef, wide_coef, bx, by, desc, box, region, now),
-        [PART] * 2 + EDGES + [REGION, BOX, REGION, (80, 384)],
-    )
-    base_e, base_h, base_p = e, h, p
+    relay2 = to_coarse(relay2)
+    h, bx, by, relay3 = call(h3_kernel, (e, h, ax, ay), [PART] + EDGES + [(64, 384)])
+    fine_bx, fine_by = exchange(bx, by, 1, (1,))
+    bx, by = exchange(bx, by, 1, (0,))
+    base_e, base_p, sent = call(
+        base_kernel, (e, h, p, slab_coef, bx, by, desc), [PART] * 2 + [REGION]
+    )
     region = to_fine(sent)
-    ax, ay = exchange(ax, ay, -1, (1,))
-    relay2 = to_coarse(relay2)
-    h, bx, by, relay3 = call(h4_kernel, (e, h, ax, ay), [PART] + EDGES + [(64, 384)])
-    bx, by = exchange(bx, by, 1, (1,))
     relay3 = to_coarse(relay3)
-    box, relay4 = call(
-        e4_kernel,
-        (e, h, p, coef, wide_coef, bx, by, desc, box, region, now),
-        [BOX, (80, 384)],
-        scratch=[pltpu.VMEM((3, 2, 24, 384), F32)],
+    box, relay4, *fix = call(
+        f3_kernel,
+        (e, h, p, coef, slab_coef, fine_bx, fine_by, desc, box, region, now)
+        + (relay1, relay2, relay3, fix_h),
+        [BOX, (80, 384)] + [PART] * 3,
+        scratch=[pltpu.VMEM((3, 2, 24, 384), F32), pltpu.VMEM(PART, F32)],
     )
     relay4 = to_coarse(relay4)
-    fix = call(
-        redo_kernel,
-        (coef, desc, relay1, relay2, relay3),
-        [PART] * 3,
-        scratch=[pltpu.VMEM(PART, F32)] * 2,
-    )
     (out,) = call(
         finish_kernel,
-        (base_e, base_h, base_p, *fix, coef, desc, relay4, box),
+        (base_e, h, base_p, *fix, coef, desc, relay4, box),
         [SLAB],
         scratch=[pltpu.VMEM((9, 6, 3, 24, 128), F32)],
     )

time: 84.8 us -> 80.5 us (0.949)
  starting transfers between devices: 52.6 us -> 45 us
  waiting for transfers between devices: 22.7 us -> 26.5 us
    ppermute x8, starting transfers between devices: 19.9 us -> 14.1 us  [shifted(): return lax.ppermute(value, axis, pairs)]
    ppermute x8, waiting for transfers between devices: 9.83 us -> 14.4 us  [shifted(): return lax.ppermute(value, axis, pairs)]
    ppermute x8, starting transfers between devices: 16.6 us -> 14.1 us  [exchange(): lax.ppermute(y_edge, AXES, pairs(0, by))]
    ppermute x8, waiting for transfers between devices: 6.4 us -> 5.42 us  [exchange(): lax.ppermute(x_edge, AXES, pairs(by, 0))]
    unnamed x16 -> x14, local copies, waits for them, and re-layouts: 2.29 us -> 1.58 us
    pallas_call x11 -> x12, Pallas kernels: 6.23 us -> 6.42 us  [call(): pl.pallas_call(kernel, out_shape=shapes, in_specs=specs or [VM] * len(ope...]
  transfers between devices with their start and end apart: 24 -> 24, of which waited for: 11 -> 13; matrix products, arithmetic and copies ran while one was open for 0% -> 0% of each run, Pallas kernels for 3% -> 3%
where the time goes in v4:
time: 80.5 us; the launch traced here: 79.9 us
  starting transfers between devices  45 us (56%)
  waiting for transfers between devices  26.5 us (33%)
  Pallas kernels  6.42 us (8%)
  local copies, waits for them, and re-layouts  1.58 us (2%)
    ppermute x8, starting transfers between devices, exchange(): lax.ppermute(x_edge, AXES, pairs(by, 0))  16.8 us
    ppermute x8, waiting for transfers between devices, shifted(): return lax.ppermute(value, axis, pairs)  14.4 us
    ppermute x8, starting transfers between devices, exchange(): lax.ppermute(y_edge, AXES, pairs(0, by))  14.1 us
    ppermute x8, starting transfers between devices, shifted(): return lax.ppermute(value, axis, pairs)  14.1 us
    ppermute x8, waiting for transfers between devices, exchange(): lax.ppermute(y_edge, AXES, pairs(0, by))  6.67 us
    pallas_call x12, Pallas kernels, call(): pl.pallas_call(kernel, out_shape=shapes, in_specs=specs or [VM] * len(ope...  6.42 us
    ppermute x8, waiting for transfers between devices, exchange(): lax.ppermute(x_edge, AXES, pairs(by, 0))  5.42 us
  transfers between devices with their start and end apart: 24, of which 13 were waited for; matrix products, arithmetic and copies ran while one was open for 0% of the time, Pallas kernels for 3%

profile of v4, /device:TPU:0, one launch (start us, length us, event | category | flops | bytes accessed | tf_op | source)
XLA Modules:
  0.0 79.9 jit_solution(14089298873362970125)
XLA Ops:
  0.0 1.6 %copy-done = f32[1,9,6,24,384]{4,3,2,1,0:T(8,128)S(1)} copy-done((f32[1,9,6,24,384]{4,3,2,1,0:T(8,128)S(1)}, f32[1,9,6,24,384]{4,3,2,1,0:T(8,128)}, u32[]{:S(2)}) %copy-start) | copy-done | bytes 1990680
  1.6 1.4 %collective-permute-start = (f32[2,24,384]{2,1,0:T(8,128)S(1)}, f32[2,24,384]{2,1,0:T(8,128)S(1)}, u32[]{:S(2)}, u32[]{:S(2)}) collective-permute-start(f32[2,24,384]{2,1,0:T(8,128)S(1)} %get-tuple-element.59), channel_id=1, source_target_pairs={{4,0},{5,1},{6,2},{7,3},{8,4},{9,5},{10,6},{11,7},{12,8},{13,9},{1... | collective-permute-start | bytes 221192 | tf_op jit(solution)/shard_map/ppermute | solution.py:632
  3.1 1.3 %collective-permute-start.1 = (f32[2,6,384]{2,1,0:T(8,128)S(1)}, f32[2,6,384]{2,1,0:T(8,128)S(1)}, u32[]{:S(2)}, u32[]{:S(2)}) collective-permute-start(f32[2,6,384]{2,1,0:T(8,128)S(1)} %get-tuple-element.60), channel_id=1, source_target_pairs={{1,0},{2,1},{3,2},{5,4},{6,5},{7,6},{9,8},{10,9},{11,10},{13,12},{... | collective-permute-start | bytes 55304 | tf_op jit(solution)/shard_map/ppermute | solution.py:633
  4.4 1.1 %shard_map.73 = (f32[3,6,24,384]{3,2,1,0:T(8,128)S(1)}, f32[3,6,24,384]{3,2,1,0:T(8,128)S(1)}, f32[3,6,24,384]{3,2,1,0:T(8,128)S(1)}, f32[9,6,9,8,128]{4,3,2,1,0...) custom-call(f32[1,9,6,24,384]{4,3,2,1,0:T(8,128)S(1)} %copy-done, ...), custom_call_target="tpu_custom_call" | custom-call | tf_op jit(solution)/shard_map/pallas_call | solution.py:597
  5.6 0.6 collective-permute-done.1.ay
  6.1 2.9 %collective-permute-done.ax = f32[2,24,384]{2,1,0:T(8,128)S(1)} collective-permute-done((f32[2,24,384]{2,1,0:T(8,128)S(1)}, f32[2,24,384]{2,1,0:T(8,128)S(1)}, u32[]{:S(2)}, u32[]{:S(2)}) %collective-permute-start) | collective-permute-done | bytes 73760 | tf_op jit(solution)/shard_map/ppermute | solution.py:632
  9.0 0.2 shard_map.75
  9.2 3.9 %collective-permute-start.2 = (f32[2,24,384]{2,1,0:T(8,128)S(1)}, f32[2,24,384]{2,1,0:T(8,128)S(1)}, u32[]{:S(2)}, u32[]{:S(2)}) collective-permute-start(f32[2,24,384]{2,1,0:T(8,128)S(1)} %get-tuple-element.64), channel_id=1, source_target_pairs={{0,4},{1,5},{2,6},{3,7},{4,8},{5,9},{6,10},{7,11},{8,12},{9,13},{1... | collective-permute-start | bytes 221192 | tf_op jit(solution)/shard_map/ppermute | solution.py:632
  13.2 2.8 %collective-permute-start.3 = (f32[2,6,384]{2,1,0:T(8,128)S(1)}, f32[2,6,384]{2,1,0:T(8,128)S(1)}, u32[]{:S(2)}, u32[]{:S(2)}) collective-permute-start(f32[2,6,384]{2,1,0:T(8,128)S(1)} %get-tuple-element.65), channel_id=1, source_target_pairs={{0,1},{1,2},{2,3},{4,5},{5,6},{6,7},{8,9},{9,10},{10,11},{12,13},{... | collective-permute-start | bytes 55304 | tf_op jit(solution)/shard_map/ppermute | solution.py:633
  16.0 0.8 %collective-permute-done.3.by = f32[2,6,384]{2,1,0:T(8,128)S(1)} collective-permute-done((f32[2,6,384]{2,1,0:T(8,128)S(1)}, f32[2,6,384]{2,1,0:T(8,128)S(1)}, u32[]{:S(2)}, u32[]{:S(2)}) %collective-permute-start.3) | collective-permute-done | bytes 18464 | tf_op jit(solution)/shard_map/ppermute | solution.py:633
  16.8 0.5 shard_map.76
  17.3 1.3 %collective-permute-start.7 = (s32[1,6,24,384]{3,2,1,0:T(8,128)S(1)}, s32[1,6,24,384]{3,2,1,0:T(8,128)S(1)}, u32[]{:S(2)}, u32[]{:S(2)}) collective-permute-start(s32[1,6,24,384]{3,2,1,0:T(8,128)S(1)} %get-tuple-element.76), channel_id=1, source_target_pairs={{0,16},{1,17},{2,18},{3,19},{4,20},{5,21},{6,22},{7,23},{8,24},{9,... | collective-permute-start | bytes 663560 | tf_op jit(solution)/shard_map/ppermute | solution.py:20
  18.7 1.3 %collective-permute-start.4 = (f32[2,3,2,8,128]{4,3,2,1,0:T(8,128)S(1)}, f32[2,3,2,8,128]{4,3,2,1,0:T(8,128)S(1)}, u32[]{:S(2)}, u32[]{:S(2)}) collective-permute-start(f32[2,3,2,8,128]{4,3,2,1,0:T(8,128)S(1)} %get-tuple-element.70), channel_id=1, source_target_pairs={{0,16},{1,17},{2,18},{3,19},{4,20},{5,21},{6,22},{7,23},{8,24},{9,... | collective-permute-start | bytes 147464 | tf_op jit(solution)/shard_map/ppermute | solution.py:20
  20.0 5.4 %collective-permute-done.4.region = f32[2,3,2,8,128]{4,3,2,1,0:T(8,128)S(1)} collective-permute-done((f32[2,3,2,8,128]{4,3,2,1,0:T(8,128)S(1)}, f32[2,3,2,8,128]{4,3,2,1,0:T(8,128)S(1)}, u32[]{:S(2)}, u32[]{:S(2)}) %collective-permute-start.4) | collective-permute-done | bytes 49184 | tf_op jit(solution)/shard_map/ppermute | solution.py:20
  25.5 1.3 %collective-permute-start.5 = (f32[2,24,384]{2,1,0:T(8,128)S(1)}, f32[2,24,384]{2,1,0:T(8,128)S(1)}, u32[]{:S(2)}, u32[]{:S(2)}) collective-permute-start(f32[2,24,384]{2,1,0:T(8,128)S(1)} %get-tuple-element.73), channel_id=1, source_target_pairs={{4,0},{5,1},{6,2},{7,3},{8,4},{9,5},{10,6},{11,7},{12,8},{13,9},{1... | collective-permute-start | bytes 221192 | tf_op jit(solution)/shard_map/ppermute | solution.py:632
  26.8 1.3 %collective-permute-start.6 = (f32[2,6,384]{2,1,0:T(8,128)S(1)}, f32[2,6,384]{2,1,0:T(8,128)S(1)}, u32[]{:S(2)}, u32[]{:S(2)}) collective-permute-start(f32[2,6,384]{2,1,0:T(8,128)S(1)} %get-tuple-element.74), channel_id=1, source_target_pairs={{1,0},{2,1},{3,2},{5,4},{6,5},{7,6},{9,8},{10,9},{11,10},{13,12},{... | collective-permute-start | bytes 55304 | tf_op jit(solution)/shard_map/ppermute | solution.py:633
  28.1 1.8 %collective-permute-done.6.ay = f32[2,6,384]{2,1,0:T(8,128)S(1)} collective-permute-done((f32[2,6,384]{2,1,0:T(8,128)S(1)}, f32[2,6,384]{2,1,0:T(8,128)S(1)}, u32[]{:S(2)}, u32[]{:S(2)}) %collective-permute-start.6) | collective-permute-done | bytes 18464 | tf_op jit(solution)/shard_map/ppermute | solution.py:633
  29.9 2.0 %collective-permute-done.5.ax = f32[2,24,384]{2,1,0:T(8,128)S(1)} collective-permute-done((f32[2,24,384]{2,1,0:T(8,128)S(1)}, f32[2,24,384]{2,1,0:T(8,128)S(1)}, u32[]{:S(2)}, u32[]{:S(2)}) %collective-permute-start.5) | collective-permute-done | bytes 73760 | tf_op jit(solution)/shard_map/ppermute | solution.py:632
  31.9 0.3 shard_map.78
  32.2 1.3 %collective-permute-start.13 = (f32[80,384]{1,0:T(8,128)S(1)}, f32[80,384]{1,0:T(8,128)S(1)}, u32[]{:S(2)}, u32[]{:S(2)}) collective-permute-start(f32[80,384]{1,0:T(8,128)S(1)} %get-tuple-element.88), channel_id=1, source_target_pairs={{16,0},{17,1},{18,2},{19,3},{20,4},{21,5},{22,6},{23,7},{24,8},{25... | collective-permute-start | bytes 368648 | tf_op jit(solution)/shard_map/ppermute | solution.py:20
  33.5 3.5 %collective-permute-start.8 = (f32[2,24,384]{2,1,0:T(8,128)S(1)}, f32[2,24,384]{2,1,0:T(8,128)S(1)}, u32[]{:S(2)}, u32[]{:S(2)}) collective-permute-start(f32[2,24,384]{2,1,0:T(8,128)S(1)} %get-tuple-element.81), channel_id=1, source_target_pairs={{0,4},{1,5},{2,6},{3,7},{4,8},{5,9},{6,10},{7,11},{8,12},{9,13},{1... | collective-permute-start | bytes 221192 | tf_op jit(solution)/shard_map/ppermute | solution.py:632
  37.0 0.7 collective-permute-start.10
  37.7 2.8 %collective-permute-start.9 = (f32[2,6,384]{2,1,0:T(8,128)S(1)}, f32[2,6,384]{2,1,0:T(8,128)S(1)}, u32[]{:S(2)}, u32[]{:S(2)}) collective-permute-start(f32[2,6,384]{2,1,0:T(8,128)S(1)} %get-tuple-element.82), channel_id=1, source_target_pairs={{0,1},{1,2},{2,3},{4,5},{5,6},{6,7},{8,9},{9,10},{10,11},{12,13},{... | collective-permute-start | bytes 55304 | tf_op jit(solution)/shard_map/ppermute | solution.py:633
  40.4 0.8 %collective-permute-done.9.by = f32[2,6,384]{2,1,0:T(8,128)S(1)} collective-permute-done((f32[2,6,384]{2,1,0:T(8,128)S(1)}, f32[2,6,384]{2,1,0:T(8,128)S(1)}, u32[]{:S(2)}, u32[]{:S(2)}) %collective-permute-start.9) | collective-permute-done | bytes 18464 | tf_op jit(solution)/shard_map/ppermute | solution.py:633
  41.3 0.5 shard_map.79
  41.8 3.0 %collective-permute-start.12 = (f32[3,2,8,128]{3,2,1,0:T(8,128)S(1)}, f32[3,2,8,128]{3,2,1,0:T(8,128)S(1)}, u32[]{:S(2)}, u32[]{:S(2)}) collective-permute-start(f32[3,2,8,128]{3,2,1,0:T(8,128)S(1)} %get-tuple-element.86), channel_id=1, source_target_pairs={{0,16},{1,17},{2,18},{3,19},{4,20},{5,21},{6,22},{7,23},{8,24},{9,... | collective-permute-start | bytes 73736 | tf_op jit(solution)/shard_map/ppermute | solution.py:20
  44.8 0.7 collective-permute-start.11
  45.5 0.8 %collective-permute-done.12.region = f32[3,2,8,128]{3,2,1,0:T(8,128)S(1)} collective-permute-done((f32[3,2,8,128]{3,2,1,0:T(8,128)S(1)}, f32[3,2,8,128]{3,2,1,0:T(8,128)S(1)}, u32[]{:S(2)}, u32[]{:S(2)}) %collective-permute-start.12) | collective-permute-done | bytes 24608 | tf_op jit(solution)/shard_map/ppermute | solution.py:20
  46.3 0.4 shard_map.80
  46.7 1.3 %collective-permute-start.14 = (f32[2,24,384]{2,1,0:T(8,128)S(1)}, f32[2,24,384]{2,1,0:T(8,128)S(1)}, u32[]{:S(2)}, u32[]{:S(2)}) collective-permute-start(f32[2,24,384]{2,1,0:T(8,128)S(1)} %get-tuple-element.90), channel_id=1, source_target_pairs={{4,0},{5,1},{6,2},{7,3},{8,4},{9,5},{10,6},{11,7},{12,8},{13,9},{1... | collective-permute-start | bytes 221192 | tf_op jit(solution)/shard_map/ppermute | solution.py:632
  48.0 1.3 %collective-permute-start.21 = (f32[80,384]{1,0:T(8,128)S(1)}, f32[80,384]{1,0:T(8,128)S(1)}, u32[]{:S(2)}, u32[]{:S(2)}) collective-permute-start(f32[80,384]{1,0:T(8,128)S(1)} %get-tuple-element.101), channel_id=1, source_target_pairs={{16,0},{17,1},{18,2},{19,3},{20,4},{21,5},{22,6},{23,7},{24,8},{25... | collective-permute-start | bytes 368648 | tf_op jit(solution)/shard_map/ppermute | solution.py:20
  49.3 1.3 %collective-permute-start.15 = (f32[2,6,384]{2,1,0:T(8,128)S(1)}, f32[2,6,384]{2,1,0:T(8,128)S(1)}, u32[]{:S(2)}, u32[]{:S(2)}) collective-permute-start(f32[2,6,384]{2,1,0:T(8,128)S(1)} %get-tuple-element.91), channel_id=1, source_target_pairs={{1,0},{2,1},{3,2},{5,4},{6,5},{7,6},{9,8},{10,9},{11,10},{13,12},{... | collective-permute-start | bytes 55304 | tf_op jit(solution)/shard_map/ppermute | solution.py:633
  50.6 1.8 %collective-permute-done.15.ay = f32[2,6,384]{2,1,0:T(8,128)S(1)} collective-permute-done((f32[2,6,384]{2,1,0:T(8,128)S(1)}, f32[2,6,384]{2,1,0:T(8,128)S(1)}, u32[]{:S(2)}, u32[]{:S(2)}) %collective-permute-start.15) | collective-permute-done | bytes 18464 | tf_op jit(solution)/shard_map/ppermute | solution.py:633
  52.4 0.6 collective-permute-done.14.ax
  53.0 0.2 shard_map.81
  53.2 4.0 %collective-permute-start.16 = (f32[2,24,384]{2,1,0:T(8,128)S(1)}, f32[2,24,384]{2,1,0:T(8,128)S(1)}, u32[]{:S(2)}, u32[]{:S(2)}) collective-permute-start(f32[2,24,384]{2,1,0:T(8,128)S(1)} %get-tuple-element.94), channel_id=1, source_target_pairs={{0,4},{1,5},{2,6},{3,7},{4,8},{5,9},{6,10},{7,11},{8,12},{9,13},{1... | collective-permute-start | bytes 221192 | tf_op jit(solution)/shard_map/ppermute | solution.py:632
  57.2 1.3 %collective-permute-start.22 = (f32[64,384]{1,0:T(8,128)S(1)}, f32[64,384]{1,0:T(8,128)S(1)}, u32[]{:S(2)}, u32[]{:S(2)}) collective-permute-start(f32[64,384]{1,0:T(8,128)S(1)} %get-tuple-element.102), channel_id=1, source_target_pairs={{16,0},{17,1},{18,2},{19,3},{20,4},{21,5},{22,6},{23,7},{24,8},{25... | collective-permute-start | bytes 294920 | tf_op jit(solution)/shard_map/ppermute | solution.py:20
  58.5 0.7 collective-permute-start.18
  59.2 3.4 %collective-permute-start.17 = (f32[2,6,384]{2,1,0:T(8,128)S(1)}, f32[2,6,384]{2,1,0:T(8,128)S(1)}, u32[]{:S(2)}, u32[]{:S(2)}) collective-permute-start(f32[2,6,384]{2,1,0:T(8,128)S(1)} %get-tuple-element.95), channel_id=1, source_target_pairs={{0,1},{1,2},{2,3},{4,5},{5,6},{6,7},{8,9},{9,10},{10,11},{12,13},{... | collective-permute-start | bytes 55304 | tf_op jit(solution)/shard_map/ppermute | solution.py:633
  62.6 0.8 %collective-permute-done.17.by = f32[2,6,384]{2,1,0:T(8,128)S(1)} collective-permute-done((f32[2,6,384]{2,1,0:T(8,128)S(1)}, f32[2,6,384]{2,1,0:T(8,128)S(1)}, u32[]{:S(2)}, u32[]{:S(2)}) %collective-permute-start.17) | collective-permute-done | bytes 18464 | tf_op jit(solution)/shard_map/ppermute | solution.py:633
  63.4 0.5 shard_map.82
  63.9 3.3 %collective-permute-start.20 = (f32[3,2,8,128]{3,2,1,0:T(8,128)S(1)}, f32[3,2,8,128]{3,2,1,0:T(8,128)S(1)}, u32[]{:S(2)}, u32[]{:S(2)}) collective-permute-start(f32[3,2,8,128]{3,2,1,0:T(8,128)S(1)} %get-tuple-element.99), channel_id=1, source_target_pairs={{0,16},{1,17},{2,18},{3,19},{4,20},{5,21},{6,22},{7,23},{8,24},{9,... | collective-permute-start | bytes 73736 | tf_op jit(solution)/shard_map/ppermute | solution.py:20
  67.2 0.7 collective-permute-start.19
  67.9 0.8 %collective-permute-done.20.region = f32[3,2,8,128]{3,2,1,0:T(8,128)S(1)} collective-permute-done((f32[3,2,8,128]{3,2,1,0:T(8,128)S(1)}, f32[3,2,8,128]{3,2,1,0:T(8,128)S(1)}, u32[]{:S(2)}, u32[]{:S(2)}) %collective-permute-start.20) | collective-permute-done | bytes 24608 | tf_op jit(solution)/shard_map/ppermute | solution.py:20
  68.7 0.6 shard_map.83
  69.4 1.3 %collective-permute-start.23 = (f32[80,384]{1,0:T(8,128)S(1)}, f32[80,384]{1,0:T(8,128)S(1)}, u32[]{:S(2)}, u32[]{:S(2)}) collective-permute-start(f32[80,384]{1,0:T(8,128)S(1)} %get-tuple-element.107), channel_id=1, source_target_pairs={{16,0},{17,1},{18,2},{19,3},{20,4},{21,5},{22,6},{23,7},{24,8},{25... | collective-permute-start | bytes 368648 | tf_op jit(solution)/shard_map/ppermute | solution.py:20
  70.7 7.4 %collective-permute-done.23.relay = f32[80,384]{1,0:T(8,128)S(1)} collective-permute-done((f32[80,384]{1,0:T(8,128)S(1)}, f32[80,384]{1,0:T(8,128)S(1)}, u32[]{:S(2)}, u32[]{:S(2)}) %collective-permute-start.23) | collective-permute-done | bytes 122912 | tf_op jit(solution)/shard_map/ppermute | solution.py:20
  78.1 1.8 %shard_map.84 = f32[9,6,24,384]{3,2,1,0:T(8,128)} custom-call(f32[3,6,24,384]{3,2,1,0:T(8,128)S(1)} %get-tuple-element.96.e, f32[3,6,24,384]{3,2,1,0:T(8,128)S(1)} %get-tuple-element.92.h, f32[3,6,24,384]{3,2,1,0:T(8,128)S(1)} %get-tuple-element.97.p, f32[3,6,24,384]{3,2,1,0:T(8,128)S(1)} %get-tuple-element.104.fix_e, ...), custom_call_target="tpu_custom_call" | custom-call | tf_op jit(solution)/shard_map/pallas_call | solution.py:597
  (26 shorter events, 0.2 us)
Async XLA Ops:
  0.0 1.6 %copy-start = (f32[1,9,6,24,384]{4,3,2,1,0:T(8,128)S(1)}, f32[1,9,6,24,384]{4,3,2,1,0:T(8,128)}, u32[]{:S(2)}) copy-start(f32[1,9,6,24,384]{4,3,2,1,0:T(8,128)} %near_y.1) | copy-start | bytes 5971972
  1.6 2.8 %copy-start.1 = (s32[1,6,24,384]{3,2,1,0:T(8,128)S(1)}, s32[1,6,24,384]{3,2,1,0:T(8,128)}, u32[]{:S(2)}) copy-start(s32[1,6,24,384]{3,2,1,0:T(8,128)} %material.1) | copy-start | bytes 663556
  1.6 2.8 %copy-start.2 = (f32[8]{0:T(128)S(1)}, f32[8]{0:T(128)}, u32[]{:S(2)}) copy-start(f32[8]{0:T(128)} %perm.1) | copy-start | bytes 100
  1.6 2.8 %copy-start.3 = (f32[8]{0:T(128)S(1)}, f32[8]{0:T(128)}, u32[]{:S(2)}) copy-start(f32[8]{0:T(128)} %cond.1) | copy-start | bytes 100
  1.6 2.8 %copy-start.4 = (f32[8]{0:T(128)S(1)}, f32[8]{0:T(128)}, u32[]{:S(2)}) copy-start(f32[8]{0:T(128)} %relax.1) | copy-start | bytes 100
  1.6 2.8 %copy-start.5 = (f32[8]{0:T(128)S(1)}, f32[8]{0:T(128)}, u32[]{:S(2)}) copy-start(f32[8]{0:T(128)} %debye.1) | copy-start | bytes 100
  1.6 2.8 %copy-start.6 = (s32[1,1,6]{2,1,0:T(1,128)S(1)}, s32[1,1,6]{2,1,0:T(1,128)}, u32[]{:S(2)}) copy-start(s32[1,1,6]{2,1,0:T(1,128)} %sub.1) | copy-start | bytes 76
  1.6 7.4 %collective-permute-start = (f32[2,24,384]{2,1,0:T(8,128)S(1)}, f32[2,24,384]{2,1,0:T(8,128)S(1)}, u32[]{:S(2)}, u32[]{:S(2)}) collective-permute-start(f32[2,24,384]{2,1,0:T(8,128)S(1)} %get-tuple-element.59), channel_id=1, source_target_pairs={{4,0},{5,1},{6,2},{7,3},{8,4},{9,5},{10,6},{11,7},{12,8},{13,9},{1... | collective-permute-start | bytes 221192 | tf_op jit(solution)/shard_map/ppermute | solution.py:632
  3.1 3.1 %collective-permute-start.1 = (f32[2,6,384]{2,1,0:T(8,128)S(1)}, f32[2,6,384]{2,1,0:T(8,128)S(1)}, u32[]{:S(2)}, u32[]{:S(2)}) collective-permute-start(f32[2,6,384]{2,1,0:T(8,128)S(1)} %get-tuple-element.60), channel_id=1, source_target_pairs={{1,0},{2,1},{3,2},{5,4},{6,5},{7,6},{9,8},{10,9},{11,10},{13,12},{... | collective-permute-start | bytes 55304 | tf_op jit(solution)/shard_map/ppermute | solution.py:633
  9.2 7.6 %collective-permute-start.2 = (f32[2,24,384]{2,1,0:T(8,128)S(1)}, f32[2,24,384]{2,1,0:T(8,128)S(1)}, u32[]{:S(2)}, u32[]{:S(2)}) collective-permute-start(f32[2,24,384]{2,1,0:T(8,128)S(1)} %get-tuple-element.64), channel_id=1, source_target_pairs={{0,4},{1,5},{2,6},{3,7},{4,8},{5,9},{6,10},{7,11},{8,12},{9,13},{1... | collective-permute-start | bytes 221192 | tf_op jit(solution)/shard_map/ppermute | solution.py:632
  13.2 3.6 %collective-permute-start.3 = (f32[2,6,384]{2,1,0:T(8,128)S(1)}, f32[2,6,384]{2,1,0:T(8,128)S(1)}, u32[]{:S(2)}, u32[]{:S(2)}) collective-permute-start(f32[2,6,384]{2,1,0:T(8,128)S(1)} %get-tuple-element.65), channel_id=1, source_target_pairs={{0,1},{1,2},{2,3},{4,5},{5,6},{6,7},{8,9},{9,10},{10,11},{12,13},{... | collective-permute-start | bytes 55304 | tf_op jit(solution)/shard_map/ppermute | solution.py:633
  17.3 14.5 %collective-permute-start.7 = (s32[1,6,24,384]{3,2,1,0:T(8,128)S(1)}, s32[1,6,24,384]{3,2,1,0:T(8,128)S(1)}, u32[]{:S(2)}, u32[]{:S(2)}) collective-permute-start(s32[1,6,24,384]{3,2,1,0:T(8,128)S(1)} %get-tuple-element.76), channel_id=1, source_target_pairs={{0,16},{1,17},{2,18},{3,19},{4,20},{5,21},{6,22},{7,23},{8,24},{9,... | collective-permute-start | bytes 663560 | tf_op jit(solution)/shard_map/ppermute | solution.py:20
  18.7 6.7 %collective-permute-start.4 = (f32[2,3,2,8,128]{4,3,2,1,0:T(8,128)S(1)}, f32[2,3,2,8,128]{4,3,2,1,0:T(8,128)S(1)}, u32[]{:S(2)}, u32[]{:S(2)}) collective-permute-start(f32[2,3,2,8,128]{4,3,2,1,0:T(8,128)S(1)} %get-tuple-element.70), channel_id=1, source_target_pairs={{0,16},{1,17},{2,18},{3,19},{4,20},{5,21},{6,22},{7,23},{8,24},{9,... | collective-permute-start | bytes 147464 | tf_op jit(solution)/shard_map/ppermute | solution.py:20
  25.5 6.4 %collective-permute-start.5 = (f32[2,24,384]{2,1,0:T(8,128)S(1)}, f32[2,24,384]{2,1,0:T(8,128)S(1)}, u32[]{:S(2)}, u32[]{:S(2)}) collective-permute-start(f32[2,24,384]{2,1,0:T(8,128)S(1)} %get-tuple-element.73), channel_id=1, source_target_pairs={{4,0},{5,1},{6,2},{7,3},{8,4},{9,5},{10,6},{11,7},{12,8},{13,9},{1... | collective-permute-start | bytes 221192 | tf_op jit(solution)/shard_map/ppermute | solution.py:632
  26.8 3.1 %collective-permute-start.6 = (f32[2,6,384]{2,1,0:T(8,128)S(1)}, f32[2,6,384]{2,1,0:T(8,128)S(1)}, u32[]{:S(2)}, u32[]{:S(2)}) collective-permute-start(f32[2,6,384]{2,1,0:T(8,128)S(1)} %get-tuple-element.74), channel_id=1, source_target_pairs={{1,0},{2,1},{3,2},{5,4},{6,5},{7,6},{9,8},{10,9},{11,10},{13,12},{... | collective-permute-start | bytes 55304 | tf_op jit(solution)/shard_map/ppermute | solution.py:633
  32.2 14.2 %collective-permute-start.13 = (f32[80,384]{1,0:T(8,128)S(1)}, f32[80,384]{1,0:T(8,128)S(1)}, u32[]{:S(2)}, u32[]{:S(2)}) collective-permute-start(f32[80,384]{1,0:T(8,128)S(1)} %get-tuple-element.88), channel_id=1, source_target_pairs={{16,0},{17,1},{18,2},{19,3},{20,4},{21,5},{22,6},{23,7},{24,8},{25... | collective-permute-start | bytes 368648 | tf_op jit(solution)/shard_map/ppermute | solution.py:20
  33.5 7.8 %collective-permute-start.8 = (f32[2,24,384]{2,1,0:T(8,128)S(1)}, f32[2,24,384]{2,1,0:T(8,128)S(1)}, u32[]{:S(2)}, u32[]{:S(2)}) collective-permute-start(f32[2,24,384]{2,1,0:T(8,128)S(1)} %get-tuple-element.81), channel_id=1, source_target_pairs={{0,4},{1,5},{2,6},{3,7},{4,8},{5,9},{6,10},{7,11},{8,12},{9,13},{1... | collective-permute-start | bytes 221192 | tf_op jit(solution)/shard_map/ppermute | solution.py:632
  37.0 8.5 %collective-permute-start.10 = (f32[2,24,384]{2,1,0:T(8,128)S(1)}, f32[2,24,384]{2,1,0:T(8,128)S(1)}, u32[]{:S(2)}, u32[]{:S(2)}) collective-permute-start(f32[2,24,384]{2,1,0:T(8,128)S(1)} %get-tuple-element.81), channel_id=1, source_target_pairs={{16,20},{17,21},{18,22},{19,23},{20,24},{21,25},{22,26},{23,27},{2... | collective-permute-start | bytes 221192 | tf_op jit(solution)/shard_map/ppermute | solution.py:632
  37.7 3.6 %collective-permute-start.9 = (f32[2,6,384]{2,1,0:T(8,128)S(1)}, f32[2,6,384]{2,1,0:T(8,128)S(1)}, u32[]{:S(2)}, u32[]{:S(2)}) collective-permute-start(f32[2,6,384]{2,1,0:T(8,128)S(1)} %get-tuple-element.82), channel_id=1, source_target_pairs={{0,1},{1,2},{2,3},{4,5},{5,6},{6,7},{8,9},{9,10},{10,11},{12,13},{... | collective-permute-start | bytes 55304 | tf_op jit(solution)/shard_map/ppermute | solution.py:633
  41.8 4.5 %collective-permute-start.12 = (f32[3,2,8,128]{3,2,1,0:T(8,128)S(1)}, f32[3,2,8,128]{3,2,1,0:T(8,128)S(1)}, u32[]{:S(2)}, u32[]{:S(2)}) collective-permute-start(f32[3,2,8,128]{3,2,1,0:T(8,128)S(1)} %get-tuple-element.86), channel_id=1, source_target_pairs={{0,16},{1,17},{2,18},{3,19},{4,20},{5,21},{6,22},{7,23},{8,24},{9,... | collective-permute-start | bytes 73736 | tf_op jit(solution)/shard_map/ppermute | solution.py:20
  44.8 0.7 collective-permute-start.11
  46.7 6.2 %collective-permute-start.14 = (f32[2,24,384]{2,1,0:T(8,128)S(1)}, f32[2,24,384]{2,1,0:T(8,128)S(1)}, u32[]{:S(2)}, u32[]{:S(2)}) collective-permute-start(f32[2,24,384]{2,1,0:T(8,128)S(1)} %get-tuple-element.90), channel_id=1, source_target_pairs={{4,0},{5,1},{6,2},{7,3},{8,4},{9,5},{10,6},{11,7},{12,8},{13,9},{1... | collective-permute-start | bytes 221192 | tf_op jit(solution)/shard_map/ppermute | solution.py:632
  48.0 19.9 %collective-permute-start.21 = (f32[80,384]{1,0:T(8,128)S(1)}, f32[80,384]{1,0:T(8,128)S(1)}, u32[]{:S(2)}, u32[]{:S(2)}) collective-permute-start(f32[80,384]{1,0:T(8,128)S(1)} %get-tuple-element.101), channel_id=1, source_target_pairs={{16,0},{17,1},{18,2},{19,3},{20,4},{21,5},{22,6},{23,7},{24,8},{25... | collective-permute-start | bytes 368648 | tf_op jit(solution)/shard_map/ppermute | solution.py:20
  49.3 3.1 %collective-permute-start.15 = (f32[2,6,384]{2,1,0:T(8,128)S(1)}, f32[2,6,384]{2,1,0:T(8,128)S(1)}, u32[]{:S(2)}, u32[]{:S(2)}) collective-permute-start(f32[2,6,384]{2,1,0:T(8,128)S(1)} %get-tuple-element.91), channel_id=1, source_target_pairs={{1,0},{2,1},{3,2},{5,4},{6,5},{7,6},{9,8},{10,9},{11,10},{13,12},{... | collective-permute-start | bytes 55304 | tf_op jit(solution)/shard_map/ppermute | solution.py:633
  53.2 10.2 %collective-permute-start.16 = (f32[2,24,384]{2,1,0:T(8,128)S(1)}, f32[2,24,384]{2,1,0:T(8,128)S(1)}, u32[]{:S(2)}, u32[]{:S(2)}) collective-permute-start(f32[2,24,384]{2,1,0:T(8,128)S(1)} %get-tuple-element.94), channel_id=1, source_target_pairs={{0,4},{1,5},{2,6},{3,7},{4,8},{5,9},{6,10},{7,11},{8,12},{9,13},{1... | collective-permute-start | bytes 221192 | tf_op jit(solution)/shard_map/ppermute | solution.py:632
  57.2 10.7 %collective-permute-start.22 = (f32[64,384]{1,0:T(8,128)S(1)}, f32[64,384]{1,0:T(8,128)S(1)}, u32[]{:S(2)}, u32[]{:S(2)}) collective-permute-start(f32[64,384]{1,0:T(8,128)S(1)} %get-tuple-element.102), channel_id=1, source_target_pairs={{16,0},{17,1},{18,2},{19,3},{20,4},{21,5},{22,6},{23,7},{24,8},{25... | collective-permute-start | bytes 294920 | tf_op jit(solution)/shard_map/ppermute | solution.py:20
  58.5 9.4 %collective-permute-start.18 = (f32[2,24,384]{2,1,0:T(8,128)S(1)}, f32[2,24,384]{2,1,0:T(8,128)S(1)}, u32[]{:S(2)}, u32[]{:S(2)}) collective-permute-start(f32[2,24,384]{2,1,0:T(8,128)S(1)} %get-tuple-element.94), channel_id=1, source_target_pairs={{16,20},{17,21},{18,22},{19,23},{20,24},{21,25},{22,26},{23,27},{2... | collective-permute-start | bytes 221192 | tf_op jit(solution)/shard_map/ppermute | solution.py:632
  59.2 4.2 %collective-permute-start.17 = (f32[2,6,384]{2,1,0:T(8,128)S(1)}, f32[2,6,384]{2,1,0:T(8,128)S(1)}, u32[]{:S(2)}, u32[]{:S(2)}) collective-permute-start(f32[2,6,384]{2,1,0:T(8,128)S(1)} %get-tuple-element.95), channel_id=1, source_target_pairs={{0,1},{1,2},{2,3},{4,5},{5,6},{6,7},{8,9},{9,10},{10,11},{12,13},{... | collective-permute-start | bytes 55304 | tf_op jit(solution)/shard_map/ppermute | solution.py:633
  63.9 4.8 %collective-permute-start.20 = (f32[3,2,8,128]{3,2,1,0:T(8,128)S(1)}, f32[3,2,8,128]{3,2,1,0:T(8,128)S(1)}, u32[]{:S(2)}, u32[]{:S(2)}) collective-permute-start(f32[3,2,8,128]{3,2,1,0:T(8,128)S(1)} %get-tuple-element.99), channel_id=1, source_target_pairs={{0,16},{1,17},{2,18},{3,19},{4,20},{5,21},{6,22},{7,23},{8,24},{9,... | collective-permute-start | bytes 73736 | tf_op jit(solution)/shard_map/ppermute | solution.py:20
  67.2 0.7 collective-permute-start.19
  69.4 8.7 %collective-permute-start.23 = (f32[80,384]{1,0:T(8,128)S(1)}, f32[80,384]{1,0:T(8,128)S(1)}, u32[]{:S(2)}, u32[]{:S(2)}) collective-permute-start(f32[80,384]{1,0:T(8,128)S(1)} %get-tuple-element.107), channel_id=1, source_target_pairs={{16,0},{17,1},{18,2},{19,3},{20,4},{21,5},{22,6},{23,7},{24,8},{25... | collective-permute-start | bytes 368648 | tf_op jit(solution)/shard_map/ppermute | solution.py:20

commit v5 on v3

--- a/solution.py
+++ b/solution.py
@@ -125,23 +125,90 @@
     )
 
 
-def magnetic(e, h, next_x, next_y, out):
-    row, lane = rows((24, 384)), lanes((24, 384))
-
-    def ahead_y(value, edge):
-        return jnp.where(row == 23, edge, pltpu.roll(value, 23, 0))
-
-    def ahead_z(value):
-        return jnp.where(lane == 383, 0.0, pltpu.roll(value, 383, 1))
-
+def ahead_y(value, edge):
+    return jnp.where(rows(value.shape) == 23, edge, pltpu.roll(value, 23, 0))
+
+
+def ahead_z(value):
+    return jnp.where(lanes(value.shape) == 383, 0.0, pltpu.roll(value, 383, 1))
+
+
+def behind_y(value, edge):
+    return jnp.where(rows(value.shape) == 0, edge, pltpu.roll(value, 1, 0))
+
+
+def behind_z(value):
+    return jnp.where(lanes(value.shape) == 0, 0.0, pltpu.roll(value, 1, 1))
+
+
+def send_edges(e, h, outs):
+    ax, ay, bx, by, d1, d2 = outs
+    ax[0], ax[1] = e[1, 0], e[2, 0]
+    ex, ey, ez = (e[c, 5] for c in range(3))
+    hy, hz = (0.0, 0.0) if h is None else (h[1, 5], h[2, 5])
+    bx[0] = hy - 0.5 * ((ahead_z(ex) - ex) + ez)
+    bx[1] = hz + 0.5 * (ey + (ahead_y(ex, 0.0) - ex))
+    for x in range(6):
+        ay[0, x : x + 1] = e[0, x, 0:1]
+        ay[1, x : x + 1] = e[2, x, 0:1]
+        ex, ey, ez = (e[c, x, 23:24] for c in range(3))
+        ey_x = e[1, x + 1, 23:24] if x < 5 else 0.0
+        hx, hz = (0.0, 0.0) if h is None else (h[0, x, 23:24], h[2, x, 23:24])
+        by[0, x : x + 1] = hx + 0.5 * (ez + (ahead_z(ey) - ey))
+        by[1, x : x + 1] = hz - 0.5 * ((ey_x - ey) + ex)
+    d1[...] = e[0, 5, 0:1]
+    d2[...] = e[1, 0, 23:24]
+
+
+class Edges:
+    def __init__(self, refs=None, packed=None, at=0):
+        self.refs, self.packed, self.at = refs, packed, at
+
+    def layer(self, which, k):
+        if self.packed is None:
+            return self.refs[which][k]
+        return self.packed[pl.ds(self.at + 32 * which + 24 * k, 24)]
+
+    def row(self, which, k, x):
+        if self.packed is None:
+            return self.refs[which][k, x : x + 1]
+        return self.packed[pl.ds(self.at + 48 + 64 * (which // 2) + 8 * k + x, 1)]
+
+    def diagonal(self, which):
+        if self.packed is None:
+            return self.refs[which][...]
+        return self.packed[pl.ds(self.at + 124 + which, 1)]
+
+
+def pack(out, boxes, edges):
+    at = 0
+    for box in boxes:
+        for c in range(3):
+            for i in range(2):
+                out[pl.ds(at + 8 * i, 8), pl.ds(128 * c, 128)] = box[c][i]
+        at += 16
+    for which in (0, 2):
+        for k in range(2):
+            out[pl.ds(at + 32 * which + 24 * k, 24)] = edges[which][k]
+            row = at + 48 + 64 * (which // 2) + 8 * k
+            out[pl.ds(row, 6)] = edges[which + 1][k]
+    for which in (4, 5):
+        out[pl.ds(at + 124 + which, 1)] = edges[which][...]
+
+
+def packed_box(ref, at=0):
+    return lambda c, i: ref[pl.ds(at + 8 * i, 8), pl.ds(128 * c, 128)]
+
+
+def magnetic(e, h, edges, out):
     for x in range(6):
         ex, ey, ez = (e[c, x] for c in range(3))
         if x < 5:
             ey_x, ez_x = e[1, x + 1], e[2, x + 1]
         else:
-            ey_x, ez_x = next_x(0), next_x(1)
-        ex_y = ahead_y(ex, next_y(0, x))
-        ez_y = ahead_y(ez, next_y(1, x))
+            ey_x, ez_x = edges.layer(0, 0), edges.layer(0, 1)
+        ex_y = ahead_y(ex, edges.row(1, 0, x))
+        ez_y = ahead_y(ez, edges.row(1, 1, x))
         ex_z, ey_z = ahead_z(ex), ahead_z(ey)
         turn = ((ez_y - ez) - (ey_z - ey), (ex_z - ex) - (ez_x - ez), (ey_x - ey) - (ex_y - ex))
         for c in range(3):
@@ -151,65 +218,49 @@
                 out[c, x] = h[c, x] - 0.5 * turn[c]
 
 
-def last_layers(h, out_x, out_y):
-    out_x[0], out_x[1] = h[1, 5], h[2, 5]
+def behind(e, edges):
+    has_x = (lax.axis_index("gx") > 0).astype(F32)
+    has_y = (lax.axis_index("gy") > 0).astype(F32)
+    row = rows((24, 384))
+    corner_row = jnp.where(row == 23, 0.5 * edges.diagonal(4), 0.0)
+    hy = has_x * (edges.layer(2, 0) + 0.5 * e[2, 0])
+    hz = has_x * (edges.layer(2, 1) - 0.5 * e[1, 0] + corner_row)
+    hx_rows, hz_rows = [], []
     for x in range(6):
-        out_y[0, x : x + 1] = h[0, x, 23:24]
-        out_y[1, x : x + 1] = h[2, x, 23:24]
-
-
-def first_layers(e, out_x, out_y):
-    out_x[0], out_x[1] = e[1, 0], e[2, 0]
-    for x in range(6):
-        out_y[0, x : x + 1] = e[0, x, 0:1]
-        out_y[1, x : x + 1] = e[2, x, 0:1]
-
-
-def curl_behind(h, x, prev_x, prev_y):
-    row, lane = rows((24, 384)), lanes((24, 384))
-
-    def behind_y(value, edge):
-        return jnp.where(row == 0, edge, pltpu.roll(value, 1, 0))
-
-    def behind_z(value):
-        return jnp.where(lane == 0, 0.0, pltpu.roll(value, 1, 1))
-
+        hx_rows.append(has_y * (edges.row(3, 0, x) - 0.5 * e[2, x, 0:1]))
+        value = edges.row(3, 1, x) + 0.5 * e[0, x, 0:1]
+        if x == 5:
+            value = value - 0.5 * edges.diagonal(5)
+        hz_rows.append(has_y * value)
+    return hy, hz, hx_rows, hz_rows
+
+
+def curl_behind(h, x, hy_x, hz_x, hx_row, hz_row):
     hx, hy, hz = (h[c, x] for c in range(3))
-    if isinstance(x, int):
-        hy_x, hz_x = (h[1, x - 1], h[2, x - 1]) if x > 0 else (prev_x(0), prev_x(1))
-    else:
-        before = jnp.maximum(x - 1, 0)
-        first = jnp.full((24, 384), x, jnp.int32) == 0
-        hy_x = jnp.where(first, prev_x(0), h[1, before])
-        hz_x = jnp.where(first, prev_x(1), h[2, before])
-    hx_y = behind_y(hx, prev_y(0, x))
-    hz_y = behind_y(hz, prev_y(1, x))
+    hx_y, hz_y = behind_y(hx, hx_row), behind_y(hz, hz_row)
     hx_z, hy_z = behind_z(hx), behind_z(hy)
     return ((hz - hz_y) - (hy - hy_z), (hx - hx_z) - (hz - hz_x), (hy - hy_x) - (hx - hx_y))
 
 
-def electric(e, h, p, coef, prev_x, prev_y, out_e, out_p, more=None):
+def step(e, h, p, coef, edges, out_e, out_h, out_p, more=None):
+    magnetic(e, h, edges, out_h)
+    hy_x, hz_x, hx_rows, hz_rows = behind(e, edges)
     for x in range(6):
-        rotation = curl_behind(h, x, prev_x, prev_y)
+        rotation = curl_behind(out_h, x, hy_x, hz_x, hx_rows[x], hz_rows[x])
+        hy_x, hz_x = out_h[1, x], out_h[2, x]
         a, b, q, f3, g = (whole(coef, k, x) for k in range(5))
         for c in range(3):
             new = a * e[c, x] + b * rotation[c]
-            old = None if p is None else p[c, x]
-            if old is not None:
+            if p is None:
+                last = g * new
+            else:
+                old = p[c, x]
                 new = new + q * old
-            last = g * new if old is None else f3 * old + g * new
+                last = f3 * old + g * new
             if more is not None:
                 new, last = new + more[0][c, x], last + more[1][c, x]
             out_e[c, x] = new
             out_p[c, x] = last
-
-
-def edge_x(ref):
-    return lambda k: ref[k]
-
-
-def edge_y(ref):
-    return lambda k, x: ref[k, pl.ds(x, 1)]
 
 
 def corner(desc):
@@ -259,29 +310,6 @@
                     e[spot] = e[spot] + pair
                 else:
                     e[spot] = jnp.where(keep, pair, e[spot])
-
-
-def pack(out, box, in_x, in_y, at=0):
-    if box is not None:
-        for c in range(3):
-            for i in range(2):
-                out[pl.ds(8 * i, 8), pl.ds(128 * c, 128)] = box[c][i]
-        at += 16
-    for k in range(2):
-        out[pl.ds(at + 24 * k, 24)] = in_x[k]
-        out[pl.ds(at + 48 + 8 * k, 6)] = in_y[k]
-
-
-def packed_box(ref):
-    return lambda c, i: ref[pl.ds(8 * i, 8), pl.ds(128 * c, 128)]
-
-
-def packed_x(ref, at):
-    return lambda k: ref[pl.ds(at + 24 * k, 24)]
-
-
-def packed_y(ref, at):
-    return lambda k, x: ref[pl.ds(at + 48 + 8 * k + x, 1)]
 
 
 def fine_steps(box, coef, desc, earlier, latest):
@@ -418,39 +446,57 @@
     return lax.axis_index("grid") == 1
 
 
-def h1_kernel(e, h, ax, ay, out_h, bx, by):
+def edge_kernel(fields, *outs):
     @pl.when(is_coarse())
     def _():
-        magnetic(e, h, edge_x(ax), edge_y(ay), out_h)
-        last_layers(out_h, bx, by)
-
-
-def e1_kernel(e, h, p, coef, bx, by, desc, out_e, out_p, ax, ay, sent):
+        send_edges(fields.at[0, pl.ds(0, 3)], fields.at[0, pl.ds(3, 3)], outs)
+
+
+def first_kernel(*refs):
+    e, h, p, coef, desc, material, table = refs[:7]
+    edges, refs = Edges(refs[7:13]), refs[13:]
+    out_e, out_h, out_p, sent, slab_coef = refs[:5]
+    outs = refs[5:]
+
     @pl.when(is_coarse())
     def _():
         spot = corner(desc)
         before = cut_region(e, desc, spot)
-        electric(e, h, p, coef, edge_x(bx), edge_y(by), out_e, out_p)
-        first_layers(out_e, ax, ay)
+        step(e, h, p, coef, edges, out_e, out_h, out_p)
+        send_edges(out_e, out_h, outs)
         after = cut_region(out_e, desc, spot)
         for c in range(3):
             for i in range(2):
                 sent[0, c, i] = before[c][i]
                 sent[1, c, i] = after[c][i]
 
-
-def h2_kernel(e, h, ax, ay, box_in, coef, region, desc, out_e, out_h, bx, by, box, now, change):
+    @pl.when(is_fine())
+    def _():
+        tiles = [table[k] for k in range(5)]
+        for x in range(6):
+            for yt in range(3):
+                for zt in range(3):
+                    index = material[0, x, pl.ds(8 * yt, 8), pl.ds(128 * zt, 128)]
+                    for k in range(5):
+                        slab_coef[k, x, 3 * yt + zt] = gather(tiles[k], index)
+
+
+def second_kernel(*refs):
+    e, h, p, coef, desc, box_in, region = refs[:7]
+    edges, refs = Edges(refs[7:13]), refs[13:]
+    out_e, out_h, out_p, sent, box, now, change = refs[:7]
+    outs = refs[7:]
+
     @pl.when(is_coarse())
     def _():
-        out_e[...] = e[...]
-        magnetic(e, h, edge_x(ax), edge_y(ay), out_h)
-        last_layers(out_h, bx, by)
+        step(e, h, p, coef, edges, out_e, out_h, out_p)
+        send_edges(out_e, out_h, outs)
+        store_box(sent, cut_region(out_e, desc, corner(desc)))
 
     @pl.when(is_fine())
     def _():
         box[...] = box_in[...]
         out_e[...] = jnp.zeros(out_e.shape, F32)
-        out_h[...] = jnp.zeros(out_h.shape, F32)
         earlier = [[region[0, c, i] for i in range(2)] for c in range(3)]
         latest = [[region[1, c, i] for i in range(2)] for c in range(3)]
         restricted = fine_steps(box, coef, desc, earlier, latest)
@@ -458,111 +504,83 @@
         store_box(now, after)
         store_box(change, delta)
         put(out_e, lambda c, i: delta[c][i], desc, corner(desc))
-
-
-def e2_kernel(e, h, p, coef, bx, by, desc, material, table, out_e, out_p, ax, ay, sent, wide_coef):
+        send_edges(out_e, None, outs)
+
+
+def third_kernel(*refs):
+    e, h, p, coef, slab_coef, desc, box_in, region, was, change = refs[:10]
+    arrived, refs = refs[10:16], refs[16:]
+    edges = Edges(arrived)
+    out_e, out_h, out_p, sent, box, now, relay = refs[:7]
+    outs = refs[7:]
+
     @pl.when(is_coarse())
     def _():
-        electric(e, h, p, coef, edge_x(bx), edge_y(by), out_e, out_p)
-        first_layers(out_e, ax, ay)
-        store_box(sent, cut_region(out_e, desc, corner(desc)))
-
-    @pl.when(is_fine())
-    def _():
-        out_e[...] = e[...]
-        out_p[...] = jnp.zeros(out_p.shape, F32)
-        first_layers(e, ax, ay)
-        tiles = [table[k] for k in range(5)]
-        for x in range(6):
-            for yt in range(3):
-                for zt in range(3):
-                    index = material[0, x, pl.ds(8 * yt, 8), pl.ds(128 * zt, 128)]
-                    for k in range(5):
-                        wide_coef[k, x, 3 * yt + zt] = gather(tiles[k], index)
-
-
-def h3_kernel(e, h, ax, ay, change, out_h, bx, by, relay):
-    magnetic(e, h, edge_x(ax), edge_y(ay), out_h)
-    last_layers(out_h, bx, by)
-
-    @pl.when(is_fine())
-    def _():
-        pack(relay, load_box(change), ax, ay)
-
-
-def e3_kernel(
-    e, h, p, coef, wide_coef, bx, by, desc, box_in, region, was,
-    out_e, out_p, ax, ay, sent, box, now, relay,
-):
-    @pl.when(is_coarse())
-    def _():
-        electric(e, h, p, coef, edge_x(bx), edge_y(by), out_e, out_p)
+        step(e, h, p, coef, edges, out_e, out_h, out_p)
         store_box(sent, cut_region(out_e, desc, corner(desc)))
 
     @pl.when(is_fine())
     def _():
         box[...] = box_in[...]
         spot = corner(desc)
-        electric(e, h, p, wide_coef, edge_x(bx), edge_y(by), out_e, out_p)
+        step(e, None, None, slab_coef, edges, out_e, out_h, out_p)
         fix = cut_region(out_e, desc, spot)
         latest = [[region[c, i] + fix[c][i] for i in range(2)] for c in range(3)]
         restricted = fine_steps(box, coef, desc, load_box(was), latest)
         after, delta = feed_back(restricted, latest, desc)
         store_box(now, after)
         put(out_e, lambda c, i: delta[c][i], desc, spot)
-        first_layers(out_e, ax, ay)
-        pack(relay, delta, bx, by)
-
-
-def h4_kernel(e, h, ax, ay, out_h, bx, by, relay):
-    @pl.when(is_fine())
-    def _():
-        magnetic(e, h, edge_x(ax), edge_y(ay), out_h)
-        last_layers(out_h, bx, by)
-        pack(relay, None, ax, ay)
-
-
-def e4_kernel(e, h, p, coef, wide_coef, bx, by, desc, box_in, region, was, box, relay, layer):
+        send_edges(out_e, out_h, outs)
+        pack(relay, (load_box(change), delta), arrived)
+
+
+def fourth_kernel(*refs):
+    e, h, p, coef, slab_coef, desc, box_in, region, was, relay1 = refs[:10]
+    arrived, refs = refs[10:16], refs[16:]
+    edges = Edges(arrived)
+    box, relay, fix_e, fix_h, fix_p, layer, one_e, new_h = refs
+
+    @pl.when(is_coarse())
+    def _():
+        one_e[...] = jnp.zeros(one_e.shape, F32)
+        spot = corner(desc)
+        put(one_e, packed_box(relay1), desc, spot)
+        step(one_e, None, None, coef, Edges(packed=relay1, at=32), fix_e, fix_h, fix_p)
+        put(fix_e, packed_box(relay1, 16), desc, spot)
+
     @pl.when(is_fine())
     def _():
         box[...] = box_in[...]
         spot = corner(desc)
-        x0 = spot[0]
+        magnetic(e, h, edges, new_h)
+        hy_b, hz_b, hx_rows, hz_rows = behind(e, edges)
         for i in range(2):
-            x = x0 + i
-            rotation = curl_behind(h, x, edge_x(bx), edge_y(by))
-            a, b, q = (whole(wide_coef, k, x) for k in range(3))
+            x = spot[0] + i
+            before = jnp.maximum(x - 1, 0)
+            number = jnp.full((24, 384), x, jnp.int32)
+            hy_x = jnp.where(number == 0, hy_b, new_h[1, before])
+            hz_x = jnp.where(number == 0, hz_b, new_h[2, before])
+            hx_row, hz_row = hx_rows[0], hz_rows[0]
+            for k in range(1, 6):
+                hx_row = jnp.where(number[0:1] == k, hx_rows[k], hx_row)
+                hz_row = jnp.where(number[0:1] == k, hz_rows[k], hz_row)
+            rotation = curl_behind(new_h, x, hy_x, hz_x, hx_row, hz_row)
+            a, b, q = (whole(slab_coef, k, x) for k in range(3))
             for c in range(3):
                 layer[c, i] = a * e[c, x] + b * rotation[c] + q * p[c, x]
         fix = cut_region(layer, desc, (0, *spot[1:]))
         latest = [[region[c, i] + fix[c][i] for i in range(2)] for c in range(3)]
         restricted = fine_steps(box, coef, desc, load_box(was), latest)
-        pack(relay, restricted, bx, by)
-
-
-def redo_kernel(coef, desc, relay1, relay2, relay3, out_e, out_h, out_p, one_e, one_h):
+        pack(relay, (restricted,), arrived)
+
+
+def finish_kernel(e, h, p, fix_e, fix_h, fix_p, coef, desc, relay, box, out, mixed, new_h):
     @pl.when(is_coarse())
     def _():
-        spot = corner(desc)
-        one_e[...] = jnp.zeros(one_e.shape, F32)
-        put(one_e, packed_box(relay1), desc, spot)
-        magnetic(one_e, None, packed_x(relay1, 16), packed_y(relay1, 16), one_h)
-        electric(
-            one_e, one_h, None, coef, packed_x(relay2, 16), packed_y(relay2, 16), out_e, out_p
-        )
-        put(out_e, packed_box(relay2), desc, spot)
-        magnetic(out_e, one_h, packed_x(relay3, 0), packed_y(relay3, 0), out_h)
-
-
-def finish_kernel(e, h, p, fix_e, fix_h, fix_p, coef, desc, relay, box, out, mixed):
-    @pl.when(is_coarse())
-    def _():
         view_e, view_p = out.at[pl.ds(0, 3)], out.at[pl.ds(6, 3)]
-        electric(
-            fix_e, fix_h, fix_p, coef, packed_x(relay, 16), packed_y(relay, 16),
-            view_e, view_p, (e, p),
-        )
-        out[3:6] = h[...] + fix_h[...]
+        edges = Edges(packed=relay, at=16)
+        step(fix_e, fix_h, fix_p, coef, edges, view_e, new_h, view_p, (e, p))
+        out[3:6] = h[...] + new_h[...]
         covered = [jnp.where(value, F32(1.0), 0.0) for value in covered_of(desc)]
         put(view_e, packed_box(relay), desc, corner(desc), covered)
 
@@ -600,13 +618,12 @@
 BOX = (9, 6, 9, 8, 128)
 COEF = (5, 6, 9, 8, 128)
 REGION = (3, 2, 8, 128)
-X_EDGE = (2, 24, 384)
-Y_EDGE = (2, 6, 384)
-EDGES = [X_EDGE, Y_EDGE]
+EDGES = [(2, 24, 384), (2, 6, 384), (2, 24, 384), (2, 6, 384), (1, 384), (1, 384)]
+WAYS = [(-1, 0), (0, -1), (1, 0), (0, 1), (1, -1), (-1, 1)]
 AXES = ("grid", "gx", "gy")
 
 
-def exchange(x_edge, y_edge, by, groups):
+def exchange(edges, groups):
     na, nb = lax.axis_size("gx"), lax.axis_size("gy")
 
     def pairs(da, db):
@@ -618,10 +635,7 @@
             if 0 <= a + da < na and 0 <= b + db < nb
         ]
 
-    return (
-        lax.ppermute(x_edge, AXES, pairs(by, 0)),
-        lax.ppermute(y_edge, AXES, pairs(0, by)),
-    )
+    return [lax.ppermute(edge, AXES, pairs(*way)) for edge, way in zip(edges, WAYS)]
 
 
 def to_fine(value):
@@ -633,8 +647,9 @@
 
 
 def body(fields, material, permittivity, conductivity, relax_rate, debye_strength, subgrids):
-    f = fields[0]
-    ax, ay = exchange(f[1:3, 0], f[0:3:2, :, 0], -1, (0,))
+    edges = call(edge_kernel, (fields,), EDGES)
+    edges = exchange(edges, (0,))
+    slab_material = to_fine(material)
     e, h, p, box, coef, desc, table = call(
         prep_kernel,
         (fields,) * 3
@@ -647,60 +662,44 @@
         + [SM] * 5,
         grid=(1,),
     )
-    h, bx, by = call(h1_kernel, (e, h, ax, ay), [PART] + EDGES)
-    bx, by = exchange(bx, by, 1, (0,))
-    e, p, ax, ay, sent = call(
-        e1_kernel, (e, h, p, coef, bx, by, desc), [PART] * 2 + EDGES + [(2, *REGION)]
+    e, h, p, sent, slab_coef, *edges = call(
+        first_kernel,
+        (e, h, p, coef, desc, slab_material, table, *edges),
+        [PART] * 3 + [(2, *REGION), COEF] + EDGES,
     )
     region = to_fine(sent)
-    ax, ay = exchange(ax, ay, -1, (0,))
-    slab_material = to_fine(material)
-    e, h, bx, by, box, now, change = call(
-        h2_kernel,
-        (e, h, ax, ay, box, coef, region, desc),
-        [PART] * 2 + EDGES + [BOX, REGION, REGION],
-    )
-    bx, by = exchange(bx, by, 1, (0,))
-    e, p, ax, ay, sent, wide_coef = call(
-        e2_kernel,
-        (e, h, p, coef, bx, by, desc, slab_material, table),
-        [PART] * 2 + EDGES + [REGION, COEF],
+    edges = exchange(edges, (0,))
+    e, h, p, sent, box, now, change, *edges = call(
+        second_kernel,
+        (e, h, p, coef, desc, box, region, *edges),
+        [PART] * 3 + [REGION, BOX, REGION, REGION] + EDGES,
     )
     region = to_fine(sent)
-    ax, ay = exchange(ax, ay, -1, (0, 1))
-    h, bx, by, relay1 = call(h3_kernel, (e, h, ax, ay, change), [PART] + EDGES + [(80, 384)])
-    bx, by = exchange(bx, by, 1, (0, 1))
-    relay1 = to_coarse(relay1)
-    e, p, ax, ay, sent, box, now, relay2 = call(
-        e3_kernel,
-        (e, h, p, coef, wide_coef, bx, by, desc, box, region, now),
-        [PART] * 2 + EDGES + [REGION, BOX, REGION, (80, 384)],
+    edges = exchange(edges, (0, 1))
+    e, h, p, sent, box, now, relay, *edges = call(
+        third_kernel,
+        (e, h, p, coef, slab_coef, desc, box, region, now, change, *edges),
+        [PART] * 3 + [REGION, BOX, REGION, (168, 384)] + EDGES,
     )
-    base_e, base_h, base_p = e, h, p
     region = to_fine(sent)
-    ax, ay = exchange(ax, ay, -1, (1,))
-    relay2 = to_coarse(relay2)
-    h, bx, by, relay3 = call(h4_kernel, (e, h, ax, ay), [PART] + EDGES + [(64, 384)])
-    bx, by = exchange(bx, by, 1, (1,))
-    relay3 = to_coarse(relay3)
-    box, relay4 = call(
-        e4_kernel,
-        (e, h, p, coef, wide_coef, bx, by, desc, box, region, now),
-        [BOX, (80, 384)],
-        scratch=[pltpu.VMEM((3, 2, 24, 384), F32)],
+    relay = to_coarse(relay)
+    edges = exchange(edges, (1,))
+    box, last, *fix = call(
+        fourth_kernel,
+        (e, h, p, coef, slab_coef, desc, box, region, now, relay, *edges),
+        [BOX, (152, 384)] + [PART] * 3,
+        scratch=[
+            pltpu.VMEM((3, 2, 24, 384), F32),
+            pltpu.VMEM(PART, F32),
+            pltpu.VMEM(PART, F32),
+        ],
     )
-    relay4 = to_coarse(relay4)
-    fix = call(
-        redo_kernel,
-        (coef, desc, relay1, relay2, relay3),
-        [PART] * 3,
-        scratch=[pltpu.VMEM(PART, F32)] * 2,
-    )
+    last = to_coarse(last)
     (out,) = call(
         finish_kernel,
-        (base_e, base_h, base_p, *fix, coef, desc, relay4, box),
+        (e, h, p, *fix, coef, desc, last, box),
         [SLAB],
-        scratch=[pltpu.VMEM((9, 6, 3, 24, 128), F32)],
+        scratch=[pltpu.VMEM((9, 6, 3, 24, 128), F32), pltpu.VMEM(PART, F32)],
     )
     return out[None]
 

time: 84.8 us -> 106 us (1.25)
  the two profiles are of different devices: /device:TPU:0 before, /device:TPU:12 now
where the time goes in v5:
time: 106 us; the launch traced here: 105 us
  starting transfers between devices  79.9 us (75%)
  waiting for transfers between devices  16.7 us (16%)
  Pallas kernels  6.39 us (6%)
  local copies, waits for them, and re-layouts  1.57 us (1%)
    ppermute x24, starting transfers between devices, exchange(): lax.ppermute(edge, AXES, pairs(*way))  51.7 us
    ppermute x6, starting transfers between devices, shifted(): return lax.ppermute(value, axis, pairs)  28.2 us
    ppermute x6, waiting for transfers between devices, shifted(): return lax.ppermute(value, axis, pairs)  9.31 us
    ppermute x24, waiting for transfers between devices, exchange(): lax.ppermute(edge, AXES, pairs(*way))  7.36 us
    pallas_call x7, Pallas kernels, call(): pl.pallas_call(kernel, out_shape=shapes, in_specs=specs or [VM] * len(ope...  6.39 us
  transfers between devices with their start and end apart: 30, of which 8 were waited for; matrix products, arithmetic and copies ran while one was open for 0% of the time, Pallas kernels for 1%

profile of v5, /device:TPU:12, one launch (start us, length us, event | category | flops | bytes accessed | tf_op | source)
XLA Modules:
  0.0 105.0 jit_solution(6128888586942447284)
XLA Ops:
  0.0 3.4 %collective-permute-start = (s32[1,6,24,384]{3,2,1,0:T(8,128)}, s32[1,6,24,384]{3,2,1,0:T(8,128)S(1)}, u32[]{:S(2)}, u32[]{:S(2)}) collective-permute-start(s32[1,6,24,384]{3,2,1,0:T(8,128)} %m2.1), channel_id=1, source_target_pairs={{0,16},{1,17},{2,18},{3,19},{4,20},{5,21},{6,22},{7,23},{8,24},{9,... | collective-permute-start | bytes 663560 | tf_op jit(solution)/shard_map/ppermute | solution.py:20
  3.4 1.5 %copy-done = f32[1,9,6,24,384]{4,3,2,1,0:T(8,128)S(1)} copy-done((f32[1,9,6,24,384]{4,3,2,1,0:T(8,128)S(1)}, f32[1,9,6,24,384]{4,3,2,1,0:T(8,128)}, u32[]{:S(2)}) %copy-start) | copy-done | bytes 1990680
  5.0 0.1 shard_map.74
  5.1 2.5 %collective-permute-start.1 = (f32[2,24,384]{2,1,0:T(8,128)S(1)}, f32[2,24,384]{2,1,0:T(8,128)S(1)}, u32[]{:S(2)}, u32[]{:S(2)}) collective-permute-start(f32[2,24,384]{2,1,0:T(8,128)S(1)} %get-tuple-element.66), channel_id=1, source_target_pairs={{4,0},{5,1},{6,2},{7,3},{8,4},{9,5},{10,6},{11,7},{12,8},{13,9},{1... | collective-permute-start | bytes 221192 | tf_op jit(solution)/shard_map/ppermute | solution.py:638
  7.6 3.5 %collective-permute-start.3 = (f32[2,24,384]{2,1,0:T(8,128)S(1)}, f32[2,24,384]{2,1,0:T(8,128)S(1)}, u32[]{:S(2)}, u32[]{:S(2)}) collective-permute-start(f32[2,24,384]{2,1,0:T(8,128)S(1)} %get-tuple-element.68), channel_id=1, source_target_pairs={{0,4},{1,5},{2,6},{3,7},{4,8},{5,9},{6,10},{7,11},{8,12},{9,13},{1... | collective-permute-start | bytes 221192 | tf_op jit(solution)/shard_map/ppermute | solution.py:638
  11.1 2.0 %collective-permute-start.5 = (f32[1,384]{1,0:T(1,128)S(1)}, f32[1,384]{1,0:T(1,128)S(1)}, u32[]{:S(2)}, u32[]{:S(2)}) collective-permute-start(f32[1,384]{1,0:T(1,128)S(1)} %get-tuple-element.70), channel_id=1, source_target_pairs={{1,4},{2,5},{3,6},{5,8},{6,9},{7,10},{9,12},{10,13},{11,14}} | collective-permute-start | bytes 4616 | tf_op jit(solution)/shard_map/ppermute | solution.py:638
  13.1 3.5 %collective-permute-start.6 = (f32[1,384]{1,0:T(1,128)S(1)}, f32[1,384]{1,0:T(1,128)S(1)}, u32[]{:S(2)}, u32[]{:S(2)}) collective-permute-start(f32[1,384]{1,0:T(1,128)S(1)} %get-tuple-element.71), channel_id=1, source_target_pairs={{4,1},{5,2},{6,3},{8,5},{9,6},{10,7},{12,9},{13,10},{14,11}} | collective-permute-start | bytes 4616 | tf_op jit(solution)/shard_map/ppermute | solution.py:638
  16.7 2.0 %collective-permute-start.2 = (f32[2,6,384]{2,1,0:T(8,128)S(1)}, f32[2,6,384]{2,1,0:T(8,128)S(1)}, u32[]{:S(2)}, u32[]{:S(2)}) collective-permute-start(f32[2,6,384]{2,1,0:T(8,128)S(1)} %get-tuple-element.67), channel_id=1, source_target_pairs={{1,0},{2,1},{3,2},{5,4},{6,5},{7,6},{9,8},{10,9},{11,10},{13,12},{... | collective-permute-start | bytes 55304 | tf_op jit(solution)/shard_map/ppermute | solution.py:638
  18.7 0.3 collective-permute-done.6.refs_12_
  18.9 2.6 %collective-permute-start.4 = (f32[2,6,384]{2,1,0:T(8,128)S(1)}, f32[2,6,384]{2,1,0:T(8,128)S(1)}, u32[]{:S(2)}, u32[]{:S(2)}) collective-permute-start(f32[2,6,384]{2,1,0:T(8,128)S(1)} %get-tuple-element.69), channel_id=1, source_target_pairs={{0,1},{1,2},{2,3},{4,5},{5,6},{6,7},{8,9},{9,10},{10,11},{12,13},{... | collective-permute-start | bytes 55304 | tf_op jit(solution)/shard_map/ppermute | solution.py:638
  21.6 1.1 %shard_map.73 = (f32[3,6,24,384]{3,2,1,0:T(8,128)S(1)}, f32[3,6,24,384]{3,2,1,0:T(8,128)S(1)}, f32[3,6,24,384]{3,2,1,0:T(8,128)S(1)}, f32[9,6,9,8,128]{4,3,2,1,0...) custom-call(f32[1,9,6,24,384]{4,3,2,1,0:T(8,128)S(1)} %copy-done, ...), custom_call_target="tpu_custom_call" | custom-call | tf_op jit(solution)/shard_map/pallas_call | solution.py:605
  22.7 1.4 %collective-permute-done.4.refs_10_ = f32[2,6,384]{2,1,0:T(8,128)S(1)} collective-permute-done((f32[2,6,384]{2,1,0:T(8,128)S(1)}, f32[2,6,384]{2,1,0:T(8,128)S(1)}, u32[]{:S(2)}, u32[]{:S(2)}) %collective-permute-start.4) | collective-permute-done | bytes 18464 | tf_op jit(solution)/shard_map/ppermute | solution.py:638
  24.1 0.9 shard_map.75
  25.0 2.4 %collective-permute-start.8 = (f32[2,24,384]{2,1,0:T(8,128)S(1)}, f32[2,24,384]{2,1,0:T(8,128)S(1)}, u32[]{:S(2)}, u32[]{:S(2)}) collective-permute-start(f32[2,24,384]{2,1,0:T(8,128)S(1)} %get-tuple-element.77), channel_id=1, source_target_pairs={{4,0},{5,1},{6,2},{7,3},{8,4},{9,5},{10,6},{11,7},{12,8},{13,9},{1... | collective-permute-start | bytes 221192 | tf_op jit(solution)/shard_map/ppermute | solution.py:638
  27.4 3.4 %collective-permute-start.10 = (f32[2,24,384]{2,1,0:T(8,128)S(1)}, f32[2,24,384]{2,1,0:T(8,128)S(1)}, u32[]{:S(2)}, u32[]{:S(2)}) collective-permute-start(f32[2,24,384]{2,1,0:T(8,128)S(1)} %get-tuple-element.79), channel_id=1, source_target_pairs={{0,4},{1,5},{2,6},{3,7},{4,8},{5,9},{6,10},{7,11},{8,12},{9,13},{1... | collective-permute-start | bytes 221192 | tf_op jit(solution)/shard_map/ppermute | solution.py:638
  30.8 1.3 %collective-permute-start.7 = (f32[2,3,2,8,128]{4,3,2,1,0:T(8,128)S(1)}, f32[2,3,2,8,128]{4,3,2,1,0:T(8,128)S(1)}, u32[]{:S(2)}, u32[]{:S(2)}) collective-permute-start(f32[2,3,2,8,128]{4,3,2,1,0:T(8,128)S(1)} %get-tuple-element.76), channel_id=1, source_target_pairs={{0,16},{1,17},{2,18},{3,19},{4,20},{5,21},{6,22},{7,23},{8,24},{9,... | collective-permute-start | bytes 147464 | tf_op jit(solution)/shard_map/ppermute | solution.py:20
  32.1 2.0 %collective-permute-start.12 = (f32[1,384]{1,0:T(1,128)S(1)}, f32[1,384]{1,0:T(1,128)S(1)}, u32[]{:S(2)}, u32[]{:S(2)}) collective-permute-start(f32[1,384]{1,0:T(1,128)S(1)} %get-tuple-element.81), channel_id=1, source_target_pairs={{1,4},{2,5},{3,6},{5,8},{6,9},{7,10},{9,12},{10,13},{11,14}} | collective-permute-start | bytes 4616 | tf_op jit(solution)/shard_map/ppermute | solution.py:638
  34.1 3.6 %collective-permute-start.13 = (f32[1,384]{1,0:T(1,128)S(1)}, f32[1,384]{1,0:T(1,128)S(1)}, u32[]{:S(2)}, u32[]{:S(2)}) collective-permute-start(f32[1,384]{1,0:T(1,128)S(1)} %get-tuple-element.82), channel_id=1, source_target_pairs={{4,1},{5,2},{6,3},{8,5},{9,6},{10,7},{12,9},{13,10},{14,11}} | collective-permute-start | bytes 4616 | tf_op jit(solution)/shard_map/ppermute | solution.py:638
  37.7 0.0 collective-permute-done.12.refs_11_
  37.7 2.0 %collective-permute-start.9 = (f32[2,6,384]{2,1,0:T(8,128)S(1)}, f32[2,6,384]{2,1,0:T(8,128)S(1)}, u32[]{:S(2)}, u32[]{:S(2)}) collective-permute-start(f32[2,6,384]{2,1,0:T(8,128)S(1)} %get-tuple-element.78), channel_id=1, source_target_pairs={{1,0},{2,1},{3,2},{5,4},{6,5},{7,6},{9,8},{10,9},{11,10},{13,12},{... | collective-permute-start | bytes 55304 | tf_op jit(solution)/shard_map/ppermute | solution.py:638
  39.7 0.2 collective-permute-done.13.refs_12_
  39.9 2.5 %collective-permute-start.11 = (f32[2,6,384]{2,1,0:T(8,128)S(1)}, f32[2,6,384]{2,1,0:T(8,128)S(1)}, u32[]{:S(2)}, u32[]{:S(2)}) collective-permute-start(f32[2,6,384]{2,1,0:T(8,128)S(1)} %get-tuple-element.80), channel_id=1, source_target_pairs={{0,1},{1,2},{2,3},{4,5},{5,6},{6,7},{8,9},{9,10},{10,11},{12,13},{... | collective-permute-start | bytes 55304 | tf_op jit(solution)/shard_map/ppermute | solution.py:638
  42.4 0.0 collective-permute-done.9.refs_8_
  42.4 2.6 %collective-permute-done.11.refs_10_ = f32[2,6,384]{2,1,0:T(8,128)S(1)} collective-permute-done((f32[2,6,384]{2,1,0:T(8,128)S(1)}, f32[2,6,384]{2,1,0:T(8,128)S(1)}, u32[]{:S(2)}, u32[]{:S(2)}) %collective-permute-start.11) | collective-permute-done | bytes 18464 | tf_op jit(solution)/shard_map/ppermute | solution.py:638
  45.1 0.8 shard_map.76
  45.9 2.5 %collective-permute-start.15 = (f32[2,24,384]{2,1,0:T(8,128)S(1)}, f32[2,24,384]{2,1,0:T(8,128)S(1)}, u32[]{:S(2)}, u32[]{:S(2)}) collective-permute-start(f32[2,24,384]{2,1,0:T(8,128)S(1)} %get-tuple-element.91), channel_id=1, source_target_pairs={{4,0},{5,1},{6,2},{7,3},{8,4},{9,5},{10,6},{11,7},{12,8},{13,9},{1... | collective-permute-start | bytes 221192 | tf_op jit(solution)/shard_map/ppermute | solution.py:638
  48.4 3.4 %collective-permute-start.17 = (f32[2,24,384]{2,1,0:T(8,128)S(1)}, f32[2,24,384]{2,1,0:T(8,128)S(1)}, u32[]{:S(2)}, u32[]{:S(2)}) collective-permute-start(f32[2,24,384]{2,1,0:T(8,128)S(1)} %get-tuple-element.93), channel_id=1, source_target_pairs={{0,4},{1,5},{2,6},{3,7},{4,8},{5,9},{6,10},{7,11},{8,12},{9,13},{1... | collective-permute-start | bytes 221192 | tf_op jit(solution)/shard_map/ppermute | solution.py:638
  51.8 1.3 %collective-permute-start.14 = (f32[3,2,8,128]{3,2,1,0:T(8,128)S(1)}, f32[3,2,8,128]{3,2,1,0:T(8,128)S(1)}, u32[]{:S(2)}, u32[]{:S(2)}) collective-permute-start(f32[3,2,8,128]{3,2,1,0:T(8,128)S(1)} %get-tuple-element.88), channel_id=1, source_target_pairs={{0,16},{1,17},{2,18},{3,19},{4,20},{5,21},{6,22},{7,23},{8,24},{9,... | collective-permute-start | bytes 73736 | tf_op jit(solution)/shard_map/ppermute | solution.py:20
  53.1 1.9 %collective-permute-start.19 = (f32[1,384]{1,0:T(1,128)S(1)}, f32[1,384]{1,0:T(1,128)S(1)}, u32[]{:S(2)}, u32[]{:S(2)}) collective-permute-start(f32[1,384]{1,0:T(1,128)S(1)} %get-tuple-element.95), channel_id=1, source_target_pairs={{1,4},{2,5},{3,6},{5,8},{6,9},{7,10},{9,12},{10,13},{11,14},{17,20... | collective-permute-start | bytes 4616 | tf_op jit(solution)/shard_map/ppermute | solution.py:638
  55.0 3.6 %collective-permute-start.20 = (f32[1,384]{1,0:T(1,128)S(1)}, f32[1,384]{1,0:T(1,128)S(1)}, u32[]{:S(2)}, u32[]{:S(2)}) collective-permute-start(f32[1,384]{1,0:T(1,128)S(1)} %get-tuple-element.96), channel_id=1, source_target_pairs={{4,1},{5,2},{6,3},{8,5},{9,6},{10,7},{12,9},{13,10},{14,11},{20,17... | collective-permute-start | bytes 4616 | tf_op jit(solution)/shard_map/ppermute | solution.py:638
  58.6 1.9 %collective-permute-start.16 = (f32[2,6,384]{2,1,0:T(8,128)S(1)}, f32[2,6,384]{2,1,0:T(8,128)S(1)}, u32[]{:S(2)}, u32[]{:S(2)}) collective-permute-start(f32[2,6,384]{2,1,0:T(8,128)S(1)} %get-tuple-element.92), channel_id=1, source_target_pairs={{1,0},{2,1},{3,2},{5,4},{6,5},{7,6},{9,8},{10,9},{11,10},{13,12},{... | collective-permute-start | bytes 55304 | tf_op jit(solution)/shard_map/ppermute | solution.py:638
  60.6 0.2 collective-permute-done.20.refs_15_
  60.8 2.5 %collective-permute-start.18 = (f32[2,6,384]{2,1,0:T(8,128)S(1)}, f32[2,6,384]{2,1,0:T(8,128)S(1)}, u32[]{:S(2)}, u32[]{:S(2)}) collective-permute-start(f32[2,6,384]{2,1,0:T(8,128)S(1)} %get-tuple-element.94), channel_id=1, source_target_pairs={{0,1},{1,2},{2,3},{4,5},{5,6},{6,7},{8,9},{9,10},{10,11},{12,13},{... | collective-permute-start | bytes 55304 | tf_op jit(solution)/shard_map/ppermute | solution.py:638
  63.3 2.6 %collective-permute-done.18.refs_13_ = f32[2,6,384]{2,1,0:T(8,128)S(1)} collective-permute-done((f32[2,6,384]{2,1,0:T(8,128)S(1)}, f32[2,6,384]{2,1,0:T(8,128)S(1)}, u32[]{:S(2)}, u32[]{:S(2)}) %collective-permute-start.18) | collective-permute-done | bytes 18464 | tf_op jit(solution)/shard_map/ppermute | solution.py:638
  65.9 0.8 shard_map.77
  66.7 1.3 %collective-permute-start.22 = (f32[168,384]{1,0:T(8,128)S(1)}, f32[168,384]{1,0:T(8,128)S(1)}, u32[]{:S(2)}, u32[]{:S(2)}) collective-permute-start(f32[168,384]{1,0:T(8,128)S(1)} %get-tuple-element.103), channel_id=1, source_target_pairs={{16,0},{17,1},{18,2},{19,3},{20,4},{21,5},{22,6},{23,7},{24,8},{25... | collective-permute-start | bytes 774152 | tf_op jit(solution)/shard_map/ppermute | solution.py:20
  68.0 0.7 collective-permute-start.23
  68.7 0.7 collective-permute-start.25
  69.3 0.7 collective-permute-start.24
  70.0 0.7 collective-permute-start.27
  70.7 0.7 collective-permute-start.28
  71.4 19.6 %collective-permute-start.21 = (f32[3,2,8,128]{3,2,1,0:T(8,128)S(1)}, f32[3,2,8,128]{3,2,1,0:T(8,128)S(1)}, u32[]{:S(2)}, u32[]{:S(2)}) collective-permute-start(f32[3,2,8,128]{3,2,1,0:T(8,128)S(1)} %get-tuple-element.101), channel_id=1, source_target_pairs={{0,16},{1,17},{2,18},{3,19},{4,20},{5,21},{6,22},{7,23},{8,24},{9,... | collective-permute-start | bytes 73736 | tf_op jit(solution)/shard_map/ppermute | solution.py:20
  91.0 0.7 collective-permute-start.26
  91.7 0.8 collective-permute-done.21.refs_7_
  92.5 0.7 shard_map.78
  93.2 1.3 %collective-permute-start.29 = (f32[152,384]{1,0:T(8,128)S(1)}, f32[152,384]{1,0:T(8,128)S(1)}, u32[]{:S(2)}, u32[]{:S(2)}) collective-permute-start(f32[152,384]{1,0:T(8,128)S(1)} %get-tuple-element.113), channel_id=1, source_target_pairs={{16,0},{17,1},{18,2},{19,3},{20,4},{21,5},{22,6},{23,7},{24,8},{25... | collective-permute-start | bytes 700424 | tf_op jit(solution)/shard_map/ppermute | solution.py:20
  94.5 8.5 %collective-permute-done.29.relay = f32[152,384]{1,0:T(8,128)S(1)} collective-permute-done((f32[152,384]{1,0:T(8,128)S(1)}, f32[152,384]{1,0:T(8,128)S(1)}, u32[]{:S(2)}, u32[]{:S(2)}) %collective-permute-start.29) | collective-permute-done | bytes 233504 | tf_op jit(solution)/shard_map/ppermute | solution.py:20
  103.0 2.0 %shard_map.79 = f32[9,6,24,384]{3,2,1,0:T(8,128)} custom-call(f32[3,6,24,384]{3,2,1,0:T(8,128)S(1)} %get-tuple-element.97.refs_0_.e, f32[3,6,24,384]{3,2,1,0:T(8,128)S(1)} %get-tuple-element.98.refs_1_.h, f32[3,6,24,384]{3,2,1,0:T(8,128)S(1)} %get-tuple-element.99.refs_2_.p, f32[3,6,24,384]{3,2,1,0:T(8,128)S(1)} %get-tuple-element.110.fix_e, ...), custom_call_target="tpu_custom_call" | custom-call | tf_op jit(solution)/shard_map/pallas_call | solution.py:605
  (33 shorter events, 0.1 us)
Async XLA Ops:
  0.0 24.1 %collective-permute-start = (s32[1,6,24,384]{3,2,1,0:T(8,128)}, s32[1,6,24,384]{3,2,1,0:T(8,128)S(1)}, u32[]{:S(2)}, u32[]{:S(2)}) collective-permute-start(s32[1,6,24,384]{3,2,1,0:T(8,128)} %m2.1), channel_id=1, source_target_pairs={{0,16},{1,17},{2,18},{3,19},{4,20},{5,21},{6,22},{7,23},{8,24},{9,... | collective-permute-start | bytes 663560 | tf_op jit(solution)/shard_map/ppermute | solution.py:20
  3.4 1.6 %copy-start = (f32[1,9,6,24,384]{4,3,2,1,0:T(8,128)S(1)}, f32[1,9,6,24,384]{4,3,2,1,0:T(8,128)}, u32[]{:S(2)}) copy-start(f32[1,9,6,24,384]{4,3,2,1,0:T(8,128)} %fields.1) | copy-start | bytes 5971972
  5.0 16.6 %copy-start.1 = (s32[1,6,24,384]{3,2,1,0:T(8,128)S(1)}, s32[1,6,24,384]{3,2,1,0:T(8,128)}, u32[]{:S(2)}) copy-start(s32[1,6,24,384]{3,2,1,0:T(8,128)} %m2.1) | copy-start | bytes 663556
  5.0 16.6 %copy-start.2 = (f32[8]{0:T(128)S(1)}, f32[8]{0:T(128)}, u32[]{:S(2)}) copy-start(f32[8]{0:T(128)} %perm.1) | copy-start | bytes 100
  5.0 16.6 %copy-start.3 = (f32[8]{0:T(128)S(1)}, f32[8]{0:T(128)}, u32[]{:S(2)}) copy-start(f32[8]{0:T(128)} %cond.1) | copy-start | bytes 100
  5.0 16.6 %copy-start.4 = (f32[8]{0:T(128)S(1)}, f32[8]{0:T(128)}, u32[]{:S(2)}) copy-start(f32[8]{0:T(128)} %relax.1) | copy-start | bytes 100
  5.0 16.6 %copy-start.5 = (f32[8]{0:T(128)S(1)}, f32[8]{0:T(128)}, u32[]{:S(2)}) copy-start(f32[8]{0:T(128)} %debye.1) | copy-start | bytes 100
  5.0 16.6 %copy-start.6 = (s32[1,1,6]{2,1,0:T(1,128)S(1)}, s32[1,1,6]{2,1,0:T(1,128)}, u32[]{:S(2)}) copy-start(s32[1,1,6]{2,1,0:T(1,128)} %sub.1) | copy-start | bytes 76
  5.1 19.0 %collective-permute-start.1 = (f32[2,24,384]{2,1,0:T(8,128)S(1)}, f32[2,24,384]{2,1,0:T(8,128)S(1)}, u32[]{:S(2)}, u32[]{:S(2)}) collective-permute-start(f32[2,24,384]{2,1,0:T(8,128)S(1)} %get-tuple-element.66), channel_id=1, source_target_pairs={{4,0},{5,1},{6,2},{7,3},{8,4},{9,5},{10,6},{11,7},{12,8},{13,9},{1... | collective-permute-start | bytes 221192 | tf_op jit(solution)/shard_map/ppermute | solution.py:638
  7.6 16.5 %collective-permute-start.3 = (f32[2,24,384]{2,1,0:T(8,128)S(1)}, f32[2,24,384]{2,1,0:T(8,128)S(1)}, u32[]{:S(2)}, u32[]{:S(2)}) collective-permute-start(f32[2,24,384]{2,1,0:T(8,128)S(1)} %get-tuple-element.68), channel_id=1, source_target_pairs={{0,4},{1,5},{2,6},{3,7},{4,8},{5,9},{6,10},{7,11},{8,12},{9,13},{1... | collective-permute-start | bytes 221192 | tf_op jit(solution)/shard_map/ppermute | solution.py:638
  11.1 5.6 %collective-permute-start.5 = (f32[1,384]{1,0:T(1,128)S(1)}, f32[1,384]{1,0:T(1,128)S(1)}, u32[]{:S(2)}, u32[]{:S(2)}) collective-permute-start(f32[1,384]{1,0:T(1,128)S(1)} %get-tuple-element.70), channel_id=1, source_target_pairs={{1,4},{2,5},{3,6},{5,8},{6,9},{7,10},{9,12},{10,13},{11,14}} | collective-permute-start | bytes 4616 | tf_op jit(solution)/shard_map/ppermute | solution.py:638
  13.1 5.8 %collective-permute-start.6 = (f32[1,384]{1,0:T(1,128)S(1)}, f32[1,384]{1,0:T(1,128)S(1)}, u32[]{:S(2)}, u32[]{:S(2)}) collective-permute-start(f32[1,384]{1,0:T(1,128)S(1)} %get-tuple-element.71), channel_id=1, source_target_pairs={{4,1},{5,2},{6,3},{8,5},{9,6},{10,7},{12,9},{13,10},{14,11}} | collective-permute-start | bytes 4616 | tf_op jit(solution)/shard_map/ppermute | solution.py:638
  16.7 6.0 %collective-permute-start.2 = (f32[2,6,384]{2,1,0:T(8,128)S(1)}, f32[2,6,384]{2,1,0:T(8,128)S(1)}, u32[]{:S(2)}, u32[]{:S(2)}) collective-permute-start(f32[2,6,384]{2,1,0:T(8,128)S(1)} %get-tuple-element.67), channel_id=1, source_target_pairs={{1,0},{2,1},{3,2},{5,4},{6,5},{7,6},{9,8},{10,9},{11,10},{13,12},{... | collective-permute-start | bytes 55304 | tf_op jit(solution)/shard_map/ppermute | solution.py:638
  18.9 5.1 %collective-permute-start.4 = (f32[2,6,384]{2,1,0:T(8,128)S(1)}, f32[2,6,384]{2,1,0:T(8,128)S(1)}, u32[]{:S(2)}, u32[]{:S(2)}) collective-permute-start(f32[2,6,384]{2,1,0:T(8,128)S(1)} %get-tuple-element.69), channel_id=1, source_target_pairs={{0,1},{1,2},{2,3},{4,5},{5,6},{6,7},{8,9},{9,10},{10,11},{12,13},{... | collective-permute-start | bytes 55304 | tf_op jit(solution)/shard_map/ppermute | solution.py:638
  25.0 20.1 %collective-permute-start.8 = (f32[2,24,384]{2,1,0:T(8,128)S(1)}, f32[2,24,384]{2,1,0:T(8,128)S(1)}, u32[]{:S(2)}, u32[]{:S(2)}) collective-permute-start(f32[2,24,384]{2,1,0:T(8,128)S(1)} %get-tuple-element.77), channel_id=1, source_target_pairs={{4,0},{5,1},{6,2},{7,3},{8,4},{9,5},{10,6},{11,7},{12,8},{13,9},{1... | collective-permute-start | bytes 221192 | tf_op jit(solution)/shard_map/ppermute | solution.py:638
  27.4 17.7 %collective-permute-start.10 = (f32[2,24,384]{2,1,0:T(8,128)S(1)}, f32[2,24,384]{2,1,0:T(8,128)S(1)}, u32[]{:S(2)}, u32[]{:S(2)}) collective-permute-start(f32[2,24,384]{2,1,0:T(8,128)S(1)} %get-tuple-element.79), channel_id=1, source_target_pairs={{0,4},{1,5},{2,6},{3,7},{4,8},{5,9},{6,10},{7,11},{8,12},{9,13},{1... | collective-permute-start | bytes 221192 | tf_op jit(solution)/shard_map/ppermute | solution.py:638
  30.8 14.2 %collective-permute-start.7 = (f32[2,3,2,8,128]{4,3,2,1,0:T(8,128)S(1)}, f32[2,3,2,8,128]{4,3,2,1,0:T(8,128)S(1)}, u32[]{:S(2)}, u32[]{:S(2)}) collective-permute-start(f32[2,3,2,8,128]{4,3,2,1,0:T(8,128)S(1)} %get-tuple-element.76), channel_id=1, source_target_pairs={{0,16},{1,17},{2,18},{3,19},{4,20},{5,21},{6,22},{7,23},{8,24},{9,... | collective-permute-start | bytes 147464 | tf_op jit(solution)/shard_map/ppermute | solution.py:20
  32.1 5.6 %collective-permute-start.12 = (f32[1,384]{1,0:T(1,128)S(1)}, f32[1,384]{1,0:T(1,128)S(1)}, u32[]{:S(2)}, u32[]{:S(2)}) collective-permute-start(f32[1,384]{1,0:T(1,128)S(1)} %get-tuple-element.81), channel_id=1, source_target_pairs={{1,4},{2,5},{3,6},{5,8},{6,9},{7,10},{9,12},{10,13},{11,14}} | collective-permute-start | bytes 4616 | tf_op jit(solution)/shard_map/ppermute | solution.py:638
  34.1 5.8 %collective-permute-start.13 = (f32[1,384]{1,0:T(1,128)S(1)}, f32[1,384]{1,0:T(1,128)S(1)}, u32[]{:S(2)}, u32[]{:S(2)}) collective-permute-start(f32[1,384]{1,0:T(1,128)S(1)} %get-tuple-element.82), channel_id=1, source_target_pairs={{4,1},{5,2},{6,3},{8,5},{9,6},{10,7},{12,9},{13,10},{14,11}} | collective-permute-start | bytes 4616 | tf_op jit(solution)/shard_map/ppermute | solution.py:638
  37.7 4.7 %collective-permute-start.9 = (f32[2,6,384]{2,1,0:T(8,128)S(1)}, f32[2,6,384]{2,1,0:T(8,128)S(1)}, u32[]{:S(2)}, u32[]{:S(2)}) collective-permute-start(f32[2,6,384]{2,1,0:T(8,128)S(1)} %get-tuple-element.78), channel_id=1, source_target_pairs={{1,0},{2,1},{3,2},{5,4},{6,5},{7,6},{9,8},{10,9},{11,10},{13,12},{... | collective-permute-start | bytes 55304 | tf_op jit(solution)/shard_map/ppermute | solution.py:638
  39.9 5.1 %collective-permute-start.11 = (f32[2,6,384]{2,1,0:T(8,128)S(1)}, f32[2,6,384]{2,1,0:T(8,128)S(1)}, u32[]{:S(2)}, u32[]{:S(2)}) collective-permute-start(f32[2,6,384]{2,1,0:T(8,128)S(1)} %get-tuple-element.80), channel_id=1, source_target_pairs={{0,1},{1,2},{2,3},{4,5},{5,6},{6,7},{8,9},{9,10},{10,11},{12,13},{... | collective-permute-start | bytes 55304 | tf_op jit(solution)/shard_map/ppermute | solution.py:638
  45.9 20.0 %collective-permute-start.15 = (f32[2,24,384]{2,1,0:T(8,128)S(1)}, f32[2,24,384]{2,1,0:T(8,128)S(1)}, u32[]{:S(2)}, u32[]{:S(2)}) collective-permute-start(f32[2,24,384]{2,1,0:T(8,128)S(1)} %get-tuple-element.91), channel_id=1, source_target_pairs={{4,0},{5,1},{6,2},{7,3},{8,4},{9,5},{10,6},{11,7},{12,8},{13,9},{1... | collective-permute-start | bytes 221192 | tf_op jit(solution)/shard_map/ppermute | solution.py:638
  48.4 17.6 %collective-permute-start.17 = (f32[2,24,384]{2,1,0:T(8,128)S(1)}, f32[2,24,384]{2,1,0:T(8,128)S(1)}, u32[]{:S(2)}, u32[]{:S(2)}) collective-permute-start(f32[2,24,384]{2,1,0:T(8,128)S(1)} %get-tuple-element.93), channel_id=1, source_target_pairs={{0,4},{1,5},{2,6},{3,7},{4,8},{5,9},{6,10},{7,11},{8,12},{9,13},{1... | collective-permute-start | bytes 221192 | tf_op jit(solution)/shard_map/ppermute | solution.py:638
  51.8 14.2 %collective-permute-start.14 = (f32[3,2,8,128]{3,2,1,0:T(8,128)S(1)}, f32[3,2,8,128]{3,2,1,0:T(8,128)S(1)}, u32[]{:S(2)}, u32[]{:S(2)}) collective-permute-start(f32[3,2,8,128]{3,2,1,0:T(8,128)S(1)} %get-tuple-element.88), channel_id=1, source_target_pairs={{0,16},{1,17},{2,18},{3,19},{4,20},{5,21},{6,22},{7,23},{8,24},{9,... | collective-permute-start | bytes 73736 | tf_op jit(solution)/shard_map/ppermute | solution.py:20
  53.1 5.6 %collective-permute-start.19 = (f32[1,384]{1,0:T(1,128)S(1)}, f32[1,384]{1,0:T(1,128)S(1)}, u32[]{:S(2)}, u32[]{:S(2)}) collective-permute-start(f32[1,384]{1,0:T(1,128)S(1)} %get-tuple-element.95), channel_id=1, source_target_pairs={{1,4},{2,5},{3,6},{5,8},{6,9},{7,10},{9,12},{10,13},{11,14},{17,20... | collective-permute-start | bytes 4616 | tf_op jit(solution)/shard_map/ppermute | solution.py:638
  55.0 5.8 %collective-permute-start.20 = (f32[1,384]{1,0:T(1,128)S(1)}, f32[1,384]{1,0:T(1,128)S(1)}, u32[]{:S(2)}, u32[]{:S(2)}) collective-permute-start(f32[1,384]{1,0:T(1,128)S(1)} %get-tuple-element.96), channel_id=1, source_target_pairs={{4,1},{5,2},{6,3},{8,5},{9,6},{10,7},{12,9},{13,10},{14,11},{20,17... | collective-permute-start | bytes 4616 | tf_op jit(solution)/shard_map/ppermute | solution.py:638
  58.6 4.6 %collective-permute-start.16 = (f32[2,6,384]{2,1,0:T(8,128)S(1)}, f32[2,6,384]{2,1,0:T(8,128)S(1)}, u32[]{:S(2)}, u32[]{:S(2)}) collective-permute-start(f32[2,6,384]{2,1,0:T(8,128)S(1)} %get-tuple-element.92), channel_id=1, source_target_pairs={{1,0},{2,1},{3,2},{5,4},{6,5},{7,6},{9,8},{10,9},{11,10},{13,12},{... | collective-permute-start | bytes 55304 | tf_op jit(solution)/shard_map/ppermute | solution.py:638
  60.8 5.1 %collective-permute-start.18 = (f32[2,6,384]{2,1,0:T(8,128)S(1)}, f32[2,6,384]{2,1,0:T(8,128)S(1)}, u32[]{:S(2)}, u32[]{:S(2)}) collective-permute-start(f32[2,6,384]{2,1,0:T(8,128)S(1)} %get-tuple-element.94), channel_id=1, source_target_pairs={{0,1},{1,2},{2,3},{4,5},{5,6},{6,7},{8,9},{9,10},{10,11},{12,13},{... | collective-permute-start | bytes 55304 | tf_op jit(solution)/shard_map/ppermute | solution.py:638
  66.7 25.8 %collective-permute-start.22 = (f32[168,384]{1,0:T(8,128)S(1)}, f32[168,384]{1,0:T(8,128)S(1)}, u32[]{:S(2)}, u32[]{:S(2)}) collective-permute-start(f32[168,384]{1,0:T(8,128)S(1)} %get-tuple-element.103), channel_id=1, source_target_pairs={{16,0},{17,1},{18,2},{19,3},{20,4},{21,5},{22,6},{23,7},{24,8},{25... | collective-permute-start | bytes 774152 | tf_op jit(solution)/shard_map/ppermute | solution.py:20
  68.0 24.5 %collective-permute-start.23 = (f32[2,24,384]{2,1,0:T(8,128)S(1)}, f32[2,24,384]{2,1,0:T(8,128)S(1)}, u32[]{:S(2)}, u32[]{:S(2)}) collective-permute-start(f32[2,24,384]{2,1,0:T(8,128)S(1)} %get-tuple-element.104), channel_id=1, source_target_pairs={{20,16},{21,17},{22,18},{23,19},{24,20},{25,21},{26,22},{27,23},{2... | collective-permute-start | bytes 221192 | tf_op jit(solution)/shard_map/ppermute | solution.py:638
  68.7 23.9 %collective-permute-start.25 = (f32[2,24,384]{2,1,0:T(8,128)S(1)}, f32[2,24,384]{2,1,0:T(8,128)S(1)}, u32[]{:S(2)}, u32[]{:S(2)}) collective-permute-start(f32[2,24,384]{2,1,0:T(8,128)S(1)} %get-tuple-element.106), channel_id=1, source_target_pairs={{16,20},{17,21},{18,22},{19,23},{20,24},{21,25},{22,26},{23,27},{2... | collective-permute-start | bytes 221192 | tf_op jit(solution)/shard_map/ppermute | solution.py:638
  69.3 21.7 %collective-permute-start.24 = (f32[2,6,384]{2,1,0:T(8,128)S(1)}, f32[2,6,384]{2,1,0:T(8,128)S(1)}, u32[]{:S(2)}, u32[]{:S(2)}) collective-permute-start(f32[2,6,384]{2,1,0:T(8,128)S(1)} %get-tuple-element.105), channel_id=1, source_target_pairs={{17,16},{18,17},{19,18},{21,20},{22,21},{23,22},{25,24},{26,25},{2... | collective-permute-start | bytes 55304 | tf_op jit(solution)/shard_map/ppermute | solution.py:638
  70.0 0.7 collective-permute-start.27
  70.7 0.7 collective-permute-start.28
  71.4 21.2 %collective-permute-start.21 = (f32[3,2,8,128]{3,2,1,0:T(8,128)S(1)}, f32[3,2,8,128]{3,2,1,0:T(8,128)S(1)}, u32[]{:S(2)}, u32[]{:S(2)}) collective-permute-start(f32[3,2,8,128]{3,2,1,0:T(8,128)S(1)} %get-tuple-element.101), channel_id=1, source_target_pairs={{0,16},{1,17},{2,18},{3,19},{4,20},{5,21},{6,22},{7,23},{8,24},{9,... | collective-permute-start | bytes 73736 | tf_op jit(solution)/shard_map/ppermute | solution.py:20
  91.0 0.7 collective-permute-start.26
  93.2 9.8 %collective-permute-start.29 = (f32[152,384]{1,0:T(8,128)S(1)}, f32[152,384]{1,0:T(8,128)S(1)}, u32[]{:S(2)}, u32[]{:S(2)}) collective-permute-start(f32[152,384]{1,0:T(8,128)S(1)} %get-tuple-element.113), channel_id=1, source_target_pairs={{16,0},{17,1},{18,2},{19,3},{20,4},{21,5},{22,6},{23,7},{24,8},{25... | collective-permute-start | bytes 700424 | tf_op jit(solution)/shard_map/ppermute | solution.py:20

commit v6 on v4

--- a/solution.py
+++ b/solution.py
@@ -261,19 +261,19 @@
                     e[spot] = jnp.where(keep, pair, e[spot])
 
 
-def pack(out, box, in_x, in_y, at=0):
+def pack(out, box, in_x, in_y, at):
     if box is not None:
         for c in range(3):
             for i in range(2):
-                out[pl.ds(8 * i, 8), pl.ds(128 * c, 128)] = box[c][i]
+                out[pl.ds(at + 8 * i, 8), pl.ds(128 * c, 128)] = box[c][i]
         at += 16
     for k in range(2):
         out[pl.ds(at + 24 * k, 24)] = in_x[k]
-        out[pl.ds(at + 48 + 8 * k, 6)] = in_y[k]
-
-
-def packed_box(ref):
-    return lambda c, i: ref[pl.ds(8 * i, 8), pl.ds(128 * c, 128)]
+        out[pl.ds(at + 48 + 8 * k, 6)] = in_y[k, 0:6]
+
+
+def packed_box(ref, at):
+    return lambda c, i: ref[pl.ds(at + 8 * i, 8), pl.ds(128 * c, 128)]
 
 
 def packed_x(ref, at):
@@ -434,7 +434,7 @@
         last_layers(out_h, bx, by)
 
 
-def e1_kernel(e, h, p, coef, bx, by, desc, material, out_e, out_p, sent, out_material):
+def e1_kernel(e, h, p, coef, bx, by, desc, material, table, out_e, out_p, sent, slab_coef):
     @pl.when(is_coarse())
     def _():
         spot = corner(desc)
@@ -445,7 +445,17 @@
             for i in range(2):
                 sent[0, c, i] = before[c][i]
                 sent[1, c, i] = after[c][i]
-        out_material[...] = material[...]
+        slab_coef[...] = coef[...]
+
+    @pl.when(is_fine())
+    def _():
+        tiles = [table[k] for k in range(5)]
+        for x in range(6):
+            for yt in range(3):
+                for zt in range(3):
+                    index = material[0, x, pl.ds(8 * yt, 8), pl.ds(128 * zt, 128)]
+                    for k in range(5):
+                        slab_coef[k, x, 3 * yt + zt] = gather(tiles[k], index)
 
 
 def f1_kernel(e, h, p, box_in, coef, region, desc, out_e, out_h, out_p, ax, ay, box, now, change):
@@ -469,25 +479,10 @@
         first_layers(out_e, ax, ay)
 
 
-def h2_kernel(e, h, ax, ay, change, coef, material, table, out_h, bx, by, relay, slab_coef):
+def h2_kernel(e, h, ax, ay, out_h, bx, by):
     magnetic(e, h, edge_x(ax), edge_y(ay), out_h)
     last_layers(out_h, bx, by)
 
-    @pl.when(is_coarse())
-    def _():
-        slab_coef[...] = coef[...]
-
-    @pl.when(is_fine())
-    def _():
-        pack(relay, load_box(change), ax, ay)
-        tiles = [table[k] for k in range(5)]
-        for x in range(6):
-            for yt in range(3):
-                for zt in range(3):
-                    index = material[0, x, pl.ds(8 * yt, 8), pl.ds(128 * zt, 128)]
-                    for k in range(5):
-                        slab_coef[k, x, 3 * yt + zt] = gather(tiles[k], index)
-
 
 def base_kernel(e, h, p, coef, bx, by, desc, out_e, out_p, sent):
     @pl.when(is_coarse())
@@ -497,16 +492,13 @@
 
 
 def f2_kernel(
-    e, h, p, base_e, base_p, coef, slab_coef, bx, by, desc, box_in, region, was, relay1,
-    out_e, out_p, ax, ay, box, now, relay, fix_h, one_e,
+    e, h, p, base_e, base_p, coef, slab_coef, bx, by, desc, box_in, region, was,
+    out_e, out_p, ax, ay, box, now, change,
 ):
     @pl.when(is_coarse())
     def _():
         out_e[...], out_p[...] = base_e[...], base_p[...]
         first_layers(base_e, ax, ay)
-        one_e[...] = jnp.zeros(one_e.shape, F32)
-        put(one_e, packed_box(relay1), desc, corner(desc))
-        magnetic(one_e, None, packed_x(relay1, 16), packed_y(relay1, 16), fix_h)
 
     @pl.when(is_fine())
     def _():
@@ -518,34 +510,39 @@
         restricted = fine_steps(box, coef, desc, load_box(was), latest)
         after, delta = feed_back(restricted, latest, desc)
         store_box(now, after)
+        store_box(change, delta)
         put(out_e, lambda c, i: delta[c][i], desc, spot)
         first_layers(out_e, ax, ay)
-        pack(relay, delta, bx, by)
-
-
-def h3_kernel(e, h, ax, ay, out_h, bx, by, relay):
+
+
+def h3_kernel(
+    e, h, ax, ay, change1, ax2, ay2, change2, bx2, by2, out_h, bx, by, relay,
+):
     magnetic(e, h, edge_x(ax), edge_y(ay), out_h)
     last_layers(out_h, bx, by)
 
     @pl.when(is_fine())
     def _():
-        pack(relay, None, ax, ay)
+        pack(relay, load_box(change1), ax2, ay2, 0)
+        pack(relay, load_box(change2), bx2, by2, 80)
+        pack(relay, None, ax, ay, 160)
 
 
 def f3_kernel(
-    e, h, p, coef, slab_coef, bx, by, desc, box_in, region, was, relay1, relay2, relay3, one_h,
-    box, relay, fix_e, fix_h, fix_p, layer, one_e,
+    e, h, p, coef, slab_coef, bx, by, desc, box_in, region, was, relay_in,
+    box, relay, fix_e, fix_h, fix_p, layer, one_e, one_h,
 ):
     @pl.when(is_coarse())
     def _():
         one_e[...] = jnp.zeros(one_e.shape, F32)
         spot = corner(desc)
-        put(one_e, packed_box(relay1), desc, spot)
+        put(one_e, packed_box(relay_in, 0), desc, spot)
+        magnetic(one_e, None, packed_x(relay_in, 16), packed_y(relay_in, 16), one_h)
         electric(
-            one_e, one_h, None, coef, packed_x(relay2, 16), packed_y(relay2, 16), fix_e, fix_p
+            one_e, one_h, None, coef, packed_x(relay_in, 96), packed_y(relay_in, 96), fix_e, fix_p
         )
-        put(fix_e, packed_box(relay2), desc, spot)
-        magnetic(fix_e, one_h, packed_x(relay3, 0), packed_y(relay3, 0), fix_h)
+        put(fix_e, packed_box(relay_in, 80), desc, spot)
+        magnetic(fix_e, one_h, packed_x(relay_in, 160), packed_y(relay_in, 160), fix_h)
 
     @pl.when(is_fine())
     def _():
@@ -561,7 +558,7 @@
         fix = cut_region(layer, desc, (0, *spot[1:]))
         latest = [[region[c, i] + fix[c][i] for i in range(2)] for c in range(3)]
         restricted = fine_steps(box, coef, desc, load_box(was), latest)
-        pack(relay, restricted, bx, by)
+        pack(relay, restricted, bx, by, 0)
 
 
 def finish_kernel(e, h, p, fix_e, fix_h, fix_p, coef, desc, relay, box, out, mixed):
@@ -574,7 +571,7 @@
         )
         out[3:6] = h[...] + fix_h[...]
         covered = [jnp.where(value, F32(1.0), 0.0) for value in covered_of(desc)]
-        put(view_e, packed_box(relay), desc, corner(desc), covered)
+        put(view_e, packed_box(relay, 0), desc, corner(desc), covered)
 
     @pl.when(is_fine())
     def _():
@@ -613,6 +610,7 @@
 X_EDGE = (2, 24, 384)
 Y_EDGE = (2, 6, 384)
 EDGES = [X_EDGE, Y_EDGE]
+LAST = [X_EDGE, (2, 16, 384)]
 AXES = ("grid", "gx", "gy")
 
 
@@ -666,55 +664,55 @@
         + [SM] * 5,
         grid=(1,),
     )
-    h, bx, by = call(h1_kernel, (e, h, ax, ay), [PART] + EDGES)
+    slab_material = to_fine(material)
+    h, bx, by = call(h1_kernel, (e, h, ax, ay), [PART] + LAST)
     bx, by = exchange(bx, by, 1, (0,))
-    e, p, sent, slab_material = call(
+    e, p, sent, slab_coef = call(
         e1_kernel,
-        (e, h, p, coef, bx, by, desc, material),
-        [PART] * 2 + [(2, *REGION), jax.ShapeDtypeStruct(material.shape, jnp.int32)],
+        (e, h, p, coef, bx, by, desc, slab_material, table),
+        [PART] * 2 + [(2, *REGION), COEF],
     )
     region = to_fine(sent)
-    slab_material = to_fine(slab_material)
-    e, h, p, ax, ay, box, now, change = call(
+    e, h, p, ax, ay, box, now, change1 = call(
         f1_kernel,
         (e, h, p, box, coef, region, desc),
         [PART] * 3 + EDGES + [BOX, REGION, REGION],
     )
+    ax2, ay2 = exchange(ax, ay, -1, (0, 1))
+    h, bx, by = call(h2_kernel, (e, h, ax2, ay2), [PART] + LAST)
+    bx2, by2 = exchange(bx, by, 1, (1,))
+    bx, by = exchange(bx, by, 1, (0,))
+    base_e, base_p, sent = call(
+        base_kernel, (e, h, p, slab_coef, bx, by, desc), [PART] * 2 + [REGION]
+    )
+    region = to_fine(sent)
+    e, p, ax, ay, box, now, change2 = call(
+        f2_kernel,
+        (e, h, p, base_e, base_p, coef, slab_coef, bx2, by2, desc, box, region, now),
+        [PART] * 2 + EDGES + [BOX, REGION, REGION],
+    )
     ax, ay = exchange(ax, ay, -1, (0, 1))
-    h, bx, by, relay1, slab_coef = call(
-        h2_kernel,
-        (e, h, ax, ay, change, coef, slab_material, table),
-        [PART] + EDGES + [(80, 384), COEF],
-    )
+    h, bx, by, relay = call(
+        h3_kernel,
+        (e, h, ax, ay, change1, ax2, ay2, change2, bx2, by2),
+        [PART] + LAST + [(224, 384)],
+    )
+    relay = to_coarse(relay)
     fine_bx, fine_by = exchange(bx, by, 1, (1,))
     bx, by = exchange(bx, by, 1, (0,))
     base_e, base_p, sent = call(
         base_kernel, (e, h, p, slab_coef, bx, by, desc), [PART] * 2 + [REGION]
     )
     region = to_fine(sent)
-    relay1 = to_coarse(relay1)
-    e, p, ax, ay, box, now, relay2, fix_h = call(
-        f2_kernel,
-        (e, h, p, base_e, base_p, coef, slab_coef, fine_bx, fine_by, desc, box, region, now, relay1),
-        [PART] * 2 + EDGES + [BOX, REGION, (80, 384), PART],
-        scratch=[pltpu.VMEM(PART, F32)],
-    )
-    ax, ay = exchange(ax, ay, -1, (0, 1))
-    relay2 = to_coarse(relay2)
-    h, bx, by, relay3 = call(h3_kernel, (e, h, ax, ay), [PART] + EDGES + [(64, 384)])
-    fine_bx, fine_by = exchange(bx, by, 1, (1,))
-    bx, by = exchange(bx, by, 1, (0,))
-    base_e, base_p, sent = call(
-        base_kernel, (e, h, p, slab_coef, bx, by, desc), [PART] * 2 + [REGION]
-    )
-    region = to_fine(sent)
-    relay3 = to_coarse(relay3)
     box, relay4, *fix = call(
         f3_kernel,
-        (e, h, p, coef, slab_coef, fine_bx, fine_by, desc, box, region, now)
-        + (relay1, relay2, relay3, fix_h),
+        (e, h, p, coef, slab_coef, fine_bx, fine_by, desc, box, region, now, relay),
         [BOX, (80, 384)] + [PART] * 3,
-        scratch=[pltpu.VMEM((3, 2, 24, 384), F32), pltpu.VMEM(PART, F32)],
+        scratch=[
+            pltpu.VMEM((3, 2, 24, 384), F32),
+            pltpu.VMEM(PART, F32),
+            pltpu.VMEM(PART, F32),
+        ],
     )
     relay4 = to_coarse(relay4)
     (out,) = call(

time: 80.5 us -> 81.2 us (level)
  starting transfers between devices: 45 us -> 50.6 us
  waiting for transfers between devices: 26.5 us -> 21.8 us
    ppermute x8 -> x6, starting transfers between devices: 14.1 us -> 20 us  [shifted(): return lax.ppermute(value, axis, pairs)]
    ppermute x8 -> x6, waiting for transfers between devices: 14.4 us -> 10.9 us  [shifted(): return lax.ppermute(value, axis, pairs)]
    ppermute x8, waiting for transfers between devices: 6.67 us -> 5.04 us  [exchange(): lax.ppermute(y_edge, AXES, pairs(0, by))]
    ppermute x8, starting transfers between devices: 16.8 us -> 15.8 us  [exchange(): lax.ppermute(x_edge, AXES, pairs(by, 0))]
  transfers between devices with their start and end apart: 24 -> 22, of which waited for: 13 -> 11; matrix products, arithmetic and copies ran while one was open for 0% -> 0% of each run, Pallas kernels for 3% -> 3%
where the time goes in v6:
time: 81.2 us; the launch traced here: 80.6 us
  starting transfers between devices  50.6 us (62%)
  waiting for transfers between devices  21.8 us (27%)
  Pallas kernels  6.31 us (8%)
  local copies, waits for them, and re-layouts  1.57 us (2%)
    ppermute x6, starting transfers between devices, shifted(): return lax.ppermute(value, axis, pairs)  20 us
    ppermute x8, starting transfers between devices, exchange(): lax.ppermute(x_edge, AXES, pairs(by, 0))  15.8 us
    ppermute x8, starting transfers between devices, exchange(): lax.ppermute(y_edge, AXES, pairs(0, by))  14.7 us
    ppermute x6, waiting for transfers between devices, shifted(): return lax.ppermute(value, axis, pairs)  10.9 us
    pallas_call x12, Pallas kernels, call(): pl.pallas_call(kernel, out_shape=shapes, in_specs=specs or [VM] * len(ope...  6.31 us
    ppermute x8, waiting for transfers between devices, exchange(): lax.ppermute(x_edge, AXES, pairs(by, 0))  5.78 us
    ppermute x8, waiting for transfers between devices, exchange(): lax.ppermute(y_edge, AXES, pairs(0, by))  5.04 us
  transfers between devices with their start and end apart: 22, of which 11 were waited for; matrix products, arithmetic and copies ran while one was open for 0% of the time, Pallas kernels for 3%

profile of v6, /device:TPU:0, one launch (start us, length us, event | category | flops | bytes accessed | tf_op | source)
XLA Modules:
  0.0 80.6 jit_solution(13312524386185037114)
XLA Ops:
  0.0 4.8 %collective-permute-start.4 = (s32[1,6,24,384]{3,2,1,0:T(8,128)}, s32[1,6,24,384]{3,2,1,0:T(8,128)S(1)}, u32[]{:S(2)}, u32[]{:S(2)}) collective-permute-start(s32[1,6,24,384]{3,2,1,0:T(8,128)} %m2.1), channel_id=1, source_target_pairs={{0,16},{1,17},{2,18},{3,19},{4,20},{5,21},{6,22},{7,23},{8,24},{9,... | collective-permute-start | bytes 663560 | tf_op jit(solution)/shard_map/ppermute | solution.py:20
  4.9 1.5 %copy-done = f32[1,9,6,24,384]{4,3,2,1,0:T(8,128)S(1)} copy-done((f32[1,9,6,24,384]{4,3,2,1,0:T(8,128)S(1)}, f32[1,9,6,24,384]{4,3,2,1,0:T(8,128)}, u32[]{:S(2)}) %copy-start) | copy-done | bytes 1990680
  6.5 1.4 %collective-permute-start = (f32[2,24,384]{2,1,0:T(8,128)S(1)}, f32[2,24,384]{2,1,0:T(8,128)S(1)}, u32[]{:S(2)}, u32[]{:S(2)}) collective-permute-start(f32[2,24,384]{2,1,0:T(8,128)S(1)} %get-tuple-element.56), channel_id=1, source_target_pairs={{4,0},{5,1},{6,2},{7,3},{8,4},{9,5},{10,6},{11,7},{12,8},{13,9},{1... | collective-permute-start | bytes 221192 | tf_op jit(solution)/shard_map/ppermute | solution.py:630
  7.9 1.3 %collective-permute-start.1 = (f32[2,6,384]{2,1,0:T(8,128)S(1)}, f32[2,6,384]{2,1,0:T(8,128)S(1)}, u32[]{:S(2)}, u32[]{:S(2)}) collective-permute-start(f32[2,6,384]{2,1,0:T(8,128)S(1)} %get-tuple-element.57), channel_id=1, source_target_pairs={{1,0},{2,1},{3,2},{5,4},{6,5},{7,6},{9,8},{10,9},{11,10},{13,12},{... | collective-permute-start | bytes 55304 | tf_op jit(solution)/shard_map/ppermute | solution.py:631
  9.3 1.1 %shard_map.73 = (f32[3,6,24,384]{3,2,1,0:T(8,128)S(1)}, f32[3,6,24,384]{3,2,1,0:T(8,128)S(1)}, f32[3,6,24,384]{3,2,1,0:T(8,128)S(1)}, f32[9,6,9,8,128]{4,3,2,1,0...) custom-call(f32[1,9,6,24,384]{4,3,2,1,0:T(8,128)S(1)} %copy-done, ...), custom_call_target="tpu_custom_call" | custom-call | tf_op jit(solution)/shard_map/pallas_call | solution.py:594
  10.4 0.6 collective-permute-done.1.ay
  11.0 1.9 %collective-permute-done.ax = f32[2,24,384]{2,1,0:T(8,128)S(1)} collective-permute-done((f32[2,24,384]{2,1,0:T(8,128)S(1)}, f32[2,24,384]{2,1,0:T(8,128)S(1)}, u32[]{:S(2)}, u32[]{:S(2)}) %collective-permute-start) | collective-permute-done | bytes 73760 | tf_op jit(solution)/shard_map/ppermute | solution.py:630
  12.9 0.2 shard_map.75
  13.1 3.5 %collective-permute-start.2 = (f32[2,24,384]{2,1,0:T(8,128)S(1)}, f32[2,24,384]{2,1,0:T(8,128)S(1)}, u32[]{:S(2)}, u32[]{:S(2)}) collective-permute-start(f32[2,24,384]{2,1,0:T(8,128)S(1)} %get-tuple-element.61), channel_id=1, source_target_pairs={{0,4},{1,5},{2,6},{3,7},{4,8},{5,9},{6,10},{7,11},{8,12},{9,13},{1... | collective-permute-start | bytes 221192 | tf_op jit(solution)/shard_map/ppermute | solution.py:630
  16.6 2.8 %collective-permute-start.3 = (f32[2,16,384]{2,1,0:T(8,128)S(1)}, f32[2,16,384]{2,1,0:T(8,128)S(1)}, u32[]{:S(2)}, u32[]{:S(2)}) collective-permute-start(f32[2,16,384]{2,1,0:T(8,128)S(1)} %get-tuple-element.62), channel_id=1, source_target_pairs={{0,1},{1,2},{2,3},{4,5},{5,6},{6,7},{8,9},{9,10},{10,11},{12,13},{... | collective-permute-start | bytes 147464 | tf_op jit(solution)/shard_map/ppermute | solution.py:631
  19.4 0.9 %collective-permute-done.3.by = f32[2,16,384]{2,1,0:T(8,128)S(1)} collective-permute-done((f32[2,16,384]{2,1,0:T(8,128)S(1)}, f32[2,16,384]{2,1,0:T(8,128)S(1)}, u32[]{:S(2)}, u32[]{:S(2)}) %collective-permute-start.3) | collective-permute-done | bytes 49184 | tf_op jit(solution)/shard_map/ppermute | solution.py:631
  20.2 0.6 shard_map.76
  20.8 1.3 %collective-permute-start.5 = (f32[2,3,2,8,128]{4,3,2,1,0:T(8,128)S(1)}, f32[2,3,2,8,128]{4,3,2,1,0:T(8,128)S(1)}, u32[]{:S(2)}, u32[]{:S(2)}) collective-permute-start(f32[2,3,2,8,128]{4,3,2,1,0:T(8,128)S(1)} %get-tuple-element.68), channel_id=1, source_target_pairs={{0,16},{1,17},{2,18},{3,19},{4,20},{5,21},{6,22},{7,23},{8,24},{9,... | collective-permute-start | bytes 147464 | tf_op jit(solution)/shard_map/ppermute | solution.py:20
  22.1 1.9 %collective-permute-done.5.region = f32[2,3,2,8,128]{4,3,2,1,0:T(8,128)S(1)} collective-permute-done((f32[2,3,2,8,128]{4,3,2,1,0:T(8,128)S(1)}, f32[2,3,2,8,128]{4,3,2,1,0:T(8,128)S(1)}, u32[]{:S(2)}, u32[]{:S(2)}) %collective-permute-start.5) | collective-permute-done | bytes 49184 | tf_op jit(solution)/shard_map/ppermute | solution.py:20
  24.0 0.1 shard_map.77
  24.1 1.3 %collective-permute-start.6 = (f32[2,24,384]{2,1,0:T(8,128)S(1)}, f32[2,24,384]{2,1,0:T(8,128)S(1)}, u32[]{:S(2)}, u32[]{:S(2)}) collective-permute-start(f32[2,24,384]{2,1,0:T(8,128)S(1)} %get-tuple-element.71), channel_id=1, source_target_pairs={{4,0},{5,1},{6,2},{7,3},{8,4},{9,5},{10,6},{11,7},{12,8},{13,9},{1... | collective-permute-start | bytes 221192 | tf_op jit(solution)/shard_map/ppermute | solution.py:630
  25.4 1.3 %collective-permute-start.7 = (f32[2,6,384]{2,1,0:T(8,128)S(1)}, f32[2,6,384]{2,1,0:T(8,128)S(1)}, u32[]{:S(2)}, u32[]{:S(2)}) collective-permute-start(f32[2,6,384]{2,1,0:T(8,128)S(1)} %get-tuple-element.72), channel_id=1, source_target_pairs={{1,0},{2,1},{3,2},{5,4},{6,5},{7,6},{9,8},{10,9},{11,10},{13,12},{... | collective-permute-start | bytes 55304 | tf_op jit(solution)/shard_map/ppermute | solution.py:631
  26.7 1.8 %collective-permute-done.7.ay.ay2 = f32[2,6,384]{2,1,0:T(8,128)S(1)} collective-permute-done((f32[2,6,384]{2,1,0:T(8,128)S(1)}, f32[2,6,384]{2,1,0:T(8,128)S(1)}, u32[]{:S(2)}, u32[]{:S(2)}) %collective-permute-start.7) | collective-permute-done | bytes 18464 | tf_op jit(solution)/shard_map/ppermute | solution.py:631
  28.5 2.1 %collective-permute-done.6.ax.ax2 = f32[2,24,384]{2,1,0:T(8,128)S(1)} collective-permute-done((f32[2,24,384]{2,1,0:T(8,128)S(1)}, f32[2,24,384]{2,1,0:T(8,128)S(1)}, u32[]{:S(2)}, u32[]{:S(2)}) %collective-permute-start.6) | collective-permute-done | bytes 73760 | tf_op jit(solution)/shard_map/ppermute | solution.py:630
  30.6 0.2 shard_map.78
  30.8 3.5 %collective-permute-start.8 = (f32[2,24,384]{2,1,0:T(8,128)S(1)}, f32[2,24,384]{2,1,0:T(8,128)S(1)}, u32[]{:S(2)}, u32[]{:S(2)}) collective-permute-start(f32[2,24,384]{2,1,0:T(8,128)S(1)} %get-tuple-element.76), channel_id=1, source_target_pairs={{0,4},{1,5},{2,6},{3,7},{4,8},{5,9},{6,10},{7,11},{8,12},{9,13},{1... | collective-permute-start | bytes 221192 | tf_op jit(solution)/shard_map/ppermute | solution.py:630
  34.3 4.2 %collective-permute-start.9 = (f32[2,16,384]{2,1,0:T(8,128)S(1)}, f32[2,16,384]{2,1,0:T(8,128)S(1)}, u32[]{:S(2)}, u32[]{:S(2)}) collective-permute-start(f32[2,16,384]{2,1,0:T(8,128)S(1)} %get-tuple-element.77), channel_id=1, source_target_pairs={{0,1},{1,2},{2,3},{4,5},{5,6},{6,7},{8,9},{9,10},{10,11},{12,13},{... | collective-permute-start | bytes 147464 | tf_op jit(solution)/shard_map/ppermute | solution.py:631
  38.5 0.7 collective-permute-start.10
  39.2 0.7 collective-permute-start.11
  39.9 0.0 collective-permute-done.9.by
  39.9 0.5 shard_map.79
  40.4 5.5 %collective-permute-start.12 = (f32[3,2,8,128]{3,2,1,0:T(8,128)S(1)}, f32[3,2,8,128]{3,2,1,0:T(8,128)S(1)}, u32[]{:S(2)}, u32[]{:S(2)}) collective-permute-start(f32[3,2,8,128]{3,2,1,0:T(8,128)S(1)} %get-tuple-element.81), channel_id=1, source_target_pairs={{0,16},{1,17},{2,18},{3,19},{4,20},{5,21},{6,22},{7,23},{8,24},{9,... | collective-permute-start | bytes 73736 | tf_op jit(solution)/shard_map/ppermute | solution.py:20
  45.9 0.0 collective-permute-done.10.bx.bx2
  45.9 1.5 %collective-permute-done.12.region = f32[3,2,8,128]{3,2,1,0:T(8,128)S(1)} collective-permute-done((f32[3,2,8,128]{3,2,1,0:T(8,128)S(1)}, f32[3,2,8,128]{3,2,1,0:T(8,128)S(1)}, u32[]{:S(2)}, u32[]{:S(2)}) %collective-permute-start.12) | collective-permute-done | bytes 24608 | tf_op jit(solution)/shard_map/ppermute | solution.py:20
  47.4 0.1 shard_map.80
  47.5 1.3 %collective-permute-start.13 = (f32[2,24,384]{2,1,0:T(8,128)S(1)}, f32[2,24,384]{2,1,0:T(8,128)S(1)}, u32[]{:S(2)}, u32[]{:S(2)}) collective-permute-start(f32[2,24,384]{2,1,0:T(8,128)S(1)} %get-tuple-element.84), channel_id=1, source_target_pairs={{4,0},{5,1},{6,2},{7,3},{8,4},{9,5},{10,6},{11,7},{12,8},{13,9},{1... | collective-permute-start | bytes 221192 | tf_op jit(solution)/shard_map/ppermute | solution.py:630
  48.8 1.3 %collective-permute-start.14 = (f32[2,6,384]{2,1,0:T(8,128)S(1)}, f32[2,6,384]{2,1,0:T(8,128)S(1)}, u32[]{:S(2)}, u32[]{:S(2)}) collective-permute-start(f32[2,6,384]{2,1,0:T(8,128)S(1)} %get-tuple-element.85), channel_id=1, source_target_pairs={{1,0},{2,1},{3,2},{5,4},{6,5},{7,6},{9,8},{10,9},{11,10},{13,12},{... | collective-permute-start | bytes 55304 | tf_op jit(solution)/shard_map/ppermute | solution.py:631
  50.1 1.8 %collective-permute-done.14.ay = f32[2,6,384]{2,1,0:T(8,128)S(1)} collective-permute-done((f32[2,6,384]{2,1,0:T(8,128)S(1)}, f32[2,6,384]{2,1,0:T(8,128)S(1)}, u32[]{:S(2)}, u32[]{:S(2)}) %collective-permute-start.14) | collective-permute-done | bytes 18464 | tf_op jit(solution)/shard_map/ppermute | solution.py:631
  51.9 1.9 %collective-permute-done.13.ax = f32[2,24,384]{2,1,0:T(8,128)S(1)} collective-permute-done((f32[2,24,384]{2,1,0:T(8,128)S(1)}, f32[2,24,384]{2,1,0:T(8,128)S(1)}, u32[]{:S(2)}, u32[]{:S(2)}) %collective-permute-start.13) | collective-permute-done | bytes 73760 | tf_op jit(solution)/shard_map/ppermute | solution.py:630
  53.7 0.2 shard_map.81
  54.0 1.3 %collective-permute-start.20 = (f32[224,384]{1,0:T(8,128)S(1)}, f32[224,384]{1,0:T(8,128)S(1)}, u32[]{:S(2)}, u32[]{:S(2)}) collective-permute-start(f32[224,384]{1,0:T(8,128)S(1)} %get-tuple-element.97), channel_id=1, source_target_pairs={{16,0},{17,1},{18,2},{19,3},{20,4},{21,5},{22,6},{23,7},{24,8},{25... | collective-permute-start | bytes 1032200 | tf_op jit(solution)/shard_map/ppermute | solution.py:20
  55.3 3.5 %collective-permute-start.15 = (f32[2,24,384]{2,1,0:T(8,128)S(1)}, f32[2,24,384]{2,1,0:T(8,128)S(1)}, u32[]{:S(2)}, u32[]{:S(2)}) collective-permute-start(f32[2,24,384]{2,1,0:T(8,128)S(1)} %get-tuple-element.90), channel_id=1, source_target_pairs={{0,4},{1,5},{2,6},{3,7},{4,8},{5,9},{6,10},{7,11},{8,12},{9,13},{1... | collective-permute-start | bytes 221192 | tf_op jit(solution)/shard_map/ppermute | solution.py:630
  58.8 2.5 %collective-permute-start.16 = (f32[2,16,384]{2,1,0:T(8,128)S(1)}, f32[2,16,384]{2,1,0:T(8,128)S(1)}, u32[]{:S(2)}, u32[]{:S(2)}) collective-permute-start(f32[2,16,384]{2,1,0:T(8,128)S(1)} %get-tuple-element.91), channel_id=1, source_target_pairs={{0,1},{1,2},{2,3},{4,5},{5,6},{6,7},{8,9},{9,10},{10,11},{12,13},{... | collective-permute-start | bytes 147464 | tf_op jit(solution)/shard_map/ppermute | solution.py:631
  61.3 0.7 collective-permute-start.17
  62.0 0.7 collective-permute-start.18
  62.6 0.0 collective-permute-done.16.by
  62.7 0.5 shard_map.82
  63.2 5.8 %collective-permute-start.19 = (f32[3,2,8,128]{3,2,1,0:T(8,128)S(1)}, f32[3,2,8,128]{3,2,1,0:T(8,128)S(1)}, u32[]{:S(2)}, u32[]{:S(2)}) collective-permute-start(f32[3,2,8,128]{3,2,1,0:T(8,128)S(1)} %get-tuple-element.95), channel_id=1, source_target_pairs={{0,16},{1,17},{2,18},{3,19},{4,20},{5,21},{6,22},{7,23},{8,24},{9,... | collective-permute-start | bytes 73736 | tf_op jit(solution)/shard_map/ppermute | solution.py:20
  69.0 1.5 %collective-permute-done.19.region = f32[3,2,8,128]{3,2,1,0:T(8,128)S(1)} collective-permute-done((f32[3,2,8,128]{3,2,1,0:T(8,128)S(1)}, f32[3,2,8,128]{3,2,1,0:T(8,128)S(1)}, u32[]{:S(2)}, u32[]{:S(2)}) %collective-permute-start.19) | collective-permute-done | bytes 24608 | tf_op jit(solution)/shard_map/ppermute | solution.py:20
  70.5 0.8 %shard_map.83 = (f32[9,6,9,8,128]{4,3,2,1,0:T(8,128)S(1)}, f32[80,384]{1,0:T(8,128)S(1)}, f32[3,6,24,384]{3,2,1,0:T(8,128)S(1)}, f32[3,6,24,384]{3,2,1,0:T(8,128)S(1)}, f32[3,6,24,384]{3,2,1,0:T(8,128)S(1)}) custom-call(f32[3,6,24,384]{3,2,1,0:T(8,128)S(1)} %get-tuple-element.83.e, f32[3,6,24,384]{3,2,1,0:T(8,128)S(1)} %get-tuple-element.88.h, ...), custom_call_target="tpu_custom_call" | custom-call | tf_op jit(solution)/shard_map/pallas_call | solution.py:594
  71.3 1.3 %collective-permute-start.21 = (f32[80,384]{1,0:T(8,128)S(1)}, f32[80,384]{1,0:T(8,128)S(1)}, u32[]{:S(2)}, u32[]{:S(2)}) collective-permute-start(f32[80,384]{1,0:T(8,128)S(1)} %get-tuple-element.101), channel_id=1, source_target_pairs={{16,0},{17,1},{18,2},{19,3},{20,4},{21,5},{22,6},{23,7},{24,8},{25... | collective-permute-start | bytes 368648 | tf_op jit(solution)/shard_map/ppermute | solution.py:20
  72.6 6.1 %collective-permute-done.21.relay = f32[80,384]{1,0:T(8,128)S(1)} collective-permute-done((f32[80,384]{1,0:T(8,128)S(1)}, f32[80,384]{1,0:T(8,128)S(1)}, u32[]{:S(2)}, u32[]{:S(2)}) %collective-permute-start.21) | collective-permute-done | bytes 122912 | tf_op jit(solution)/shard_map/ppermute | solution.py:20
  78.7 1.9 %shard_map.84 = f32[9,6,24,384]{3,2,1,0:T(8,128)} custom-call(f32[3,6,24,384]{3,2,1,0:T(8,128)S(1)} %get-tuple-element.92.e, f32[3,6,24,384]{3,2,1,0:T(8,128)S(1)} %get-tuple-element.88.h, f32[3,6,24,384]{3,2,1,0:T(8,128)S(1)} %get-tuple-element.93.p, f32[3,6,24,384]{3,2,1,0:T(8,128)S(1)} %get-tuple-element.98.fix_e, ...), custom_call_target="tpu_custom_call" | custom-call | tf_op jit(solution)/shard_map/pallas_call | solution.py:594
  (22 shorter events, 0.1 us)
Async XLA Ops:
  0.0 20.2 %collective-permute-start.4 = (s32[1,6,24,384]{3,2,1,0:T(8,128)}, s32[1,6,24,384]{3,2,1,0:T(8,128)S(1)}, u32[]{:S(2)}, u32[]{:S(2)}) collective-permute-start(s32[1,6,24,384]{3,2,1,0:T(8,128)} %m2.1), channel_id=1, source_target_pairs={{0,16},{1,17},{2,18},{3,19},{4,20},{5,21},{6,22},{7,23},{8,24},{9,... | collective-permute-start | bytes 663560 | tf_op jit(solution)/shard_map/ppermute | solution.py:20
  4.9 1.6 %copy-start = (f32[1,9,6,24,384]{4,3,2,1,0:T(8,128)S(1)}, f32[1,9,6,24,384]{4,3,2,1,0:T(8,128)}, u32[]{:S(2)}) copy-start(f32[1,9,6,24,384]{4,3,2,1,0:T(8,128)} %near_y.1) | copy-start | bytes 5971972
  6.4 2.8 %copy-start.1 = (s32[1,6,24,384]{3,2,1,0:T(8,128)S(1)}, s32[1,6,24,384]{3,2,1,0:T(8,128)}, u32[]{:S(2)}) copy-start(s32[1,6,24,384]{3,2,1,0:T(8,128)} %m2.1) | copy-start | bytes 663556
  6.4 2.8 %copy-start.2 = (f32[8]{0:T(128)S(1)}, f32[8]{0:T(128)}, u32[]{:S(2)}) copy-start(f32[8]{0:T(128)} %perm.1) | copy-start | bytes 100
  6.4 2.8 %copy-start.3 = (f32[8]{0:T(128)S(1)}, f32[8]{0:T(128)}, u32[]{:S(2)}) copy-start(f32[8]{0:T(128)} %cond.1) | copy-start | bytes 100
  6.4 2.8 %copy-start.4 = (f32[8]{0:T(128)S(1)}, f32[8]{0:T(128)}, u32[]{:S(2)}) copy-start(f32[8]{0:T(128)} %relax.1) | copy-start | bytes 100
  6.4 2.8 %copy-start.5 = (f32[8]{0:T(128)S(1)}, f32[8]{0:T(128)}, u32[]{:S(2)}) copy-start(f32[8]{0:T(128)} %debye.1) | copy-start | bytes 100
  6.4 2.8 %copy-start.6 = (s32[1,1,6]{2,1,0:T(1,128)S(1)}, s32[1,1,6]{2,1,0:T(1,128)}, u32[]{:S(2)}) copy-start(s32[1,1,6]{2,1,0:T(1,128)} %sub.1) | copy-start | bytes 76
  6.5 6.4 %collective-permute-start = (f32[2,24,384]{2,1,0:T(8,128)S(1)}, f32[2,24,384]{2,1,0:T(8,128)S(1)}, u32[]{:S(2)}, u32[]{:S(2)}) collective-permute-start(f32[2,24,384]{2,1,0:T(8,128)S(1)} %get-tuple-element.56), channel_id=1, source_target_pairs={{4,0},{5,1},{6,2},{7,3},{8,4},{9,5},{10,6},{11,7},{12,8},{13,9},{1... | collective-permute-start | bytes 221192 | tf_op jit(solution)/shard_map/ppermute | solution.py:630
  7.9 3.1 %collective-permute-start.1 = (f32[2,6,384]{2,1,0:T(8,128)S(1)}, f32[2,6,384]{2,1,0:T(8,128)S(1)}, u32[]{:S(2)}, u32[]{:S(2)}) collective-permute-start(f32[2,6,384]{2,1,0:T(8,128)S(1)} %get-tuple-element.57), channel_id=1, source_target_pairs={{1,0},{2,1},{3,2},{5,4},{6,5},{7,6},{9,8},{10,9},{11,10},{13,12},{... | collective-permute-start | bytes 55304 | tf_op jit(solution)/shard_map/ppermute | solution.py:631
  13.1 7.2 %collective-permute-start.2 = (f32[2,24,384]{2,1,0:T(8,128)S(1)}, f32[2,24,384]{2,1,0:T(8,128)S(1)}, u32[]{:S(2)}, u32[]{:S(2)}) collective-permute-start(f32[2,24,384]{2,1,0:T(8,128)S(1)} %get-tuple-element.61), channel_id=1, source_target_pairs={{0,4},{1,5},{2,6},{3,7},{4,8},{5,9},{6,10},{7,11},{8,12},{9,13},{1... | collective-permute-start | bytes 221192 | tf_op jit(solution)/shard_map/ppermute | solution.py:630
  16.6 3.7 %collective-permute-start.3 = (f32[2,16,384]{2,1,0:T(8,128)S(1)}, f32[2,16,384]{2,1,0:T(8,128)S(1)}, u32[]{:S(2)}, u32[]{:S(2)}) collective-permute-start(f32[2,16,384]{2,1,0:T(8,128)S(1)} %get-tuple-element.62), channel_id=1, source_target_pairs={{0,1},{1,2},{2,3},{4,5},{5,6},{6,7},{8,9},{9,10},{10,11},{12,13},{... | collective-permute-start | bytes 147464 | tf_op jit(solution)/shard_map/ppermute | solution.py:631
  20.8 3.2 %collective-permute-start.5 = (f32[2,3,2,8,128]{4,3,2,1,0:T(8,128)S(1)}, f32[2,3,2,8,128]{4,3,2,1,0:T(8,128)S(1)}, u32[]{:S(2)}, u32[]{:S(2)}) collective-permute-start(f32[2,3,2,8,128]{4,3,2,1,0:T(8,128)S(1)} %get-tuple-element.68), channel_id=1, source_target_pairs={{0,16},{1,17},{2,18},{3,19},{4,20},{5,21},{6,22},{7,23},{8,24},{9,... | collective-permute-start | bytes 147464 | tf_op jit(solution)/shard_map/ppermute | solution.py:20
  24.1 6.4 %collective-permute-start.6 = (f32[2,24,384]{2,1,0:T(8,128)S(1)}, f32[2,24,384]{2,1,0:T(8,128)S(1)}, u32[]{:S(2)}, u32[]{:S(2)}) collective-permute-start(f32[2,24,384]{2,1,0:T(8,128)S(1)} %get-tuple-element.71), channel_id=1, source_target_pairs={{4,0},{5,1},{6,2},{7,3},{8,4},{9,5},{10,6},{11,7},{12,8},{13,9},{1... | collective-permute-start | bytes 221192 | tf_op jit(solution)/shard_map/ppermute | solution.py:630
  25.4 3.1 %collective-permute-start.7 = (f32[2,6,384]{2,1,0:T(8,128)S(1)}, f32[2,6,384]{2,1,0:T(8,128)S(1)}, u32[]{:S(2)}, u32[]{:S(2)}) collective-permute-start(f32[2,6,384]{2,1,0:T(8,128)S(1)} %get-tuple-element.72), channel_id=1, source_target_pairs={{1,0},{2,1},{3,2},{5,4},{6,5},{7,6},{9,8},{10,9},{11,10},{13,12},{... | collective-permute-start | bytes 55304 | tf_op jit(solution)/shard_map/ppermute | solution.py:631
  30.8 9.1 %collective-permute-start.8 = (f32[2,24,384]{2,1,0:T(8,128)S(1)}, f32[2,24,384]{2,1,0:T(8,128)S(1)}, u32[]{:S(2)}, u32[]{:S(2)}) collective-permute-start(f32[2,24,384]{2,1,0:T(8,128)S(1)} %get-tuple-element.76), channel_id=1, source_target_pairs={{0,4},{1,5},{2,6},{3,7},{4,8},{5,9},{6,10},{7,11},{8,12},{9,13},{1... | collective-permute-start | bytes 221192 | tf_op jit(solution)/shard_map/ppermute | solution.py:630
  34.3 5.6 %collective-permute-start.9 = (f32[2,16,384]{2,1,0:T(8,128)S(1)}, f32[2,16,384]{2,1,0:T(8,128)S(1)}, u32[]{:S(2)}, u32[]{:S(2)}) collective-permute-start(f32[2,16,384]{2,1,0:T(8,128)S(1)} %get-tuple-element.77), channel_id=1, source_target_pairs={{0,1},{1,2},{2,3},{4,5},{5,6},{6,7},{8,9},{9,10},{10,11},{12,13},{... | collective-permute-start | bytes 147464 | tf_op jit(solution)/shard_map/ppermute | solution.py:631
  38.5 7.4 %collective-permute-start.10 = (f32[2,24,384]{2,1,0:T(8,128)S(1)}, f32[2,24,384]{2,1,0:T(8,128)S(1)}, u32[]{:S(2)}, u32[]{:S(2)}) collective-permute-start(f32[2,24,384]{2,1,0:T(8,128)S(1)} %get-tuple-element.76), channel_id=1, source_target_pairs={{16,20},{17,21},{18,22},{19,23},{20,24},{21,25},{22,26},{23,27},{2... | collective-permute-start | bytes 221192 | tf_op jit(solution)/shard_map/ppermute | solution.py:630
  39.2 6.7 %collective-permute-start.11 = (f32[2,16,384]{2,1,0:T(8,128)S(1)}, f32[2,16,384]{2,1,0:T(8,128)S(1)}, u32[]{:S(2)}, u32[]{:S(2)}) collective-permute-start(f32[2,16,384]{2,1,0:T(8,128)S(1)} %get-tuple-element.77), channel_id=1, source_target_pairs={{16,17},{17,18},{18,19},{20,21},{21,22},{22,23},{24,25},{25,26},{2... | collective-permute-start | bytes 147464 | tf_op jit(solution)/shard_map/ppermute | solution.py:631
  40.4 7.0 %collective-permute-start.12 = (f32[3,2,8,128]{3,2,1,0:T(8,128)S(1)}, f32[3,2,8,128]{3,2,1,0:T(8,128)S(1)}, u32[]{:S(2)}, u32[]{:S(2)}) collective-permute-start(f32[3,2,8,128]{3,2,1,0:T(8,128)S(1)} %get-tuple-element.81), channel_id=1, source_target_pairs={{0,16},{1,17},{2,18},{3,19},{4,20},{5,21},{6,22},{7,23},{8,24},{9,... | collective-permute-start | bytes 73736 | tf_op jit(solution)/shard_map/ppermute | solution.py:20
  47.5 6.2 %collective-permute-start.13 = (f32[2,24,384]{2,1,0:T(8,128)S(1)}, f32[2,24,384]{2,1,0:T(8,128)S(1)}, u32[]{:S(2)}, u32[]{:S(2)}) collective-permute-start(f32[2,24,384]{2,1,0:T(8,128)S(1)} %get-tuple-element.84), channel_id=1, source_target_pairs={{4,0},{5,1},{6,2},{7,3},{8,4},{9,5},{10,6},{11,7},{12,8},{13,9},{1... | collective-permute-start | bytes 221192 | tf_op jit(solution)/shard_map/ppermute | solution.py:630
  48.8 3.1 %collective-permute-start.14 = (f32[2,6,384]{2,1,0:T(8,128)S(1)}, f32[2,6,384]{2,1,0:T(8,128)S(1)}, u32[]{:S(2)}, u32[]{:S(2)}) collective-permute-start(f32[2,6,384]{2,1,0:T(8,128)S(1)} %get-tuple-element.85), channel_id=1, source_target_pairs={{1,0},{2,1},{3,2},{5,4},{6,5},{7,6},{9,8},{10,9},{11,10},{13,12},{... | collective-permute-start | bytes 55304 | tf_op jit(solution)/shard_map/ppermute | solution.py:631
  54.0 16.5 %collective-permute-start.20 = (f32[224,384]{1,0:T(8,128)S(1)}, f32[224,384]{1,0:T(8,128)S(1)}, u32[]{:S(2)}, u32[]{:S(2)}) collective-permute-start(f32[224,384]{1,0:T(8,128)S(1)} %get-tuple-element.97), channel_id=1, source_target_pairs={{16,0},{17,1},{18,2},{19,3},{20,4},{21,5},{22,6},{23,7},{24,8},{25... | collective-permute-start | bytes 1032200 | tf_op jit(solution)/shard_map/ppermute | solution.py:20
  55.3 7.4 %collective-permute-start.15 = (f32[2,24,384]{2,1,0:T(8,128)S(1)}, f32[2,24,384]{2,1,0:T(8,128)S(1)}, u32[]{:S(2)}, u32[]{:S(2)}) collective-permute-start(f32[2,24,384]{2,1,0:T(8,128)S(1)} %get-tuple-element.90), channel_id=1, source_target_pairs={{0,4},{1,5},{2,6},{3,7},{4,8},{5,9},{6,10},{7,11},{8,12},{9,13},{1... | collective-permute-start | bytes 221192 | tf_op jit(solution)/shard_map/ppermute | solution.py:630
  58.8 3.9 %collective-permute-start.16 = (f32[2,16,384]{2,1,0:T(8,128)S(1)}, f32[2,16,384]{2,1,0:T(8,128)S(1)}, u32[]{:S(2)}, u32[]{:S(2)}) collective-permute-start(f32[2,16,384]{2,1,0:T(8,128)S(1)} %get-tuple-element.91), channel_id=1, source_target_pairs={{0,1},{1,2},{2,3},{4,5},{5,6},{6,7},{8,9},{9,10},{10,11},{12,13},{... | collective-permute-start | bytes 147464 | tf_op jit(solution)/shard_map/ppermute | solution.py:631
  61.3 7.7 %collective-permute-start.17 = (f32[2,24,384]{2,1,0:T(8,128)S(1)}, f32[2,24,384]{2,1,0:T(8,128)S(1)}, u32[]{:S(2)}, u32[]{:S(2)}) collective-permute-start(f32[2,24,384]{2,1,0:T(8,128)S(1)} %get-tuple-element.90), channel_id=1, source_target_pairs={{16,20},{17,21},{18,22},{19,23},{20,24},{21,25},{22,26},{23,27},{2... | collective-permute-start | bytes 221192 | tf_op jit(solution)/shard_map/ppermute | solution.py:630
  62.0 7.0 %collective-permute-start.18 = (f32[2,16,384]{2,1,0:T(8,128)S(1)}, f32[2,16,384]{2,1,0:T(8,128)S(1)}, u32[]{:S(2)}, u32[]{:S(2)}) collective-permute-start(f32[2,16,384]{2,1,0:T(8,128)S(1)} %get-tuple-element.91), channel_id=1, source_target_pairs={{16,17},{17,18},{18,19},{20,21},{21,22},{22,23},{24,25},{25,26},{2... | collective-permute-start | bytes 147464 | tf_op jit(solution)/shard_map/ppermute | solution.py:631
  63.2 7.3 %collective-permute-start.19 = (f32[3,2,8,128]{3,2,1,0:T(8,128)S(1)}, f32[3,2,8,128]{3,2,1,0:T(8,128)S(1)}, u32[]{:S(2)}, u32[]{:S(2)}) collective-permute-start(f32[3,2,8,128]{3,2,1,0:T(8,128)S(1)} %get-tuple-element.95), channel_id=1, source_target_pairs={{0,16},{1,17},{2,18},{3,19},{4,20},{5,21},{6,22},{7,23},{8,24},{9,... | collective-permute-start | bytes 73736 | tf_op jit(solution)/shard_map/ppermute | solution.py:20
  71.3 7.4 %collective-permute-start.21 = (f32[80,384]{1,0:T(8,128)S(1)}, f32[80,384]{1,0:T(8,128)S(1)}, u32[]{:S(2)}, u32[]{:S(2)}) collective-permute-start(f32[80,384]{1,0:T(8,128)S(1)} %get-tuple-element.101), channel_id=1, source_target_pairs={{16,0},{17,1},{18,2},{19,3},{20,4},{21,5},{22,6},{23,7},{24,8},{25... | collective-permute-start | bytes 368648 | tf_op jit(solution)/shard_map/ppermute | solution.py:20

commit v7 on v6

--- a/solution.py
+++ b/solution.py
@@ -406,6 +406,12 @@
             ref[c, i] = values[c][i]
 
 
+def store_tiles(ref, values):
+    for c in range(3):
+        for i in range(2):
+            ref[2 * c + i] = values[c][i]
+
+
 def load_box(ref):
     return [[ref[c, i] for i in range(2)] for c in range(3)]
 
@@ -427,9 +433,10 @@
             ay[1, x : x + 1] = near_y[0, 2, x, 0:1]
 
 
-def h1_kernel(e, h, ax, ay, out_h, bx, by):
+def h1_kernel(e, h, ax, ay, material, out_h, bx, by, sent):
     @pl.when(is_coarse())
     def _():
+        sent[...] = material[...]
         magnetic(e, h, edge_x(ax), edge_y(ay), out_h)
         last_layers(out_h, bx, by)
 
@@ -488,7 +495,7 @@
     @pl.when(is_coarse())
     def _():
         electric(e, h, p, coef, edge_x(bx), edge_y(by), out_e, out_p)
-        store_box(sent, cut_region(out_e, desc, corner(desc)))
+        store_tiles(sent, cut_region(out_e, desc, corner(desc)))
 
 
 def f2_kernel(
@@ -506,7 +513,7 @@
         spot = corner(desc)
         electric(e, h, p, slab_coef, edge_x(bx), edge_y(by), out_e, out_p)
         fix = cut_region(out_e, desc, spot)
-        latest = [[region[c, i] + fix[c][i] for i in range(2)] for c in range(3)]
+        latest = [[region[2 * c + i] + fix[c][i] for i in range(2)] for c in range(3)]
         restricted = fine_steps(box, coef, desc, load_box(was), latest)
         after, delta = feed_back(restricted, latest, desc)
         store_box(now, after)
@@ -556,7 +563,7 @@
             for c in range(3):
                 layer[c, i] = a * e[c, x] + b * rotation[c] + q * p[c, x]
         fix = cut_region(layer, desc, (0, *spot[1:]))
-        latest = [[region[c, i] + fix[c][i] for i in range(2)] for c in range(3)]
+        latest = [[region[2 * c + i] + fix[c][i] for i in range(2)] for c in range(3)]
         restricted = fine_steps(box, coef, desc, load_box(was), latest)
         pack(relay, restricted, bx, by, 0)
 
@@ -664,8 +671,12 @@
         + [SM] * 5,
         grid=(1,),
     )
-    slab_material = to_fine(material)
-    h, bx, by = call(h1_kernel, (e, h, ax, ay), [PART] + LAST)
+    h, bx, by, slab_material = call(
+        h1_kernel,
+        (e, h, ax, ay, material),
+        [PART] + LAST + [jax.ShapeDtypeStruct(material.shape, jnp.int32)],
+    )
+    slab_material = to_fine(slab_material)
     bx, by = exchange(bx, by, 1, (0,))
     e, p, sent, slab_coef = call(
         e1_kernel,
@@ -683,7 +694,7 @@
     bx2, by2 = exchange(bx, by, 1, (1,))
     bx, by = exchange(bx, by, 1, (0,))
     base_e, base_p, sent = call(
-        base_kernel, (e, h, p, slab_coef, bx, by, desc), [PART] * 2 + [REGION]
+        base_kernel, (e, h, p, slab_coef, bx, by, desc), [PART] * 2 + [(19, 8, 128)]
     )
     region = to_fine(sent)
     e, p, ax, ay, box, now, change2 = call(
@@ -701,7 +712,7 @@
     fine_bx, fine_by = exchange(bx, by, 1, (1,))
     bx, by = exchange(bx, by, 1, (0,))
     base_e, base_p, sent = call(
-        base_kernel, (e, h, p, slab_coef, bx, by, desc), [PART] * 2 + [REGION]
+        base_kernel, (e, h, p, slab_coef, bx, by, desc), [PART] * 2 + [(19, 8, 128)]
     )
     region = to_fine(sent)
     box, relay4, *fix = call(

time: 81.2 us -> 76.1 us (0.937)
  starting transfers between devices: 50.6 us -> 40.9 us
  waiting for transfers between devices: 21.8 us -> 26.2 us
    ppermute x6, starting transfers between devices: 20 us -> 10.4 us  [shifted(): return lax.ppermute(value, axis, pairs)]
    ppermute x8, waiting for transfers between devices: 5.04 us -> 6.76 us  [exchange(): lax.ppermute(y_edge, AXES, pairs(0, by))]
    ppermute x6, waiting for transfers between devices: 10.9 us -> 12.5 us  [shifted(): return lax.ppermute(value, axis, pairs)]
    ppermute x8, waiting for transfers between devices: 5.78 us -> 6.96 us  [exchange(): lax.ppermute(x_edge, AXES, pairs(by, 0))]
  transfers between devices with their start and end apart: 22 -> 22, of which waited for: 11 -> 14; matrix products, arithmetic and copies ran while one was open for 0% -> 0% of each run, Pallas kernels for 3% -> 2%
where the time goes in v7:
time: 76.1 us; the launch traced here: 75.4 us
  starting transfers between devices  40.9 us (54%)
  waiting for transfers between devices  26.2 us (34%)
  Pallas kernels  6.47 us (9%)
  local copies, waits for them, and re-layouts  1.58 us (2%)
    ppermute x8, starting transfers between devices, exchange(): lax.ppermute(x_edge, AXES, pairs(by, 0))  16.2 us
    ppermute x8, starting transfers between devices, exchange(): lax.ppermute(y_edge, AXES, pairs(0, by))  14.3 us
    ppermute x6, waiting for transfers between devices, shifted(): return lax.ppermute(value, axis, pairs)  12.5 us
    ppermute x6, starting transfers between devices, shifted(): return lax.ppermute(value, axis, pairs)  10.4 us
    ppermute x8, waiting for transfers between devices, exchange(): lax.ppermute(x_edge, AXES, pairs(by, 0))  6.96 us
    ppermute x8, waiting for transfers between devices, exchange(): lax.ppermute(y_edge, AXES, pairs(0, by))  6.76 us
    pallas_call x12, Pallas kernels, call(): pl.pallas_call(kernel, out_shape=shapes, in_specs=specs or [VM] * len(ope...  6.47 us
    unnamed x14, local copies, waits for them, and re-layouts  1.58 us
  transfers between devices with their start and end apart: 22, of which 14 were waited for; matrix products, arithmetic and copies ran while one was open for 0% of the time, Pallas kernels for 2%

profile of v7, /device:TPU:0, one launch (start us, length us, event | category | flops | bytes accessed | tf_op | source)
XLA Modules:
  0.0 75.4 jit_solution(8714842190010584973)
XLA Ops:
  0.0 1.6 %copy-done = f32[1,9,6,24,384]{4,3,2,1,0:T(8,128)S(1)} copy-done((f32[1,9,6,24,384]{4,3,2,1,0:T(8,128)S(1)}, f32[1,9,6,24,384]{4,3,2,1,0:T(8,128)}, u32[]{:S(2)}) %copy-start) | copy-done | bytes 1990680
  1.6 1.4 %collective-permute-start = (f32[2,24,384]{2,1,0:T(8,128)S(1)}, f32[2,24,384]{2,1,0:T(8,128)S(1)}, u32[]{:S(2)}, u32[]{:S(2)}) collective-permute-start(f32[2,24,384]{2,1,0:T(8,128)S(1)} %get-tuple-element.57), channel_id=1, source_target_pairs={{4,0},{5,1},{6,2},{7,3},{8,4},{9,5},{10,6},{11,7},{12,8},{13,9},{1... | collective-permute-start | bytes 221192 | tf_op jit(solution)/shard_map/ppermute | solution.py:637
  3.1 1.3 %collective-permute-start.1 = (f32[2,6,384]{2,1,0:T(8,128)S(1)}, f32[2,6,384]{2,1,0:T(8,128)S(1)}, u32[]{:S(2)}, u32[]{:S(2)}) collective-permute-start(f32[2,6,384]{2,1,0:T(8,128)S(1)} %get-tuple-element.58), channel_id=1, source_target_pairs={{1,0},{2,1},{3,2},{5,4},{6,5},{7,6},{9,8},{10,9},{11,10},{13,12},{... | collective-permute-start | bytes 55304 | tf_op jit(solution)/shard_map/ppermute | solution.py:638
  4.4 1.1 %shard_map.73 = (f32[3,6,24,384]{3,2,1,0:T(8,128)S(1)}, f32[3,6,24,384]{3,2,1,0:T(8,128)S(1)}, f32[3,6,24,384]{3,2,1,0:T(8,128)S(1)}, f32[9,6,9,8,128]{4,3,2,1,0...) custom-call(f32[1,9,6,24,384]{4,3,2,1,0:T(8,128)S(1)} %copy-done, ...), custom_call_target="tpu_custom_call" | custom-call | tf_op jit(solution)/shard_map/pallas_call | solution.py:601
  5.6 0.6 collective-permute-done.1.ay
  6.1 2.9 %collective-permute-done.ax = f32[2,24,384]{2,1,0:T(8,128)S(1)} collective-permute-done((f32[2,24,384]{2,1,0:T(8,128)S(1)}, f32[2,24,384]{2,1,0:T(8,128)S(1)}, u32[]{:S(2)}, u32[]{:S(2)}) %collective-permute-start) | collective-permute-done | bytes 73760 | tf_op jit(solution)/shard_map/ppermute | solution.py:637
  9.0 0.2 shard_map.75
  9.3 2.5 %collective-permute-start.4 = (s32[1,6,24,384]{3,2,1,0:T(8,128)S(1)}, s32[1,6,24,384]{3,2,1,0:T(8,128)S(1)}, u32[]{:S(2)}, u32[]{:S(2)}) collective-permute-start(s32[1,6,24,384]{3,2,1,0:T(8,128)S(1)} %get-tuple-element.65), channel_id=1, source_target_pairs={{0,16},{1,17},{2,18},{3,19},{4,20},{5,21},{6,22},{7,23},{8,24},{9,... | collective-permute-start | bytes 663560 | tf_op jit(solution)/shard_map/ppermute | solution.py:20
  11.8 3.5 %collective-permute-start.2 = (f32[2,24,384]{2,1,0:T(8,128)S(1)}, f32[2,24,384]{2,1,0:T(8,128)S(1)}, u32[]{:S(2)}, u32[]{:S(2)}) collective-permute-start(f32[2,24,384]{2,1,0:T(8,128)S(1)} %get-tuple-element.62), channel_id=1, source_target_pairs={{0,4},{1,5},{2,6},{3,7},{4,8},{5,9},{6,10},{7,11},{8,12},{9,13},{1... | collective-permute-start | bytes 221192 | tf_op jit(solution)/shard_map/ppermute | solution.py:637
  15.3 2.0 %collective-permute-start.3 = (f32[2,16,384]{2,1,0:T(8,128)S(1)}, f32[2,16,384]{2,1,0:T(8,128)S(1)}, u32[]{:S(2)}, u32[]{:S(2)}) collective-permute-start(f32[2,16,384]{2,1,0:T(8,128)S(1)} %get-tuple-element.63), channel_id=1, source_target_pairs={{0,1},{1,2},{2,3},{4,5},{5,6},{6,7},{8,9},{9,10},{10,11},{12,13},{... | collective-permute-start | bytes 147464 | tf_op jit(solution)/shard_map/ppermute | solution.py:638
  17.3 0.9 %collective-permute-done.3.by = f32[2,16,384]{2,1,0:T(8,128)S(1)} collective-permute-done((f32[2,16,384]{2,1,0:T(8,128)S(1)}, f32[2,16,384]{2,1,0:T(8,128)S(1)}, u32[]{:S(2)}, u32[]{:S(2)}) %collective-permute-start.3) | collective-permute-done | bytes 49184 | tf_op jit(solution)/shard_map/ppermute | solution.py:638
  18.2 0.6 shard_map.76
  18.7 2.6 %collective-permute-start.5 = (f32[2,3,2,8,128]{4,3,2,1,0:T(8,128)S(1)}, f32[2,3,2,8,128]{4,3,2,1,0:T(8,128)S(1)}, u32[]{:S(2)}, u32[]{:S(2)}) collective-permute-start(f32[2,3,2,8,128]{4,3,2,1,0:T(8,128)S(1)} %get-tuple-element.70), channel_id=1, source_target_pairs={{0,16},{1,17},{2,18},{3,19},{4,20},{5,21},{6,22},{7,23},{8,24},{9,... | collective-permute-start | bytes 147464 | tf_op jit(solution)/shard_map/ppermute | solution.py:20
  21.4 1.9 %collective-permute-done.5.region = f32[2,3,2,8,128]{4,3,2,1,0:T(8,128)S(1)} collective-permute-done((f32[2,3,2,8,128]{4,3,2,1,0:T(8,128)S(1)}, f32[2,3,2,8,128]{4,3,2,1,0:T(8,128)S(1)}, u32[]{:S(2)}, u32[]{:S(2)}) %collective-permute-start.5) | collective-permute-done | bytes 49184 | tf_op jit(solution)/shard_map/ppermute | solution.py:20
  23.3 0.1 shard_map.77
  23.5 1.3 %collective-permute-start.6 = (f32[2,24,384]{2,1,0:T(8,128)S(1)}, f32[2,24,384]{2,1,0:T(8,128)S(1)}, u32[]{:S(2)}, u32[]{:S(2)}) collective-permute-start(f32[2,24,384]{2,1,0:T(8,128)S(1)} %get-tuple-element.73), channel_id=1, source_target_pairs={{4,0},{5,1},{6,2},{7,3},{8,4},{9,5},{10,6},{11,7},{12,8},{13,9},{1... | collective-permute-start | bytes 221192 | tf_op jit(solution)/shard_map/ppermute | solution.py:637
  24.8 1.3 %collective-permute-start.7 = (f32[2,6,384]{2,1,0:T(8,128)S(1)}, f32[2,6,384]{2,1,0:T(8,128)S(1)}, u32[]{:S(2)}, u32[]{:S(2)}) collective-permute-start(f32[2,6,384]{2,1,0:T(8,128)S(1)} %get-tuple-element.74), channel_id=1, source_target_pairs={{1,0},{2,1},{3,2},{5,4},{6,5},{7,6},{9,8},{10,9},{11,10},{13,12},{... | collective-permute-start | bytes 55304 | tf_op jit(solution)/shard_map/ppermute | solution.py:638
  26.1 1.8 %collective-permute-done.7.ay.ay2 = f32[2,6,384]{2,1,0:T(8,128)S(1)} collective-permute-done((f32[2,6,384]{2,1,0:T(8,128)S(1)}, f32[2,6,384]{2,1,0:T(8,128)S(1)}, u32[]{:S(2)}, u32[]{:S(2)}) %collective-permute-start.7) | collective-permute-done | bytes 18464 | tf_op jit(solution)/shard_map/ppermute | solution.py:638
  27.8 2.0 %collective-permute-done.6.ax.ax2 = f32[2,24,384]{2,1,0:T(8,128)S(1)} collective-permute-done((f32[2,24,384]{2,1,0:T(8,128)S(1)}, f32[2,24,384]{2,1,0:T(8,128)S(1)}, u32[]{:S(2)}, u32[]{:S(2)}) %collective-permute-start.6) | collective-permute-done | bytes 73760 | tf_op jit(solution)/shard_map/ppermute | solution.py:637
  29.9 0.2 shard_map.78
  30.1 3.9 %collective-permute-start.8 = (f32[2,24,384]{2,1,0:T(8,128)S(1)}, f32[2,24,384]{2,1,0:T(8,128)S(1)}, u32[]{:S(2)}, u32[]{:S(2)}) collective-permute-start(f32[2,24,384]{2,1,0:T(8,128)S(1)} %get-tuple-element.78), channel_id=1, source_target_pairs={{0,4},{1,5},{2,6},{3,7},{4,8},{5,9},{6,10},{7,11},{8,12},{9,13},{1... | collective-permute-start | bytes 221192 | tf_op jit(solution)/shard_map/ppermute | solution.py:637
  34.0 3.2 %collective-permute-start.9 = (f32[2,16,384]{2,1,0:T(8,128)S(1)}, f32[2,16,384]{2,1,0:T(8,128)S(1)}, u32[]{:S(2)}, u32[]{:S(2)}) collective-permute-start(f32[2,16,384]{2,1,0:T(8,128)S(1)} %get-tuple-element.79), channel_id=1, source_target_pairs={{0,1},{1,2},{2,3},{4,5},{5,6},{6,7},{8,9},{9,10},{10,11},{12,13},{... | collective-permute-start | bytes 147464 | tf_op jit(solution)/shard_map/ppermute | solution.py:638
  37.2 0.9 %collective-permute-done.9.by = f32[2,16,384]{2,1,0:T(8,128)S(1)} collective-permute-done((f32[2,16,384]{2,1,0:T(8,128)S(1)}, f32[2,16,384]{2,1,0:T(8,128)S(1)}, u32[]{:S(2)}, u32[]{:S(2)}) %collective-permute-start.9) | collective-permute-done | bytes 49184 | tf_op jit(solution)/shard_map/ppermute | solution.py:638
  38.1 0.5 shard_map.79
  38.7 1.3 %collective-permute-start.12 = (f32[19,8,128]{2,1,0:T(8,128)S(1)}, f32[19,8,128]{2,1,0:T(8,128)S(1)}, u32[]{:S(2)}, u32[]{:S(2)}) collective-permute-start(f32[19,8,128]{2,1,0:T(8,128)S(1)} %get-tuple-element.83), channel_id=1, source_target_pairs={{0,16},{1,17},{2,18},{3,19},{4,20},{5,21},{6,22},{7,23},{8,24},{9,... | collective-permute-start | bytes 233480 | tf_op jit(solution)/shard_map/ppermute | solution.py:20
  40.0 0.7 collective-permute-start.10
  40.6 0.7 collective-permute-start.11
  41.3 1.1 %collective-permute-done.12.region = f32[19,8,128]{2,1,0:T(8,128)S(1)} collective-permute-done((f32[19,8,128]{2,1,0:T(8,128)S(1)}, f32[19,8,128]{2,1,0:T(8,128)S(1)}, u32[]{:S(2)}, u32[]{:S(2)}) %collective-permute-start.12) | collective-permute-done | bytes 77856 | tf_op jit(solution)/shard_map/ppermute | solution.py:20
  42.4 0.1 shard_map.80
  42.5 1.3 %collective-permute-start.13 = (f32[2,24,384]{2,1,0:T(8,128)S(1)}, f32[2,24,384]{2,1,0:T(8,128)S(1)}, u32[]{:S(2)}, u32[]{:S(2)}) collective-permute-start(f32[2,24,384]{2,1,0:T(8,128)S(1)} %get-tuple-element.86), channel_id=1, source_target_pairs={{4,0},{5,1},{6,2},{7,3},{8,4},{9,5},{10,6},{11,7},{12,8},{13,9},{1... | collective-permute-start | bytes 221192 | tf_op jit(solution)/shard_map/ppermute | solution.py:637
  43.8 1.3 %collective-permute-start.14 = (f32[2,6,384]{2,1,0:T(8,128)S(1)}, f32[2,6,384]{2,1,0:T(8,128)S(1)}, u32[]{:S(2)}, u32[]{:S(2)}) collective-permute-start(f32[2,6,384]{2,1,0:T(8,128)S(1)} %get-tuple-element.87), channel_id=1, source_target_pairs={{1,0},{2,1},{3,2},{5,4},{6,5},{7,6},{9,8},{10,9},{11,10},{13,12},{... | collective-permute-start | bytes 55304 | tf_op jit(solution)/shard_map/ppermute | solution.py:638
  45.1 1.8 %collective-permute-done.14.ay = f32[2,6,384]{2,1,0:T(8,128)S(1)} collective-permute-done((f32[2,6,384]{2,1,0:T(8,128)S(1)}, f32[2,6,384]{2,1,0:T(8,128)S(1)}, u32[]{:S(2)}, u32[]{:S(2)}) %collective-permute-start.14) | collective-permute-done | bytes 18464 | tf_op jit(solution)/shard_map/ppermute | solution.py:638
  46.9 2.1 %collective-permute-done.13.ax = f32[2,24,384]{2,1,0:T(8,128)S(1)} collective-permute-done((f32[2,24,384]{2,1,0:T(8,128)S(1)}, f32[2,24,384]{2,1,0:T(8,128)S(1)}, u32[]{:S(2)}, u32[]{:S(2)}) %collective-permute-start.13) | collective-permute-done | bytes 73760 | tf_op jit(solution)/shard_map/ppermute | solution.py:637
  49.0 0.2 shard_map.81
  49.2 1.3 %collective-permute-start.20 = (f32[224,384]{1,0:T(8,128)S(1)}, f32[224,384]{1,0:T(8,128)S(1)}, u32[]{:S(2)}, u32[]{:S(2)}) collective-permute-start(f32[224,384]{1,0:T(8,128)S(1)} %get-tuple-element.99), channel_id=1, source_target_pairs={{16,0},{17,1},{18,2},{19,3},{20,4},{21,5},{22,6},{23,7},{24,8},{25... | collective-permute-start | bytes 1032200 | tf_op jit(solution)/shard_map/ppermute | solution.py:20
  50.5 3.5 %collective-permute-start.15 = (f32[2,24,384]{2,1,0:T(8,128)S(1)}, f32[2,24,384]{2,1,0:T(8,128)S(1)}, u32[]{:S(2)}, u32[]{:S(2)}) collective-permute-start(f32[2,24,384]{2,1,0:T(8,128)S(1)} %get-tuple-element.92), channel_id=1, source_target_pairs={{0,4},{1,5},{2,6},{3,7},{4,8},{5,9},{6,10},{7,11},{8,12},{9,13},{1... | collective-permute-start | bytes 221192 | tf_op jit(solution)/shard_map/ppermute | solution.py:637
  54.0 3.9 %collective-permute-start.16 = (f32[2,16,384]{2,1,0:T(8,128)S(1)}, f32[2,16,384]{2,1,0:T(8,128)S(1)}, u32[]{:S(2)}, u32[]{:S(2)}) collective-permute-start(f32[2,16,384]{2,1,0:T(8,128)S(1)} %get-tuple-element.93), channel_id=1, source_target_pairs={{0,1},{1,2},{2,3},{4,5},{5,6},{6,7},{8,9},{9,10},{10,11},{12,13},{... | collective-permute-start | bytes 147464 | tf_op jit(solution)/shard_map/ppermute | solution.py:638
  57.9 0.9 %collective-permute-done.16.by = f32[2,16,384]{2,1,0:T(8,128)S(1)} collective-permute-done((f32[2,16,384]{2,1,0:T(8,128)S(1)}, f32[2,16,384]{2,1,0:T(8,128)S(1)}, u32[]{:S(2)}, u32[]{:S(2)}) %collective-permute-start.16) | collective-permute-done | bytes 49184 | tf_op jit(solution)/shard_map/ppermute | solution.py:638
  58.7 0.5 shard_map.82
  59.3 1.3 %collective-permute-start.19 = (f32[19,8,128]{2,1,0:T(8,128)S(1)}, f32[19,8,128]{2,1,0:T(8,128)S(1)}, u32[]{:S(2)}, u32[]{:S(2)}) collective-permute-start(f32[19,8,128]{2,1,0:T(8,128)S(1)} %get-tuple-element.97), channel_id=1, source_target_pairs={{0,16},{1,17},{2,18},{3,19},{4,20},{5,21},{6,22},{7,23},{8,24},{9,... | collective-permute-start | bytes 233480 | tf_op jit(solution)/shard_map/ppermute | solution.py:20
  60.6 0.7 collective-permute-start.17
  61.3 0.7 collective-permute-start.18
  62.0 1.1 %collective-permute-done.19.region = f32[19,8,128]{2,1,0:T(8,128)S(1)} collective-permute-done((f32[19,8,128]{2,1,0:T(8,128)S(1)}, f32[19,8,128]{2,1,0:T(8,128)S(1)}, u32[]{:S(2)}, u32[]{:S(2)}) %collective-permute-start.19) | collective-permute-done | bytes 77856 | tf_op jit(solution)/shard_map/ppermute | solution.py:20
  63.1 1.1 %collective-permute-done.20.relay_in = f32[224,384]{1,0:T(8,128)S(1)} collective-permute-done((f32[224,384]{1,0:T(8,128)S(1)}, f32[224,384]{1,0:T(8,128)S(1)}, u32[]{:S(2)}, u32[]{:S(2)}) %collective-permute-start.20) | collective-permute-done | bytes 344096 | tf_op jit(solution)/shard_map/ppermute | solution.py:20
  64.2 0.9 %shard_map.83 = (f32[9,6,9,8,128]{4,3,2,1,0:T(8,128)S(1)}, f32[80,384]{1,0:T(8,128)S(1)}, f32[3,6,24,384]{3,2,1,0:T(8,128)S(1)}, f32[3,6,24,384]{3,2,1,0:T(8,128)S(1)}, f32[3,6,24,384]{3,2,1,0:T(8,128)S(1)}) custom-call(f32[3,6,24,384]{3,2,1,0:T(8,128)S(1)} %get-tuple-element.85.e, f32[3,6,24,384]{3,2,1,0:T(8,128)S(1)} %get-tuple-element.90.h, ...), custom_call_target="tpu_custom_call" | custom-call | tf_op jit(solution)/shard_map/pallas_call | solution.py:601
  65.0 1.3 %collective-permute-start.21 = (f32[80,384]{1,0:T(8,128)S(1)}, f32[80,384]{1,0:T(8,128)S(1)}, u32[]{:S(2)}, u32[]{:S(2)}) collective-permute-start(f32[80,384]{1,0:T(8,128)S(1)} %get-tuple-element.103), channel_id=1, source_target_pairs={{16,0},{17,1},{18,2},{19,3},{20,4},{21,5},{22,6},{23,7},{24,8},{25... | collective-permute-start | bytes 368648 | tf_op jit(solution)/shard_map/ppermute | solution.py:20
  66.3 7.2 %collective-permute-done.21.relay = f32[80,384]{1,0:T(8,128)S(1)} collective-permute-done((f32[80,384]{1,0:T(8,128)S(1)}, f32[80,384]{1,0:T(8,128)S(1)}, u32[]{:S(2)}, u32[]{:S(2)}) %collective-permute-start.21) | collective-permute-done | bytes 122912 | tf_op jit(solution)/shard_map/ppermute | solution.py:20
  73.6 1.9 %shard_map.84 = f32[9,6,24,384]{3,2,1,0:T(8,128)} custom-call(f32[3,6,24,384]{3,2,1,0:T(8,128)S(1)} %get-tuple-element.94.e, f32[3,6,24,384]{3,2,1,0:T(8,128)S(1)} %get-tuple-element.90.h, f32[3,6,24,384]{3,2,1,0:T(8,128)S(1)} %get-tuple-element.95.p, f32[3,6,24,384]{3,2,1,0:T(8,128)S(1)} %get-tuple-element.100.fix_e, ...), custom_call_target="tpu_custom_call" | custom-call | tf_op jit(solution)/shard_map/pallas_call | solution.py:601
  (22 shorter events, 0.1 us)
Async XLA Ops:
  0.0 1.6 %copy-start = (f32[1,9,6,24,384]{4,3,2,1,0:T(8,128)S(1)}, f32[1,9,6,24,384]{4,3,2,1,0:T(8,128)}, u32[]{:S(2)}) copy-start(f32[1,9,6,24,384]{4,3,2,1,0:T(8,128)} %near_y.1) | copy-start | bytes 5971972
  1.6 2.8 %copy-start.1 = (s32[1,6,24,384]{3,2,1,0:T(8,128)S(1)}, s32[1,6,24,384]{3,2,1,0:T(8,128)}, u32[]{:S(2)}) copy-start(s32[1,6,24,384]{3,2,1,0:T(8,128)} %material.1) | copy-start | bytes 663556
  1.6 2.8 %copy-start.2 = (f32[8]{0:T(128)S(1)}, f32[8]{0:T(128)}, u32[]{:S(2)}) copy-start(f32[8]{0:T(128)} %perm.1) | copy-start | bytes 100
  1.6 2.8 %copy-start.3 = (f32[8]{0:T(128)S(1)}, f32[8]{0:T(128)}, u32[]{:S(2)}) copy-start(f32[8]{0:T(128)} %cond.1) | copy-start | bytes 100
  1.6 2.8 %copy-start.4 = (f32[8]{0:T(128)S(1)}, f32[8]{0:T(128)}, u32[]{:S(2)}) copy-start(f32[8]{0:T(128)} %relax.1) | copy-start | bytes 100
  1.6 2.8 %copy-start.5 = (f32[8]{0:T(128)S(1)}, f32[8]{0:T(128)}, u32[]{:S(2)}) copy-start(f32[8]{0:T(128)} %debye.1) | copy-start | bytes 100
  1.6 2.8 %copy-start.6 = (s32[1,1,6]{2,1,0:T(1,128)S(1)}, s32[1,1,6]{2,1,0:T(1,128)}, u32[]{:S(2)}) copy-start(s32[1,1,6]{2,1,0:T(1,128)} %sub.1) | copy-start | bytes 76
  1.6 7.4 %collective-permute-start = (f32[2,24,384]{2,1,0:T(8,128)S(1)}, f32[2,24,384]{2,1,0:T(8,128)S(1)}, u32[]{:S(2)}, u32[]{:S(2)}) collective-permute-start(f32[2,24,384]{2,1,0:T(8,128)S(1)} %get-tuple-element.57), channel_id=1, source_target_pairs={{4,0},{5,1},{6,2},{7,3},{8,4},{9,5},{10,6},{11,7},{12,8},{13,9},{1... | collective-permute-start | bytes 221192 | tf_op jit(solution)/shard_map/ppermute | solution.py:637
  3.1 3.1 %collective-permute-start.1 = (f32[2,6,384]{2,1,0:T(8,128)S(1)}, f32[2,6,384]{2,1,0:T(8,128)S(1)}, u32[]{:S(2)}, u32[]{:S(2)}) collective-permute-start(f32[2,6,384]{2,1,0:T(8,128)S(1)} %get-tuple-element.58), channel_id=1, source_target_pairs={{1,0},{2,1},{3,2},{5,4},{6,5},{7,6},{9,8},{10,9},{11,10},{13,12},{... | collective-permute-start | bytes 55304 | tf_op jit(solution)/shard_map/ppermute | solution.py:638
  9.3 8.9 %collective-permute-start.4 = (s32[1,6,24,384]{3,2,1,0:T(8,128)S(1)}, s32[1,6,24,384]{3,2,1,0:T(8,128)S(1)}, u32[]{:S(2)}, u32[]{:S(2)}) collective-permute-start(s32[1,6,24,384]{3,2,1,0:T(8,128)S(1)} %get-tuple-element.65), channel_id=1, source_target_pairs={{0,16},{1,17},{2,18},{3,19},{4,20},{5,21},{6,22},{7,23},{8,24},{9,... | collective-permute-start | bytes 663560 | tf_op jit(solution)/shard_map/ppermute | solution.py:20
  11.8 6.4 %collective-permute-start.2 = (f32[2,24,384]{2,1,0:T(8,128)S(1)}, f32[2,24,384]{2,1,0:T(8,128)S(1)}, u32[]{:S(2)}, u32[]{:S(2)}) collective-permute-start(f32[2,24,384]{2,1,0:T(8,128)S(1)} %get-tuple-element.62), channel_id=1, source_target_pairs={{0,4},{1,5},{2,6},{3,7},{4,8},{5,9},{6,10},{7,11},{8,12},{9,13},{1... | collective-permute-start | bytes 221192 | tf_op jit(solution)/shard_map/ppermute | solution.py:637
  15.3 2.8 %collective-permute-start.3 = (f32[2,16,384]{2,1,0:T(8,128)S(1)}, f32[2,16,384]{2,1,0:T(8,128)S(1)}, u32[]{:S(2)}, u32[]{:S(2)}) collective-permute-start(f32[2,16,384]{2,1,0:T(8,128)S(1)} %get-tuple-element.63), channel_id=1, source_target_pairs={{0,1},{1,2},{2,3},{4,5},{5,6},{6,7},{8,9},{9,10},{10,11},{12,13},{... | collective-permute-start | bytes 147464 | tf_op jit(solution)/shard_map/ppermute | solution.py:638
  18.7 4.6 %collective-permute-start.5 = (f32[2,3,2,8,128]{4,3,2,1,0:T(8,128)S(1)}, f32[2,3,2,8,128]{4,3,2,1,0:T(8,128)S(1)}, u32[]{:S(2)}, u32[]{:S(2)}) collective-permute-start(f32[2,3,2,8,128]{4,3,2,1,0:T(8,128)S(1)} %get-tuple-element.70), channel_id=1, source_target_pairs={{0,16},{1,17},{2,18},{3,19},{4,20},{5,21},{6,22},{7,23},{8,24},{9,... | collective-permute-start | bytes 147464 | tf_op jit(solution)/shard_map/ppermute | solution.py:20
  23.5 6.4 %collective-permute-start.6 = (f32[2,24,384]{2,1,0:T(8,128)S(1)}, f32[2,24,384]{2,1,0:T(8,128)S(1)}, u32[]{:S(2)}, u32[]{:S(2)}) collective-permute-start(f32[2,24,384]{2,1,0:T(8,128)S(1)} %get-tuple-element.73), channel_id=1, source_target_pairs={{4,0},{5,1},{6,2},{7,3},{8,4},{9,5},{10,6},{11,7},{12,8},{13,9},{1... | collective-permute-start | bytes 221192 | tf_op jit(solution)/shard_map/ppermute | solution.py:637
  24.8 3.1 %collective-permute-start.7 = (f32[2,6,384]{2,1,0:T(8,128)S(1)}, f32[2,6,384]{2,1,0:T(8,128)S(1)}, u32[]{:S(2)}, u32[]{:S(2)}) collective-permute-start(f32[2,6,384]{2,1,0:T(8,128)S(1)} %get-tuple-element.74), channel_id=1, source_target_pairs={{1,0},{2,1},{3,2},{5,4},{6,5},{7,6},{9,8},{10,9},{11,10},{13,12},{... | collective-permute-start | bytes 55304 | tf_op jit(solution)/shard_map/ppermute | solution.py:638
  30.1 8.0 %collective-permute-start.8 = (f32[2,24,384]{2,1,0:T(8,128)S(1)}, f32[2,24,384]{2,1,0:T(8,128)S(1)}, u32[]{:S(2)}, u32[]{:S(2)}) collective-permute-start(f32[2,24,384]{2,1,0:T(8,128)S(1)} %get-tuple-element.78), channel_id=1, source_target_pairs={{0,4},{1,5},{2,6},{3,7},{4,8},{5,9},{6,10},{7,11},{8,12},{9,13},{1... | collective-permute-start | bytes 221192 | tf_op jit(solution)/shard_map/ppermute | solution.py:637
  34.0 4.1 %collective-permute-start.9 = (f32[2,16,384]{2,1,0:T(8,128)S(1)}, f32[2,16,384]{2,1,0:T(8,128)S(1)}, u32[]{:S(2)}, u32[]{:S(2)}) collective-permute-start(f32[2,16,384]{2,1,0:T(8,128)S(1)} %get-tuple-element.79), channel_id=1, source_target_pairs={{0,1},{1,2},{2,3},{4,5},{5,6},{6,7},{8,9},{9,10},{10,11},{12,13},{... | collective-permute-start | bytes 147464 | tf_op jit(solution)/shard_map/ppermute | solution.py:638
  38.7 3.8 %collective-permute-start.12 = (f32[19,8,128]{2,1,0:T(8,128)S(1)}, f32[19,8,128]{2,1,0:T(8,128)S(1)}, u32[]{:S(2)}, u32[]{:S(2)}) collective-permute-start(f32[19,8,128]{2,1,0:T(8,128)S(1)} %get-tuple-element.83), channel_id=1, source_target_pairs={{0,16},{1,17},{2,18},{3,19},{4,20},{5,21},{6,22},{7,23},{8,24},{9,... | collective-permute-start | bytes 233480 | tf_op jit(solution)/shard_map/ppermute | solution.py:20
  40.0 1.4 %collective-permute-start.10 = (f32[2,24,384]{2,1,0:T(8,128)S(1)}, f32[2,24,384]{2,1,0:T(8,128)S(1)}, u32[]{:S(2)}, u32[]{:S(2)}) collective-permute-start(f32[2,24,384]{2,1,0:T(8,128)S(1)} %get-tuple-element.78), channel_id=1, source_target_pairs={{16,20},{17,21},{18,22},{19,23},{20,24},{21,25},{22,26},{23,27},{2... | collective-permute-start | bytes 221192 | tf_op jit(solution)/shard_map/ppermute | solution.py:637
  40.6 0.7 collective-permute-start.11
  42.5 6.4 %collective-permute-start.13 = (f32[2,24,384]{2,1,0:T(8,128)S(1)}, f32[2,24,384]{2,1,0:T(8,128)S(1)}, u32[]{:S(2)}, u32[]{:S(2)}) collective-permute-start(f32[2,24,384]{2,1,0:T(8,128)S(1)} %get-tuple-element.86), channel_id=1, source_target_pairs={{4,0},{5,1},{6,2},{7,3},{8,4},{9,5},{10,6},{11,7},{12,8},{13,9},{1... | collective-permute-start | bytes 221192 | tf_op jit(solution)/shard_map/ppermute | solution.py:637
  43.8 3.1 %collective-permute-start.14 = (f32[2,6,384]{2,1,0:T(8,128)S(1)}, f32[2,6,384]{2,1,0:T(8,128)S(1)}, u32[]{:S(2)}, u32[]{:S(2)}) collective-permute-start(f32[2,6,384]{2,1,0:T(8,128)S(1)} %get-tuple-element.87), channel_id=1, source_target_pairs={{1,0},{2,1},{3,2},{5,4},{6,5},{7,6},{9,8},{10,9},{11,10},{13,12},{... | collective-permute-start | bytes 55304 | tf_op jit(solution)/shard_map/ppermute | solution.py:638
  49.2 15.0 %collective-permute-start.20 = (f32[224,384]{1,0:T(8,128)S(1)}, f32[224,384]{1,0:T(8,128)S(1)}, u32[]{:S(2)}, u32[]{:S(2)}) collective-permute-start(f32[224,384]{1,0:T(8,128)S(1)} %get-tuple-element.99), channel_id=1, source_target_pairs={{16,0},{17,1},{18,2},{19,3},{20,4},{21,5},{22,6},{23,7},{24,8},{25... | collective-permute-start | bytes 1032200 | tf_op jit(solution)/shard_map/ppermute | solution.py:20
  50.5 8.2 %collective-permute-start.15 = (f32[2,24,384]{2,1,0:T(8,128)S(1)}, f32[2,24,384]{2,1,0:T(8,128)S(1)}, u32[]{:S(2)}, u32[]{:S(2)}) collective-permute-start(f32[2,24,384]{2,1,0:T(8,128)S(1)} %get-tuple-element.92), channel_id=1, source_target_pairs={{0,4},{1,5},{2,6},{3,7},{4,8},{5,9},{6,10},{7,11},{8,12},{9,13},{1... | collective-permute-start | bytes 221192 | tf_op jit(solution)/shard_map/ppermute | solution.py:637
  54.0 4.7 %collective-permute-start.16 = (f32[2,16,384]{2,1,0:T(8,128)S(1)}, f32[2,16,384]{2,1,0:T(8,128)S(1)}, u32[]{:S(2)}, u32[]{:S(2)}) collective-permute-start(f32[2,16,384]{2,1,0:T(8,128)S(1)} %get-tuple-element.93), channel_id=1, source_target_pairs={{0,1},{1,2},{2,3},{4,5},{5,6},{6,7},{8,9},{9,10},{10,11},{12,13},{... | collective-permute-start | bytes 147464 | tf_op jit(solution)/shard_map/ppermute | solution.py:638
  59.3 3.8 %collective-permute-start.19 = (f32[19,8,128]{2,1,0:T(8,128)S(1)}, f32[19,8,128]{2,1,0:T(8,128)S(1)}, u32[]{:S(2)}, u32[]{:S(2)}) collective-permute-start(f32[19,8,128]{2,1,0:T(8,128)S(1)} %get-tuple-element.97), channel_id=1, source_target_pairs={{0,16},{1,17},{2,18},{3,19},{4,20},{5,21},{6,22},{7,23},{8,24},{9,... | collective-permute-start | bytes 233480 | tf_op jit(solution)/shard_map/ppermute | solution.py:20
  60.6 1.4 %collective-permute-start.17 = (f32[2,24,384]{2,1,0:T(8,128)S(1)}, f32[2,24,384]{2,1,0:T(8,128)S(1)}, u32[]{:S(2)}, u32[]{:S(2)}) collective-permute-start(f32[2,24,384]{2,1,0:T(8,128)S(1)} %get-tuple-element.92), channel_id=1, source_target_pairs={{16,20},{17,21},{18,22},{19,23},{20,24},{21,25},{22,26},{23,27},{2... | collective-permute-start | bytes 221192 | tf_op jit(solution)/shard_map/ppermute | solution.py:637
  61.3 0.7 collective-permute-start.18
  65.0 8.5 %collective-permute-start.21 = (f32[80,384]{1,0:T(8,128)S(1)}, f32[80,384]{1,0:T(8,128)S(1)}, u32[]{:S(2)}, u32[]{:S(2)}) collective-permute-start(f32[80,384]{1,0:T(8,128)S(1)} %get-tuple-element.103), channel_id=1, source_target_pairs={{16,0},{17,1},{18,2},{19,3},{20,4},{21,5},{22,6},{23,7},{24,8},{25... | collective-permute-start | bytes 368648 | tf_op jit(solution)/shard_map/ppermute | solution.py:20

commit v8 on v7

--- a/solution.py
+++ b/solution.py
@@ -74,41 +74,45 @@
     return out
 
 
-def prep_kernel(f0, f1, f2, m0, m1, m2, perm, cond, relax, debye, sub, e, h, p, box, coef, desc, wide):
-    coarse = lax.axis_index("grid") == 0
-    fields, material = (f0, f1, f2), (m0, m1, m2)
+def prep_kernel(fields, material, perm, cond, relax, debye, sub, e, h, p, coef, desc, wide):
     for k in range(6):
         desc[k] = jnp.full((8, 128), sub[0, 0, k], jnp.int32)
 
-    @pl.when(coarse)
+    @pl.when(is_coarse())
     def _():
         table = tables(perm, cond, relax, debye, 1.0)
         for x in range(6):
             for yt in range(3):
                 for zt in range(3):
-                    index = material[zt][0, x, pl.ds(8 * yt, 8)]
+                    index = material[0, x, pl.ds(8 * yt, 8), pl.ds(128 * zt, 128)]
                     for k in range(5):
                         coef[k, x, 3 * yt + zt] = gather(table[k], index)
-        for a in range(3):
-            for k, part in enumerate((e, h, p)):
-                part[:, :, :, pl.ds(128 * a, 128)] = fields[a][0, 3 * k : 3 * k + 3]
-
-    @pl.when(jnp.logical_not(coarse))
+        for k, part in enumerate((e, h, p)):
+            part[...] = fields[0, 3 * k : 3 * k + 3]
+
+    @pl.when(is_fine())
     def _():
         for k, tile in enumerate(tables(perm, cond, relax, debye, 1.0)):
             wide[k] = tile
-        table = tables(perm, cond, relax, debye, F32(1.0 / 3.0))
-        row, lane = rows(), lanes()
-        ly, lz = sub[0, 0, 4], sub[0, 0, 5]
-        within = (row < ly) & (lane < lz)
+        for k, tile in enumerate(tables(perm, cond, relax, debye, F32(1.0 / 3.0))):
+            wide[5 + k] = tile
+
+
+def fine_prep_kernel(f0, f1, f2, m0, m1, m2, table, desc, box, coef):
+    fields, material = (f0, f1, f2), (m0, m1, m2)
+
+    @pl.when(is_fine())
+    def _():
+        tiles = [table[5 + k] for k in range(5)]
+        covered = covered_of(desc)
         for x in range(6):
-            inside = within & (x < 3 * sub[0, 0, 3])
+            inside = covered[x // 3]
             for u in range(3):
                 cut = pl.ds(u, 8, stride=3)
                 parts = [material[a][0, x, cut] for a in range(3)]
                 for t, index in enumerate(to_tiles(parts)):
                     for k in range(5):
-                        coef[k, x, 3 * u + t] = gather(table[k], index)
+                        coef[k, x, 3 * u + t] = gather(tiles[k], index)
                 for c in range(9):
                     parts = [fields[a][0, c, x, cut] for a in range(3)]
                     for t, tile in enumerate(to_tiles(parts)):
@@ -284,7 +288,7 @@
     return lambda k, x: ref[pl.ds(at + 48 + 8 * k + x, 1)]
 
 
-def fine_steps(box, coef, desc, earlier, latest):
+def fine_steps(box_in, box, coef, desc, earlier, latest):
     row, lane = rows(), lanes()
     lx, ly, lz = desc[3], desc[4], desc[5]
     inside = covered_of(desc)
@@ -322,18 +326,18 @@
 
     zero = jnp.zeros((8, 128), F32)
 
-    def substep(number, carry):
-        weight = (number.astype(F32) + 1.0) / 3.0
+    def substep(number, old_box):
+        weight = (jnp.asarray(number, F32) + 1.0) / 3.0
         driven = [
             [earlier[c][i] + weight * (latest[c][i] - earlier[c][i]) for i in range(2)]
             for c in range(3)
         ]
         for x in range(6):
             part = x // 3
-            e = [[box[c, x, k] for k in range(9)] for c in range(3)]
+            e = [[old_box[c, x, k] for k in range(9)] for c in range(3)]
             if x < 5:
-                ey_x = [box[1, x + 1, k] for k in range(9)]
-                ez_x = [box[2, x + 1, k] for k in range(9)]
+                ey_x = [old_box[1, x + 1, k] for k in range(9)]
+                ez_x = [old_box[2, x + 1, k] for k in range(9)]
             else:
                 ey_x = ez_x = [zero] * 9
             h = [[], [], []]
@@ -347,7 +351,7 @@
                         (ey_x[k] - ey) - (ahead_y(e[0], u, t) - ex),
                     )
                     for c in range(3):
-                        value = box[3 + c, x, k] - 0.5 * turn[c]
+                        value = old_box[3 + c, x, k] - 0.5 * turn[c]
                         box[3 + c, x, k] = value
                         h[c].append(value)
             x_face = x == 0
@@ -371,7 +375,7 @@
                         None if x_face is True else either(x_face if x in (2, 5) else None, y_face[u]),
                     )
                     for c in range(3):
-                        old = box[6 + c, x, k]
+                        old = old_box[6 + c, x, k]
                         new = a * e[c][k] + b * rotation[c] + p * old
                         if c > 0 and x_face is True:
                             new = driven[c][part]
@@ -380,9 +384,14 @@
                         new = jnp.where(inside[part], new, 0.0)
                         box[c, x, k] = new
                         box[6 + c, x, k] = f3 * old + g * new
+
+    substep(0, box_in)
+
+    def further(number, carry):
+        substep(number, box)
         return carry
 
-    lax.fori_loop(0, 3, substep, 0)
+    lax.fori_loop(1, 3, further, 0)
     restricted = [[zero, zero] for c in range(3)]
     for c in range(3):
         for i in range(2):
@@ -433,39 +442,45 @@
             ay[1, x : x + 1] = near_y[0, 2, x, 0:1]
 
 
-def h1_kernel(e, h, ax, ay, material, out_h, bx, by, sent):
-    @pl.when(is_coarse())
-    def _():
-        sent[...] = material[...]
+def h1_kernel(e, h, ax, ay, material, desc, out_h, bx, by, sent):
+    @pl.when(is_coarse())
+    def _():
+        sent[0:6] = material[0].astype(F32)
+        before = cut_region(e, desc, corner(desc))
+        for c in range(3):
+            for i in range(2):
+                sent[6, pl.ds(8 * i, 8), pl.ds(128 * c, 128)] = before[c][i]
         magnetic(e, h, edge_x(ax), edge_y(ay), out_h)
         last_layers(out_h, bx, by)
 
 
-def e1_kernel(e, h, p, coef, bx, by, desc, material, table, out_e, out_p, sent, slab_coef):
-    @pl.when(is_coarse())
-    def _():
-        spot = corner(desc)
-        before = cut_region(e, desc, spot)
+def e1_kernel(
+    e, h, p, coef, bx, by, desc, material, table, out_e, out_p, sent, slab_coef, first
+):
+    @pl.when(is_coarse())
+    def _():
         electric(e, h, p, coef, edge_x(bx), edge_y(by), out_e, out_p)
-        after = cut_region(out_e, desc, spot)
+        for k, tile in enumerate(sum(cut_region(out_e, desc, corner(desc)), [])):
+            sent[k] = tile
+        slab_coef[...] = coef[...]
+
+    @pl.when(is_fine())
+    def _():
         for c in range(3):
             for i in range(2):
-                sent[0, c, i] = before[c][i]
-                sent[1, c, i] = after[c][i]
-        slab_coef[...] = coef[...]
-
-    @pl.when(is_fine())
-    def _():
+                first[c, i] = material[6, pl.ds(8 * i, 8), pl.ds(128 * c, 128)]
         tiles = [table[k] for k in range(5)]
         for x in range(6):
             for yt in range(3):
                 for zt in range(3):
-                    index = material[0, x, pl.ds(8 * yt, 8), pl.ds(128 * zt, 128)]
+                    index = material[x, pl.ds(8 * yt, 8), pl.ds(128 * zt, 128)].astype(jnp.int32)
                     for k in range(5):
                         slab_coef[k, x, 3 * yt + zt] = gather(tiles[k], index)
 
 
-def f1_kernel(e, h, p, box_in, coef, region, desc, out_e, out_h, out_p, ax, ay, box, now, change):
+def f1_kernel(
+    e, h, p, box_in, coef, first, region, desc, out_e, out_h, out_p, ax, ay, box, now, change
+):
     @pl.when(is_coarse())
     def _():
         out_e[...], out_h[...], out_p[...] = e[...], h[...], p[...]
@@ -473,12 +488,11 @@
 
     @pl.when(is_fine())
     def _():
-        box[...] = box_in[...]
         for out in (out_e, out_h, out_p):
             out[...] = jnp.zeros(out.shape, F32)
-        earlier = [[region[0, c, i] for i in range(2)] for c in range(3)]
-        latest = [[region[1, c, i] for i in range(2)] for c in range(3)]
-        restricted = fine_steps(box, coef, desc, earlier, latest)
+        earlier = load_box(first)
+        latest = [[region[2 * c + i] for i in range(2)] for c in range(3)]
+        restricted = fine_steps(box_in, box, coef, desc, earlier, latest)
         after, delta = feed_back(restricted, latest, desc)
         store_box(now, after)
         store_box(change, delta)
@@ -509,12 +523,11 @@
 
     @pl.when(is_fine())
     def _():
-        box[...] = box_in[...]
         spot = corner(desc)
         electric(e, h, p, slab_coef, edge_x(bx), edge_y(by), out_e, out_p)
         fix = cut_region(out_e, desc, spot)
         latest = [[region[2 * c + i] + fix[c][i] for i in range(2)] for c in range(3)]
-        restricted = fine_steps(box, coef, desc, load_box(was), latest)
+        restricted = fine_steps(box_in, box, coef, desc, load_box(was), latest)
         after, delta = feed_back(restricted, latest, desc)
         store_box(now, after)
         store_box(change, delta)
@@ -546,14 +559,13 @@
         put(one_e, packed_box(relay_in, 0), desc, spot)
         magnetic(one_e, None, packed_x(relay_in, 16), packed_y(relay_in, 16), one_h)
         electric(
-            one_e, one_h, None, coef, packed_x(relay_in, 96), packed_y(relay_in, 96), fix_e, fix_p
+            one_e, one_h, None, slab_coef, packed_x(relay_in, 96), packed_y(relay_in, 96), fix_e, fix_p
         )
         put(fix_e, packed_box(relay_in, 80), desc, spot)
         magnetic(fix_e, one_h, packed_x(relay_in, 160), packed_y(relay_in, 160), fix_h)
 
     @pl.when(is_fine())
     def _():
-        box[...] = box_in[...]
         spot = corner(desc)
         x0 = spot[0]
         for i in range(2):
@@ -564,7 +576,7 @@
                 layer[c, i] = a * e[c, x] + b * rotation[c] + q * p[c, x]
         fix = cut_region(layer, desc, (0, *spot[1:]))
         latest = [[region[2 * c + i] + fix[c][i] for i in range(2)] for c in range(3)]
-        restricted = fine_steps(box, coef, desc, load_box(was), latest)
+        restricted = fine_steps(box_in, box, coef, desc, load_box(was), latest)
         pack(relay, restricted, bx, by, 0)
 
 
@@ -617,7 +629,7 @@
 X_EDGE = (2, 24, 384)
 Y_EDGE = (2, 6, 384)
 EDGES = [X_EDGE, Y_EDGE]
-LAST = [X_EDGE, (2, 16, 384)]
+LAST = EDGES
 AXES = ("grid", "gx", "gy")
 
 
@@ -659,34 +671,37 @@
         grid=(1,),
     )
     ax, ay = exchange(ax, ay, -1, (0,))
-    e, h, p, box, coef, desc, table = call(
+    e, h, p, coef, desc, table = call(
         prep_kernel,
-        (fields,) * 3
-        + (material,) * 3
-        + (permittivity, conductivity, relax_rate, debye_strength, subgrids),
-        [PART] * 3
-        + [BOX, COEF, jax.ShapeDtypeStruct((6, 8, 128), jnp.int32), (5, 8, 128)],
+        (fields, material, permittivity, conductivity, relax_rate, debye_strength, subgrids),
+        [PART] * 3 + [COEF, jax.ShapeDtypeStruct((6, 8, 128), jnp.int32), (10, 8, 128)],
+        [VM] * 2 + [SM] * 5,
+    )
+    box, fine_coef = call(
+        fine_prep_kernel,
+        (fields,) * 3 + (material,) * 3 + (table, desc),
+        [BOX, COEF],
         [third((1, 9, 6, 24, 128), a) for a in range(3)]
         + [third((1, 6, 24, 128), a) for a in range(3)]
-        + [SM] * 5,
+        + [VM] * 2,
         grid=(1,),
     )
     h, bx, by, slab_material = call(
         h1_kernel,
-        (e, h, ax, ay, material),
-        [PART] + LAST + [jax.ShapeDtypeStruct(material.shape, jnp.int32)],
+        (e, h, ax, ay, material, desc),
+        [PART] + LAST + [(7, 24, 384)],
     )
     slab_material = to_fine(slab_material)
     bx, by = exchange(bx, by, 1, (0,))
-    e, p, sent, slab_coef = call(
+    e, p, sent, slab_coef, first = call(
         e1_kernel,
         (e, h, p, coef, bx, by, desc, slab_material, table),
-        [PART] * 2 + [(2, *REGION), COEF],
+        [PART] * 2 + [(6, 8, 128), COEF, REGION],
     )
     region = to_fine(sent)
     e, h, p, ax, ay, box, now, change1 = call(
         f1_kernel,
-        (e, h, p, box, coef, region, desc),
+        (e, h, p, box, fine_coef, first, region, desc),
         [PART] * 3 + EDGES + [BOX, REGION, REGION],
     )
     ax2, ay2 = exchange(ax, ay, -1, (0, 1))
@@ -699,7 +714,7 @@
     region = to_fine(sent)
     e, p, ax, ay, box, now, change2 = call(
         f2_kernel,
-        (e, h, p, base_e, base_p, coef, slab_coef, bx2, by2, desc, box, region, now),
+        (e, h, p, base_e, base_p, fine_coef, slab_coef, bx2, by2, desc, box, region, now),
         [PART] * 2 + EDGES + [BOX, REGION, REGION],
     )
     ax, ay = exchange(ax, ay, -1, (0, 1))
@@ -717,7 +732,7 @@
     region = to_fine(sent)
     box, relay4, *fix = call(
         f3_kernel,
-        (e, h, p, coef, slab_coef, fine_bx, fine_by, desc, box, region, now, relay),
+        (e, h, p, fine_coef, slab_coef, fine_bx, fine_by, desc, box, region, now, relay),
         [BOX, (80, 384)] + [PART] * 3,
         scratch=[
             pltpu.VMEM((3, 2, 24, 384), F32),

time: 76.1 us -> 74.4 us (0.978)
  waiting for transfers between devices: 26.2 us -> 25 us
  starting transfers between devices: 40.9 us -> 40.1 us
    ppermute x6, waiting for transfers between devices: 12.5 us -> 11.6 us  [shifted(): return lax.ppermute(value, axis, pairs)]
    pallas_call x12 -> x13, Pallas kernels: 6.47 us -> 6.73 us  [call(): pl.pallas_call(kernel, out_shape=shapes, in_specs=specs or [VM] * len(ope...]
    unnamed x14 -> x16, local copies, waits for them, and re-layouts: 1.58 us -> 1.58 us
where the time goes in v8:
time: 74.4 us; the launch traced here: 73.9 us
  starting transfers between devices  40.1 us (54%)
  waiting for transfers between devices  25 us (34%)
  Pallas kernels  6.73 us (9%)
  local copies, waits for them, and re-layouts  1.58 us (2%)
    ppermute x8, starting transfers between devices, exchange(): lax.ppermute(x_edge, AXES, pairs(by, 0))  16.6 us
    ppermute x8, starting transfers between devices, exchange(): lax.ppermute(y_edge, AXES, pairs(0, by))  13.8 us
    ppermute x6, waiting for transfers between devices, shifted(): return lax.ppermute(value, axis, pairs)  11.6 us
    ppermute x6, starting transfers between devices, shifted(): return lax.ppermute(value, axis, pairs)  9.82 us
    ppermute x8, waiting for transfers between devices, exchange(): lax.ppermute(x_edge, AXES, pairs(by, 0))  6.76 us
    pallas_call x13, Pallas kernels, call(): pl.pallas_call(kernel, out_shape=shapes, in_specs=specs or [VM] * len(ope...  6.73 us
    ppermute x8, waiting for transfers between devices, exchange(): lax.ppermute(y_edge, AXES, pairs(0, by))  6.67 us
    unnamed x16, local copies, waits for them, and re-layouts  1.58 us
  transfers between devices with their start and end apart: 22, of which 14 were waited for; matrix products, arithmetic and copies ran while one was open for 0% of the time, Pallas kernels for 2%

profile of v8, /device:TPU:0, one launch (start us, length us, event | category | flops | bytes accessed | tf_op | source)
XLA Modules:
  0.0 73.9 jit_solution(2360843200298034967)
XLA Ops:
  0.0 1.6 %copy-done = f32[1,9,6,24,384]{4,3,2,1,0:T(8,128)S(1)} copy-done((f32[1,9,6,24,384]{4,3,2,1,0:T(8,128)S(1)}, f32[1,9,6,24,384]{4,3,2,1,0:T(8,128)}, u32[]{:S(2)}) %copy-start) | copy-done | bytes 1990680
  1.6 1.4 %collective-permute-start = (f32[2,24,384]{2,1,0:T(8,128)S(1)}, f32[2,24,384]{2,1,0:T(8,128)S(1)}, u32[]{:S(2)}, u32[]{:S(2)}) collective-permute-start(f32[2,24,384]{2,1,0:T(8,128)S(1)} %get-tuple-element.59), channel_id=1, source_target_pairs={{4,0},{5,1},{6,2},{7,3},{8,4},{9,5},{10,6},{11,7},{12,8},{13,9},{1... | collective-permute-start | bytes 221192 | tf_op jit(solution)/shard_map/ppermute | solution.py:649
  3.1 1.3 %collective-permute-start.1 = (f32[2,6,384]{2,1,0:T(8,128)S(1)}, f32[2,6,384]{2,1,0:T(8,128)S(1)}, u32[]{:S(2)}, u32[]{:S(2)}) collective-permute-start(f32[2,6,384]{2,1,0:T(8,128)S(1)} %get-tuple-element.60), channel_id=1, source_target_pairs={{1,0},{2,1},{3,2},{5,4},{6,5},{7,6},{9,8},{10,9},{11,10},{13,12},{... | collective-permute-start | bytes 55304 | tf_op jit(solution)/shard_map/ppermute | solution.py:650
  4.4 1.1 %shard_map.73 = (f32[3,6,24,384]{3,2,1,0:T(8,128)S(1)}, f32[3,6,24,384]{3,2,1,0:T(8,128)S(1)}, f32[3,6,24,384]{3,2,1,0:T(8,128)S(1)}, f32[5,6,9,8,128]{4,3,2,1,0...) custom-call(f32[1,9,6,24,384]{4,3,2,1,0:T(8,128)S(1)} %copy-done, s32[1,6,24,384]{3,2,1,0:T(8,128)S(1)} %copy-done.2, ...), custom_call_target="tpu_custom_call" | custom-call | tf_op jit(solution)/shard_map/pallas_call | solution.py:613
  5.6 0.6 collective-permute-done.1.ay
  6.1 2.9 %collective-permute-done.ax = f32[2,24,384]{2,1,0:T(8,128)S(1)} collective-permute-done((f32[2,24,384]{2,1,0:T(8,128)S(1)}, f32[2,24,384]{2,1,0:T(8,128)S(1)}, u32[]{:S(2)}, u32[]{:S(2)}) %collective-permute-start) | collective-permute-done | bytes 73760 | tf_op jit(solution)/shard_map/ppermute | solution.py:649
  9.0 0.3 shard_map.75
  9.4 1.4 %collective-permute-start.4 = (f32[7,24,384]{2,1,0:T(8,128)S(1)}, f32[7,24,384]{2,1,0:T(8,128)S(1)}, u32[]{:S(2)}, u32[]{:S(2)}) collective-permute-start(f32[7,24,384]{2,1,0:T(8,128)S(1)} %get-tuple-element.67), channel_id=1, source_target_pairs={{0,16},{1,17},{2,18},{3,19},{4,20},{5,21},{6,22},{7,23},{8,24},{9,... | collective-permute-start | bytes 774152 | tf_op jit(solution)/shard_map/ppermute | solution.py:20
  10.8 3.9 %collective-permute-start.2 = (f32[2,24,384]{2,1,0:T(8,128)S(1)}, f32[2,24,384]{2,1,0:T(8,128)S(1)}, u32[]{:S(2)}, u32[]{:S(2)}) collective-permute-start(f32[2,24,384]{2,1,0:T(8,128)S(1)} %get-tuple-element.65), channel_id=1, source_target_pairs={{0,4},{1,5},{2,6},{3,7},{4,8},{5,9},{6,10},{7,11},{8,12},{9,13},{1... | collective-permute-start | bytes 221192 | tf_op jit(solution)/shard_map/ppermute | solution.py:649
  14.7 2.8 %collective-permute-start.3 = (f32[2,6,384]{2,1,0:T(8,128)S(1)}, f32[2,6,384]{2,1,0:T(8,128)S(1)}, u32[]{:S(2)}, u32[]{:S(2)}) collective-permute-start(f32[2,6,384]{2,1,0:T(8,128)S(1)} %get-tuple-element.66), channel_id=1, source_target_pairs={{0,1},{1,2},{2,3},{4,5},{5,6},{6,7},{8,9},{9,10},{10,11},{12,13},{... | collective-permute-start | bytes 55304 | tf_op jit(solution)/shard_map/ppermute | solution.py:650
  17.5 0.8 %collective-permute-done.3.by = f32[2,6,384]{2,1,0:T(8,128)S(1)} collective-permute-done((f32[2,6,384]{2,1,0:T(8,128)S(1)}, f32[2,6,384]{2,1,0:T(8,128)S(1)}, u32[]{:S(2)}, u32[]{:S(2)}) %collective-permute-start.3) | collective-permute-done | bytes 18464 | tf_op jit(solution)/shard_map/ppermute | solution.py:650
  18.4 0.5 shard_map.76
  18.9 3.2 %collective-permute-start.5 = (f32[6,8,128]{2,1,0:T(8,128)S(1)}, f32[6,8,128]{2,1,0:T(8,128)S(1)}, u32[]{:S(2)}, u32[]{:S(2)}) collective-permute-start(f32[6,8,128]{2,1,0:T(8,128)S(1)} %get-tuple-element.74), channel_id=1, source_target_pairs={{0,16},{1,17},{2,18},{3,19},{4,20},{5,21},{6,22},{7,23},{8,24},{9,... | collective-permute-start | bytes 73736 | tf_op jit(solution)/shard_map/ppermute | solution.py:20
  22.1 0.1 shard_map.77
  22.3 1.3 %collective-permute-done.5.region = f32[6,8,128]{2,1,0:T(8,128)S(1)} collective-permute-done((f32[6,8,128]{2,1,0:T(8,128)S(1)}, f32[6,8,128]{2,1,0:T(8,128)S(1)}, u32[]{:S(2)}, u32[]{:S(2)}) %collective-permute-start.5) | collective-permute-done | bytes 24608 | tf_op jit(solution)/shard_map/ppermute | solution.py:20
  23.6 0.1 shard_map.78
  23.8 1.3 %collective-permute-start.6 = (f32[2,24,384]{2,1,0:T(8,128)S(1)}, f32[2,24,384]{2,1,0:T(8,128)S(1)}, u32[]{:S(2)}, u32[]{:S(2)}) collective-permute-start(f32[2,24,384]{2,1,0:T(8,128)S(1)} %get-tuple-element.77), channel_id=1, source_target_pairs={{4,0},{5,1},{6,2},{7,3},{8,4},{9,5},{10,6},{11,7},{12,8},{13,9},{1... | collective-permute-start | bytes 221192 | tf_op jit(solution)/shard_map/ppermute | solution.py:649
  25.1 1.3 %collective-permute-start.7 = (f32[2,6,384]{2,1,0:T(8,128)S(1)}, f32[2,6,384]{2,1,0:T(8,128)S(1)}, u32[]{:S(2)}, u32[]{:S(2)}) collective-permute-start(f32[2,6,384]{2,1,0:T(8,128)S(1)} %get-tuple-element.78), channel_id=1, source_target_pairs={{1,0},{2,1},{3,2},{5,4},{6,5},{7,6},{9,8},{10,9},{11,10},{13,12},{... | collective-permute-start | bytes 55304 | tf_op jit(solution)/shard_map/ppermute | solution.py:650
  26.4 1.8 %collective-permute-done.7.ay.ay2 = f32[2,6,384]{2,1,0:T(8,128)S(1)} collective-permute-done((f32[2,6,384]{2,1,0:T(8,128)S(1)}, f32[2,6,384]{2,1,0:T(8,128)S(1)}, u32[]{:S(2)}, u32[]{:S(2)}) %collective-permute-start.7) | collective-permute-done | bytes 18464 | tf_op jit(solution)/shard_map/ppermute | solution.py:650
  28.2 1.9 %collective-permute-done.6.ax.ax2 = f32[2,24,384]{2,1,0:T(8,128)S(1)} collective-permute-done((f32[2,24,384]{2,1,0:T(8,128)S(1)}, f32[2,24,384]{2,1,0:T(8,128)S(1)}, u32[]{:S(2)}, u32[]{:S(2)}) %collective-permute-start.6) | collective-permute-done | bytes 73760 | tf_op jit(solution)/shard_map/ppermute | solution.py:649
  30.0 0.2 shard_map.79
  30.3 3.7 %collective-permute-start.8 = (f32[2,24,384]{2,1,0:T(8,128)S(1)}, f32[2,24,384]{2,1,0:T(8,128)S(1)}, u32[]{:S(2)}, u32[]{:S(2)}) collective-permute-start(f32[2,24,384]{2,1,0:T(8,128)S(1)} %get-tuple-element.82), channel_id=1, source_target_pairs={{0,4},{1,5},{2,6},{3,7},{4,8},{5,9},{6,10},{7,11},{8,12},{9,13},{1... | collective-permute-start | bytes 221192 | tf_op jit(solution)/shard_map/ppermute | solution.py:649
  33.9 2.2 %collective-permute-start.9 = (f32[2,6,384]{2,1,0:T(8,128)S(1)}, f32[2,6,384]{2,1,0:T(8,128)S(1)}, u32[]{:S(2)}, u32[]{:S(2)}) collective-permute-start(f32[2,6,384]{2,1,0:T(8,128)S(1)} %get-tuple-element.83), channel_id=1, source_target_pairs={{0,1},{1,2},{2,3},{4,5},{5,6},{6,7},{8,9},{9,10},{10,11},{12,13},{... | collective-permute-start | bytes 55304 | tf_op jit(solution)/shard_map/ppermute | solution.py:650
  36.2 0.8 %collective-permute-done.9.by = f32[2,6,384]{2,1,0:T(8,128)S(1)} collective-permute-done((f32[2,6,384]{2,1,0:T(8,128)S(1)}, f32[2,6,384]{2,1,0:T(8,128)S(1)}, u32[]{:S(2)}, u32[]{:S(2)}) %collective-permute-start.9) | collective-permute-done | bytes 18464 | tf_op jit(solution)/shard_map/ppermute | solution.py:650
  37.0 0.5 shard_map.80
  37.5 1.3 %collective-permute-start.12 = (f32[19,8,128]{2,1,0:T(8,128)S(1)}, f32[19,8,128]{2,1,0:T(8,128)S(1)}, u32[]{:S(2)}, u32[]{:S(2)}) collective-permute-start(f32[19,8,128]{2,1,0:T(8,128)S(1)} %get-tuple-element.87), channel_id=1, source_target_pairs={{0,16},{1,17},{2,18},{3,19},{4,20},{5,21},{6,22},{7,23},{8,24},{9,... | collective-permute-start | bytes 233480 | tf_op jit(solution)/shard_map/ppermute | solution.py:20
  38.8 0.7 collective-permute-start.10
  39.5 0.7 collective-permute-start.11
  40.2 1.1 %collective-permute-done.12.region = f32[19,8,128]{2,1,0:T(8,128)S(1)} collective-permute-done((f32[19,8,128]{2,1,0:T(8,128)S(1)}, f32[19,8,128]{2,1,0:T(8,128)S(1)}, u32[]{:S(2)}, u32[]{:S(2)}) %collective-permute-start.12) | collective-permute-done | bytes 77856 | tf_op jit(solution)/shard_map/ppermute | solution.py:20
  41.4 1.3 %collective-permute-start.13 = (f32[2,24,384]{2,1,0:T(8,128)S(1)}, f32[2,24,384]{2,1,0:T(8,128)S(1)}, u32[]{:S(2)}, u32[]{:S(2)}) collective-permute-start(f32[2,24,384]{2,1,0:T(8,128)S(1)} %get-tuple-element.90), channel_id=1, source_target_pairs={{4,0},{5,1},{6,2},{7,3},{8,4},{9,5},{10,6},{11,7},{12,8},{13,9},{1... | collective-permute-start | bytes 221192 | tf_op jit(solution)/shard_map/ppermute | solution.py:649
  42.7 1.3 %collective-permute-start.14 = (f32[2,6,384]{2,1,0:T(8,128)S(1)}, f32[2,6,384]{2,1,0:T(8,128)S(1)}, u32[]{:S(2)}, u32[]{:S(2)}) collective-permute-start(f32[2,6,384]{2,1,0:T(8,128)S(1)} %get-tuple-element.91), channel_id=1, source_target_pairs={{1,0},{2,1},{3,2},{5,4},{6,5},{7,6},{9,8},{10,9},{11,10},{13,12},{... | collective-permute-start | bytes 55304 | tf_op jit(solution)/shard_map/ppermute | solution.py:650
  44.0 1.8 %collective-permute-done.14.ay = f32[2,6,384]{2,1,0:T(8,128)S(1)} collective-permute-done((f32[2,6,384]{2,1,0:T(8,128)S(1)}, f32[2,6,384]{2,1,0:T(8,128)S(1)}, u32[]{:S(2)}, u32[]{:S(2)}) %collective-permute-start.14) | collective-permute-done | bytes 18464 | tf_op jit(solution)/shard_map/ppermute | solution.py:650
  45.8 2.0 %collective-permute-done.13.ax = f32[2,24,384]{2,1,0:T(8,128)S(1)} collective-permute-done((f32[2,24,384]{2,1,0:T(8,128)S(1)}, f32[2,24,384]{2,1,0:T(8,128)S(1)}, u32[]{:S(2)}, u32[]{:S(2)}) %collective-permute-start.13) | collective-permute-done | bytes 73760 | tf_op jit(solution)/shard_map/ppermute | solution.py:649
  47.9 0.2 shard_map.82
  48.1 1.3 %collective-permute-start.20 = (f32[224,384]{1,0:T(8,128)S(1)}, f32[224,384]{1,0:T(8,128)S(1)}, u32[]{:S(2)}, u32[]{:S(2)}) collective-permute-start(f32[224,384]{1,0:T(8,128)S(1)} %get-tuple-element.103), channel_id=1, source_target_pairs={{16,0},{17,1},{18,2},{19,3},{20,4},{21,5},{22,6},{23,7},{24,8},{25... | collective-permute-start | bytes 1032200 | tf_op jit(solution)/shard_map/ppermute | solution.py:20
  49.4 3.6 %collective-permute-start.15 = (f32[2,24,384]{2,1,0:T(8,128)S(1)}, f32[2,24,384]{2,1,0:T(8,128)S(1)}, u32[]{:S(2)}, u32[]{:S(2)}) collective-permute-start(f32[2,24,384]{2,1,0:T(8,128)S(1)} %get-tuple-element.96), channel_id=1, source_target_pairs={{0,4},{1,5},{2,6},{3,7},{4,8},{5,9},{6,10},{7,11},{8,12},{9,13},{1... | collective-permute-start | bytes 221192 | tf_op jit(solution)/shard_map/ppermute | solution.py:649
  53.0 3.6 %collective-permute-start.16 = (f32[2,6,384]{2,1,0:T(8,128)S(1)}, f32[2,6,384]{2,1,0:T(8,128)S(1)}, u32[]{:S(2)}, u32[]{:S(2)}) collective-permute-start(f32[2,6,384]{2,1,0:T(8,128)S(1)} %get-tuple-element.97), channel_id=1, source_target_pairs={{0,1},{1,2},{2,3},{4,5},{5,6},{6,7},{8,9},{9,10},{10,11},{12,13},{... | collective-permute-start | bytes 55304 | tf_op jit(solution)/shard_map/ppermute | solution.py:650
  56.6 0.8 %collective-permute-done.16.by = f32[2,6,384]{2,1,0:T(8,128)S(1)} collective-permute-done((f32[2,6,384]{2,1,0:T(8,128)S(1)}, f32[2,6,384]{2,1,0:T(8,128)S(1)}, u32[]{:S(2)}, u32[]{:S(2)}) %collective-permute-start.16) | collective-permute-done | bytes 18464 | tf_op jit(solution)/shard_map/ppermute | solution.py:650
  57.4 0.6 shard_map.83
  58.0 1.3 %collective-permute-start.19 = (f32[19,8,128]{2,1,0:T(8,128)S(1)}, f32[19,8,128]{2,1,0:T(8,128)S(1)}, u32[]{:S(2)}, u32[]{:S(2)}) collective-permute-start(f32[19,8,128]{2,1,0:T(8,128)S(1)} %get-tuple-element.101), channel_id=1, source_target_pairs={{0,16},{1,17},{2,18},{3,19},{4,20},{5,21},{6,22},{7,23},{8,24},{9,... | collective-permute-start | bytes 233480 | tf_op jit(solution)/shard_map/ppermute | solution.py:20
  59.3 0.7 collective-permute-start.17
  60.0 0.7 collective-permute-start.18
  60.7 1.2 %collective-permute-done.19.region = f32[19,8,128]{2,1,0:T(8,128)S(1)} collective-permute-done((f32[19,8,128]{2,1,0:T(8,128)S(1)}, f32[19,8,128]{2,1,0:T(8,128)S(1)}, u32[]{:S(2)}, u32[]{:S(2)}) %collective-permute-start.19) | collective-permute-done | bytes 77856 | tf_op jit(solution)/shard_map/ppermute | solution.py:20
  61.9 0.9 %collective-permute-done.20.relay_in = f32[224,384]{1,0:T(8,128)S(1)} collective-permute-done((f32[224,384]{1,0:T(8,128)S(1)}, f32[224,384]{1,0:T(8,128)S(1)}, u32[]{:S(2)}, u32[]{:S(2)}) %collective-permute-start.20) | collective-permute-done | bytes 344096 | tf_op jit(solution)/shard_map/ppermute | solution.py:20
  62.8 0.8 %shard_map.84 = (f32[9,6,9,8,128]{4,3,2,1,0:T(8,128)S(1)}, f32[80,384]{1,0:T(8,128)S(1)}, f32[3,6,24,384]{3,2,1,0:T(8,128)S(1)}, f32[3,6,24,384]{3,2,1,0:T(8,128)S(1)}, f32[3,6,24,384]{3,2,1,0:T(8,128)S(1)}) custom-call(f32[3,6,24,384]{3,2,1,0:T(8,128)S(1)} %get-tuple-element.89.e, f32[3,6,24,384]{3,2,1,0:T(8,128)S(1)} %get-tuple-element.94.h, ...), custom_call_target="tpu_custom_call" | custom-call | tf_op jit(solution)/shard_map/pallas_call | solution.py:613
  63.7 1.3 %collective-permute-start.21 = (f32[80,384]{1,0:T(8,128)S(1)}, f32[80,384]{1,0:T(8,128)S(1)}, u32[]{:S(2)}, u32[]{:S(2)}) collective-permute-start(f32[80,384]{1,0:T(8,128)S(1)} %get-tuple-element.107), channel_id=1, source_target_pairs={{16,0},{17,1},{18,2},{19,3},{20,4},{21,5},{22,6},{23,7},{24,8},{25... | collective-permute-start | bytes 368648 | tf_op jit(solution)/shard_map/ppermute | solution.py:20
  65.0 7.0 %collective-permute-done.21.relay = f32[80,384]{1,0:T(8,128)S(1)} collective-permute-done((f32[80,384]{1,0:T(8,128)S(1)}, f32[80,384]{1,0:T(8,128)S(1)}, u32[]{:S(2)}, u32[]{:S(2)}) %collective-permute-start.21) | collective-permute-done | bytes 122912 | tf_op jit(solution)/shard_map/ppermute | solution.py:20
  71.9 1.9 %shard_map.85 = f32[9,6,24,384]{3,2,1,0:T(8,128)} custom-call(f32[3,6,24,384]{3,2,1,0:T(8,128)S(1)} %get-tuple-element.98.e, f32[3,6,24,384]{3,2,1,0:T(8,128)S(1)} %get-tuple-element.94.h, f32[3,6,24,384]{3,2,1,0:T(8,128)S(1)} %get-tuple-element.99.p, f32[3,6,24,384]{3,2,1,0:T(8,128)S(1)} %get-tuple-element.104.fix_e, ...), custom_call_target="tpu_custom_call" | custom-call | tf_op jit(solution)/shard_map/pallas_call | solution.py:613
  (25 shorter events, 0.2 us)
Async XLA Ops:
  0.0 1.6 %copy-start = (f32[1,9,6,24,384]{4,3,2,1,0:T(8,128)S(1)}, f32[1,9,6,24,384]{4,3,2,1,0:T(8,128)}, u32[]{:S(2)}) copy-start(f32[1,9,6,24,384]{4,3,2,1,0:T(8,128)} %f2.1) | copy-start | bytes 5971972
  1.6 2.8 %copy-start.2 = (s32[1,6,24,384]{3,2,1,0:T(8,128)S(1)}, s32[1,6,24,384]{3,2,1,0:T(8,128)}, u32[]{:S(2)}) copy-start(s32[1,6,24,384]{3,2,1,0:T(8,128)} %m2.1) | copy-start | bytes 663556
  1.6 2.8 %copy-start.3 = (f32[8]{0:T(128)S(1)}, f32[8]{0:T(128)}, u32[]{:S(2)}) copy-start(f32[8]{0:T(128)} %perm.1) | copy-start | bytes 100
  1.6 2.8 %copy-start.4 = (f32[8]{0:T(128)S(1)}, f32[8]{0:T(128)}, u32[]{:S(2)}) copy-start(f32[8]{0:T(128)} %cond.1) | copy-start | bytes 100
  1.6 2.8 %copy-start.5 = (f32[8]{0:T(128)S(1)}, f32[8]{0:T(128)}, u32[]{:S(2)}) copy-start(f32[8]{0:T(128)} %relax.1) | copy-start | bytes 100
  1.6 2.8 %copy-start.6 = (f32[8]{0:T(128)S(1)}, f32[8]{0:T(128)}, u32[]{:S(2)}) copy-start(f32[8]{0:T(128)} %debye.1) | copy-start | bytes 100
  1.6 2.8 %copy-start.7 = (s32[1,1,6]{2,1,0:T(1,128)S(1)}, s32[1,1,6]{2,1,0:T(1,128)}, u32[]{:S(2)}) copy-start(s32[1,1,6]{2,1,0:T(1,128)} %sub.1) | copy-start | bytes 76
  1.6 7.4 %collective-permute-start = (f32[2,24,384]{2,1,0:T(8,128)S(1)}, f32[2,24,384]{2,1,0:T(8,128)S(1)}, u32[]{:S(2)}, u32[]{:S(2)}) collective-permute-start(f32[2,24,384]{2,1,0:T(8,128)S(1)} %get-tuple-element.59), channel_id=1, source_target_pairs={{4,0},{5,1},{6,2},{7,3},{8,4},{9,5},{10,6},{11,7},{12,8},{13,9},{1... | collective-permute-start | bytes 221192 | tf_op jit(solution)/shard_map/ppermute | solution.py:649
  3.1 3.1 %collective-permute-start.1 = (f32[2,6,384]{2,1,0:T(8,128)S(1)}, f32[2,6,384]{2,1,0:T(8,128)S(1)}, u32[]{:S(2)}, u32[]{:S(2)}) collective-permute-start(f32[2,6,384]{2,1,0:T(8,128)S(1)} %get-tuple-element.60), channel_id=1, source_target_pairs={{1,0},{2,1},{3,2},{5,4},{6,5},{7,6},{9,8},{10,9},{11,10},{13,12},{... | collective-permute-start | bytes 55304 | tf_op jit(solution)/shard_map/ppermute | solution.py:650
  9.3 12.8 %copy-start.1 = (f32[1,9,6,24,384]{4,3,2,1,0:T(8,128)S(1)}, f32[1,9,6,24,384]{4,3,2,1,0:T(8,128)}, u32[]{:S(2)}) copy-start(f32[1,9,6,24,384]{4,3,2,1,0:T(8,128)} %f2.1) | copy-start | bytes 5971972
  9.4 9.0 %collective-permute-start.4 = (f32[7,24,384]{2,1,0:T(8,128)S(1)}, f32[7,24,384]{2,1,0:T(8,128)S(1)}, u32[]{:S(2)}, u32[]{:S(2)}) collective-permute-start(f32[7,24,384]{2,1,0:T(8,128)S(1)} %get-tuple-element.67), channel_id=1, source_target_pairs={{0,16},{1,17},{2,18},{3,19},{4,20},{5,21},{6,22},{7,23},{8,24},{9,... | collective-permute-start | bytes 774152 | tf_op jit(solution)/shard_map/ppermute | solution.py:20
  10.8 7.6 %collective-permute-start.2 = (f32[2,24,384]{2,1,0:T(8,128)S(1)}, f32[2,24,384]{2,1,0:T(8,128)S(1)}, u32[]{:S(2)}, u32[]{:S(2)}) collective-permute-start(f32[2,24,384]{2,1,0:T(8,128)S(1)} %get-tuple-element.65), channel_id=1, source_target_pairs={{0,4},{1,5},{2,6},{3,7},{4,8},{5,9},{6,10},{7,11},{8,12},{9,13},{1... | collective-permute-start | bytes 221192 | tf_op jit(solution)/shard_map/ppermute | solution.py:649
  14.7 3.6 %collective-permute-start.3 = (f32[2,6,384]{2,1,0:T(8,128)S(1)}, f32[2,6,384]{2,1,0:T(8,128)S(1)}, u32[]{:S(2)}, u32[]{:S(2)}) collective-permute-start(f32[2,6,384]{2,1,0:T(8,128)S(1)} %get-tuple-element.66), channel_id=1, source_target_pairs={{0,1},{1,2},{2,3},{4,5},{5,6},{6,7},{8,9},{9,10},{10,11},{12,13},{... | collective-permute-start | bytes 55304 | tf_op jit(solution)/shard_map/ppermute | solution.py:650
  18.9 4.7 %collective-permute-start.5 = (f32[6,8,128]{2,1,0:T(8,128)S(1)}, f32[6,8,128]{2,1,0:T(8,128)S(1)}, u32[]{:S(2)}, u32[]{:S(2)}) collective-permute-start(f32[6,8,128]{2,1,0:T(8,128)S(1)} %get-tuple-element.74), channel_id=1, source_target_pairs={{0,16},{1,17},{2,18},{3,19},{4,20},{5,21},{6,22},{7,23},{8,24},{9,... | collective-permute-start | bytes 73736 | tf_op jit(solution)/shard_map/ppermute | solution.py:20
  23.8 6.2 %collective-permute-start.6 = (f32[2,24,384]{2,1,0:T(8,128)S(1)}, f32[2,24,384]{2,1,0:T(8,128)S(1)}, u32[]{:S(2)}, u32[]{:S(2)}) collective-permute-start(f32[2,24,384]{2,1,0:T(8,128)S(1)} %get-tuple-element.77), channel_id=1, source_target_pairs={{4,0},{5,1},{6,2},{7,3},{8,4},{9,5},{10,6},{11,7},{12,8},{13,9},{1... | collective-permute-start | bytes 221192 | tf_op jit(solution)/shard_map/ppermute | solution.py:649
  25.1 3.1 %collective-permute-start.7 = (f32[2,6,384]{2,1,0:T(8,128)S(1)}, f32[2,6,384]{2,1,0:T(8,128)S(1)}, u32[]{:S(2)}, u32[]{:S(2)}) collective-permute-start(f32[2,6,384]{2,1,0:T(8,128)S(1)} %get-tuple-element.78), channel_id=1, source_target_pairs={{1,0},{2,1},{3,2},{5,4},{6,5},{7,6},{9,8},{10,9},{11,10},{13,12},{... | collective-permute-start | bytes 55304 | tf_op jit(solution)/shard_map/ppermute | solution.py:650
  30.3 6.7 %collective-permute-start.8 = (f32[2,24,384]{2,1,0:T(8,128)S(1)}, f32[2,24,384]{2,1,0:T(8,128)S(1)}, u32[]{:S(2)}, u32[]{:S(2)}) collective-permute-start(f32[2,24,384]{2,1,0:T(8,128)S(1)} %get-tuple-element.82), channel_id=1, source_target_pairs={{0,4},{1,5},{2,6},{3,7},{4,8},{5,9},{6,10},{7,11},{8,12},{9,13},{1... | collective-permute-start | bytes 221192 | tf_op jit(solution)/shard_map/ppermute | solution.py:649
  33.9 3.0 %collective-permute-start.9 = (f32[2,6,384]{2,1,0:T(8,128)S(1)}, f32[2,6,384]{2,1,0:T(8,128)S(1)}, u32[]{:S(2)}, u32[]{:S(2)}) collective-permute-start(f32[2,6,384]{2,1,0:T(8,128)S(1)} %get-tuple-element.83), channel_id=1, source_target_pairs={{0,1},{1,2},{2,3},{4,5},{5,6},{6,7},{8,9},{9,10},{10,11},{12,13},{... | collective-permute-start | bytes 55304 | tf_op jit(solution)/shard_map/ppermute | solution.py:650
  37.5 3.8 %collective-permute-start.12 = (f32[19,8,128]{2,1,0:T(8,128)S(1)}, f32[19,8,128]{2,1,0:T(8,128)S(1)}, u32[]{:S(2)}, u32[]{:S(2)}) collective-permute-start(f32[19,8,128]{2,1,0:T(8,128)S(1)} %get-tuple-element.87), channel_id=1, source_target_pairs={{0,16},{1,17},{2,18},{3,19},{4,20},{5,21},{6,22},{7,23},{8,24},{9,... | collective-permute-start | bytes 233480 | tf_op jit(solution)/shard_map/ppermute | solution.py:20
  38.8 1.4 %collective-permute-start.10 = (f32[2,24,384]{2,1,0:T(8,128)S(1)}, f32[2,24,384]{2,1,0:T(8,128)S(1)}, u32[]{:S(2)}, u32[]{:S(2)}) collective-permute-start(f32[2,24,384]{2,1,0:T(8,128)S(1)} %get-tuple-element.82), channel_id=1, source_target_pairs={{16,20},{17,21},{18,22},{19,23},{20,24},{21,25},{22,26},{23,27},{2... | collective-permute-start | bytes 221192 | tf_op jit(solution)/shard_map/ppermute | solution.py:649
  39.5 0.7 collective-permute-start.11
  41.4 6.4 %collective-permute-start.13 = (f32[2,24,384]{2,1,0:T(8,128)S(1)}, f32[2,24,384]{2,1,0:T(8,128)S(1)}, u32[]{:S(2)}, u32[]{:S(2)}) collective-permute-start(f32[2,24,384]{2,1,0:T(8,128)S(1)} %get-tuple-element.90), channel_id=1, source_target_pairs={{4,0},{5,1},{6,2},{7,3},{8,4},{9,5},{10,6},{11,7},{12,8},{13,9},{1... | collective-permute-start | bytes 221192 | tf_op jit(solution)/shard_map/ppermute | solution.py:649
  42.7 3.1 %collective-permute-start.14 = (f32[2,6,384]{2,1,0:T(8,128)S(1)}, f32[2,6,384]{2,1,0:T(8,128)S(1)}, u32[]{:S(2)}, u32[]{:S(2)}) collective-permute-start(f32[2,6,384]{2,1,0:T(8,128)S(1)} %get-tuple-element.91), channel_id=1, source_target_pairs={{1,0},{2,1},{3,2},{5,4},{6,5},{7,6},{9,8},{10,9},{11,10},{13,12},{... | collective-permute-start | bytes 55304 | tf_op jit(solution)/shard_map/ppermute | solution.py:650
  48.1 14.7 %collective-permute-start.20 = (f32[224,384]{1,0:T(8,128)S(1)}, f32[224,384]{1,0:T(8,128)S(1)}, u32[]{:S(2)}, u32[]{:S(2)}) collective-permute-start(f32[224,384]{1,0:T(8,128)S(1)} %get-tuple-element.103), channel_id=1, source_target_pairs={{16,0},{17,1},{18,2},{19,3},{20,4},{21,5},{22,6},{23,7},{24,8},{25... | collective-permute-start | bytes 1032200 | tf_op jit(solution)/shard_map/ppermute | solution.py:20
  49.4 8.0 %collective-permute-start.15 = (f32[2,24,384]{2,1,0:T(8,128)S(1)}, f32[2,24,384]{2,1,0:T(8,128)S(1)}, u32[]{:S(2)}, u32[]{:S(2)}) collective-permute-start(f32[2,24,384]{2,1,0:T(8,128)S(1)} %get-tuple-element.96), channel_id=1, source_target_pairs={{0,4},{1,5},{2,6},{3,7},{4,8},{5,9},{6,10},{7,11},{8,12},{9,13},{1... | collective-permute-start | bytes 221192 | tf_op jit(solution)/shard_map/ppermute | solution.py:649
  53.0 4.4 %collective-permute-start.16 = (f32[2,6,384]{2,1,0:T(8,128)S(1)}, f32[2,6,384]{2,1,0:T(8,128)S(1)}, u32[]{:S(2)}, u32[]{:S(2)}) collective-permute-start(f32[2,6,384]{2,1,0:T(8,128)S(1)} %get-tuple-element.97), channel_id=1, source_target_pairs={{0,1},{1,2},{2,3},{4,5},{5,6},{6,7},{8,9},{9,10},{10,11},{12,13},{... | collective-permute-start | bytes 55304 | tf_op jit(solution)/shard_map/ppermute | solution.py:650
  58.0 3.9 %collective-permute-start.19 = (f32[19,8,128]{2,1,0:T(8,128)S(1)}, f32[19,8,128]{2,1,0:T(8,128)S(1)}, u32[]{:S(2)}, u32[]{:S(2)}) collective-permute-start(f32[19,8,128]{2,1,0:T(8,128)S(1)} %get-tuple-element.101), channel_id=1, source_target_pairs={{0,16},{1,17},{2,18},{3,19},{4,20},{5,21},{6,22},{7,23},{8,24},{9,... | collective-permute-start | bytes 233480 | tf_op jit(solution)/shard_map/ppermute | solution.py:20
  59.3 1.4 %collective-permute-start.17 = (f32[2,24,384]{2,1,0:T(8,128)S(1)}, f32[2,24,384]{2,1,0:T(8,128)S(1)}, u32[]{:S(2)}, u32[]{:S(2)}) collective-permute-start(f32[2,24,384]{2,1,0:T(8,128)S(1)} %get-tuple-element.96), channel_id=1, source_target_pairs={{16,20},{17,21},{18,22},{19,23},{20,24},{21,25},{22,26},{23,27},{2... | collective-permute-start | bytes 221192 | tf_op jit(solution)/shard_map/ppermute | solution.py:649
  60.0 0.7 collective-permute-start.18
  63.7 8.3 %collective-permute-start.21 = (f32[80,384]{1,0:T(8,128)S(1)}, f32[80,384]{1,0:T(8,128)S(1)}, u32[]{:S(2)}, u32[]{:S(2)}) collective-permute-start(f32[80,384]{1,0:T(8,128)S(1)} %get-tuple-element.107), channel_id=1, source_target_pairs={{16,0},{17,1},{18,2},{19,3},{20,4},{21,5},{22,6},{23,7},{24,8},{25... | collective-permute-start | bytes 368648 | tf_op jit(solution)/shard_map/ppermute | solution.py:20

commit v9 on v8

--- a/solution.py
+++ b/solution.py
@@ -179,6 +179,8 @@
         return jnp.where(lane == 0, 0.0, pltpu.roll(value, 1, 1))
 
     hx, hy, hz = (h[c, x] for c in range(3))
+    if prev_x is None:
+        prev_x, prev_y = lambda k: 0.0, lambda k, x: 0.0
     if isinstance(x, int):
         hy_x, hz_x = (h[1, x - 1], h[2, x - 1]) if x > 0 else (prev_x(0), prev_x(1))
     else:
@@ -206,6 +208,21 @@
                 new, last = new + more[0][c, x], last + more[1][c, x]
             out_e[c, x] = new
             out_p[c, x] = last
+
+
+def complete(part_e, part_p, coef, prev_x, prev_y, out_e, out_p):
+    for x in range(6):
+        b, g = (jnp.concatenate([coef[k, x, zt, 0:1] for zt in range(3)], axis=1) for k in (1, 4))
+        for c in range(3):
+            new, last = part_e[c, x], part_p[c, x]
+            if x == 0 and c > 0:
+                more = whole(coef, 1, 0) * (prev_x(1) if c == 1 else -prev_x(0))
+                new, last = new + more, last + whole(coef, 4, 0) * more
+            out_e[c, x], out_p[c, x] = new, last
+            if c != 1:
+                more = b * (-prev_y(1, x) if c == 0 else prev_y(0, x))
+                out_e[c, x, 0:1] = new[0:1] + more
+                out_p[c, x, 0:1] = last[0:1] + g * more
 
 
 def edge_x(ref):
@@ -442,6 +459,18 @@
             ay[1, x : x + 1] = near_y[0, 2, x, 0:1]
 
 
+def coarse_part_kernel(e, h, p, coef, out_e, out_p):
+    @pl.when(is_coarse())
+    def _():
+        electric(e, h, p, coef, None, None, out_e, out_p)
+
+
+def fine_part_kernel(e, h, p, coef, out_e, out_p):
+    @pl.when(is_fine())
+    def _():
+        electric(e, h, p, coef, None, None, out_e, out_p)
+
+
 def h1_kernel(e, h, ax, ay, material, desc, out_h, bx, by, sent):
     @pl.when(is_coarse())
     def _():
@@ -455,11 +484,11 @@
 
 
 def e1_kernel(
-    e, h, p, coef, bx, by, desc, material, table, out_e, out_p, sent, slab_coef, first
+    e, p, coef, bx, by, desc, material, table, out_e, out_p, sent, slab_coef, first
 ):
     @pl.when(is_coarse())
     def _():
-        electric(e, h, p, coef, edge_x(bx), edge_y(by), out_e, out_p)
+        complete(e, p, coef, edge_x(bx), edge_y(by), out_e, out_p)
         for k, tile in enumerate(sum(cut_region(out_e, desc, corner(desc)), [])):
             sent[k] = tile
         slab_coef[...] = coef[...]
@@ -513,7 +542,7 @@
 
 
 def f2_kernel(
-    e, h, p, base_e, base_p, coef, slab_coef, bx, by, desc, box_in, region, was,
+    e, p, base_e, base_p, coef, slab_coef, bx, by, desc, box_in, region, was,
     out_e, out_p, ax, ay, box, now, change,
 ):
     @pl.when(is_coarse())
@@ -524,7 +553,7 @@
     @pl.when(is_fine())
     def _():
         spot = corner(desc)
-        electric(e, h, p, slab_coef, edge_x(bx), edge_y(by), out_e, out_p)
+        complete(e, p, slab_coef, edge_x(bx), edge_y(by), out_e, out_p)
         fix = cut_region(out_e, desc, spot)
         latest = [[region[2 * c + i] + fix[c][i] for i in range(2)] for c in range(3)]
         restricted = fine_steps(box_in, box, coef, desc, load_box(was), latest)
@@ -580,17 +609,12 @@
         pack(relay, restricted, bx, by, 0)
 
 
-def finish_kernel(e, h, p, fix_e, fix_h, fix_p, coef, desc, relay, box, out, mixed):
+def late_kernel(e, h, p, fix_e, fix_h, fix_p, coef, box, out, mixed):
     @pl.when(is_coarse())
     def _():
         view_e, view_p = out.at[pl.ds(0, 3)], out.at[pl.ds(6, 3)]
-        electric(
-            fix_e, fix_h, fix_p, coef, packed_x(relay, 16), packed_y(relay, 16),
-            view_e, view_p, (e, p),
-        )
+        electric(fix_e, fix_h, fix_p, coef, None, None, view_e, view_p, (e, p))
         out[3:6] = h[...] + fix_h[...]
-        covered = [jnp.where(value, F32(1.0), 0.0) for value in covered_of(desc)]
-        put(view_e, packed_box(relay, 0), desc, corner(desc), covered)
 
     @pl.when(is_fine())
     def _():
@@ -602,6 +626,23 @@
                         mixed[c, x, a, pl.ds(u, 8, stride=3)] = parts[a]
                 for a in range(3):
                     out[c, x, :, pl.ds(128 * a, 128)] = mixed[c, x, a]
+
+
+def finish_kernel(late, coef, desc, relay, out):
+    @pl.when(is_coarse())
+    def _():
+        view_e, view_p = out.at[pl.ds(0, 3)], out.at[pl.ds(6, 3)]
+        out[3:6] = late[3:6]
+        complete(
+            late.at[pl.ds(0, 3)], late.at[pl.ds(6, 3)], coef,
+            packed_x(relay, 16), packed_y(relay, 16), view_e, view_p,
+        )
+        covered = [jnp.where(value, F32(1.0), 0.0) for value in covered_of(desc)]
+        put(view_e, packed_box(relay, 0), desc, corner(desc), covered)
+
+    @pl.when(is_fine())
+    def _():
+        out[...] = late[...]
 
 
 def third(shape, a):
@@ -693,9 +734,10 @@
     )
     slab_material = to_fine(slab_material)
     bx, by = exchange(bx, by, 1, (0,))
+    e, p = call(coarse_part_kernel, (e, h, p, coef), [PART] * 2)
     e, p, sent, slab_coef, first = call(
         e1_kernel,
-        (e, h, p, coef, bx, by, desc, slab_material, table),
+        (e, p, coef, bx, by, desc, slab_material, table),
         [PART] * 2 + [(6, 8, 128), COEF, REGION],
     )
     region = to_fine(sent)
@@ -712,9 +754,10 @@
         base_kernel, (e, h, p, slab_coef, bx, by, desc), [PART] * 2 + [(19, 8, 128)]
     )
     region = to_fine(sent)
+    e, p = call(fine_part_kernel, (e, h, p, slab_coef), [PART] * 2)
     e, p, ax, ay, box, now, change2 = call(
         f2_kernel,
-        (e, h, p, base_e, base_p, fine_coef, slab_coef, bx2, by2, desc, box, region, now),
+        (e, p, base_e, base_p, fine_coef, slab_coef, bx2, by2, desc, box, region, now),
         [PART] * 2 + EDGES + [BOX, REGION, REGION],
     )
     ax, ay = exchange(ax, ay, -1, (0, 1))
@@ -741,12 +784,13 @@
         ],
     )
     relay4 = to_coarse(relay4)
-    (out,) = call(
-        finish_kernel,
-        (base_e, h, base_p, *fix, coef, desc, relay4, box),
+    (late,) = call(
+        late_kernel,
+        (base_e, h, base_p, *fix, slab_coef, box),
         [SLAB],
         scratch=[pltpu.VMEM((9, 6, 3, 24, 128), F32)],
     )
+    (out,) = call(finish_kernel, (late, slab_coef, desc, relay4), [SLAB])
     return out[None]
 
 

time: 74.4 us -> 73.5 us (0.988)
  waiting for transfers between devices: 25 us -> 23.9 us
    ppermute x6, waiting for transfers between devices: 11.6 us -> 10.4 us  [shifted(): return lax.ppermute(value, axis, pairs)]
    pallas_call x13 -> x16, Pallas kernels: 6.73 us -> 6.96 us  [call(): pl.pallas_call(kernel, out_shape=shapes, in_specs=specs or [VM] * len(ope...]
  transfers between devices with their start and end apart: 22 -> 22, of which waited for: 14 -> 14; matrix products, arithmetic and copies ran while one was open for 0% -> 0% of each run, Pallas kernels for 2% -> 4%
where the time goes in v9:
time: 73.5 us; the launch traced here: 73 us
  starting transfers between devices  40.1 us (55%)
  waiting for transfers between devices  23.9 us (33%)
  Pallas kernels  6.96 us (9%)
  local copies, waits for them, and re-layouts  1.58 us (2%)
    ppermute x8, starting transfers between devices, exchange(): lax.ppermute(x_edge, AXES, pairs(by, 0))  16.6 us
    ppermute x8, starting transfers between devices, exchange(): lax.ppermute(y_edge, AXES, pairs(0, by))  13.5 us
    ppermute x6, waiting for transfers between devices, shifted(): return lax.ppermute(value, axis, pairs)  10.4 us
    ppermute x6, starting transfers between devices, shifted(): return lax.ppermute(value, axis, pairs)  9.99 us
    ppermute x8, waiting for transfers between devices, exchange(): lax.ppermute(x_edge, AXES, pairs(by, 0))  7.17 us
    pallas_call x16, Pallas kernels, call(): pl.pallas_call(kernel, out_shape=shapes, in_specs=specs or [VM] * len(ope...  6.96 us
    ppermute x8, waiting for transfers between devices, exchange(): lax.ppermute(y_edge, AXES, pairs(0, by))  6.35 us
    unnamed x16, local copies, waits for them, and re-layouts  1.58 us
  transfers between devices with their start and end apart: 22, of which 14 were waited for; matrix products, arithmetic and copies ran while one was open for 0% of the time, Pallas kernels for 4%

profile of v9, /device:TPU:0, one launch (start us, length us, event | category | flops | bytes accessed | tf_op | source)
XLA Modules:
  0.0 73.0 jit_solution(17020512877250013114)
XLA Ops:
  0.0 1.6 %copy-done = f32[1,9,6,24,384]{4,3,2,1,0:T(8,128)S(1)} copy-done((f32[1,9,6,24,384]{4,3,2,1,0:T(8,128)S(1)}, f32[1,9,6,24,384]{4,3,2,1,0:T(8,128)}, u32[]{:S(2)}) %copy-start) | copy-done | bytes 1990680
  1.6 1.4 %collective-permute-start = (f32[2,24,384]{2,1,0:T(8,128)S(1)}, f32[2,24,384]{2,1,0:T(8,128)S(1)}, u32[]{:S(2)}, u32[]{:S(2)}) collective-permute-start(f32[2,24,384]{2,1,0:T(8,128)S(1)} %get-tuple-element.63), channel_id=1, source_target_pairs={{4,0},{5,1},{6,2},{7,3},{8,4},{9,5},{10,6},{11,7},{12,8},{13,9},{1... | collective-permute-start | bytes 221192 | tf_op jit(solution)/shard_map/ppermute | solution.py:690
  3.1 1.3 %collective-permute-start.1 = (f32[2,6,384]{2,1,0:T(8,128)S(1)}, f32[2,6,384]{2,1,0:T(8,128)S(1)}, u32[]{:S(2)}, u32[]{:S(2)}) collective-permute-start(f32[2,6,384]{2,1,0:T(8,128)S(1)} %get-tuple-element.64), channel_id=1, source_target_pairs={{1,0},{2,1},{3,2},{5,4},{6,5},{7,6},{9,8},{10,9},{11,10},{13,12},{... | collective-permute-start | bytes 55304 | tf_op jit(solution)/shard_map/ppermute | solution.py:691
  4.4 1.1 %shard_map.73 = (f32[3,6,24,384]{3,2,1,0:T(8,128)S(1)}, f32[3,6,24,384]{3,2,1,0:T(8,128)S(1)}, f32[3,6,24,384]{3,2,1,0:T(8,128)S(1)}, f32[5,6,9,8,128]{4,3,2,1,0...) custom-call(f32[1,9,6,24,384]{4,3,2,1,0:T(8,128)S(1)} %copy-done, s32[1,6,24,384]{3,2,1,0:T(8,128)S(1)} %copy-done.2, ...), custom_call_target="tpu_custom_call" | custom-call | tf_op jit(solution)/shard_map/pallas_call | solution.py:654
  5.6 0.6 collective-permute-done.1.ay
  6.1 2.9 %collective-permute-done.ax = f32[2,24,384]{2,1,0:T(8,128)S(1)} collective-permute-done((f32[2,24,384]{2,1,0:T(8,128)S(1)}, f32[2,24,384]{2,1,0:T(8,128)S(1)}, u32[]{:S(2)}, u32[]{:S(2)}) %collective-permute-start) | collective-permute-done | bytes 73760 | tf_op jit(solution)/shard_map/ppermute | solution.py:690
  9.0 0.3 shard_map.75
  9.3 1.3 %collective-permute-start.4 = (f32[7,24,384]{2,1,0:T(8,128)S(1)}, f32[7,24,384]{2,1,0:T(8,128)S(1)}, u32[]{:S(2)}, u32[]{:S(2)}) collective-permute-start(f32[7,24,384]{2,1,0:T(8,128)S(1)} %get-tuple-element.73), channel_id=1, source_target_pairs={{0,16},{1,17},{2,18},{3,19},{4,20},{5,21},{6,22},{7,23},{8,24},{9,... | collective-permute-start | bytes 774152 | tf_op jit(solution)/shard_map/ppermute | solution.py:20
  10.6 3.9 %collective-permute-start.2 = (f32[2,24,384]{2,1,0:T(8,128)S(1)}, f32[2,24,384]{2,1,0:T(8,128)S(1)}, u32[]{:S(2)}, u32[]{:S(2)}) collective-permute-start(f32[2,24,384]{2,1,0:T(8,128)S(1)} %get-tuple-element.71), channel_id=1, source_target_pairs={{0,4},{1,5},{2,6},{3,7},{4,8},{5,9},{6,10},{7,11},{8,12},{9,13},{1... | collective-permute-start | bytes 221192 | tf_op jit(solution)/shard_map/ppermute | solution.py:690
  14.6 2.8 %collective-permute-start.3 = (f32[2,6,384]{2,1,0:T(8,128)S(1)}, f32[2,6,384]{2,1,0:T(8,128)S(1)}, u32[]{:S(2)}, u32[]{:S(2)}) collective-permute-start(f32[2,6,384]{2,1,0:T(8,128)S(1)} %get-tuple-element.72), channel_id=1, source_target_pairs={{0,1},{1,2},{2,3},{4,5},{5,6},{6,7},{8,9},{9,10},{10,11},{12,13},{... | collective-permute-start | bytes 55304 | tf_op jit(solution)/shard_map/ppermute | solution.py:691
  17.4 0.4 shard_map.76
  17.8 0.4 collective-permute-done.3.by
  18.2 0.2 shard_map.77
  18.5 3.5 %collective-permute-start.5 = (f32[6,8,128]{2,1,0:T(8,128)S(1)}, f32[6,8,128]{2,1,0:T(8,128)S(1)}, u32[]{:S(2)}, u32[]{:S(2)}) collective-permute-start(f32[6,8,128]{2,1,0:T(8,128)S(1)} %get-tuple-element.80), channel_id=1, source_target_pairs={{0,16},{1,17},{2,18},{3,19},{4,20},{5,21},{6,22},{7,23},{8,24},{9,... | collective-permute-start | bytes 73736 | tf_op jit(solution)/shard_map/ppermute | solution.py:20
  22.1 1.3 %collective-permute-done.5.region = f32[6,8,128]{2,1,0:T(8,128)S(1)} collective-permute-done((f32[6,8,128]{2,1,0:T(8,128)S(1)}, f32[6,8,128]{2,1,0:T(8,128)S(1)}, u32[]{:S(2)}, u32[]{:S(2)}) %collective-permute-start.5) | collective-permute-done | bytes 24608 | tf_op jit(solution)/shard_map/ppermute | solution.py:20
  23.6 1.3 %collective-permute-start.6 = (f32[2,24,384]{2,1,0:T(8,128)S(1)}, f32[2,24,384]{2,1,0:T(8,128)S(1)}, u32[]{:S(2)}, u32[]{:S(2)}) collective-permute-start(f32[2,24,384]{2,1,0:T(8,128)S(1)} %get-tuple-element.83), channel_id=1, source_target_pairs={{4,0},{5,1},{6,2},{7,3},{8,4},{9,5},{10,6},{11,7},{12,8},{13,9},{1... | collective-permute-start | bytes 221192 | tf_op jit(solution)/shard_map/ppermute | solution.py:690
  24.9 1.3 %collective-permute-start.7 = (f32[2,6,384]{2,1,0:T(8,128)S(1)}, f32[2,6,384]{2,1,0:T(8,128)S(1)}, u32[]{:S(2)}, u32[]{:S(2)}) collective-permute-start(f32[2,6,384]{2,1,0:T(8,128)S(1)} %get-tuple-element.84), channel_id=1, source_target_pairs={{1,0},{2,1},{3,2},{5,4},{6,5},{7,6},{9,8},{10,9},{11,10},{13,12},{... | collective-permute-start | bytes 55304 | tf_op jit(solution)/shard_map/ppermute | solution.py:691
  26.2 1.8 %collective-permute-done.7.ay.ay2 = f32[2,6,384]{2,1,0:T(8,128)S(1)} collective-permute-done((f32[2,6,384]{2,1,0:T(8,128)S(1)}, f32[2,6,384]{2,1,0:T(8,128)S(1)}, u32[]{:S(2)}, u32[]{:S(2)}) %collective-permute-start.7) | collective-permute-done | bytes 18464 | tf_op jit(solution)/shard_map/ppermute | solution.py:691
  28.0 1.9 %collective-permute-done.6.ax.ax2 = f32[2,24,384]{2,1,0:T(8,128)S(1)} collective-permute-done((f32[2,24,384]{2,1,0:T(8,128)S(1)}, f32[2,24,384]{2,1,0:T(8,128)S(1)}, u32[]{:S(2)}, u32[]{:S(2)}) %collective-permute-start.6) | collective-permute-done | bytes 73760 | tf_op jit(solution)/shard_map/ppermute | solution.py:690
  29.9 0.2 shard_map.80
  30.1 3.7 %collective-permute-start.8 = (f32[2,24,384]{2,1,0:T(8,128)S(1)}, f32[2,24,384]{2,1,0:T(8,128)S(1)}, u32[]{:S(2)}, u32[]{:S(2)}) collective-permute-start(f32[2,24,384]{2,1,0:T(8,128)S(1)} %get-tuple-element.90), channel_id=1, source_target_pairs={{0,4},{1,5},{2,6},{3,7},{4,8},{5,9},{6,10},{7,11},{8,12},{9,13},{1... | collective-permute-start | bytes 221192 | tf_op jit(solution)/shard_map/ppermute | solution.py:690
  33.8 1.9 %collective-permute-start.9 = (f32[2,6,384]{2,1,0:T(8,128)S(1)}, f32[2,6,384]{2,1,0:T(8,128)S(1)}, u32[]{:S(2)}, u32[]{:S(2)}) collective-permute-start(f32[2,6,384]{2,1,0:T(8,128)S(1)} %get-tuple-element.91), channel_id=1, source_target_pairs={{0,1},{1,2},{2,3},{4,5},{5,6},{6,7},{8,9},{9,10},{10,11},{12,13},{... | collective-permute-start | bytes 55304 | tf_op jit(solution)/shard_map/ppermute | solution.py:691
  35.7 0.8 %collective-permute-done.9.by = f32[2,6,384]{2,1,0:T(8,128)S(1)} collective-permute-done((f32[2,6,384]{2,1,0:T(8,128)S(1)}, f32[2,6,384]{2,1,0:T(8,128)S(1)}, u32[]{:S(2)}, u32[]{:S(2)}) %collective-permute-start.9) | collective-permute-done | bytes 18464 | tf_op jit(solution)/shard_map/ppermute | solution.py:691
  36.5 0.5 shard_map.82
  37.1 1.3 %collective-permute-start.12 = (f32[19,8,128]{2,1,0:T(8,128)S(1)}, f32[19,8,128]{2,1,0:T(8,128)S(1)}, u32[]{:S(2)}, u32[]{:S(2)}) collective-permute-start(f32[19,8,128]{2,1,0:T(8,128)S(1)} %get-tuple-element.95), channel_id=1, source_target_pairs={{0,16},{1,17},{2,18},{3,19},{4,20},{5,21},{6,22},{7,23},{8,24},{9,... | collective-permute-start | bytes 233480 | tf_op jit(solution)/shard_map/ppermute | solution.py:20
  38.4 0.7 collective-permute-start.10
  39.0 0.7 collective-permute-start.11
  39.8 0.9 %collective-permute-done.12.region = f32[19,8,128]{2,1,0:T(8,128)S(1)} collective-permute-done((f32[19,8,128]{2,1,0:T(8,128)S(1)}, f32[19,8,128]{2,1,0:T(8,128)S(1)}, u32[]{:S(2)}, u32[]{:S(2)}) %collective-permute-start.12) | collective-permute-done | bytes 77856 | tf_op jit(solution)/shard_map/ppermute | solution.py:20
  40.7 1.3 %collective-permute-start.13 = (f32[2,24,384]{2,1,0:T(8,128)S(1)}, f32[2,24,384]{2,1,0:T(8,128)S(1)}, u32[]{:S(2)}, u32[]{:S(2)}) collective-permute-start(f32[2,24,384]{2,1,0:T(8,128)S(1)} %get-tuple-element.98), channel_id=1, source_target_pairs={{4,0},{5,1},{6,2},{7,3},{8,4},{9,5},{10,6},{11,7},{12,8},{13,9},{1... | collective-permute-start | bytes 221192 | tf_op jit(solution)/shard_map/ppermute | solution.py:690
  42.0 1.3 %collective-permute-start.14 = (f32[2,6,384]{2,1,0:T(8,128)S(1)}, f32[2,6,384]{2,1,0:T(8,128)S(1)}, u32[]{:S(2)}, u32[]{:S(2)}) collective-permute-start(f32[2,6,384]{2,1,0:T(8,128)S(1)} %get-tuple-element.99), channel_id=1, source_target_pairs={{1,0},{2,1},{3,2},{5,4},{6,5},{7,6},{9,8},{10,9},{11,10},{13,12},{... | collective-permute-start | bytes 55304 | tf_op jit(solution)/shard_map/ppermute | solution.py:691
  43.3 1.9 %collective-permute-done.14.ay = f32[2,6,384]{2,1,0:T(8,128)S(1)} collective-permute-done((f32[2,6,384]{2,1,0:T(8,128)S(1)}, f32[2,6,384]{2,1,0:T(8,128)S(1)}, u32[]{:S(2)}, u32[]{:S(2)}) %collective-permute-start.14) | collective-permute-done | bytes 18464 | tf_op jit(solution)/shard_map/ppermute | solution.py:691
  45.2 2.4 %collective-permute-done.13.ax = f32[2,24,384]{2,1,0:T(8,128)S(1)} collective-permute-done((f32[2,24,384]{2,1,0:T(8,128)S(1)}, f32[2,24,384]{2,1,0:T(8,128)S(1)}, u32[]{:S(2)}, u32[]{:S(2)}) %collective-permute-start.13) | collective-permute-done | bytes 73760 | tf_op jit(solution)/shard_map/ppermute | solution.py:690
  47.6 0.2 shard_map.84
  47.9 1.3 %collective-permute-start.20 = (f32[224,384]{1,0:T(8,128)S(1)}, f32[224,384]{1,0:T(8,128)S(1)}, u32[]{:S(2)}, u32[]{:S(2)}) collective-permute-start(f32[224,384]{1,0:T(8,128)S(1)} %get-tuple-element.111), channel_id=1, source_target_pairs={{16,0},{17,1},{18,2},{19,3},{20,4},{21,5},{22,6},{23,7},{24,8},{25... | collective-permute-start | bytes 1032200 | tf_op jit(solution)/shard_map/ppermute | solution.py:20
  49.2 3.6 %collective-permute-start.15 = (f32[2,24,384]{2,1,0:T(8,128)S(1)}, f32[2,24,384]{2,1,0:T(8,128)S(1)}, u32[]{:S(2)}, u32[]{:S(2)}) collective-permute-start(f32[2,24,384]{2,1,0:T(8,128)S(1)} %get-tuple-element.104), channel_id=1, source_target_pairs={{0,4},{1,5},{2,6},{3,7},{4,8},{5,9},{6,10},{7,11},{8,12},{9,13},{1... | collective-permute-start | bytes 221192 | tf_op jit(solution)/shard_map/ppermute | solution.py:690
  52.8 3.6 %collective-permute-start.16 = (f32[2,6,384]{2,1,0:T(8,128)S(1)}, f32[2,6,384]{2,1,0:T(8,128)S(1)}, u32[]{:S(2)}, u32[]{:S(2)}) collective-permute-start(f32[2,6,384]{2,1,0:T(8,128)S(1)} %get-tuple-element.105), channel_id=1, source_target_pairs={{0,1},{1,2},{2,3},{4,5},{5,6},{6,7},{8,9},{9,10},{10,11},{12,13},{... | collective-permute-start | bytes 55304 | tf_op jit(solution)/shard_map/ppermute | solution.py:691
  56.4 0.8 %collective-permute-done.16.by = f32[2,6,384]{2,1,0:T(8,128)S(1)} collective-permute-done((f32[2,6,384]{2,1,0:T(8,128)S(1)}, f32[2,6,384]{2,1,0:T(8,128)S(1)}, u32[]{:S(2)}, u32[]{:S(2)}) %collective-permute-start.16) | collective-permute-done | bytes 18464 | tf_op jit(solution)/shard_map/ppermute | solution.py:691
  57.3 0.5 shard_map.85
  57.8 1.3 %collective-permute-start.19 = (f32[19,8,128]{2,1,0:T(8,128)S(1)}, f32[19,8,128]{2,1,0:T(8,128)S(1)}, u32[]{:S(2)}, u32[]{:S(2)}) collective-permute-start(f32[19,8,128]{2,1,0:T(8,128)S(1)} %get-tuple-element.109), channel_id=1, source_target_pairs={{0,16},{1,17},{2,18},{3,19},{4,20},{5,21},{6,22},{7,23},{8,24},{9,... | collective-permute-start | bytes 233480 | tf_op jit(solution)/shard_map/ppermute | solution.py:20
  59.1 0.7 collective-permute-start.17
  59.8 0.7 collective-permute-start.18
  60.5 1.2 %collective-permute-done.19.region = f32[19,8,128]{2,1,0:T(8,128)S(1)} collective-permute-done((f32[19,8,128]{2,1,0:T(8,128)S(1)}, f32[19,8,128]{2,1,0:T(8,128)S(1)}, u32[]{:S(2)}, u32[]{:S(2)}) %collective-permute-start.19) | collective-permute-done | bytes 77856 | tf_op jit(solution)/shard_map/ppermute | solution.py:20
  61.7 0.5 collective-permute-done.20.relay_in
  62.2 0.8 %shard_map.86 = (f32[9,6,9,8,128]{4,3,2,1,0:T(8,128)S(1)}, f32[80,384]{1,0:T(8,128)S(1)}, f32[3,6,24,384]{3,2,1,0:T(8,128)S(1)}, f32[3,6,24,384]{3,2,1,0:T(8,128)S(1)}, f32[3,6,24,384]{3,2,1,0:T(8,128)S(1)}) custom-call(f32[3,6,24,384]{3,2,1,0:T(8,128)S(1)} %get-tuple-element.97.e, f32[3,6,24,384]{3,2,1,0:T(8,128)S(1)} %get-tuple-element.102.h, ...), custom_call_target="tpu_custom_call" | custom-call | tf_op jit(solution)/shard_map/pallas_call | solution.py:654
  63.1 1.3 %collective-permute-start.21 = (f32[80,384]{1,0:T(8,128)S(1)}, f32[80,384]{1,0:T(8,128)S(1)}, u32[]{:S(2)}, u32[]{:S(2)}) collective-permute-start(f32[80,384]{1,0:T(8,128)S(1)} %get-tuple-element.116), channel_id=1, source_target_pairs={{16,0},{17,1},{18,2},{19,3},{20,4},{21,5},{22,6},{23,7},{24,8},{25... | collective-permute-start | bytes 368648 | tf_op jit(solution)/shard_map/ppermute | solution.py:20
  64.4 0.6 shard_map.87.late
  65.0 6.5 %collective-permute-done.21.relay = f32[80,384]{1,0:T(8,128)S(1)} collective-permute-done((f32[80,384]{1,0:T(8,128)S(1)}, f32[80,384]{1,0:T(8,128)S(1)}, u32[]{:S(2)}, u32[]{:S(2)}) %collective-permute-start.21) | collective-permute-done | bytes 122912 | tf_op jit(solution)/shard_map/ppermute | solution.py:20
  71.4 1.5 %shard_map.88 = f32[9,6,24,384]{3,2,1,0:T(8,128)} custom-call(f32[9,6,24,384]{3,2,1,0:T(8,128)S(1)} %shard_map.87.late, f32[5,6,9,8,128]{4,3,2,1,0:T(8,128)S(1)} %get-tuple-element.87.coef.slab_coef, s32[6,8,128]{2,1,0:T(8,128)S(1)} %get-tuple-element.65.desc, f32[80,384]{1,0:T(8,128)S(1)} %collective-permute-done.21.relay), custom_call_target="tpu_custom_call" | custom-call | tf_op jit(solution)/shard_map/pallas_call | solution.py:654
  (28 shorter events, 0.5 us)
Async XLA Ops:
  0.0 1.6 %copy-start = (f32[1,9,6,24,384]{4,3,2,1,0:T(8,128)S(1)}, f32[1,9,6,24,384]{4,3,2,1,0:T(8,128)}, u32[]{:S(2)}) copy-start(f32[1,9,6,24,384]{4,3,2,1,0:T(8,128)} %f2.1) | copy-start | bytes 5971972
  1.6 2.8 %copy-start.2 = (s32[1,6,24,384]{3,2,1,0:T(8,128)S(1)}, s32[1,6,24,384]{3,2,1,0:T(8,128)}, u32[]{:S(2)}) copy-start(s32[1,6,24,384]{3,2,1,0:T(8,128)} %m2.1) | copy-start | bytes 663556
  1.6 2.8 %copy-start.3 = (f32[8]{0:T(128)S(1)}, f32[8]{0:T(128)}, u32[]{:S(2)}) copy-start(f32[8]{0:T(128)} %perm.1) | copy-start | bytes 100
  1.6 2.8 %copy-start.4 = (f32[8]{0:T(128)S(1)}, f32[8]{0:T(128)}, u32[]{:S(2)}) copy-start(f32[8]{0:T(128)} %cond.1) | copy-start | bytes 100
  1.6 2.8 %copy-start.5 = (f32[8]{0:T(128)S(1)}, f32[8]{0:T(128)}, u32[]{:S(2)}) copy-start(f32[8]{0:T(128)} %relax.1) | copy-start | bytes 100
  1.6 2.8 %copy-start.6 = (f32[8]{0:T(128)S(1)}, f32[8]{0:T(128)}, u32[]{:S(2)}) copy-start(f32[8]{0:T(128)} %debye.1) | copy-start | bytes 100
  1.6 2.8 %copy-start.7 = (s32[1,1,6]{2,1,0:T(1,128)S(1)}, s32[1,1,6]{2,1,0:T(1,128)}, u32[]{:S(2)}) copy-start(s32[1,1,6]{2,1,0:T(1,128)} %sub.1) | copy-start | bytes 76
  1.6 7.4 %collective-permute-start = (f32[2,24,384]{2,1,0:T(8,128)S(1)}, f32[2,24,384]{2,1,0:T(8,128)S(1)}, u32[]{:S(2)}, u32[]{:S(2)}) collective-permute-start(f32[2,24,384]{2,1,0:T(8,128)S(1)} %get-tuple-element.63), channel_id=1, source_target_pairs={{4,0},{5,1},{6,2},{7,3},{8,4},{9,5},{10,6},{11,7},{12,8},{13,9},{1... | collective-permute-start | bytes 221192 | tf_op jit(solution)/shard_map/ppermute | solution.py:690
  3.1 3.1 %collective-permute-start.1 = (f32[2,6,384]{2,1,0:T(8,128)S(1)}, f32[2,6,384]{2,1,0:T(8,128)S(1)}, u32[]{:S(2)}, u32[]{:S(2)}) collective-permute-start(f32[2,6,384]{2,1,0:T(8,128)S(1)} %get-tuple-element.64), channel_id=1, source_target_pairs={{1,0},{2,1},{3,2},{5,4},{6,5},{7,6},{9,8},{10,9},{11,10},{13,12},{... | collective-permute-start | bytes 55304 | tf_op jit(solution)/shard_map/ppermute | solution.py:691
  9.3 8.9 %collective-permute-start.4 = (f32[7,24,384]{2,1,0:T(8,128)S(1)}, f32[7,24,384]{2,1,0:T(8,128)S(1)}, u32[]{:S(2)}, u32[]{:S(2)}) collective-permute-start(f32[7,24,384]{2,1,0:T(8,128)S(1)} %get-tuple-element.73), channel_id=1, source_target_pairs={{0,16},{1,17},{2,18},{3,19},{4,20},{5,21},{6,22},{7,23},{8,24},{9,... | collective-permute-start | bytes 774152 | tf_op jit(solution)/shard_map/ppermute | solution.py:20
  10.6 7.6 %collective-permute-start.2 = (f32[2,24,384]{2,1,0:T(8,128)S(1)}, f32[2,24,384]{2,1,0:T(8,128)S(1)}, u32[]{:S(2)}, u32[]{:S(2)}) collective-permute-start(f32[2,24,384]{2,1,0:T(8,128)S(1)} %get-tuple-element.71), channel_id=1, source_target_pairs={{0,4},{1,5},{2,6},{3,7},{4,8},{5,9},{6,10},{7,11},{8,12},{9,13},{1... | collective-permute-start | bytes 221192 | tf_op jit(solution)/shard_map/ppermute | solution.py:690
  14.6 3.6 %collective-permute-start.3 = (f32[2,6,384]{2,1,0:T(8,128)S(1)}, f32[2,6,384]{2,1,0:T(8,128)S(1)}, u32[]{:S(2)}, u32[]{:S(2)}) collective-permute-start(f32[2,6,384]{2,1,0:T(8,128)S(1)} %get-tuple-element.72), channel_id=1, source_target_pairs={{0,1},{1,2},{2,3},{4,5},{5,6},{6,7},{8,9},{9,10},{10,11},{12,13},{... | collective-permute-start | bytes 55304 | tf_op jit(solution)/shard_map/ppermute | solution.py:691
  17.8 4.2 %copy-start.1 = (f32[1,9,6,24,384]{4,3,2,1,0:T(8,128)S(1)}, f32[1,9,6,24,384]{4,3,2,1,0:T(8,128)}, u32[]{:S(2)}) copy-start(f32[1,9,6,24,384]{4,3,2,1,0:T(8,128)} %f2.1) | copy-start | bytes 5971972
  18.5 5.0 %collective-permute-start.5 = (f32[6,8,128]{2,1,0:T(8,128)S(1)}, f32[6,8,128]{2,1,0:T(8,128)S(1)}, u32[]{:S(2)}, u32[]{:S(2)}) collective-permute-start(f32[6,8,128]{2,1,0:T(8,128)S(1)} %get-tuple-element.80), channel_id=1, source_target_pairs={{0,16},{1,17},{2,18},{3,19},{4,20},{5,21},{6,22},{7,23},{8,24},{9,... | collective-permute-start | bytes 73736 | tf_op jit(solution)/shard_map/ppermute | solution.py:20
  23.6 6.2 %collective-permute-start.6 = (f32[2,24,384]{2,1,0:T(8,128)S(1)}, f32[2,24,384]{2,1,0:T(8,128)S(1)}, u32[]{:S(2)}, u32[]{:S(2)}) collective-permute-start(f32[2,24,384]{2,1,0:T(8,128)S(1)} %get-tuple-element.83), channel_id=1, source_target_pairs={{4,0},{5,1},{6,2},{7,3},{8,4},{9,5},{10,6},{11,7},{12,8},{13,9},{1... | collective-permute-start | bytes 221192 | tf_op jit(solution)/shard_map/ppermute | solution.py:690
  24.9 3.1 %collective-permute-start.7 = (f32[2,6,384]{2,1,0:T(8,128)S(1)}, f32[2,6,384]{2,1,0:T(8,128)S(1)}, u32[]{:S(2)}, u32[]{:S(2)}) collective-permute-start(f32[2,6,384]{2,1,0:T(8,128)S(1)} %get-tuple-element.84), channel_id=1, source_target_pairs={{1,0},{2,1},{3,2},{5,4},{6,5},{7,6},{9,8},{10,9},{11,10},{13,12},{... | collective-permute-start | bytes 55304 | tf_op jit(solution)/shard_map/ppermute | solution.py:691
  30.1 6.4 %collective-permute-start.8 = (f32[2,24,384]{2,1,0:T(8,128)S(1)}, f32[2,24,384]{2,1,0:T(8,128)S(1)}, u32[]{:S(2)}, u32[]{:S(2)}) collective-permute-start(f32[2,24,384]{2,1,0:T(8,128)S(1)} %get-tuple-element.90), channel_id=1, source_target_pairs={{0,4},{1,5},{2,6},{3,7},{4,8},{5,9},{6,10},{7,11},{8,12},{9,13},{1... | collective-permute-start | bytes 221192 | tf_op jit(solution)/shard_map/ppermute | solution.py:690
  33.8 2.7 %collective-permute-start.9 = (f32[2,6,384]{2,1,0:T(8,128)S(1)}, f32[2,6,384]{2,1,0:T(8,128)S(1)}, u32[]{:S(2)}, u32[]{:S(2)}) collective-permute-start(f32[2,6,384]{2,1,0:T(8,128)S(1)} %get-tuple-element.91), channel_id=1, source_target_pairs={{0,1},{1,2},{2,3},{4,5},{5,6},{6,7},{8,9},{9,10},{10,11},{12,13},{... | collective-permute-start | bytes 55304 | tf_op jit(solution)/shard_map/ppermute | solution.py:691
  37.1 3.6 %collective-permute-start.12 = (f32[19,8,128]{2,1,0:T(8,128)S(1)}, f32[19,8,128]{2,1,0:T(8,128)S(1)}, u32[]{:S(2)}, u32[]{:S(2)}) collective-permute-start(f32[19,8,128]{2,1,0:T(8,128)S(1)} %get-tuple-element.95), channel_id=1, source_target_pairs={{0,16},{1,17},{2,18},{3,19},{4,20},{5,21},{6,22},{7,23},{8,24},{9,... | collective-permute-start | bytes 233480 | tf_op jit(solution)/shard_map/ppermute | solution.py:20
  38.4 1.4 %collective-permute-start.10 = (f32[2,24,384]{2,1,0:T(8,128)S(1)}, f32[2,24,384]{2,1,0:T(8,128)S(1)}, u32[]{:S(2)}, u32[]{:S(2)}) collective-permute-start(f32[2,24,384]{2,1,0:T(8,128)S(1)} %get-tuple-element.90), channel_id=1, source_target_pairs={{16,20},{17,21},{18,22},{19,23},{20,24},{21,25},{22,26},{23,27},{2... | collective-permute-start | bytes 221192 | tf_op jit(solution)/shard_map/ppermute | solution.py:690
  39.0 0.7 collective-permute-start.11
  40.7 6.9 %collective-permute-start.13 = (f32[2,24,384]{2,1,0:T(8,128)S(1)}, f32[2,24,384]{2,1,0:T(8,128)S(1)}, u32[]{:S(2)}, u32[]{:S(2)}) collective-permute-start(f32[2,24,384]{2,1,0:T(8,128)S(1)} %get-tuple-element.98), channel_id=1, source_target_pairs={{4,0},{5,1},{6,2},{7,3},{8,4},{9,5},{10,6},{11,7},{12,8},{13,9},{1... | collective-permute-start | bytes 221192 | tf_op jit(solution)/shard_map/ppermute | solution.py:690
  42.0 3.2 %collective-permute-start.14 = (f32[2,6,384]{2,1,0:T(8,128)S(1)}, f32[2,6,384]{2,1,0:T(8,128)S(1)}, u32[]{:S(2)}, u32[]{:S(2)}) collective-permute-start(f32[2,6,384]{2,1,0:T(8,128)S(1)} %get-tuple-element.99), channel_id=1, source_target_pairs={{1,0},{2,1},{3,2},{5,4},{6,5},{7,6},{9,8},{10,9},{11,10},{13,12},{... | collective-permute-start | bytes 55304 | tf_op jit(solution)/shard_map/ppermute | solution.py:691
  47.9 14.4 %collective-permute-start.20 = (f32[224,384]{1,0:T(8,128)S(1)}, f32[224,384]{1,0:T(8,128)S(1)}, u32[]{:S(2)}, u32[]{:S(2)}) collective-permute-start(f32[224,384]{1,0:T(8,128)S(1)} %get-tuple-element.111), channel_id=1, source_target_pairs={{16,0},{17,1},{18,2},{19,3},{20,4},{21,5},{22,6},{23,7},{24,8},{25... | collective-permute-start | bytes 1032200 | tf_op jit(solution)/shard_map/ppermute | solution.py:20
  49.2 8.1 %collective-permute-start.15 = (f32[2,24,384]{2,1,0:T(8,128)S(1)}, f32[2,24,384]{2,1,0:T(8,128)S(1)}, u32[]{:S(2)}, u32[]{:S(2)}) collective-permute-start(f32[2,24,384]{2,1,0:T(8,128)S(1)} %get-tuple-element.104), channel_id=1, source_target_pairs={{0,4},{1,5},{2,6},{3,7},{4,8},{5,9},{6,10},{7,11},{8,12},{9,13},{1... | collective-permute-start | bytes 221192 | tf_op jit(solution)/shard_map/ppermute | solution.py:690
  52.8 4.4 %collective-permute-start.16 = (f32[2,6,384]{2,1,0:T(8,128)S(1)}, f32[2,6,384]{2,1,0:T(8,128)S(1)}, u32[]{:S(2)}, u32[]{:S(2)}) collective-permute-start(f32[2,6,384]{2,1,0:T(8,128)S(1)} %get-tuple-element.105), channel_id=1, source_target_pairs={{0,1},{1,2},{2,3},{4,5},{5,6},{6,7},{8,9},{9,10},{10,11},{12,13},{... | collective-permute-start | bytes 55304 | tf_op jit(solution)/shard_map/ppermute | solution.py:691
  57.8 3.9 %collective-permute-start.19 = (f32[19,8,128]{2,1,0:T(8,128)S(1)}, f32[19,8,128]{2,1,0:T(8,128)S(1)}, u32[]{:S(2)}, u32[]{:S(2)}) collective-permute-start(f32[19,8,128]{2,1,0:T(8,128)S(1)} %get-tuple-element.109), channel_id=1, source_target_pairs={{0,16},{1,17},{2,18},{3,19},{4,20},{5,21},{6,22},{7,23},{8,24},{9,... | collective-permute-start | bytes 233480 | tf_op jit(solution)/shard_map/ppermute | solution.py:20
  59.1 1.4 %collective-permute-start.17 = (f32[2,24,384]{2,1,0:T(8,128)S(1)}, f32[2,24,384]{2,1,0:T(8,128)S(1)}, u32[]{:S(2)}, u32[]{:S(2)}) collective-permute-start(f32[2,24,384]{2,1,0:T(8,128)S(1)} %get-tuple-element.104), channel_id=1, source_target_pairs={{16,20},{17,21},{18,22},{19,23},{20,24},{21,25},{22,26},{23,27},{2... | collective-permute-start | bytes 221192 | tf_op jit(solution)/shard_map/ppermute | solution.py:690
  59.8 0.7 collective-permute-start.18
  63.1 8.3 %collective-permute-start.21 = (f32[80,384]{1,0:T(8,128)S(1)}, f32[80,384]{1,0:T(8,128)S(1)}, u32[]{:S(2)}, u32[]{:S(2)}) collective-permute-start(f32[80,384]{1,0:T(8,128)S(1)} %get-tuple-element.116), channel_id=1, source_target_pairs={{16,0},{17,1},{18,2},{19,3},{20,4},{21,5},{22,6},{23,7},{24,8},{25... | collective-permute-start | bytes 368648 | tf_op jit(solution)/shard_map/ppermute | solution.py:20

commit v10 on v9

--- a/solution.py
+++ b/solution.py
@@ -577,9 +577,15 @@
         pack(relay, None, ax, ay, 160)
 
 
+def halo_kernel(bx, by, out):
+    @pl.when(is_fine())
+    def _():
+        pack(out, None, bx, by, 0)
+
+
 def f3_kernel(
     e, h, p, coef, slab_coef, bx, by, desc, box_in, region, was, relay_in,
-    box, relay, fix_e, fix_h, fix_p, layer, one_e, one_h,
+    box, averaged, fix_e, fix_h, fix_p, layer, one_e, one_h,
 ):
     @pl.when(is_coarse())
     def _():
@@ -606,7 +612,7 @@
         fix = cut_region(layer, desc, (0, *spot[1:]))
         latest = [[region[2 * c + i] + fix[c][i] for i in range(2)] for c in range(3)]
         restricted = fine_steps(box_in, box, coef, desc, load_box(was), latest)
-        pack(relay, restricted, bx, by, 0)
+        store_box(averaged, restricted)
 
 
 def late_kernel(e, h, p, fix_e, fix_h, fix_p, coef, box, out, mixed):
@@ -628,17 +634,17 @@
                     out[c, x, :, pl.ds(128 * a, 128)] = mixed[c, x, a]
 
 
-def finish_kernel(late, coef, desc, relay, out):
+def finish_kernel(late, coef, desc, averaged, halos, out):
     @pl.when(is_coarse())
     def _():
         view_e, view_p = out.at[pl.ds(0, 3)], out.at[pl.ds(6, 3)]
         out[3:6] = late[3:6]
         complete(
             late.at[pl.ds(0, 3)], late.at[pl.ds(6, 3)], coef,
-            packed_x(relay, 16), packed_y(relay, 16), view_e, view_p,
+            packed_x(halos, 0), packed_y(halos, 0), view_e, view_p,
         )
         covered = [jnp.where(value, F32(1.0), 0.0) for value in covered_of(desc)]
-        put(view_e, packed_box(relay, 0), desc, corner(desc), covered)
+        put(view_e, lambda c, i: averaged[c, i], desc, corner(desc), covered)
 
     @pl.when(is_fine())
     def _():
@@ -773,24 +779,26 @@
         base_kernel, (e, h, p, slab_coef, bx, by, desc), [PART] * 2 + [(19, 8, 128)]
     )
     region = to_fine(sent)
-    box, relay4, *fix = call(
+    (halos,) = call(halo_kernel, (fine_bx, fine_by), [(64, 384)])
+    halos = to_coarse(halos)
+    box, averaged, *fix = call(
         f3_kernel,
         (e, h, p, fine_coef, slab_coef, fine_bx, fine_by, desc, box, region, now, relay),
-        [BOX, (80, 384)] + [PART] * 3,
+        [BOX, REGION] + [PART] * 3,
         scratch=[
             pltpu.VMEM((3, 2, 24, 384), F32),
             pltpu.VMEM(PART, F32),
             pltpu.VMEM(PART, F32),
         ],
     )
-    relay4 = to_coarse(relay4)
+    averaged = to_coarse(averaged)
     (late,) = call(
         late_kernel,
         (base_e, h, base_p, *fix, slab_coef, box),
         [SLAB],
         scratch=[pltpu.VMEM((9, 6, 3, 24, 128), F32)],
     )
-    (out,) = call(finish_kernel, (late, slab_coef, desc, relay4), [SLAB])
+    (out,) = call(finish_kernel, (late, slab_coef, desc, averaged, halos), [SLAB])
     return out[None]
 
 

time: 73.5 us -> 76.1 us (1.035)
  starting transfers between devices: 40.1 us -> 45.8 us
  waiting for transfers between devices: 23.9 us -> 20.7 us
    ppermute x6 -> x7, starting transfers between devices: 9.99 us -> 15.7 us  [shifted(): return lax.ppermute(value, axis, pairs)]
    ppermute x6 -> x7, waiting for transfers between devices: 10.4 us -> 7.83 us  [shifted(): return lax.ppermute(value, axis, pairs)]
    pallas_call x16 -> x17, Pallas kernels: 6.96 us -> 6.97 us  [call(): pl.pallas_call(kernel, out_shape=shapes, in_specs=specs or [VM] * len(ope...]
  transfers between devices with their start and end apart: 22 -> 23, of which waited for: 14 -> 14; matrix products, arithmetic and copies ran while one was open for 0% -> 0% of each run, Pallas kernels for 4% -> 5%
where the time goes in v10:
time: 76.1 us; the launch traced here: 75.5 us
  starting transfers between devices  45.8 us (60%)
  waiting for transfers between devices  20.7 us (27%)
  Pallas kernels  6.97 us (9%)
  local copies, waits for them, and re-layouts  1.58 us (2%)
    ppermute x8, starting transfers between devices, exchange(): lax.ppermute(x_edge, AXES, pairs(by, 0))  16.6 us
    ppermute x7, starting transfers between devices, shifted(): return lax.ppermute(value, axis, pairs)  15.7 us
    ppermute x8, starting transfers between devices, exchange(): lax.ppermute(y_edge, AXES, pairs(0, by))  13.5 us
    ppermute x7, waiting for transfers between devices, shifted(): return lax.ppermute(value, axis, pairs)  7.83 us
    ppermute x8, waiting for transfers between devices, exchange(): lax.ppermute(x_edge, AXES, pairs(by, 0))  7.17 us
    pallas_call x17, Pallas kernels, call(): pl.pallas_call(kernel, out_shape=shapes, in_specs=specs or [VM] * len(ope...  6.97 us
    ppermute x8, waiting for transfers between devices, exchange(): lax.ppermute(y_edge, AXES, pairs(0, by))  5.68 us
    unnamed x16, local copies, waits for them, and re-layouts  1.58 us
  transfers between devices with their start and end apart: 23, of which 14 were waited for; matrix products, arithmetic and copies ran while one was open for 0% of the time, Pallas kernels for 5%

profile of v10, /device:TPU:0, one launch (start us, length us, event | category | flops | bytes accessed | tf_op | source)
XLA Modules:
  0.0 75.5 jit_solution(10132242170588828777)
XLA Ops:
  0.0 1.6 %copy-done = f32[1,9,6,24,384]{4,3,2,1,0:T(8,128)S(1)} copy-done((f32[1,9,6,24,384]{4,3,2,1,0:T(8,128)S(1)}, f32[1,9,6,24,384]{4,3,2,1,0:T(8,128)}, u32[]{:S(2)}) %copy-start) | copy-done | bytes 1990680
  1.6 1.4 %collective-permute-start = (f32[2,24,384]{2,1,0:T(8,128)S(1)}, f32[2,24,384]{2,1,0:T(8,128)S(1)}, u32[]{:S(2)}, u32[]{:S(2)}) collective-permute-start(f32[2,24,384]{2,1,0:T(8,128)S(1)} %get-tuple-element.63), channel_id=1, source_target_pairs={{4,0},{5,1},{6,2},{7,3},{8,4},{9,5},{10,6},{11,7},{12,8},{13,9},{1... | collective-permute-start | bytes 221192 | tf_op jit(solution)/shard_map/ppermute | solution.py:696
  3.1 1.3 %collective-permute-start.1 = (f32[2,6,384]{2,1,0:T(8,128)S(1)}, f32[2,6,384]{2,1,0:T(8,128)S(1)}, u32[]{:S(2)}, u32[]{:S(2)}) collective-permute-start(f32[2,6,384]{2,1,0:T(8,128)S(1)} %get-tuple-element.64), channel_id=1, source_target_pairs={{1,0},{2,1},{3,2},{5,4},{6,5},{7,6},{9,8},{10,9},{11,10},{13,12},{... | collective-permute-start | bytes 55304 | tf_op jit(solution)/shard_map/ppermute | solution.py:697
  4.4 1.1 %shard_map.73 = (f32[3,6,24,384]{3,2,1,0:T(8,128)S(1)}, f32[3,6,24,384]{3,2,1,0:T(8,128)S(1)}, f32[3,6,24,384]{3,2,1,0:T(8,128)S(1)}, f32[5,6,9,8,128]{4,3,2,1,0...) custom-call(f32[1,9,6,24,384]{4,3,2,1,0:T(8,128)S(1)} %copy-done, s32[1,6,24,384]{3,2,1,0:T(8,128)S(1)} %copy-done.2, ...), custom_call_target="tpu_custom_call" | custom-call | tf_op jit(solution)/shard_map/pallas_call | solution.py:660
  5.6 0.6 collective-permute-done.1.ay
  6.1 2.9 %collective-permute-done.ax = f32[2,24,384]{2,1,0:T(8,128)S(1)} collective-permute-done((f32[2,24,384]{2,1,0:T(8,128)S(1)}, f32[2,24,384]{2,1,0:T(8,128)S(1)}, u32[]{:S(2)}, u32[]{:S(2)}) %collective-permute-start) | collective-permute-done | bytes 73760 | tf_op jit(solution)/shard_map/ppermute | solution.py:696
  9.0 0.3 shard_map.75
  9.3 1.3 %collective-permute-start.4 = (f32[7,24,384]{2,1,0:T(8,128)S(1)}, f32[7,24,384]{2,1,0:T(8,128)S(1)}, u32[]{:S(2)}, u32[]{:S(2)}) collective-permute-start(f32[7,24,384]{2,1,0:T(8,128)S(1)} %get-tuple-element.73), channel_id=1, source_target_pairs={{0,16},{1,17},{2,18},{3,19},{4,20},{5,21},{6,22},{7,23},{8,24},{9,... | collective-permute-start | bytes 774152 | tf_op jit(solution)/shard_map/ppermute | solution.py:20
  10.6 3.9 %collective-permute-start.2 = (f32[2,24,384]{2,1,0:T(8,128)S(1)}, f32[2,24,384]{2,1,0:T(8,128)S(1)}, u32[]{:S(2)}, u32[]{:S(2)}) collective-permute-start(f32[2,24,384]{2,1,0:T(8,128)S(1)} %get-tuple-element.71), channel_id=1, source_target_pairs={{0,4},{1,5},{2,6},{3,7},{4,8},{5,9},{6,10},{7,11},{8,12},{9,13},{1... | collective-permute-start | bytes 221192 | tf_op jit(solution)/shard_map/ppermute | solution.py:696
  14.6 2.8 %collective-permute-start.3 = (f32[2,6,384]{2,1,0:T(8,128)S(1)}, f32[2,6,384]{2,1,0:T(8,128)S(1)}, u32[]{:S(2)}, u32[]{:S(2)}) collective-permute-start(f32[2,6,384]{2,1,0:T(8,128)S(1)} %get-tuple-element.72), channel_id=1, source_target_pairs={{0,1},{1,2},{2,3},{4,5},{5,6},{6,7},{8,9},{9,10},{10,11},{12,13},{... | collective-permute-start | bytes 55304 | tf_op jit(solution)/shard_map/ppermute | solution.py:697
  17.4 0.4 shard_map.76
  17.8 0.4 collective-permute-done.3.by
  18.2 0.2 shard_map.77
  18.5 3.5 %collective-permute-start.5 = (f32[6,8,128]{2,1,0:T(8,128)S(1)}, f32[6,8,128]{2,1,0:T(8,128)S(1)}, u32[]{:S(2)}, u32[]{:S(2)}) collective-permute-start(f32[6,8,128]{2,1,0:T(8,128)S(1)} %get-tuple-element.80), channel_id=1, source_target_pairs={{0,16},{1,17},{2,18},{3,19},{4,20},{5,21},{6,22},{7,23},{8,24},{9,... | collective-permute-start | bytes 73736 | tf_op jit(solution)/shard_map/ppermute | solution.py:20
  22.1 1.3 %collective-permute-done.5.region = f32[6,8,128]{2,1,0:T(8,128)S(1)} collective-permute-done((f32[6,8,128]{2,1,0:T(8,128)S(1)}, f32[6,8,128]{2,1,0:T(8,128)S(1)}, u32[]{:S(2)}, u32[]{:S(2)}) %collective-permute-start.5) | collective-permute-done | bytes 24608 | tf_op jit(solution)/shard_map/ppermute | solution.py:20
  23.6 1.3 %collective-permute-start.6 = (f32[2,24,384]{2,1,0:T(8,128)S(1)}, f32[2,24,384]{2,1,0:T(8,128)S(1)}, u32[]{:S(2)}, u32[]{:S(2)}) collective-permute-start(f32[2,24,384]{2,1,0:T(8,128)S(1)} %get-tuple-element.83), channel_id=1, source_target_pairs={{4,0},{5,1},{6,2},{7,3},{8,4},{9,5},{10,6},{11,7},{12,8},{13,9},{1... | collective-permute-start | bytes 221192 | tf_op jit(solution)/shard_map/ppermute | solution.py:696
  24.9 1.3 %collective-permute-start.7 = (f32[2,6,384]{2,1,0:T(8,128)S(1)}, f32[2,6,384]{2,1,0:T(8,128)S(1)}, u32[]{:S(2)}, u32[]{:S(2)}) collective-permute-start(f32[2,6,384]{2,1,0:T(8,128)S(1)} %get-tuple-element.84), channel_id=1, source_target_pairs={{1,0},{2,1},{3,2},{5,4},{6,5},{7,6},{9,8},{10,9},{11,10},{13,12},{... | collective-permute-start | bytes 55304 | tf_op jit(solution)/shard_map/ppermute | solution.py:697
  26.2 1.8 %collective-permute-done.7.ay.ay2 = f32[2,6,384]{2,1,0:T(8,128)S(1)} collective-permute-done((f32[2,6,384]{2,1,0:T(8,128)S(1)}, f32[2,6,384]{2,1,0:T(8,128)S(1)}, u32[]{:S(2)}, u32[]{:S(2)}) %collective-permute-start.7) | collective-permute-done | bytes 18464 | tf_op jit(solution)/shard_map/ppermute | solution.py:697
  28.0 1.9 %collective-permute-done.6.ax.ax2 = f32[2,24,384]{2,1,0:T(8,128)S(1)} collective-permute-done((f32[2,24,384]{2,1,0:T(8,128)S(1)}, f32[2,24,384]{2,1,0:T(8,128)S(1)}, u32[]{:S(2)}, u32[]{:S(2)}) %collective-permute-start.6) | collective-permute-done | bytes 73760 | tf_op jit(solution)/shard_map/ppermute | solution.py:696
  29.9 0.2 shard_map.80
  30.1 3.7 %collective-permute-start.8 = (f32[2,24,384]{2,1,0:T(8,128)S(1)}, f32[2,24,384]{2,1,0:T(8,128)S(1)}, u32[]{:S(2)}, u32[]{:S(2)}) collective-permute-start(f32[2,24,384]{2,1,0:T(8,128)S(1)} %get-tuple-element.90), channel_id=1, source_target_pairs={{0,4},{1,5},{2,6},{3,7},{4,8},{5,9},{6,10},{7,11},{8,12},{9,13},{1... | collective-permute-start | bytes 221192 | tf_op jit(solution)/shard_map/ppermute | solution.py:696
  33.8 1.9 %collective-permute-start.9 = (f32[2,6,384]{2,1,0:T(8,128)S(1)}, f32[2,6,384]{2,1,0:T(8,128)S(1)}, u32[]{:S(2)}, u32[]{:S(2)}) collective-permute-start(f32[2,6,384]{2,1,0:T(8,128)S(1)} %get-tuple-element.91), channel_id=1, source_target_pairs={{0,1},{1,2},{2,3},{4,5},{5,6},{6,7},{8,9},{9,10},{10,11},{12,13},{... | collective-permute-start | bytes 55304 | tf_op jit(solution)/shard_map/ppermute | solution.py:697
  35.7 0.8 %collective-permute-done.9.by = f32[2,6,384]{2,1,0:T(8,128)S(1)} collective-permute-done((f32[2,6,384]{2,1,0:T(8,128)S(1)}, f32[2,6,384]{2,1,0:T(8,128)S(1)}, u32[]{:S(2)}, u32[]{:S(2)}) %collective-permute-start.9) | collective-permute-done | bytes 18464 | tf_op jit(solution)/shard_map/ppermute | solution.py:697
  36.5 0.5 shard_map.82
  37.1 1.3 %collective-permute-start.12 = (f32[19,8,128]{2,1,0:T(8,128)S(1)}, f32[19,8,128]{2,1,0:T(8,128)S(1)}, u32[]{:S(2)}, u32[]{:S(2)}) collective-permute-start(f32[19,8,128]{2,1,0:T(8,128)S(1)} %get-tuple-element.95), channel_id=1, source_target_pairs={{0,16},{1,17},{2,18},{3,19},{4,20},{5,21},{6,22},{7,23},{8,24},{9,... | collective-permute-start | bytes 233480 | tf_op jit(solution)/shard_map/ppermute | solution.py:20
  38.4 0.7 collective-permute-start.10
  39.0 0.7 collective-permute-start.11
  39.7 0.9 %collective-permute-done.12.region = f32[19,8,128]{2,1,0:T(8,128)S(1)} collective-permute-done((f32[19,8,128]{2,1,0:T(8,128)S(1)}, f32[19,8,128]{2,1,0:T(8,128)S(1)}, u32[]{:S(2)}, u32[]{:S(2)}) %collective-permute-start.12) | collective-permute-done | bytes 77856 | tf_op jit(solution)/shard_map/ppermute | solution.py:20
  40.7 1.3 %collective-permute-start.13 = (f32[2,24,384]{2,1,0:T(8,128)S(1)}, f32[2,24,384]{2,1,0:T(8,128)S(1)}, u32[]{:S(2)}, u32[]{:S(2)}) collective-permute-start(f32[2,24,384]{2,1,0:T(8,128)S(1)} %get-tuple-element.98), channel_id=1, source_target_pairs={{4,0},{5,1},{6,2},{7,3},{8,4},{9,5},{10,6},{11,7},{12,8},{13,9},{1... | collective-permute-start | bytes 221192 | tf_op jit(solution)/shard_map/ppermute | solution.py:696
  42.0 1.3 %collective-permute-start.14 = (f32[2,6,384]{2,1,0:T(8,128)S(1)}, f32[2,6,384]{2,1,0:T(8,128)S(1)}, u32[]{:S(2)}, u32[]{:S(2)}) collective-permute-start(f32[2,6,384]{2,1,0:T(8,128)S(1)} %get-tuple-element.99), channel_id=1, source_target_pairs={{1,0},{2,1},{3,2},{5,4},{6,5},{7,6},{9,8},{10,9},{11,10},{13,12},{... | collective-permute-start | bytes 55304 | tf_op jit(solution)/shard_map/ppermute | solution.py:697
  43.3 1.9 %collective-permute-done.14.ay = f32[2,6,384]{2,1,0:T(8,128)S(1)} collective-permute-done((f32[2,6,384]{2,1,0:T(8,128)S(1)}, f32[2,6,384]{2,1,0:T(8,128)S(1)}, u32[]{:S(2)}, u32[]{:S(2)}) %collective-permute-start.14) | collective-permute-done | bytes 18464 | tf_op jit(solution)/shard_map/ppermute | solution.py:697
  45.2 2.4 %collective-permute-done.13.ax = f32[2,24,384]{2,1,0:T(8,128)S(1)} collective-permute-done((f32[2,24,384]{2,1,0:T(8,128)S(1)}, f32[2,24,384]{2,1,0:T(8,128)S(1)}, u32[]{:S(2)}, u32[]{:S(2)}) %collective-permute-start.13) | collective-permute-done | bytes 73760 | tf_op jit(solution)/shard_map/ppermute | solution.py:696
  47.6 0.2 shard_map.84
  47.9 1.3 %collective-permute-start.20 = (f32[224,384]{1,0:T(8,128)S(1)}, f32[224,384]{1,0:T(8,128)S(1)}, u32[]{:S(2)}, u32[]{:S(2)}) collective-permute-start(f32[224,384]{1,0:T(8,128)S(1)} %get-tuple-element.111), channel_id=1, source_target_pairs={{16,0},{17,1},{18,2},{19,3},{20,4},{21,5},{22,6},{23,7},{24,8},{25... | collective-permute-start | bytes 1032200 | tf_op jit(solution)/shard_map/ppermute | solution.py:20
  49.2 3.6 %collective-permute-start.15 = (f32[2,24,384]{2,1,0:T(8,128)S(1)}, f32[2,24,384]{2,1,0:T(8,128)S(1)}, u32[]{:S(2)}, u32[]{:S(2)}) collective-permute-start(f32[2,24,384]{2,1,0:T(8,128)S(1)} %get-tuple-element.104), channel_id=1, source_target_pairs={{0,4},{1,5},{2,6},{3,7},{4,8},{5,9},{6,10},{7,11},{8,12},{9,13},{1... | collective-permute-start | bytes 221192 | tf_op jit(solution)/shard_map/ppermute | solution.py:696
  52.8 0.7 collective-permute-start.17
  53.5 3.6 %collective-permute-start.16 = (f32[2,6,384]{2,1,0:T(8,128)S(1)}, f32[2,6,384]{2,1,0:T(8,128)S(1)}, u32[]{:S(2)}, u32[]{:S(2)}) collective-permute-start(f32[2,6,384]{2,1,0:T(8,128)S(1)} %get-tuple-element.105), channel_id=1, source_target_pairs={{0,1},{1,2},{2,3},{4,5},{5,6},{6,7},{8,9},{9,10},{10,11},{12,13},{... | collective-permute-start | bytes 55304 | tf_op jit(solution)/shard_map/ppermute | solution.py:697
  57.1 0.7 collective-permute-start.18
  57.9 0.5 shard_map.85
  58.5 5.8 %collective-permute-start.19 = (f32[19,8,128]{2,1,0:T(8,128)S(1)}, f32[19,8,128]{2,1,0:T(8,128)S(1)}, u32[]{:S(2)}, u32[]{:S(2)}) collective-permute-start(f32[19,8,128]{2,1,0:T(8,128)S(1)} %get-tuple-element.109), channel_id=1, source_target_pairs={{0,16},{1,17},{2,18},{3,19},{4,20},{5,21},{6,22},{7,23},{8,24},{9,... | collective-permute-start | bytes 233480 | tf_op jit(solution)/shard_map/ppermute | solution.py:20
  64.3 1.3 %collective-permute-start.22 = (f32[64,384]{1,0:T(8,128)S(1)}, f32[64,384]{1,0:T(8,128)S(1)}, u32[]{:S(2)}, u32[]{:S(2)}) collective-permute-start(f32[64,384]{1,0:T(8,128)S(1)} %shard_map.88), channel_id=1, source_target_pairs={{16,0},{17,1},{18,2},{19,3},{20,4},{21,5},{22,6},{23,7},{24,8},{25... | collective-permute-start | bytes 294920 | tf_op jit(solution)/shard_map/ppermute | solution.py:20
  65.6 1.2 %collective-permute-done.19.region = f32[19,8,128]{2,1,0:T(8,128)S(1)} collective-permute-done((f32[19,8,128]{2,1,0:T(8,128)S(1)}, f32[19,8,128]{2,1,0:T(8,128)S(1)}, u32[]{:S(2)}, u32[]{:S(2)}) %collective-permute-start.19) | collective-permute-done | bytes 77856 | tf_op jit(solution)/shard_map/ppermute | solution.py:20
  66.8 0.8 %shard_map.86 = (f32[9,6,9,8,128]{4,3,2,1,0:T(8,128)S(1)}, f32[3,2,8,128]{3,2,1,0:T(8,128)S(1)}, f32[3,6,24,384]{3,2,1,0:T(8,128)S(1)}, f32[3,6,24,384]{3,2,1,0:T(8,128)S(1)}, f32[3,6,24,384]{3,2,1,0:T(8,128)S(1)}) custom-call(f32[3,6,24,384]{3,2,1,0:T(8,128)S(1)} %get-tuple-element.97.e, f32[3,6,24,384]{3,2,1,0:T(8,128)S(1)} %get-tuple-element.102.h, ...), custom_call_target="tpu_custom_call" | custom-call | tf_op jit(solution)/shard_map/pallas_call | solution.py:660
  67.6 1.3 %collective-permute-start.21 = (f32[3,2,8,128]{3,2,1,0:T(8,128)S(1)}, f32[3,2,8,128]{3,2,1,0:T(8,128)S(1)}, u32[]{:S(2)}, u32[]{:S(2)}) collective-permute-start(f32[3,2,8,128]{3,2,1,0:T(8,128)S(1)} %get-tuple-element.116), channel_id=1, source_target_pairs={{16,0},{17,1},{18,2},{19,3},{20,4},{21,5},{22,6},{23,7},{24,8},{25... | collective-permute-start | bytes 73736 | tf_op jit(solution)/shard_map/ppermute | solution.py:20
  68.9 0.6 shard_map.87.late
  69.5 1.9 %collective-permute-done.22.halos = f32[64,384]{1,0:T(8,128)S(1)} collective-permute-done((f32[64,384]{1,0:T(8,128)S(1)}, f32[64,384]{1,0:T(8,128)S(1)}, u32[]{:S(2)}, u32[]{:S(2)}) %collective-permute-start.22) | collective-permute-done | bytes 98336 | tf_op jit(solution)/shard_map/ppermute | solution.py:20
  71.3 2.6 %collective-permute-done.21.averaged = f32[3,2,8,128]{3,2,1,0:T(8,128)S(1)} collective-permute-done((f32[3,2,8,128]{3,2,1,0:T(8,128)S(1)}, f32[3,2,8,128]{3,2,1,0:T(8,128)S(1)}, u32[]{:S(2)}, u32[]{:S(2)}) %collective-permute-start.21) | collective-permute-done | bytes 24608 | tf_op jit(solution)/shard_map/ppermute | solution.py:20
  74.0 1.5 %shard_map.89 = f32[9,6,24,384]{3,2,1,0:T(8,128)} custom-call(f32[9,6,24,384]{3,2,1,0:T(8,128)S(1)} %shard_map.87.late, f32[5,6,9,8,128]{4,3,2,1,0:T(8,128)S(1)} %get-tuple-element.87.coef.slab_coef, s32[6,8,128]{2,1,0:T(8,128)S(1)} %get-tuple-element.65.desc, f32[3,2,8,128]{3,2,1,0:T(8,128)S(1)} %collective-permute-done.21.averaged, ...), custom_call_target="tpu_custom_call" | custom-call | tf_op jit(solution)/shard_map/pallas_call | solution.py:660
  (31 shorter events, 0.7 us)
Async XLA Ops:
  0.0 1.6 %copy-start = (f32[1,9,6,24,384]{4,3,2,1,0:T(8,128)S(1)}, f32[1,9,6,24,384]{4,3,2,1,0:T(8,128)}, u32[]{:S(2)}) copy-start(f32[1,9,6,24,384]{4,3,2,1,0:T(8,128)} %f2.1) | copy-start | bytes 5971972
  1.6 2.8 %copy-start.2 = (s32[1,6,24,384]{3,2,1,0:T(8,128)S(1)}, s32[1,6,24,384]{3,2,1,0:T(8,128)}, u32[]{:S(2)}) copy-start(s32[1,6,24,384]{3,2,1,0:T(8,128)} %m2.1) | copy-start | bytes 663556
  1.6 2.8 %copy-start.3 = (f32[8]{0:T(128)S(1)}, f32[8]{0:T(128)}, u32[]{:S(2)}) copy-start(f32[8]{0:T(128)} %perm.1) | copy-start | bytes 100
  1.6 2.8 %copy-start.4 = (f32[8]{0:T(128)S(1)}, f32[8]{0:T(128)}, u32[]{:S(2)}) copy-start(f32[8]{0:T(128)} %cond.1) | copy-start | bytes 100
  1.6 2.8 %copy-start.5 = (f32[8]{0:T(128)S(1)}, f32[8]{0:T(128)}, u32[]{:S(2)}) copy-start(f32[8]{0:T(128)} %relax.1) | copy-start | bytes 100
  1.6 2.8 %copy-start.6 = (f32[8]{0:T(128)S(1)}, f32[8]{0:T(128)}, u32[]{:S(2)}) copy-start(f32[8]{0:T(128)} %debye.1) | copy-start | bytes 100
  1.6 2.8 %copy-start.7 = (s32[1,1,6]{2,1,0:T(1,128)S(1)}, s32[1,1,6]{2,1,0:T(1,128)}, u32[]{:S(2)}) copy-start(s32[1,1,6]{2,1,0:T(1,128)} %sub.1) | copy-start | bytes 76
  1.6 7.4 %collective-permute-start = (f32[2,24,384]{2,1,0:T(8,128)S(1)}, f32[2,24,384]{2,1,0:T(8,128)S(1)}, u32[]{:S(2)}, u32[]{:S(2)}) collective-permute-start(f32[2,24,384]{2,1,0:T(8,128)S(1)} %get-tuple-element.63), channel_id=1, source_target_pairs={{4,0},{5,1},{6,2},{7,3},{8,4},{9,5},{10,6},{11,7},{12,8},{13,9},{1... | collective-permute-start | bytes 221192 | tf_op jit(solution)/shard_map/ppermute | solution.py:696
  3.1 3.1 %collective-permute-start.1 = (f32[2,6,384]{2,1,0:T(8,128)S(1)}, f32[2,6,384]{2,1,0:T(8,128)S(1)}, u32[]{:S(2)}, u32[]{:S(2)}) collective-permute-start(f32[2,6,384]{2,1,0:T(8,128)S(1)} %get-tuple-element.64), channel_id=1, source_target_pairs={{1,0},{2,1},{3,2},{5,4},{6,5},{7,6},{9,8},{10,9},{11,10},{13,12},{... | collective-permute-start | bytes 55304 | tf_op jit(solution)/shard_map/ppermute | solution.py:697
  9.3 8.9 %collective-permute-start.4 = (f32[7,24,384]{2,1,0:T(8,128)S(1)}, f32[7,24,384]{2,1,0:T(8,128)S(1)}, u32[]{:S(2)}, u32[]{:S(2)}) collective-permute-start(f32[7,24,384]{2,1,0:T(8,128)S(1)} %get-tuple-element.73), channel_id=1, source_target_pairs={{0,16},{1,17},{2,18},{3,19},{4,20},{5,21},{6,22},{7,23},{8,24},{9,... | collective-permute-start | bytes 774152 | tf_op jit(solution)/shard_map/ppermute | solution.py:20
  10.6 7.6 %collective-permute-start.2 = (f32[2,24,384]{2,1,0:T(8,128)S(1)}, f32[2,24,384]{2,1,0:T(8,128)S(1)}, u32[]{:S(2)}, u32[]{:S(2)}) collective-permute-start(f32[2,24,384]{2,1,0:T(8,128)S(1)} %get-tuple-element.71), channel_id=1, source_target_pairs={{0,4},{1,5},{2,6},{3,7},{4,8},{5,9},{6,10},{7,11},{8,12},{9,13},{1... | collective-permute-start | bytes 221192 | tf_op jit(solution)/shard_map/ppermute | solution.py:696
  14.6 3.6 %collective-permute-start.3 = (f32[2,6,384]{2,1,0:T(8,128)S(1)}, f32[2,6,384]{2,1,0:T(8,128)S(1)}, u32[]{:S(2)}, u32[]{:S(2)}) collective-permute-start(f32[2,6,384]{2,1,0:T(8,128)S(1)} %get-tuple-element.72), channel_id=1, source_target_pairs={{0,1},{1,2},{2,3},{4,5},{5,6},{6,7},{8,9},{9,10},{10,11},{12,13},{... | collective-permute-start | bytes 55304 | tf_op jit(solution)/shard_map/ppermute | solution.py:697
  17.8 4.2 %copy-start.1 = (f32[1,9,6,24,384]{4,3,2,1,0:T(8,128)S(1)}, f32[1,9,6,24,384]{4,3,2,1,0:T(8,128)}, u32[]{:S(2)}) copy-start(f32[1,9,6,24,384]{4,3,2,1,0:T(8,128)} %f2.1) | copy-start | bytes 5971972
  18.5 5.0 %collective-permute-start.5 = (f32[6,8,128]{2,1,0:T(8,128)S(1)}, f32[6,8,128]{2,1,0:T(8,128)S(1)}, u32[]{:S(2)}, u32[]{:S(2)}) collective-permute-start(f32[6,8,128]{2,1,0:T(8,128)S(1)} %get-tuple-element.80), channel_id=1, source_target_pairs={{0,16},{1,17},{2,18},{3,19},{4,20},{5,21},{6,22},{7,23},{8,24},{9,... | collective-permute-start | bytes 73736 | tf_op jit(solution)/shard_map/ppermute | solution.py:20
  23.6 6.2 %collective-permute-start.6 = (f32[2,24,384]{2,1,0:T(8,128)S(1)}, f32[2,24,384]{2,1,0:T(8,128)S(1)}, u32[]{:S(2)}, u32[]{:S(2)}) collective-permute-start(f32[2,24,384]{2,1,0:T(8,128)S(1)} %get-tuple-element.83), channel_id=1, source_target_pairs={{4,0},{5,1},{6,2},{7,3},{8,4},{9,5},{10,6},{11,7},{12,8},{13,9},{1... | collective-permute-start | bytes 221192 | tf_op jit(solution)/shard_map/ppermute | solution.py:696
  24.9 3.1 %collective-permute-start.7 = (f32[2,6,384]{2,1,0:T(8,128)S(1)}, f32[2,6,384]{2,1,0:T(8,128)S(1)}, u32[]{:S(2)}, u32[]{:S(2)}) collective-permute-start(f32[2,6,384]{2,1,0:T(8,128)S(1)} %get-tuple-element.84), channel_id=1, source_target_pairs={{1,0},{2,1},{3,2},{5,4},{6,5},{7,6},{9,8},{10,9},{11,10},{13,12},{... | collective-permute-start | bytes 55304 | tf_op jit(solution)/shard_map/ppermute | solution.py:697
  30.1 6.4 %collective-permute-start.8 = (f32[2,24,384]{2,1,0:T(8,128)S(1)}, f32[2,24,384]{2,1,0:T(8,128)S(1)}, u32[]{:S(2)}, u32[]{:S(2)}) collective-permute-start(f32[2,24,384]{2,1,0:T(8,128)S(1)} %get-tuple-element.90), channel_id=1, source_target_pairs={{0,4},{1,5},{2,6},{3,7},{4,8},{5,9},{6,10},{7,11},{8,12},{9,13},{1... | collective-permute-start | bytes 221192 | tf_op jit(solution)/shard_map/ppermute | solution.py:696
  33.8 2.7 %collective-permute-start.9 = (f32[2,6,384]{2,1,0:T(8,128)S(1)}, f32[2,6,384]{2,1,0:T(8,128)S(1)}, u32[]{:S(2)}, u32[]{:S(2)}) collective-permute-start(f32[2,6,384]{2,1,0:T(8,128)S(1)} %get-tuple-element.91), channel_id=1, source_target_pairs={{0,1},{1,2},{2,3},{4,5},{5,6},{6,7},{8,9},{9,10},{10,11},{12,13},{... | collective-permute-start | bytes 55304 | tf_op jit(solution)/shard_map/ppermute | solution.py:697
  37.1 3.6 %collective-permute-start.12 = (f32[19,8,128]{2,1,0:T(8,128)S(1)}, f32[19,8,128]{2,1,0:T(8,128)S(1)}, u32[]{:S(2)}, u32[]{:S(2)}) collective-permute-start(f32[19,8,128]{2,1,0:T(8,128)S(1)} %get-tuple-element.95), channel_id=1, source_target_pairs={{0,16},{1,17},{2,18},{3,19},{4,20},{5,21},{6,22},{7,23},{8,24},{9,... | collective-permute-start | bytes 233480 | tf_op jit(solution)/shard_map/ppermute | solution.py:20
  38.4 1.4 %collective-permute-start.10 = (f32[2,24,384]{2,1,0:T(8,128)S(1)}, f32[2,24,384]{2,1,0:T(8,128)S(1)}, u32[]{:S(2)}, u32[]{:S(2)}) collective-permute-start(f32[2,24,384]{2,1,0:T(8,128)S(1)} %get-tuple-element.90), channel_id=1, source_target_pairs={{16,20},{17,21},{18,22},{19,23},{20,24},{21,25},{22,26},{23,27},{2... | collective-permute-start | bytes 221192 | tf_op jit(solution)/shard_map/ppermute | solution.py:696
  39.0 0.7 collective-permute-start.11
  40.7 6.9 %collective-permute-start.13 = (f32[2,24,384]{2,1,0:T(8,128)S(1)}, f32[2,24,384]{2,1,0:T(8,128)S(1)}, u32[]{:S(2)}, u32[]{:S(2)}) collective-permute-start(f32[2,24,384]{2,1,0:T(8,128)S(1)} %get-tuple-element.98), channel_id=1, source_target_pairs={{4,0},{5,1},{6,2},{7,3},{8,4},{9,5},{10,6},{11,7},{12,8},{13,9},{1... | collective-permute-start | bytes 221192 | tf_op jit(solution)/shard_map/ppermute | solution.py:696
  42.0 3.2 %collective-permute-start.14 = (f32[2,6,384]{2,1,0:T(8,128)S(1)}, f32[2,6,384]{2,1,0:T(8,128)S(1)}, u32[]{:S(2)}, u32[]{:S(2)}) collective-permute-start(f32[2,6,384]{2,1,0:T(8,128)S(1)} %get-tuple-element.99), channel_id=1, source_target_pairs={{1,0},{2,1},{3,2},{5,4},{6,5},{7,6},{9,8},{10,9},{11,10},{13,12},{... | collective-permute-start | bytes 55304 | tf_op jit(solution)/shard_map/ppermute | solution.py:697
  47.9 18.9 %collective-permute-start.20 = (f32[224,384]{1,0:T(8,128)S(1)}, f32[224,384]{1,0:T(8,128)S(1)}, u32[]{:S(2)}, u32[]{:S(2)}) collective-permute-start(f32[224,384]{1,0:T(8,128)S(1)} %get-tuple-element.111), channel_id=1, source_target_pairs={{16,0},{17,1},{18,2},{19,3},{20,4},{21,5},{22,6},{23,7},{24,8},{25... | collective-permute-start | bytes 1032200 | tf_op jit(solution)/shard_map/ppermute | solution.py:20
  49.2 8.8 %collective-permute-start.15 = (f32[2,24,384]{2,1,0:T(8,128)S(1)}, f32[2,24,384]{2,1,0:T(8,128)S(1)}, u32[]{:S(2)}, u32[]{:S(2)}) collective-permute-start(f32[2,24,384]{2,1,0:T(8,128)S(1)} %get-tuple-element.104), channel_id=1, source_target_pairs={{0,4},{1,5},{2,6},{3,7},{4,8},{5,9},{6,10},{7,11},{8,12},{9,13},{1... | collective-permute-start | bytes 221192 | tf_op jit(solution)/shard_map/ppermute | solution.py:696
  52.8 11.4 %collective-permute-start.17 = (f32[2,24,384]{2,1,0:T(8,128)S(1)}, f32[2,24,384]{2,1,0:T(8,128)S(1)}, u32[]{:S(2)}, u32[]{:S(2)}) collective-permute-start(f32[2,24,384]{2,1,0:T(8,128)S(1)} %get-tuple-element.104), channel_id=1, source_target_pairs={{16,20},{17,21},{18,22},{19,23},{20,24},{21,25},{22,26},{23,27},{2... | collective-permute-start | bytes 221192 | tf_op jit(solution)/shard_map/ppermute | solution.py:696
  53.5 4.4 %collective-permute-start.16 = (f32[2,6,384]{2,1,0:T(8,128)S(1)}, f32[2,6,384]{2,1,0:T(8,128)S(1)}, u32[]{:S(2)}, u32[]{:S(2)}) collective-permute-start(f32[2,6,384]{2,1,0:T(8,128)S(1)} %get-tuple-element.105), channel_id=1, source_target_pairs={{0,1},{1,2},{2,3},{4,5},{5,6},{6,7},{8,9},{9,10},{10,11},{12,13},{... | collective-permute-start | bytes 55304 | tf_op jit(solution)/shard_map/ppermute | solution.py:697
  57.1 7.1 %collective-permute-start.18 = (f32[2,6,384]{2,1,0:T(8,128)S(1)}, f32[2,6,384]{2,1,0:T(8,128)S(1)}, u32[]{:S(2)}, u32[]{:S(2)}) collective-permute-start(f32[2,6,384]{2,1,0:T(8,128)S(1)} %get-tuple-element.105), channel_id=1, source_target_pairs={{16,17},{17,18},{18,19},{20,21},{21,22},{22,23},{24,25},{25,26},{2... | collective-permute-start | bytes 55304 | tf_op jit(solution)/shard_map/ppermute | solution.py:697
  58.5 8.3 %collective-permute-start.19 = (f32[19,8,128]{2,1,0:T(8,128)S(1)}, f32[19,8,128]{2,1,0:T(8,128)S(1)}, u32[]{:S(2)}, u32[]{:S(2)}) collective-permute-start(f32[19,8,128]{2,1,0:T(8,128)S(1)} %get-tuple-element.109), channel_id=1, source_target_pairs={{0,16},{1,17},{2,18},{3,19},{4,20},{5,21},{6,22},{7,23},{8,24},{9,... | collective-permute-start | bytes 233480 | tf_op jit(solution)/shard_map/ppermute | solution.py:20
  64.3 7.1 %collective-permute-start.22 = (f32[64,384]{1,0:T(8,128)S(1)}, f32[64,384]{1,0:T(8,128)S(1)}, u32[]{:S(2)}, u32[]{:S(2)}) collective-permute-start(f32[64,384]{1,0:T(8,128)S(1)} %shard_map.88), channel_id=1, source_target_pairs={{16,0},{17,1},{18,2},{19,3},{20,4},{21,5},{22,6},{23,7},{24,8},{25... | collective-permute-start | bytes 294920 | tf_op jit(solution)/shard_map/ppermute | solution.py:20
  67.6 6.4 %collective-permute-start.21 = (f32[3,2,8,128]{3,2,1,0:T(8,128)S(1)}, f32[3,2,8,128]{3,2,1,0:T(8,128)S(1)}, u32[]{:S(2)}, u32[]{:S(2)}) collective-permute-start(f32[3,2,8,128]{3,2,1,0:T(8,128)S(1)} %get-tuple-element.116), channel_id=1, source_target_pairs={{16,0},{17,1},{18,2},{19,3},{20,4},{21,5},{22,6},{23,7},{24,8},{25... | collective-permute-start | bytes 73736 | tf_op jit(solution)/shard_map/ppermute | solution.py:20
